TPU v7x, 32 devices: a whole 2x2x4 slice. The times are simulated.
32 devices in a mesh: dp: 2 (over core), expert: 4 (over y, x), blk: 4 (over z).
Axes of the slice: x: 2, y: 2, z: 4, core: 2. Of those that a mesh axis runs over, the one named last changes fastest.
Arguments:
- tokens: bfloat16 [256, 6144], P('dp', 'blk'), may hold values from -6 to 6
- expert_ids: int32 [256, 2], P('dp'), may hold values from 0 to 7, all different within a row; in each aligned block of 128 rows (0 to 127, 128 to 255, ...) at most 48 rows name the same one
- route_weights: float32 [256, 2], P('dp'), may hold values from 0.1 to 1
- gate_weight: bfloat16 [8, 6144, 8192], P('expert', 'blk', 'dp'), may hold values from -0.078125 to 0.078125
- up_weight: bfloat16 [8, 6144, 8192], P('expert', 'blk', 'dp'), may hold values from -0.078125 to 0.078125
- down_weight: bfloat16 [8, 8192, 6144], P('expert', 'dp', 'blk'), may hold values from -0.0625 to 0.0625
Outputs:
- mixed: bfloat16 [256, 6144], P('dp', 'blk')
Inputs may be any that keep to these rules, and one draw needn't show every extreme that they name: `expert_ids`: each row names 2 different experts. Among the 128 rows of one data shard no expert is named more than 48 times, and in every draw some expert is named exactly 48 times in some shard.
All inputs are finite; a program needn't handle non-finite values.
Results may differ from a plain program's by a relative error of at most 0.0051.
Values may be sent and summed in bfloat16 or wider, within the bound.
No kernel may reach another device: no remote copies, remote signals or barrier semaphores. Data moves between devices by JAX's collectives and lax.ppermute only.
A program may use at most 128 MiB of HBM per device.

v0:
```python
import jax
import jax.numpy as jnp
from jax import lax
from jax.sharding import PartitionSpec as P

EXPERTS = 8
CAP = 48


def local(tokens, expert_ids, route_weights, gate_weight, up_weight, down_weight):
    local_count = gate_weight.shape[0]
    token_count = tokens.shape[0]
    top_count = expert_ids.shape[1]
    group_index = lax.axis_index("expert")
    flat_ids = expert_ids.reshape(-1)
    one_hot = (flat_ids[:, None] == jnp.arange(EXPERTS, dtype=jnp.int32)[None, :]).astype(jnp.int32)
    before = jnp.cumsum(one_hot, axis=0) - one_hot
    position = jnp.sum(before * one_hot, axis=1)
    local_ids = flat_ids - group_index * local_count
    is_mine = local_ids[:, None] == jnp.arange(local_count, dtype=jnp.int32)[None, :]
    in_slot = position[:, None] == jnp.arange(CAP, dtype=jnp.int32)[None, :]
    slot_hit = (is_mine[:, :, None] & in_slot[:, None, :]).reshape(
        token_count, top_count, local_count, CAP
    )
    dispatch = jnp.any(slot_hit, axis=1).astype(jnp.bfloat16)
    combine = jnp.sum(slot_hit.astype(jnp.float32) * route_weights[:, :, None, None], axis=1)
    picked = jnp.einsum("tec,tf->ecf", dispatch, tokens, preferred_element_type=jnp.float32).astype(
        jnp.bfloat16
    )
    shard_rows = lax.all_gather(picked, "dp", axis=1, tiled=True)
    gate_part = jnp.einsum(
        "enf,efh->enh", shard_rows, gate_weight, preferred_element_type=jnp.float32
    )
    up_part = jnp.einsum("enf,efh->enh", shard_rows, up_weight, preferred_element_type=jnp.float32)
    partial_value = jnp.stack([gate_part, up_part])
    summed = lax.psum(partial_value, "blk")
    hidden = (jax.nn.silu(summed[0]) * summed[1]).astype(jnp.bfloat16)
    expert_out = lax.psum_scatter(
        jnp.einsum("enh,ehd->ned", hidden, down_weight, preferred_element_type=jnp.float32),
        "dp",
        scatter_dimension=0,
        tiled=True,
    )
    mixed_part = jnp.einsum("tec,ced->td", combine, expert_out, precision=lax.Precision.HIGHEST)
    mixed = lax.psum(mixed_part, "expert")
    return mixed.astype(jnp.bfloat16)


def solution(mesh):
    placed = (
        P("dp", "blk"),
        P("dp", None),
        P("dp", None),
        P("expert", "blk", "dp"),
        P("expert", "blk", "dp"),
        P("expert", "dp", "blk"),
    )
    return jax.shard_map(
        local, mesh=mesh, in_specs=placed, out_specs=P("dp", "blk"), check_vma=False
    )
```

profile of v0, /device:TPU:0, one launch (start us, length us, event | category | flops | bytes accessed | tf_op | source)
XLA Modules:
  0.0 328.6 jit_solution(11125822579298977786)
XLA Ops:
  6.5 0.0 copy-start
  6.5 0.0 all-reduce.3.cloned.1.call-start
  6.5 0.8 copy.13
  7.4 0.1 eq.65
  7.5 0.1 reshape.70
  7.7 0.6 reduce-window.6
  8.3 0.2 slice_reduce_fusion
  8.5 0.1 fusion.7
  8.6 0.1 eq.69
  8.8 0.1 copy.15
  8.9 0.7 broadcast_subtract_fusion
  9.6 0.0 copy-done
  9.6 0.2 convolution_convert_fusion
  9.8 2.3 all_gather.3
  12.1 10.4 %convolution_bitcast_fusion = f32[1,2,96,4096]{3,2,1,0:T(8,128)S(1)} fusion(bf16[2,96,1536]{2,1,0:T(8,128)(2,1)S(1)} %all_gather.3, bf16[2,1536,4096]{2,1,0:T(8,128)(2,1)} %param.10), kind=kOutput, calls=%fused_computation.1 | convolution fusion | flops 2415919104 | bytes 28901376 | tf_op jit(solution)/shard_map/enf,efh->enh/dot_general | solution.py:34
  22.5 10.4 %convolution_bitcast_fusion.1 = f32[1,2,96,4096]{3,2,1,0:T(8,128)S(1)} fusion(bf16[2,96,1536]{2,1,0:T(8,128)(2,1)S(1)} %all_gather.3, bf16[2,1536,4096]{2,1,0:T(8,128)(2,1)} %param.9), kind=kOutput, calls=%fused_computation.2 | convolution fusion | flops 2415919104 | bytes 28901376 | tf_op jit(solution)/shard_map/enf,efh->enh/dot_general | solution.py:31
  33.0 3.1 pad_maximum_fusion
  36.0 0.0 all-reduce.3.cloned.1.call-update
  36.1 0.0 copy-start.2
  36.1 0.0 reduce-scatter.2.cloned.1.call-start
  36.1 225.6 %all-reduce.3.cloned.1.call-done = f32[2,2,96,4096]{3,2,1,0:T(8,128)} async-done(((f32[2,2,96,4096]{3,2,1,0:T(8,128)}), f32[2,2,96,4096]{3,2,1,0:T(8,128)}) %all-reduce.3.cloned.1.call-update) | async-done | bytes 6291472 | tf_op jit(solution)/shard_map/psum | solution.py:36
  261.7 0.0 copy-start.1
  261.7 15.4 %convolution_bitcast_fusion.2 = f32[96,2,1536]{2,0,1:T(8,128)} fusion(bf16[2,4096,1536]{2,1,0:T(8,128)(2,1)} %param.11, f32[2,2,96,4096]{3,2,1,0:T(8,128)} %all-reduce.3.cloned.1.call-done), kind=kOutput, calls=%fused_computation.7 | convolution fusion | flops 2420637696 | bytes 32636928 | tf_op jit(solution)/shard_map/enh,ehd->ned/dot_general | solution.py:39
  277.1 0.0 reduce-scatter.2.cloned.1.call-update
  277.1 0.0 copy-done.2
  277.2 7.7 %reduce-scatter.2.cloned.1.call-done = f32[48,2,1536]{2,0,1:T(8,128)} async-done(((f32[96,2,1536]{2,0,1:T(8,128)}), f32[48,2,1536]{2,0,1:T(8,128)}) %reduce-scatter.2.cloned.1.call-update) | async-done | bytes 589840 | tf_op jit(solution)/shard_map/reduce_scatter | solution.py:38
  284.9 1.9 convolution_bitcast_fusion.3
  286.8 34.9 %all-reduce.4 = bf16[128,1536]{1,0:T(8,128)(2,1)} all-reduce(f32[128,1536]{1,0:T(8,128)S(1)} %convolution_bitcast_fusion.3), channel_id=1, replica_groups=mesh['dp'=2,'expert'=4,'blk'=4] {'expert'}, use_global_device_ids=true, to_apply=%region_7.8 | all-reduce | flops 196608 | bytes 1179648 | tf_op jit(solution)/shard_map/psum | solution.py:45
  321.7 0.0 copy-done.1
  (7 shorter events, 0.1 us)
Async XLA Ops:
  6.5 3.0 copy-start
  6.5 255.1 %all-reduce.3.cloned.1.call-start = ((), (), s32[]{:S(2)}) async-start(), calls=%async_computation.1 | async-start | bytes 12582912 | tf_op jit(solution)/shard_map/psum | solution.py:36
  36.1 241.1 %copy-start.2 = (f32[128,2]{0,1:T(2,128)S(1)}, f32[128,2]{0,1:T(2,128)}, u32[]{:S(2)}) copy-start(f32[128,2]{0,1:T(2,128)} %param.8) | copy-start | bytes 3076
  36.1 248.8 %reduce-scatter.2.cloned.1.call-start = ((), (), s32[]{:S(2)}) async-start(), calls=%async_computation.2 | async-start | bytes 1769472 | tf_op jit(solution)/shard_map/reduce_scatter | solution.py:38
  261.7 60.0 %copy-start.1 = (bf16[128,1536]{1,0:T(8,128)(2,1)S(1)}, bf16[128,1536]{1,0:T(8,128)(2,1)}, u32[]{:S(2)}) copy-start(bf16[128,1536]{1,0:T(8,128)(2,1)} %param.6) | copy-start | bytes 1179652
Sparse Core Ops, SparseCore 0:
  36.2 225.4 all-reduce.2
  277.2 7.6 reduce-scatter.1
where the time goes:
time: 329 us
  waiting for transfers between devices  233 us (71%)
  matrix products  38.3 us (12%)
  blocking collectives  37.2 us (11%)
  between operations  13.5 us (4%)
  other arithmetic  4.55 us (1%)
    psum x1, waiting for transfers between devices, local(): summed = lax.psum(partial_value, 'blk')  226 us
    psum x1, blocking collectives, local(): mixed = lax.psum(mixed_part, 'expert')  34.9 us
    dot_general x1, matrix products, local(): jnp.einsum('enh,ehd->ned', hidden, down_weight, preferred_element_type=jn...  15.4 us
    dot_general x1, matrix products, local(): jnp.einsum('enf,efh->enh', shard_rows, gate_weight, preferred_element_typ...  10.4 us
    dot_general x1, matrix products, local(): jnp.einsum('enf,efh->enh', shard_rows, up_weight, preferred_element_type=...  10.4 us
    reduce_scatter x1, waiting for transfers between devices, local(): lax.psum_scatter(jnp.einsum('enh,ehd->ned', hidden, down_weight, preferre...  7.73 us
  transfers between devices with their start and end apart: 2, of which 2 were waited for; matrix products, arithmetic and copies ran while one was open for 0% of the time, Pallas kernels for 0%

commit v1 on v0

v1 whole, which is shorter than its diff:
```python
import functools

import jax
import jax.numpy as jnp
from jax import lax
from jax.experimental import pallas as pl
from jax.experimental.pallas import tpu as pltpu
from jax.sharding import PartitionSpec as P

CAP = 48
CHUNKS = 4
VMEM_LIMIT = 40 * 1024 * 1024
F32, BF16 = jnp.float32, jnp.bfloat16


def params(steps):
    return pltpu.CompilerParams(
        dimension_semantics=("arbitrary",) * steps, vmem_limit_bytes=VMEM_LIMIT
    )


def slot_hits(ids, group, local_count):
    rows, lanes = ids.shape[0], local_count * CAP
    lane = lax.broadcasted_iota(jnp.int32, (rows, lanes), 1)
    expert = jnp.full((rows, lanes), group * local_count, jnp.int32)
    slot = lane
    for step in range(1, local_count):
        expert = expert + (lane >= step * CAP).astype(jnp.int32)
        slot = slot - CAP * (lane >= step * CAP).astype(jnp.int32)
    named = [ids[:, k : k + 1] == expert for k in range(ids.shape[1])]
    member = functools.reduce(jnp.logical_or, named)
    earlier = lax.broadcasted_iota(jnp.int32, (rows, rows), 1) < lax.broadcasted_iota(
        jnp.int32, (rows, rows), 0
    )
    position = jnp.dot(
        earlier.astype(F32).astype(BF16),
        member.astype(F32).astype(BF16),
        preferred_element_type=F32,
    )
    hit = member & (position.astype(jnp.int32) == slot)
    return hit, named


def pick_kernel(local_count, group_ref, *refs):
    pairs, out_ref = refs[:-1], refs[-1]
    for s in range(len(pairs) // 2):
        ids_ref, tokens_ref = pairs[2 * s], pairs[2 * s + 1]
        hit, _ = slot_hits(ids_ref[...], group_ref[0], local_count)
        rows = lax.dot_general(
            hit.astype(F32).astype(BF16),
            tokens_ref[...],
            (((0,), (0,)), ((), ())),
            preferred_element_type=F32,
        ).astype(BF16)
        for e in range(local_count):
            out_ref[e, s * CAP : (s + 1) * CAP, :] = rows[e * CAP : (e + 1) * CAP, :]


def pick(group, pairs, local_count):
    shards, width = len(pairs) // 2, pairs[1].shape[1]
    return pl.pallas_call(
        functools.partial(pick_kernel, local_count),
        out_shape=jax.ShapeDtypeStruct((local_count, shards * CAP, width), BF16),
        in_specs=[pl.BlockSpec(memory_space=pltpu.SMEM)]
        + [pl.BlockSpec(memory_space=pltpu.VMEM)] * len(pairs),
        out_specs=pl.BlockSpec(memory_space=pltpu.VMEM),
        compiler_params=params(0),
        name="pick",
    )(group, *pairs)


def gate_up_kernel(steps, where_ref, x_ref, gate_ref, up_ref, full_ref, *short_ref):
    step = pl.program_id(1)
    parts = [
        jnp.dot(x_ref[0], w_ref[0], preferred_element_type=F32) for w_ref in (gate_ref, up_ref)
    ]

    @pl.when(step == 0)
    def _():
        for i in range(2):
            full_ref[i, 0] = parts[i]

    @pl.when(step > 0)
    def _():
        for i in range(2):
            full_ref[i, 0] += parts[i]

    if short_ref:

        @pl.when(step == steps - 1)
        def _():
            short_ref[0][...] = full_ref[...].astype(BF16)


def gate_up(where, rows, gate_weight, up_weight, chunk, width, short):
    local_count, count, depth = rows.shape
    chunks = gate_weight.shape[2] // 2 // width
    steps = 2
    weight = pl.BlockSpec(
        (1, depth // steps, width), lambda e, k, where: (e, k, where[0] * chunks + chunk)
    )
    out = pl.BlockSpec((2, 1, count, width), lambda e, k, where: (0, e, 0, 0))
    shape = (2, local_count, count, width)
    return pl.pallas_call(
        functools.partial(gate_up_kernel, steps),
        grid_spec=pltpu.PrefetchScalarGridSpec(
            num_scalar_prefetch=1,
            grid=(local_count, steps),
            in_specs=[
                pl.BlockSpec((1, count, depth // steps), lambda e, k, where: (e, 0, k)),
                weight,
                weight,
            ],
            out_specs=[out] * (1 + short),
        ),
        out_shape=[jax.ShapeDtypeStruct(shape, F32), jax.ShapeDtypeStruct(shape, BF16)][: 1 + short],
        cost_estimate=pl.CostEstimate(
            flops=4 * local_count * count * depth * width,
            bytes_accessed=4 * local_count * depth * width,
            transcendentals=0,
        ),
        compiler_params=params(2),
        name="gate_up",
    )(where, rows, gate_weight, up_weight)


def down_kernel(parts, first, where_ref, *refs):
    refs = list(refs)
    out_ref = refs.pop()
    step = pl.program_id(1)
    total = None
    for i in range(parts):
        at_end, inside, weight = refs[3 * i : 3 * i + 3]
        hidden = jnp.where(where_ref[0] == 1, at_end[0], inside[0])
        product = jnp.dot(hidden, weight[0], preferred_element_type=F32)
        total = product if total is None else total + product

    @pl.when(step == 0)
    def _():
        out_ref[0] = total if first else refs[-1][0] + total

    @pl.when(step > 0)
    def _():
        out_ref[0] += total


def down(where, parts, down_weight, total):
    local_count, count, width = parts[0][0].shape
    features = down_weight.shape[2]
    chunks = down_weight.shape[1] // 2 // width
    steps = 2 if width % 256 == 0 else 1
    operands, specs = [], []
    for at_end, inside, half_at, chunk in parts:
        hidden = pl.BlockSpec((1, count, width // steps), lambda e, k, where: (e, 0, k))
        operands += [at_end, inside, down_weight]
        specs += [
            hidden,
            hidden,
            pl.BlockSpec(
                (1, width // steps, features),
                lambda e, k, where, half_at=half_at, chunk=chunk: (
                    e,
                    (where[half_at] * chunks + chunk) * steps + k,
                    0,
                ),
            ),
        ]
    out = pl.BlockSpec((1, count, features), lambda e, k, where: (e, 0, 0))
    first = total is None
    if not first:
        operands.append(total)
        specs.append(out)
    return pl.pallas_call(
        functools.partial(down_kernel, len(parts), first),
        grid_spec=pltpu.PrefetchScalarGridSpec(
            num_scalar_prefetch=1, grid=(local_count, steps), in_specs=specs, out_specs=out
        ),
        out_shape=jax.ShapeDtypeStruct((local_count, count, features), F32),
        input_output_aliases={} if first else {len(operands): 0},
        cost_estimate=pl.CostEstimate(
            flops=2 * len(parts) * local_count * count * features * width,
            bytes_accessed=2 * len(parts) * local_count * features * width,
            transcendentals=0,
        ),
        compiler_params=params(2),
        name="down",
    )(where, *operands)


def combine_kernel(local_count, groups, group_ref, ids_ref, weights_ref, *refs):
    sums, own_ref, sent = refs[: -groups], refs[-groups], refs[1 - groups :]
    hit, named = slot_hits(ids_ref[...], group_ref[0], local_count)
    scale = sum(
        jnp.where(named[k], weights_ref[:, k : k + 1], 0.0) for k in range(len(named))
    )
    scale = jnp.where(hit, scale, 0.0)
    scale_high = scale.astype(BF16)
    scale_low = (scale - scale_high.astype(F32)).astype(BF16)
    rows = jnp.concatenate(
        [functools.reduce(jnp.add, [ref[e] for ref in sums]) for e in range(local_count)], axis=0
    )
    rows_high = rows.astype(BF16)
    rows_low = (rows - rows_high.astype(F32)).astype(BF16)
    mixed = (
        jnp.dot(scale_high, rows_high, preferred_element_type=F32)
        + jnp.dot(scale_high, rows_low, preferred_element_type=F32)
        + jnp.dot(scale_low, rows_high, preferred_element_type=F32)
    )
    block = own_ref.shape[0]
    for place in range(groups):
        piece = mixed[place * block : (place + 1) * block]
        step = group_ref[0] ^ place

        @pl.when(step == 0)
        def _():
            own_ref[...] = piece

        for other in range(1, groups):

            @pl.when(step == other)
            def _():
                sent[other - 1][...] = piece.astype(BF16)


def combine(group, ids, weights, sums, groups):
    local_count, _, features = sums[0].shape
    block = ids.shape[0] // groups
    return pl.pallas_call(
        functools.partial(combine_kernel, local_count, groups),
        out_shape=[jax.ShapeDtypeStruct((block, features), F32)]
        + [jax.ShapeDtypeStruct((block, features), BF16)] * (groups - 1),
        in_specs=[pl.BlockSpec(memory_space=pltpu.SMEM)]
        + [pl.BlockSpec(memory_space=pltpu.VMEM)] * (2 + len(sums)),
        out_specs=[pl.BlockSpec(memory_space=pltpu.VMEM)] * groups,
        compiler_params=params(0),
        name="combine",
    )(group, ids, weights, *sums)


def gather_kernel(group_ref, *refs):
    out_ref = refs[-1]
    block = refs[0].shape[0]
    for step, piece_ref in enumerate(refs[:-1]):
        start = pl.multiple_of((group_ref[0] ^ step) * block, block)
        out_ref[pl.ds(start, block), :] = piece_ref[...]


def place_blocks(group, pieces):
    block, features = pieces[0].shape
    return pl.pallas_call(
        gather_kernel,
        out_shape=jax.ShapeDtypeStruct((block * len(pieces), features), BF16),
        in_specs=[pl.BlockSpec(memory_space=pltpu.SMEM)]
        + [pl.BlockSpec(memory_space=pltpu.VMEM)] * len(pieces),
        out_specs=pl.BlockSpec(memory_space=pltpu.VMEM),
        compiler_params=params(0),
        name="place_blocks",
    )(group, *pieces)


def local(mesh_shape, tokens, expert_ids, route_weights, gate_weight, up_weight, down_weight):
    shards, groups, line = mesh_shape["dp"], mesh_shape["expert"], mesh_shape["blk"]
    local_count, _, hidden_count = gate_weight.shape
    group = lax.axis_index("expert").astype(jnp.int32).reshape(1)
    place = lax.axis_index("blk")
    at_end = (place == 0) | (place == line - 1)
    far = (place < line // 2).astype(jnp.int32)
    near = 1 - far
    where_far, where_near = far.reshape(1), near.reshape(1)
    where = jnp.stack([at_end.astype(jnp.int32), near, far])

    if shards == 2:
        swap = [(0, 1), (1, 0)]
        other_ids = lax.ppermute(expert_ids, "dp", swap)
        other_tokens = lax.ppermute(tokens, "dp", swap)
        rows = pick(group, [expert_ids, tokens, other_ids, other_tokens], local_count)
    else:
        rows = lax.all_gather(
            pick(group, [expert_ids, tokens], local_count), "dp", axis=1, tiled=True
        )

    hop_pairs = [[(0, 1), (3, 2)], [(1, 2), (2, 1)], [(2, 3), (1, 0)]]
    hop = [functools.partial(lax.ppermute, axis_name="blk", perm=pairs) for pairs in hop_pairs]
    width = max(128, hidden_count // 2 // CHUNKS)
    chunks = hidden_count // 2 // width
    total, before = None, None
    for c in range(chunks):
        far_full, far_short = gate_up(where_far, rows, gate_weight, up_weight, c, width, True)
        (near_full,) = gate_up(where_near, rows, gate_weight, up_weight, c, width, False)
        got = hop[0](far_short)
        got = hop[1]((far_full + got.astype(F32)).astype(BF16))
        got = hop[2]((near_full + got.astype(F32)).astype(BF16))
        summed = near_full + got.astype(F32)
        hidden = (jax.nn.silu(summed[0]) * summed[1]).astype(BF16)
        first = hop[0](hidden)
        second = hop[1](first)
        third = hop[2](second)
        parts = [(hidden, first, 1, c)] + ([before] if before else [])
        total = down(where, parts, down_weight, total)
        before = (third, second, 2, c)
    total = down(where, [before], down_weight, total)

    if shards == 2:
        sums = [total[:, :CAP], lax.ppermute(total[:, CAP:], "dp", swap)]
    else:
        sums = [lax.psum_scatter(total, "dp", scatter_dimension=1, tiled=True)]
    own, *sent = combine(group, expert_ids, route_weights, sums, groups)
    for step in range(1, groups):
        exchange = [(i, i ^ step) for i in range(groups)]
        own = own + lax.ppermute(sent[step - 1], "expert", exchange).astype(F32)
    block = own.astype(BF16)
    pieces = [block]
    for step in range(1, groups):
        pieces.append(lax.ppermute(block, "expert", [(i, i ^ step) for i in range(groups)]))
    return place_blocks(group, pieces)


def solution(mesh):
    placed = (
        P("dp", "blk"),
        P("dp", None),
        P("dp", None),
        P("expert", "blk", "dp"),
        P("expert", "blk", "dp"),
        P("expert", "dp", "blk"),
    )
    return jax.shard_map(
        functools.partial(local, dict(mesh.shape)),
        mesh=mesh,
        in_specs=placed,
        out_specs=P("dp", "blk"),
        check_vma=False,
    )
```

time: 329 us -> 161 us (0.49)
  waiting for transfers between devices: 233 us -> 38.5 us
  Pallas kernels: 0 us -> 60.8 us
  starting transfers between devices: 0.04 us -> 54 us
  matrix products: 38.3 us -> 0 us
  blocking collectives: 37.2 us -> 0 us
  between operations: 13.5 us -> 0.59 us
    psum x1 -> x0, waiting for transfers between devices: 226 us -> none  [local(): summed = lax.psum(partial_value, 'blk')]
    pallas_call x0 -> x16, Pallas kernels: none -> 60.8 us  [the longest x8 35.5 us: gate_up(): pl.pallas_call(functools.partial(gate_up_kernel, steps), grid_spec=pltpu....]
    ppermute x0 -> x33, starting transfers between devices: none -> 54 us  [the longest x4 22 us: local(): first = hop[0](hidden)]
    ppermute x0 -> x33, waiting for transfers between devices: none -> 38.5 us  [the longest x4 13.5 us: local(): got = hop[2]((near_full + got.astype(F32)).astype(BF16))]
    dot_general x5 -> x0, matrix products: 38.3 us -> none  [the longest x1 15.4 us: local(): jnp.einsum('enh,ehd->ned', hidden, down_weight, preferred_element_type=jn...]
    psum x1 -> x0, blocking collectives: 34.9 us -> none  [local(): mixed = lax.psum(mixed_part, 'expert')]
    reduce_scatter x1 -> x0, waiting for transfers between devices: 7.73 us -> none  [local(): lax.psum_scatter(jnp.einsum('enh,ehd->ned', hidden, down_weight, preferre...]
    another operation x3 -> x1, other arithmetic: 3.69 us -> 0.08 us  [local(): where = jnp.stack([at_end.astype(jnp.int32), near, far])]
  transfers between devices with their start and end apart: 2 -> 33, of which waited for: 2 -> 15; matrix products, arithmetic and copies ran while one was open for 0% -> 2% of each run, Pallas kernels for 0% -> 32%
where the time goes in v1:
time: 161 us; the launch traced here: 159 us
  Pallas kernels  60.8 us (38%)
  starting transfers between devices  54 us (34%)
  waiting for transfers between devices  38.5 us (24%)
  local copies, waits for them, and re-layouts  2.48 us (2%)
  other arithmetic  2.09 us (1%)
    pallas_call x8, Pallas kernels, gate_up(): pl.pallas_call(functools.partial(gate_up_kernel, steps), grid_spec=pltpu....  35.5 us
    pallas_call x5, Pallas kernels, down(): pl.pallas_call(functools.partial(down_kernel, len(parts), first), grid_sp...  23 us
    ppermute x4, starting transfers between devices, local(): first = hop[0](hidden)  22 us
    ppermute x4, waiting for transfers between devices, local(): got = hop[2]((near_full + got.astype(F32)).astype(BF16))  13.5 us
    ppermute x4, starting transfers between devices, local(): got = hop[0](far_short)  8.6 us
    ppermute x4, waiting for transfers between devices, local(): first = hop[0](hidden)  5.84 us
    ppermute x4, starting transfers between devices, local(): got = hop[2]((near_full + got.astype(F32)).astype(BF16))  5.17 us
    ppermute x4, starting transfers between devices, local(): third = hop[2](second)  5.16 us
  transfers between devices with their start and end apart: 33, of which 15 were waited for; matrix products, arithmetic and copies ran while one was open for 2% of the time, Pallas kernels for 32%

profile of v1, /device:TPU:0, one launch (start us, length us, event | category | flops | bytes accessed | tf_op | source)
XLA Modules:
  0.0 158.6 jit_solution(7388825535936255875)
XLA Ops:
  1.4 1.2 collective-permute-done.refs_2_
  2.6 1.0 copy-done.2
  4.3 4.5 %gate_up.15 = (f32[2,2,96,512]{3,2,1,0:T(8,128)S(1)}, bf16[2,2,96,512]{3,2,1,0:T(8,128)(2,1)S(1)}) custom-call(s32[1]{0:T(128)} %bitcast.3.where_ref, bf16[2,96,1536]{2,1,0:T(8,128)(2,1)S(1)} %pick.1.x_ref, bf16[2,1536,4096]{2,1,0:T(8,128)(2,1)} %gate_ref.15, bf16[2,1536,4096]{2,1,0:T(8,128)(2,1)} %up_ref.15), custom_call_target="tpu_custom_call" | custom-call | flops 603979776 | bytes 6291456 | tf_op jit(solution)/shard_map/gate_up/pallas_call | solution.py:104
  8.8 4.7 %collective-permute-start.20 = (bf16[2,2,96,512]{3,2,1,0:T(8,128)(2,1)S(1)}, bf16[2,2,96,512]{3,2,1,0:T(8,128)(2,1)S(1)}, u32[]{:S(2)}, u32[]{:S(2)}) collective-permute-start(bf16[2,2,96,512]{3,2,1,0:T(8,128)(2,1)S(1)} %get-tuple-element.24), channel_id=1, source_target_pairs={{0,1},{3,2},{4,5},{7,6},{8,9},{11,10},{12,13},{15,14},{16,17},{19,... | collective-permute-start | bytes 1179656 | tf_op jit(solution)/shard_map/ppermute | solution.py:290
  13.5 4.5 %gate_up.13 = (f32[2,2,96,512]{3,2,1,0:T(8,128)S(1)}, bf16[2,2,96,512]{3,2,1,0:T(8,128)(2,1)S(1)}) custom-call(s32[1]{0:T(128)} %bitcast.3.where_ref, bf16[2,96,1536]{2,1,0:T(8,128)(2,1)S(1)} %pick.1.x_ref, bf16[2,1536,4096]{2,1,0:T(8,128)(2,1)} %gate_ref.15, bf16[2,1536,4096]{2,1,0:T(8,128)(2,1)} %up_ref.15), custom_call_target="tpu_custom_call" | custom-call | flops 603979776 | bytes 6291456 | tf_op jit(solution)/shard_map/gate_up/pallas_call | solution.py:104
  18.0 1.3 collective-permute-start.14
  19.3 4.4 %gate_up.14 = f32[2,2,96,512]{3,2,1,0:T(8,128)S(1)} custom-call(s32[1]{0:T(128)} %bitcast.2.where_ref, bf16[2,96,1536]{2,1,0:T(8,128)(2,1)S(1)} %pick.1.x_ref, bf16[2,1536,4096]{2,1,0:T(8,128)(2,1)} %gate_ref.15, bf16[2,1536,4096]{2,1,0:T(8,128)(2,1)} %up_ref.15), custom_call_target="tpu_custom_call" | custom-call | flops 603979776 | bytes 6291456 | tf_op jit(solution)/shard_map/gate_up/pallas_call | solution.py:104
  23.7 4.4 %gate_up.12 = f32[2,2,96,512]{3,2,1,0:T(8,128)S(1)} custom-call(s32[1]{0:T(128)} %bitcast.2.where_ref, bf16[2,96,1536]{2,1,0:T(8,128)(2,1)S(1)} %pick.1.x_ref, bf16[2,1536,4096]{2,1,0:T(8,128)(2,1)} %gate_ref.15, bf16[2,1536,4096]{2,1,0:T(8,128)(2,1)} %up_ref.15), custom_call_target="tpu_custom_call" | custom-call | flops 603979776 | bytes 6291456 | tf_op jit(solution)/shard_map/gate_up/pallas_call | solution.py:104
  28.1 4.5 %gate_up.11 = (f32[2,2,96,512]{3,2,1,0:T(8,128)S(1)}, bf16[2,2,96,512]{3,2,1,0:T(8,128)(2,1)S(1)}) custom-call(s32[1]{0:T(128)} %bitcast.3.where_ref, bf16[2,96,1536]{2,1,0:T(8,128)(2,1)S(1)} %pick.1.x_ref, bf16[2,1536,4096]{2,1,0:T(8,128)(2,1)} %gate_ref.15, bf16[2,1536,4096]{2,1,0:T(8,128)(2,1)} %up_ref.15), custom_call_target="tpu_custom_call" | custom-call | flops 603979776 | bytes 6291456 | tf_op jit(solution)/shard_map/gate_up/pallas_call | solution.py:104
  32.6 4.5 %gate_up.9 = (f32[2,2,96,512]{3,2,1,0:T(8,128)S(1)}, bf16[2,2,96,512]{3,2,1,0:T(8,128)(2,1)S(1)}) custom-call(s32[1]{0:T(128)} %bitcast.3.where_ref, bf16[2,96,1536]{2,1,0:T(8,128)(2,1)S(1)} %pick.1.x_ref, bf16[2,1536,4096]{2,1,0:T(8,128)(2,1)} %gate_ref.15, bf16[2,1536,4096]{2,1,0:T(8,128)(2,1)} %up_ref.15), custom_call_target="tpu_custom_call" | custom-call | flops 603979776 | bytes 6291456 | tf_op jit(solution)/shard_map/gate_up/pallas_call | solution.py:104
  37.1 1.3 collective-permute-start.8
  38.4 1.3 collective-permute-start.2
  39.7 4.4 %gate_up.10 = f32[2,2,96,512]{3,2,1,0:T(8,128)S(1)} custom-call(s32[1]{0:T(128)} %bitcast.2.where_ref, bf16[2,96,1536]{2,1,0:T(8,128)(2,1)S(1)} %pick.1.x_ref, bf16[2,1536,4096]{2,1,0:T(8,128)(2,1)} %gate_ref.15, bf16[2,1536,4096]{2,1,0:T(8,128)(2,1)} %up_ref.15), custom_call_target="tpu_custom_call" | custom-call | flops 603979776 | bytes 6291456 | tf_op jit(solution)/shard_map/gate_up/pallas_call | solution.py:104
  44.1 4.4 %gate_up.8 = f32[2,2,96,512]{3,2,1,0:T(8,128)S(1)} custom-call(s32[1]{0:T(128)} %bitcast.2.where_ref, bf16[2,96,1536]{2,1,0:T(8,128)(2,1)S(1)} %pick.1.x_ref, bf16[2,1536,4096]{2,1,0:T(8,128)(2,1)} %gate_ref.15, bf16[2,1536,4096]{2,1,0:T(8,128)(2,1)} %up_ref.15), custom_call_target="tpu_custom_call" | custom-call | flops 603979776 | bytes 6291456 | tf_op jit(solution)/shard_map/gate_up/pallas_call | solution.py:104
  51.1 4.6 %collective-permute-done.2 = bf16[2,2,96,512]{3,2,1,0:T(8,128)(2,1)S(1)} collective-permute-done((bf16[2,2,96,512]{3,2,1,0:T(8,128)(2,1)S(1)}, bf16[2,2,96,512]{3,2,1,0:T(8,128)(2,1)S(1)}, u32[]{:S(2)}, u32[]{:S(2)}) %collective-permute-start.2) | collective-permute-done | bytes 393248 | tf_op jit(solution)/shard_map/ppermute | solution.py:290
  56.7 1.3 collective-permute-start.22
  58.1 1.3 collective-permute-start.16
  59.6 1.3 collective-permute-start.10
  61.0 1.3 collective-permute-start.4
  62.3 9.7 %collective-permute-done.22 = bf16[2,2,96,512]{3,2,1,0:T(8,128)(2,1)S(1)} collective-permute-done((bf16[2,2,96,512]{3,2,1,0:T(8,128)(2,1)S(1)}, bf16[2,2,96,512]{3,2,1,0:T(8,128)(2,1)S(1)}, u32[]{:S(2)}, u32[]{:S(2)}) %collective-permute-start.22) | collective-permute-done | bytes 393248 | tf_op jit(solution)/shard_map/ppermute | solution.py:292
  72.3 17.9 %collective-permute-start.23 = (bf16[2,96,512]{2,1,0:T(8,128)(2,1)S(1)}, bf16[2,96,512]{2,1,0:T(8,128)(2,1)S(1)}, u32[]{:S(2)}, u32[]{:S(2)}) collective-permute-start(bf16[2,96,512]{2,1,0:T(8,128)(2,1)S(1)} %fusion.1.refs_0_), channel_id=1, source_target_pairs={{0,1},{3,2},{4,5},{7,6},{8,9},{11,10},{12,13},{15,14},{16,17},{19,... | collective-permute-start | bytes 589832 | tf_op jit(solution)/shard_map/ppermute | solution.py:295
  90.4 1.3 collective-permute-start.17
  92.0 1.3 collective-permute-start.11
  93.3 3.8 %collective-permute-done.4 = bf16[2,2,96,512]{3,2,1,0:T(8,128)(2,1)S(1)} collective-permute-done((bf16[2,2,96,512]{3,2,1,0:T(8,128)(2,1)S(1)}, bf16[2,2,96,512]{3,2,1,0:T(8,128)(2,1)S(1)}, u32[]{:S(2)}, u32[]{:S(2)}) %collective-permute-start.4) | collective-permute-done | bytes 393248 | tf_op jit(solution)/shard_map/ppermute | solution.py:292
  97.3 1.5 collective-permute-start.5
  100.4 3.5 %collective-permute-done.11.refs_1_ = bf16[2,96,512]{2,1,0:T(8,128)(2,1)S(1)} collective-permute-done((bf16[2,96,512]{2,1,0:T(8,128)(2,1)S(1)}, bf16[2,96,512]{2,1,0:T(8,128)(2,1)S(1)}, u32[]{:S(2)}, u32[]{:S(2)}) %collective-permute-start.11) | collective-permute-done | bytes 196640 | tf_op jit(solution)/shard_map/ppermute | solution.py:295
  104.6 2.1 %collective-permute-done.5.refs_1_ = bf16[2,96,512]{2,1,0:T(8,128)(2,1)S(1)} collective-permute-done((bf16[2,96,512]{2,1,0:T(8,128)(2,1)S(1)}, bf16[2,96,512]{2,1,0:T(8,128)(2,1)S(1)}, u32[]{:S(2)}, u32[]{:S(2)}) %collective-permute-start.5) | collective-permute-done | bytes 196640 | tf_op jit(solution)/shard_map/ppermute | solution.py:295
  107.3 1.3 collective-permute-start.25
  108.6 1.3 collective-permute-start.19
  110.0 1.3 collective-permute-start.13
  111.3 1.3 collective-permute-start.7
  112.6 3.9 %down.5.refs_6_ = f32[2,96,1536]{2,1,0:T(8,128)S(1)} custom-call(s32[3]{0:T(128)S(1)} %pad_add_fusion.where_ref, bf16[2,96,512]{2,1,0:T(8,128)(2,1)S(1)} %fusion.1.refs_0_, bf16[2,96,512]{2,1,0:T(8,128)(2,1)S(1)} %collective-permute-done.23.refs_1_, bf16[2,4096,1536]{2,1,0:T(8,128)(2,1)} %refs_2_.9), custom_call_target="tpu_custom_call" | custom-call | flops 301989888 | bytes 3145728 | tf_op jit(solution)/shard_map/down/pallas_call | solution.py:173
  116.6 3.1 %collective-permute-done.25.refs_3_ = bf16[2,96,512]{2,1,0:T(8,128)(2,1)S(1)} collective-permute-done((bf16[2,96,512]{2,1,0:T(8,128)(2,1)S(1)}, bf16[2,96,512]{2,1,0:T(8,128)(2,1)S(1)}, u32[]{:S(2)}, u32[]{:S(2)}) %collective-permute-start.25) | collective-permute-done | bytes 196640 | tf_op jit(solution)/shard_map/ppermute | solution.py:297
  119.7 5.0 %down.6.refs_6_ = f32[2,96,1536]{2,1,0:T(8,128)S(1)} custom-call(s32[3]{0:T(128)S(1)} %pad_add_fusion.where_ref, bf16[2,96,512]{2,1,0:T(8,128)(2,1)S(1)} %fusion.3.refs_0_, bf16[2,96,512]{2,1,0:T(8,128)(2,1)S(1)} %collective-permute-done.17.refs_1_, bf16[2,4096,1536]{2,1,0:T(8,128)(2,1)} %refs_2_.9, ...), custom_call_target="tpu_custom_call", output_to_operand_aliasing={{}: (7, {})} | custom-call | flops 603979776 | bytes 6291456 | tf_op jit(solution)/shard_map/down/pallas_call | solution.py:173
  124.7 5.0 %down.7.refs_6_ = f32[2,96,1536]{2,1,0:T(8,128)S(1)} custom-call(s32[3]{0:T(128)S(1)} %pad_add_fusion.where_ref, bf16[2,96,512]{2,1,0:T(8,128)(2,1)S(1)} %fusion.5.refs_0_, bf16[2,96,512]{2,1,0:T(8,128)(2,1)S(1)} %collective-permute-done.11.refs_1_, bf16[2,4096,1536]{2,1,0:T(8,128)(2,1)} %refs_2_.9, ...), custom_call_target="tpu_custom_call", output_to_operand_aliasing={{}: (7, {})} | custom-call | flops 603979776 | bytes 6291456 | tf_op jit(solution)/shard_map/down/pallas_call | solution.py:173
  129.8 5.0 %down.8.refs_3_ = f32[2,96,1536]{2,1,0:T(8,128)S(1)} custom-call(s32[3]{0:T(128)S(1)} %pad_add_fusion.where_ref, bf16[2,96,512]{2,1,0:T(8,128)(2,1)S(1)} %fusion.7.refs_0_, bf16[2,96,512]{2,1,0:T(8,128)(2,1)S(1)} %collective-permute-done.5.refs_1_, bf16[2,4096,1536]{2,1,0:T(8,128)(2,1)} %refs_2_.9, ...), custom_call_target="tpu_custom_call", output_to_operand_aliasing={{}: (7, {})} | custom-call | flops 603979776 | bytes 6291456 | tf_op jit(solution)/shard_map/down/pallas_call | solution.py:173
  134.8 4.0 %down.9 = f32[2,96,1536]{2,1,0:T(8,128)S(1)} custom-call(s32[3]{0:T(128)S(1)} %pad_add_fusion.where_ref, bf16[2,96,512]{2,1,0:T(8,128)(2,1)S(1)} %collective-permute-done.7.refs_0_, bf16[2,96,512]{2,1,0:T(8,128)(2,1)S(1)} %collective-permute-done.6.refs_1_, bf16[2,4096,1536]{2,1,0:T(8,128)(2,1)} %refs_2_.9, ...), custom_call_target="tpu_custom_call", output_to_operand_aliasing={{}: (4, {})} | custom-call | flops 301989888 | bytes 3145728 | tf_op jit(solution)/shard_map/down/pallas_call | solution.py:173
  139.6 1.4 collective-permute-done.26.refs_1_
  141.8 1.6 collective-permute-start.27
  143.4 1.5 collective-permute-start.28
  145.4 1.3 collective-permute-done.27
  146.7 2.4 %collective-permute-done.28 = bf16[32,1536]{1,0:T(8,128)(2,1)S(1)} collective-permute-done((bf16[32,1536]{1,0:T(8,128)(2,1)S(1)}, bf16[32,1536]{1,0:T(8,128)(2,1)S(1)}, u32[]{:S(2)}, u32[]{:S(2)}) %collective-permute-start.28) | collective-permute-done | bytes 98336 | tf_op jit(solution)/shard_map/ppermute | solution.py:310
  149.2 1.3 collective-permute-done.29
  150.5 0.9 collective-permute-start.30
  151.4 0.9 collective-permute-start.31
  152.3 1.7 %collective-permute-start.32 = (bf16[32,1536]{1,0:T(8,128)(2,1)S(1)}, bf16[32,1536]{1,0:T(8,128)(2,1)S(1)}, u32[]{:S(2)}, u32[]{:S(2)}) collective-permute-start(bf16[32,1536]{1,0:T(8,128)(2,1)S(1)} %add_convert_fusion.8.refs_0_), channel_id=1, source_target_pairs={{0,12},{4,8},{8,4},{12,0},{1,13},{5,9},{9,5},{13,1},{2,14},{6,10},... | collective-permute-start | bytes 294920 | tf_op jit(solution)/shard_map/ppermute | solution.py:314
  154.0 2.0 %collective-permute-done.30.refs_1_ = bf16[32,1536]{1,0:T(8,128)(2,1)S(1)} collective-permute-done((bf16[32,1536]{1,0:T(8,128)(2,1)S(1)}, bf16[32,1536]{1,0:T(8,128)(2,1)S(1)}, u32[]{:S(2)}, u32[]{:S(2)}) %collective-permute-start.30) | collective-permute-done | bytes 98336 | tf_op jit(solution)/shard_map/ppermute | solution.py:314
  156.4 1.4 collective-permute-done.32.refs_3_
  (63 shorter events, 13.1 us)
Async XLA Ops:
  0.0 2.6 %collective-permute-start.1 = (bf16[128,1536]{1,0:T(8,128)(2,1)}, bf16[128,1536]{1,0:T(8,128)(2,1)S(1)}, u32[]{:S(2)}, u32[]{:S(2)}) collective-permute-start(bf16[128,1536]{1,0:T(8,128)(2,1)} %refs_1_.1), channel_id=1, source_target_pairs={{0,16},{16,0},{1,17},{17,1},{2,18},{18,2},{3,19},{19,3},{4,20},{20... | collective-permute-start | bytes 1179656 | tf_op jit(solution)/shard_map/ppermute | solution.py:275
  1.2 7.6 %copy-start = (s32[128,2]{1,0:T(8,128)}, s32[128,2]{1,0:T(8,128)S(1)}, u32[]{:S(2)}) copy-start(s32[128,2]{1,0:T(8,128)S(1)} %copy.13.refs_0_.ids_ref) | copy-start | bytes 3076
  1.2 1.3 collective-permute-start
  2.6 1.0 copy-start.2
  8.8 39.7 %collective-permute-start.20 = (bf16[2,2,96,512]{3,2,1,0:T(8,128)(2,1)S(1)}, bf16[2,2,96,512]{3,2,1,0:T(8,128)(2,1)S(1)}, u32[]{:S(2)}, u32[]{:S(2)}) collective-permute-start(bf16[2,2,96,512]{3,2,1,0:T(8,128)(2,1)S(1)} %get-tuple-element.24), channel_id=1, source_target_pairs={{0,1},{3,2},{4,5},{7,6},{8,9},{11,10},{12,13},{15,14},{16,17},{19,... | collective-permute-start | bytes 1179656 | tf_op jit(solution)/shard_map/ppermute | solution.py:290
  18.0 31.4 %collective-permute-start.14 = (bf16[2,2,96,512]{3,2,1,0:T(8,128)(2,1)S(1)}, bf16[2,2,96,512]{3,2,1,0:T(8,128)(2,1)S(1)}, u32[]{:S(2)}, u32[]{:S(2)}) collective-permute-start(bf16[2,2,96,512]{3,2,1,0:T(8,128)(2,1)S(1)} %get-tuple-element.22), channel_id=1, source_target_pairs={{0,1},{3,2},{4,5},{7,6},{8,9},{11,10},{12,13},{15,14},{16,17},{19,... | collective-permute-start | bytes 1179656 | tf_op jit(solution)/shard_map/ppermute | solution.py:290
  37.1 13.1 %collective-permute-start.8 = (bf16[2,2,96,512]{3,2,1,0:T(8,128)(2,1)S(1)}, bf16[2,2,96,512]{3,2,1,0:T(8,128)(2,1)S(1)}, u32[]{:S(2)}, u32[]{:S(2)}) collective-permute-start(bf16[2,2,96,512]{3,2,1,0:T(8,128)(2,1)S(1)} %get-tuple-element.20), channel_id=1, source_target_pairs={{0,1},{3,2},{4,5},{7,6},{8,9},{11,10},{12,13},{15,14},{16,17},{19,... | collective-permute-start | bytes 1179656 | tf_op jit(solution)/shard_map/ppermute | solution.py:290
  38.4 17.3 %collective-permute-start.2 = (bf16[2,2,96,512]{3,2,1,0:T(8,128)(2,1)S(1)}, bf16[2,2,96,512]{3,2,1,0:T(8,128)(2,1)S(1)}, u32[]{:S(2)}, u32[]{:S(2)}) collective-permute-start(bf16[2,2,96,512]{3,2,1,0:T(8,128)(2,1)S(1)} %get-tuple-element.18), channel_id=1, source_target_pairs={{0,1},{3,2},{4,5},{7,6},{8,9},{11,10},{12,13},{15,14},{16,17},{19,... | collective-permute-start | bytes 1179656 | tf_op jit(solution)/shard_map/ppermute | solution.py:290
  48.7 7.8 %collective-permute-start.21 = (bf16[2,2,96,512]{3,2,1,0:T(8,128)(2,1)S(1)}, bf16[2,2,96,512]{3,2,1,0:T(8,128)(2,1)S(1)}, u32[]{:S(2)}, u32[]{:S(2)}) collective-permute-start(bf16[2,2,96,512]{3,2,1,0:T(8,128)(2,1)S(1)} %add_convert_fusion.1), channel_id=1, source_target_pairs={{1,2},{2,1},{5,6},{6,5},{9,10},{10,9},{13,14},{14,13},{17,18},{18,... | collective-permute-start | bytes 1179656 | tf_op jit(solution)/shard_map/ppermute | solution.py:291
  49.5 8.4 %collective-permute-start.15 = (bf16[2,2,96,512]{3,2,1,0:T(8,128)(2,1)S(1)}, bf16[2,2,96,512]{3,2,1,0:T(8,128)(2,1)S(1)}, u32[]{:S(2)}, u32[]{:S(2)}) collective-permute-start(bf16[2,2,96,512]{3,2,1,0:T(8,128)(2,1)S(1)} %add_convert_fusion.3), channel_id=1, source_target_pairs={{1,2},{2,1},{5,6},{6,5},{9,10},{10,9},{13,14},{14,13},{17,18},{18,... | collective-permute-start | bytes 1179656 | tf_op jit(solution)/shard_map/ppermute | solution.py:291
  50.4 9.0 %collective-permute-start.9 = (bf16[2,2,96,512]{3,2,1,0:T(8,128)(2,1)S(1)}, bf16[2,2,96,512]{3,2,1,0:T(8,128)(2,1)S(1)}, u32[]{:S(2)}, u32[]{:S(2)}) collective-permute-start(bf16[2,2,96,512]{3,2,1,0:T(8,128)(2,1)S(1)} %add_convert_fusion.5), channel_id=1, source_target_pairs={{1,2},{2,1},{5,6},{6,5},{9,10},{10,9},{13,14},{14,13},{17,18},{18,... | collective-permute-start | bytes 1179656 | tf_op jit(solution)/shard_map/ppermute | solution.py:291
  55.8 5.0 %collective-permute-start.3 = (bf16[2,2,96,512]{3,2,1,0:T(8,128)(2,1)S(1)}, bf16[2,2,96,512]{3,2,1,0:T(8,128)(2,1)S(1)}, u32[]{:S(2)}, u32[]{:S(2)}) collective-permute-start(bf16[2,2,96,512]{3,2,1,0:T(8,128)(2,1)S(1)} %add_convert_fusion.7), channel_id=1, source_target_pairs={{1,2},{2,1},{5,6},{6,5},{9,10},{10,9},{13,14},{14,13},{17,18},{18,... | collective-permute-start | bytes 1179656 | tf_op jit(solution)/shard_map/ppermute | solution.py:291
  56.7 15.3 %collective-permute-start.22 = (bf16[2,2,96,512]{3,2,1,0:T(8,128)(2,1)S(1)}, bf16[2,2,96,512]{3,2,1,0:T(8,128)(2,1)S(1)}, u32[]{:S(2)}, u32[]{:S(2)}) collective-permute-start(bf16[2,2,96,512]{3,2,1,0:T(8,128)(2,1)S(1)} %add_convert_fusion), channel_id=1, source_target_pairs={{2,3},{1,0},{6,7},{5,4},{10,11},{9,8},{14,15},{13,12},{18,19},{17,... | collective-permute-start | bytes 1179656 | tf_op jit(solution)/shard_map/ppermute | solution.py:292
  58.1 32.1 %collective-permute-start.16 = (bf16[2,2,96,512]{3,2,1,0:T(8,128)(2,1)S(1)}, bf16[2,2,96,512]{3,2,1,0:T(8,128)(2,1)S(1)}, u32[]{:S(2)}, u32[]{:S(2)}) collective-permute-start(bf16[2,2,96,512]{3,2,1,0:T(8,128)(2,1)S(1)} %add_convert_fusion.2), channel_id=1, source_target_pairs={{2,3},{1,0},{6,7},{5,4},{10,11},{9,8},{14,15},{13,12},{18,19},{17,... | collective-permute-start | bytes 1179656 | tf_op jit(solution)/shard_map/ppermute | solution.py:292
  59.6 32.2 %collective-permute-start.10 = (bf16[2,2,96,512]{3,2,1,0:T(8,128)(2,1)S(1)}, bf16[2,2,96,512]{3,2,1,0:T(8,128)(2,1)S(1)}, u32[]{:S(2)}, u32[]{:S(2)}) collective-permute-start(bf16[2,2,96,512]{3,2,1,0:T(8,128)(2,1)S(1)} %add_convert_fusion.4), channel_id=1, source_target_pairs={{2,3},{1,0},{6,7},{5,4},{10,11},{9,8},{14,15},{13,12},{18,19},{17,... | collective-permute-start | bytes 1179656 | tf_op jit(solution)/shard_map/ppermute | solution.py:292
  61.0 36.1 %collective-permute-start.4 = (bf16[2,2,96,512]{3,2,1,0:T(8,128)(2,1)S(1)}, bf16[2,2,96,512]{3,2,1,0:T(8,128)(2,1)S(1)}, u32[]{:S(2)}, u32[]{:S(2)}) collective-permute-start(bf16[2,2,96,512]{3,2,1,0:T(8,128)(2,1)S(1)} %add_convert_fusion.6), channel_id=1, source_target_pairs={{2,3},{1,0},{6,7},{5,4},{10,11},{9,8},{14,15},{13,12},{18,19},{17,... | collective-permute-start | bytes 1179656 | tf_op jit(solution)/shard_map/ppermute | solution.py:292
  72.3 26.5 %collective-permute-start.23 = (bf16[2,96,512]{2,1,0:T(8,128)(2,1)S(1)}, bf16[2,96,512]{2,1,0:T(8,128)(2,1)S(1)}, u32[]{:S(2)}, u32[]{:S(2)}) collective-permute-start(bf16[2,96,512]{2,1,0:T(8,128)(2,1)S(1)} %fusion.1.refs_0_), channel_id=1, source_target_pairs={{0,1},{3,2},{4,5},{7,6},{8,9},{11,10},{12,13},{15,14},{16,17},{19,... | collective-permute-start | bytes 589832 | tf_op jit(solution)/shard_map/ppermute | solution.py:295
  90.4 9.3 %collective-permute-start.17 = (bf16[2,96,512]{2,1,0:T(8,128)(2,1)S(1)}, bf16[2,96,512]{2,1,0:T(8,128)(2,1)S(1)}, u32[]{:S(2)}, u32[]{:S(2)}) collective-permute-start(bf16[2,96,512]{2,1,0:T(8,128)(2,1)S(1)} %fusion.3.refs_0_), channel_id=1, source_target_pairs={{0,1},{3,2},{4,5},{7,6},{8,9},{11,10},{12,13},{15,14},{16,17},{19,... | collective-permute-start | bytes 589832 | tf_op jit(solution)/shard_map/ppermute | solution.py:295
  92.0 11.9 %collective-permute-start.11 = (bf16[2,96,512]{2,1,0:T(8,128)(2,1)S(1)}, bf16[2,96,512]{2,1,0:T(8,128)(2,1)S(1)}, u32[]{:S(2)}, u32[]{:S(2)}) collective-permute-start(bf16[2,96,512]{2,1,0:T(8,128)(2,1)S(1)} %fusion.5.refs_0_), channel_id=1, source_target_pairs={{0,1},{3,2},{4,5},{7,6},{8,9},{11,10},{12,13},{15,14},{16,17},{19,... | collective-permute-start | bytes 589832 | tf_op jit(solution)/shard_map/ppermute | solution.py:295
  97.3 9.3 %collective-permute-start.5 = (bf16[2,96,512]{2,1,0:T(8,128)(2,1)S(1)}, bf16[2,96,512]{2,1,0:T(8,128)(2,1)S(1)}, u32[]{:S(2)}, u32[]{:S(2)}) collective-permute-start(bf16[2,96,512]{2,1,0:T(8,128)(2,1)S(1)} %fusion.7.refs_0_), channel_id=1, source_target_pairs={{0,1},{3,2},{4,5},{7,6},{8,9},{11,10},{12,13},{15,14},{16,17},{19,... | collective-permute-start | bytes 589832 | tf_op jit(solution)/shard_map/ppermute | solution.py:295
  98.8 8.5 %collective-permute-start.24 = (bf16[2,96,512]{2,1,0:T(8,128)(2,1)S(1)}, bf16[2,96,512]{2,1,0:T(8,128)(2,1)S(1)}, u32[]{:S(2)}, u32[]{:S(2)}) collective-permute-start(bf16[2,96,512]{2,1,0:T(8,128)(2,1)S(1)} %collective-permute-done.23.refs_1_), channel_id=1, source_target_pairs={{1,2},{2,1},{5,6},{6,5},{9,10},{10,9},{13,14},{14,13},{17,18},{18,... | collective-permute-start | bytes 589832 | tf_op jit(solution)/shard_map/ppermute | solution.py:296
  99.7 8.9 %collective-permute-start.18 = (bf16[2,96,512]{2,1,0:T(8,128)(2,1)S(1)}, bf16[2,96,512]{2,1,0:T(8,128)(2,1)S(1)}, u32[]{:S(2)}, u32[]{:S(2)}) collective-permute-start(bf16[2,96,512]{2,1,0:T(8,128)(2,1)S(1)} %collective-permute-done.17.refs_1_), channel_id=1, source_target_pairs={{1,2},{2,1},{5,6},{6,5},{9,10},{10,9},{13,14},{14,13},{17,18},{18,... | collective-permute-start | bytes 589832 | tf_op jit(solution)/shard_map/ppermute | solution.py:296
  103.9 6.0 %collective-permute-start.12 = (bf16[2,96,512]{2,1,0:T(8,128)(2,1)S(1)}, bf16[2,96,512]{2,1,0:T(8,128)(2,1)S(1)}, u32[]{:S(2)}, u32[]{:S(2)}) collective-permute-start(bf16[2,96,512]{2,1,0:T(8,128)(2,1)S(1)} %collective-permute-done.11.refs_1_), channel_id=1, source_target_pairs={{1,2},{2,1},{5,6},{6,5},{9,10},{10,9},{13,14},{14,13},{17,18},{18,... | collective-permute-start | bytes 589832 | tf_op jit(solution)/shard_map/ppermute | solution.py:296
  106.6 4.7 %collective-permute-start.6 = (bf16[2,96,512]{2,1,0:T(8,128)(2,1)S(1)}, bf16[2,96,512]{2,1,0:T(8,128)(2,1)S(1)}, u32[]{:S(2)}, u32[]{:S(2)}) collective-permute-start(bf16[2,96,512]{2,1,0:T(8,128)(2,1)S(1)} %collective-permute-done.5.refs_1_), channel_id=1, source_target_pairs={{1,2},{2,1},{5,6},{6,5},{9,10},{10,9},{13,14},{14,13},{17,18},{18,... | collective-permute-start | bytes 589832 | tf_op jit(solution)/shard_map/ppermute | solution.py:296
  107.3 12.4 %collective-permute-start.25 = (bf16[2,96,512]{2,1,0:T(8,128)(2,1)S(1)}, bf16[2,96,512]{2,1,0:T(8,128)(2,1)S(1)}, u32[]{:S(2)}, u32[]{:S(2)}) collective-permute-start(bf16[2,96,512]{2,1,0:T(8,128)(2,1)S(1)} %collective-permute-done.24.refs_4_), channel_id=1, source_target_pairs={{2,3},{1,0},{6,7},{5,4},{10,11},{9,8},{14,15},{13,12},{18,19},{17,... | collective-permute-start | bytes 589832 | tf_op jit(solution)/shard_map/ppermute | solution.py:297
  108.6 16.1 %collective-permute-start.19 = (bf16[2,96,512]{2,1,0:T(8,128)(2,1)S(1)}, bf16[2,96,512]{2,1,0:T(8,128)(2,1)S(1)}, u32[]{:S(2)}, u32[]{:S(2)}) collective-permute-start(bf16[2,96,512]{2,1,0:T(8,128)(2,1)S(1)} %collective-permute-done.18.refs_4_), channel_id=1, source_target_pairs={{2,3},{1,0},{6,7},{5,4},{10,11},{9,8},{14,15},{13,12},{18,19},{17,... | collective-permute-start | bytes 589832 | tf_op jit(solution)/shard_map/ppermute | solution.py:297
  110.0 19.8 %collective-permute-start.13 = (bf16[2,96,512]{2,1,0:T(8,128)(2,1)S(1)}, bf16[2,96,512]{2,1,0:T(8,128)(2,1)S(1)}, u32[]{:S(2)}, u32[]{:S(2)}) collective-permute-start(bf16[2,96,512]{2,1,0:T(8,128)(2,1)S(1)} %collective-permute-done.12.refs_4_), channel_id=1, source_target_pairs={{2,3},{1,0},{6,7},{5,4},{10,11},{9,8},{14,15},{13,12},{18,19},{17,... | collective-permute-start | bytes 589832 | tf_op jit(solution)/shard_map/ppermute | solution.py:297
  111.3 23.5 %collective-permute-start.7 = (bf16[2,96,512]{2,1,0:T(8,128)(2,1)S(1)}, bf16[2,96,512]{2,1,0:T(8,128)(2,1)S(1)}, u32[]{:S(2)}, u32[]{:S(2)}) collective-permute-start(bf16[2,96,512]{2,1,0:T(8,128)(2,1)S(1)} %collective-permute-done.6.refs_1_), channel_id=1, source_target_pairs={{2,3},{1,0},{6,7},{5,4},{10,11},{9,8},{14,15},{13,12},{18,19},{17,... | collective-permute-start | bytes 589832 | tf_op jit(solution)/shard_map/ppermute | solution.py:297
  138.8 0.7 copy-start.3
  138.9 2.2 %copy-start.1 = (s32[128,2]{1,0:T(8,128)S(1)}, s32[128,2]{1,0:T(8,128)}, u32[]{:S(2)}) copy-start(s32[128,2]{1,0:T(8,128)} %copy-done) | copy-start | bytes 3076
  139.0 2.1 %collective-permute-start.26 = (f32[2,48,1536]{2,1,0:T(8,128)S(1)}, f32[2,48,1536]{2,1,0:T(8,128)S(1)}, u32[]{:S(2)}, u32[]{:S(2)}) collective-permute-start(f32[2,48,1536]{2,1,0:T(8,128)S(1)} %get-tuple-element.29), channel_id=1, source_target_pairs={{0,16},{16,0},{1,17},{17,1},{2,18},{18,2},{3,19},{19,3},{4,20},{20... | collective-permute-start | bytes 1769480 | tf_op jit(solution)/shard_map/ppermute | solution.py:304
  141.8 4.9 %collective-permute-start.27 = (bf16[32,1536]{1,0:T(8,128)(2,1)S(1)}, bf16[32,1536]{1,0:T(8,128)(2,1)S(1)}, u32[]{:S(2)}, u32[]{:S(2)}) collective-permute-start(bf16[32,1536]{1,0:T(8,128)(2,1)S(1)} %get-tuple-element.26), channel_id=1, source_target_pairs={{0,4},{4,0},{8,12},{12,8},{1,5},{5,1},{9,13},{13,9},{2,6},{6,2},{1... | collective-permute-start | bytes 294920 | tf_op jit(solution)/shard_map/ppermute | solution.py:310
  143.4 5.8 %collective-permute-start.28 = (bf16[32,1536]{1,0:T(8,128)(2,1)S(1)}, bf16[32,1536]{1,0:T(8,128)(2,1)S(1)}, u32[]{:S(2)}, u32[]{:S(2)}) collective-permute-start(bf16[32,1536]{1,0:T(8,128)(2,1)S(1)} %get-tuple-element.27), channel_id=1, source_target_pairs={{0,8},{4,12},{8,0},{12,4},{1,9},{5,13},{9,1},{13,5},{2,10},{6,14},... | collective-permute-start | bytes 294920 | tf_op jit(solution)/shard_map/ppermute | solution.py:310
  144.9 5.5 %collective-permute-start.29 = (bf16[32,1536]{1,0:T(8,128)(2,1)S(1)}, bf16[32,1536]{1,0:T(8,128)(2,1)S(1)}, u32[]{:S(2)}, u32[]{:S(2)}) collective-permute-start(bf16[32,1536]{1,0:T(8,128)(2,1)S(1)} %get-tuple-element.28), channel_id=1, source_target_pairs={{0,12},{4,8},{8,4},{12,0},{1,13},{5,9},{9,5},{13,1},{2,14},{6,10},... | collective-permute-start | bytes 294920 | tf_op jit(solution)/shard_map/ppermute | solution.py:310
  150.5 5.6 %collective-permute-start.30 = (bf16[32,1536]{1,0:T(8,128)(2,1)S(1)}, bf16[32,1536]{1,0:T(8,128)(2,1)S(1)}, u32[]{:S(2)}, u32[]{:S(2)}) collective-permute-start(bf16[32,1536]{1,0:T(8,128)(2,1)S(1)} %add_convert_fusion.8.refs_0_), channel_id=1, source_target_pairs={{0,4},{4,0},{8,12},{12,8},{1,5},{5,1},{9,13},{13,9},{2,6},{6,2},{1... | collective-permute-start | bytes 294920 | tf_op jit(solution)/shard_map/ppermute | solution.py:314
  151.4 5.0 %collective-permute-start.31 = (bf16[32,1536]{1,0:T(8,128)(2,1)S(1)}, bf16[32,1536]{1,0:T(8,128)(2,1)S(1)}, u32[]{:S(2)}, u32[]{:S(2)}) collective-permute-start(bf16[32,1536]{1,0:T(8,128)(2,1)S(1)} %add_convert_fusion.8.refs_0_), channel_id=1, source_target_pairs={{0,8},{4,12},{8,0},{12,4},{1,9},{5,13},{9,1},{13,5},{2,10},{6,14},... | collective-permute-start | bytes 294920 | tf_op jit(solution)/shard_map/ppermute | solution.py:314
  152.3 5.5 %collective-permute-start.32 = (bf16[32,1536]{1,0:T(8,128)(2,1)S(1)}, bf16[32,1536]{1,0:T(8,128)(2,1)S(1)}, u32[]{:S(2)}, u32[]{:S(2)}) collective-permute-start(bf16[32,1536]{1,0:T(8,128)(2,1)S(1)} %add_convert_fusion.8.refs_0_), channel_id=1, source_target_pairs={{0,12},{4,8},{8,4},{12,0},{1,13},{5,9},{9,5},{13,1},{2,14},{6,10},... | collective-permute-start | bytes 294920 | tf_op jit(solution)/shard_map/ppermute | solution.py:314

commit v2 on v0

v2 whole, which is shorter than its diff:
```python
import functools

import jax
import jax.numpy as jnp
from jax import lax
from jax.experimental import pallas as pl
from jax.experimental.pallas import tpu as pltpu
from jax.sharding import PartitionSpec as P

CAP = 48
F32, BF16 = jnp.float32, jnp.bfloat16
MIB = 1024 * 1024

CHUNKS = ((3, "end"), (4, "end"), (4, "end"), (3, "end"), (2, "inner"))

ROUTES = {
    "end": {
        "m0": (0, 1, None), "m1": (1, 2, "m0"), "m2": (2, 3, "m1"),
        "a0": (3, 2, None), "a1": (2, 1, "a0"), "a2": (1, 0, "a1"),
    },
    "inner": {
        "m0": (0, 1, None), "mb": (3, 2, None), "m1": (1, 2, "m0"),
        "a0": (2, 1, None), "a1": (2, 3, None), "a2": (1, 0, "a0"),
    },
}
OWNER = {"end": (3, ("m2",)), "inner": (2, ("m1", "mb"))}
HELD = {"end": ("a2", "a1", "a0", None), "inner": ("a2", "a0", None, "a1")}

ORDER = (
    ("g", 0), ("m0", 0), ("g", 1), ("m0", 1), ("m1", 0), ("g", 2), ("m0", 2), ("m1", 1),
    ("m2", 0), ("g", 3), ("m0", 3), ("m1", 2), ("m2", 1), ("g", 4), ("m0", 4), ("m1", 3),
    ("h", 0), ("a0", 0), ("m2", 2), ("h", 1), ("a0", 1), ("m1", 4), ("mb", 4), ("m2", 3),
    ("a1", 0), ("a1", 1), ("h", 2), ("a0", 2), ("h", 4), ("a0", 4), ("a2", 0), ("a1", 4),
    ("h", 3), ("a0", 3), ("a2", 1), ("a1", 2), ("a2", 4), ("d", 0), ("a1", 3), ("a2", 2),
    ("d", 1), ("a2", 3), ("d", 4), ("d", 2), ("d", 3),
)

SMEM = pl.BlockSpec(memory_space=pltpu.SMEM)
VMEM = pl.BlockSpec(memory_space=pltpu.VMEM)
ANY = pl.BlockSpec(memory_space=pl.ANY)
HBM = pl.BlockSpec(memory_space=pltpu.HBM)


def call(kernel, name, outs, operands, specs, after, scratch=(), aliases=None, limit=42, cost=(0, 0)):
    count = len(operands)

    def body(*refs):
        kernel(*refs[:count], *refs[count + len(after) :])

    return pl.pallas_call(
        body,
        out_shape=outs,
        in_specs=list(specs) + [ANY] * len(after),
        out_specs=jax.tree.map(lambda _: VMEM, outs) if aliases is None else ANY,
        scratch_shapes=list(scratch),
        input_output_aliases=aliases or {},
        cost_estimate=pl.CostEstimate(flops=cost[0], bytes_accessed=cost[1], transcendentals=0),
        compiler_params=pltpu.CompilerParams(vmem_limit_bytes=limit * MIB),
        name=name,
    )(*operands, *after)


def chunk_widths(count):
    unit = 256 if count % 4096 == 0 else 128
    widths, start = [], 0
    for share, _ in CHUNKS:
        widths.append(max(unit, share * count // 16 // unit * unit))
    kept = []
    for width in widths:
        width = min(width, count - start)
        if width:
            kept.append(width)
        start += width
    kept[-1] += count - start
    return kept


def slot_hits(ids, group, local_count):
    tokens, lanes = ids.shape[1], local_count * CAP
    slot = lax.broadcasted_iota(jnp.int32, (lanes, tokens), 0)
    expert = jnp.full((lanes, tokens), group * local_count, jnp.int32)
    for step in range(1, local_count):
        passed = (slot >= CAP).astype(jnp.int32) if step == 1 else passed_next
        expert = expert + passed
        slot = slot - CAP * passed
        passed_next = (slot >= CAP).astype(jnp.int32)
    named = [ids[k : k + 1, :] == expert for k in range(ids.shape[0])]
    member = functools.reduce(jnp.logical_or, named)
    earlier = lax.broadcasted_iota(jnp.int32, (tokens, tokens), 0) < lax.broadcasted_iota(
        jnp.int32, (tokens, tokens), 1
    )
    position = jnp.dot(
        member.astype(F32).astype(BF16),
        earlier.astype(F32).astype(BF16),
        preferred_element_type=F32,
    )
    return member & (position.astype(jnp.int32) == slot), named


def pick(group, ids, tokens, local_count):
    def kernel(group_ref, ids_ref, tokens_ref, out_ref):
        hit, _ = slot_hits(ids_ref[...], group_ref[0], local_count)
        rows = jnp.dot(
            hit.astype(F32).astype(BF16), tokens_ref[...], preferred_element_type=F32
        ).astype(BF16)
        for e in range(local_count):
            out_ref[e] = rows[e * CAP : (e + 1) * CAP]

    shape = jax.ShapeDtypeStruct((local_count, CAP, tokens.shape[1]), BF16)
    return call(kernel, "pick", shape, [group, ids, tokens], [SMEM, VMEM, VMEM], [])


def gate_up(place, rows, weights, start, width, after):
    local_count, _, depth = rows[0].shape
    count = sum(part.shape[1] for part in rows)
    pieces = 3
    block = depth // pieces

    def kernel(place_ref, *refs):
        row_refs = refs[: len(rows)]
        weight_refs, full_ref, short_ref, held, sems = refs[len(rows) : len(rows) + 2], *refs[len(rows) + 2 :]
        copies = []
        for e in range(local_count):
            for i in range(2):
                for k in range(pieces):
                    at = (e * 2 + i) * pieces + k
                    copies.append(
                        pltpu.make_async_copy(
                            weight_refs[i].at[e, pl.ds(k * block, block), pl.ds(start, width)],
                            held.at[at],
                            sems.at[at],
                        )
                    )
        for copy in copies:
            copy.start()
        for e in range(local_count):
            x = jnp.concatenate([ref[e] for ref in row_refs], axis=0)
            for i in range(2):
                total = None
                for k in range(pieces):
                    at = (e * 2 + i) * pieces + k
                    copies[at].wait()
                    part = jnp.dot(
                        x[:, k * block : (k + 1) * block], held[at], preferred_element_type=F32
                    )
                    total = part if total is None else total + part
                full_ref[i, e] = total

                @pl.when(place_ref[0] == 0)
                def _():
                    short_ref[i, e] = total.astype(BF16)

    shape = (2, local_count, count, width)
    slots = 2 * local_count * pieces
    return call(
        kernel,
        "gate_up",
        [jax.ShapeDtypeStruct(shape, F32), jax.ShapeDtypeStruct(shape, BF16)],
        [place, *rows, *weights],
        [SMEM] + [VMEM] * len(rows) + [HBM, HBM],
        after,
        [pltpu.VMEM((slots, block, width), BF16), pltpu.SemaphoreType.DMA((slots,))],
        limit=42,
        cost=(4 * local_count * count * depth * width, 4 * local_count * depth * width),
    )


def add_to_send(place, at, full, got, after):
    def kernel(place_ref, full_ref, got_ref, out_ref):
        @pl.when(place_ref[0] == at)
        def _():
            for e in range(full_ref.shape[1]):
                for i in range(2):
                    out_ref[i, e] = (full_ref[i, e] + got_ref[i, e].astype(F32)).astype(BF16)

    shape = jax.ShapeDtypeStruct(full.shape, BF16)
    return call(kernel, "add_to_send", shape, [place, full, got], [SMEM, VMEM, VMEM], after)


def round_to_send(place, at, full, after):
    def kernel(place_ref, full_ref, out_ref):
        @pl.when(place_ref[0] == at)
        def _():
            out_ref[...] = full_ref[...].astype(BF16)

    shape = jax.ShapeDtypeStruct(full.shape, BF16)
    return call(kernel, "round_to_send", shape, [place, full], [SMEM, VMEM], after)


def hidden_values(place, at, full, got, after):
    def kernel(place_ref, full_ref, *refs):
        got_refs, out_ref = refs[:-1], refs[-1]

        @pl.when(place_ref[0] == at)
        def _():
            for e in range(full_ref.shape[1]):
                gate, up = full_ref[0, e], full_ref[1, e]
                for ref in got_refs:
                    gate, up = gate + ref[0, e].astype(F32), up + ref[1, e].astype(F32)
                out_ref[e] = (gate / (1.0 + jnp.exp(-gate)) * up).astype(BF16)

    shape = jax.ShapeDtypeStruct(full.shape[1:], BF16)
    return call(
        kernel, "hidden_values", shape, [place, full, *got], [SMEM] + [VMEM] * (1 + len(got)), after
    )


def pass_on(value, after):
    def kernel(value_ref, out_ref):
        del value_ref, out_ref

    shape = jax.ShapeDtypeStruct(value.shape, value.dtype)
    return call(kernel, "pass_on", shape, [value], [ANY], after, aliases={0: 0})


def down(place, held, down_weight, start, totals, row_counts, after):
    local_count, count, width = held[0].shape
    features = down_weight.shape[2]
    block = 256 if width % 256 == 0 else 128
    pieces = width // block
    places = len(held)

    def kernel(place_ref, *refs):
        held_refs, weight_ref = refs[:places], refs[places]
        total_refs = refs[places + 1 : places + 1 + len(totals)]
        out_refs = refs[places + 1 + len(totals) :][: len(row_counts)]
        hidden, weights, sems = refs[-3:]
        copies = []
        for e in range(local_count):
            for k in range(pieces):
                at = e * pieces + k
                copies.append(
                    pltpu.make_async_copy(
                        weight_ref.at[e, pl.ds(start + k * block, block), :],
                        weights.at[at],
                        sems.at[at],
                    )
                )
        for copy in copies:
            copy.start()
        for i in range(places):

            @pl.when(place_ref[0] == i)
            def _():
                hidden[...] = held_refs[i][...]

        for e in range(local_count):
            product = None
            for k in range(pieces):
                copies[e * pieces + k].wait()
                part = jnp.dot(
                    hidden[e, :, k * block : (k + 1) * block],
                    weights[e * pieces + k],
                    preferred_element_type=F32,
                )
                product = part if product is None else product + part
            first = 0
            for i, rows in enumerate(row_counts):
                value = product[first : first + rows]
                out_refs[i][e] = total_refs[i][e] + value if totals else value
                first += rows

    shapes = [jax.ShapeDtypeStruct((local_count, rows, features), F32) for rows in row_counts]
    operands = [place, *held, down_weight, *totals]
    return call(
        kernel,
        "down",
        shapes,
        operands,
        [SMEM] + [VMEM] * places + [HBM] + [VMEM] * len(totals),
        after,
        [
            pltpu.VMEM(held[0].shape, BF16),
            pltpu.VMEM((local_count * pieces, block, features), BF16),
            pltpu.SemaphoreType.DMA((local_count * pieces,)),
        ],
        limit=42,
        cost=(2 * local_count * count * features * width, 2 * local_count * features * width),
    )


def combine(group, ids, weights, sums, groups):
    local_count, _, features = sums[0].shape
    tokens = ids.shape[1]
    block = tokens // groups

    def kernel(group_ref, ids_ref, weights_ref, *refs):
        sum_refs, own_ref, sent = refs[: len(sums)], refs[len(sums)], refs[len(sums) + 1 :]
        hit, named = slot_hits(ids_ref[...], group_ref[0], local_count)
        scale = sum(
            jnp.where(named[k], weights_ref[k : k + 1, :], 0.0) for k in range(len(named))
        )
        scale = jnp.where(hit, scale, 0.0)
        scale_high = scale.astype(BF16)
        scale_low = (scale - scale_high.astype(F32)).astype(BF16)
        rows = jnp.concatenate(
            [functools.reduce(jnp.add, [ref[e] for ref in sum_refs]) for e in range(local_count)],
            axis=0,
        )
        rows_high = rows.astype(BF16)
        rows_low = (rows - rows_high.astype(F32)).astype(BF16)

        def product(a, b):
            return lax.dot_general(
                a, b, (((0,), (0,)), ((), ())), preferred_element_type=F32
            )

        mixed = (
            product(scale_high, rows_high)
            + product(scale_high, rows_low)
            + product(scale_low, rows_high)
        )
        for place in range(groups):
            piece = mixed[place * block : (place + 1) * block]
            step = group_ref[0] ^ place

            @pl.when(step == 0)
            def _():
                own_ref[...] = piece

            for other in range(1, groups):

                @pl.when(step == other)
                def _():
                    sent[other - 1][...] = piece.astype(BF16)

    return call(
        kernel,
        "combine",
        [jax.ShapeDtypeStruct((block, features), F32)]
        + [jax.ShapeDtypeStruct((block, features), BF16)] * (groups - 1),
        [group, ids, weights, *sums],
        [SMEM] + [VMEM] * (2 + len(sums)),
        [],
    )


def place_blocks(group, pieces):
    block, features = pieces[0].shape

    def kernel(group_ref, *refs):
        out_ref = refs[-1]
        for step, piece_ref in enumerate(refs[:-1]):
            start = pl.multiple_of((group_ref[0] ^ step) * block, block)
            out_ref[pl.ds(start, block), :] = piece_ref[...]

    shape = jax.ShapeDtypeStruct((block * len(pieces), features), BF16)
    return call(
        kernel, "place_blocks", shape, [group, *pieces], [SMEM] + [VMEM] * len(pieces), []
    )


def local(mesh_shape, tokens, expert_ids, route_weights, gate_weight, up_weight, down_weight):
    shards, groups, line = mesh_shape["dp"], mesh_shape["expert"], mesh_shape["blk"]
    local_count, _, hidden_count = gate_weight.shape
    group = lax.axis_index("expert").astype(jnp.int32).reshape(1)
    line_at = lax.axis_index("blk")
    odd = lax.axis_index("dp") % 2
    place = jnp.where(odd == 1, line - 1 - line_at, line_at).astype(jnp.int32).reshape(1)
    ids, choice_weights = expert_ids.T, route_weights.T
    swap = [(0, 1), (1, 0)]

    def hop(value, source, target):
        pairs = []
        for shard in range(shards):
            ends = (line - 1 - source, line - 1 - target) if shard % 2 else (source, target)
            pairs.append((shard * line + ends[0], shard * line + ends[1]))
        return lax.ppermute(value, ("dp", "blk"), pairs)

    rows = pick(group, ids, tokens, local_count)
    if shards == 2:
        rows = [rows, lax.ppermute(rows, "dp", swap)]
    else:
        rows = [lax.all_gather(rows, "dp", axis=1, tiled=True)]
    row_counts = [part.shape[1] for part in rows]

    widths = chunk_widths(hidden_count)
    starts = [sum(widths[:c]) for c in range(len(widths))]
    full, short, values, got, totals, after = {}, {}, {}, {}, [], []
    for name, c in ORDER:
        if c >= len(widths):
            continue
        kind = CHUNKS[c][1]
        route = ROUTES[kind]
        owner, summed_by = OWNER[kind]
        if name == "g":
            full[c], short[c] = gate_up(
                place, rows, (gate_weight, up_weight), starts[c], widths[c], after
            )
            after = [full[c]]
        elif name == "h":
            values[c] = hidden_values(place, owner, full[c], [got[c, m] for m in summed_by], after)
            after = [values[c]]
        elif name == "d":
            held = [values[c] if m is None else got[c, m] for m in HELD[kind]]
            totals = down(place, held, down_weight, starts[c], totals, row_counts, after)
            after = [totals[0]]
        else:
            source, target, needed = route[name]
            if name == "m0":
                sent = short[c]
            elif name == "mb":
                sent = round_to_send(place, source, full[c], after)
                after = [sent]
            elif name[0] == "m":
                sent = add_to_send(place, source, full[c], got[c, needed], after)
                after = [sent]
            elif needed is None:
                sent = values[c]
            else:
                sent = got[c, needed] = pass_on(got[c, needed], after)
                after = [sent]
            got[c, name] = hop(sent, source, target)

    if shards == 2:
        sums = [totals[0], lax.ppermute(totals[1], "dp", swap)]
    else:
        sums = [lax.psum_scatter(totals[0], "dp", scatter_dimension=1, tiled=True)]
    own, *sent = combine(group, ids, choice_weights, sums, groups)
    for step in range(groups - 1, 0, -1):
        exchange = [(i, i ^ step) for i in range(groups)]
        own = own + lax.ppermute(sent[step - 1], "expert", exchange).astype(F32)
    block = own.astype(BF16)
    pieces = [block]
    for step in range(1, groups):
        pieces.append(lax.ppermute(block, "expert", [(i, i ^ step) for i in range(groups)]))
    return place_blocks(group, pieces)


def solution(mesh):
    placed = (
        P("dp", "blk"),
        P("dp", None),
        P("dp", None),
        P("expert", "blk", "dp"),
        P("expert", "blk", "dp"),
        P("expert", "dp", "blk"),
    )
    return jax.shard_map(
        functools.partial(local, dict(mesh.shape)),
        mesh=mesh,
        in_specs=placed,
        out_specs=P("dp", "blk"),
        check_vma=False,
    )
```

time: 329 us -> 156 us (0.47)
  waiting for transfers between devices: 233 us -> 60.8 us
  starting transfers between devices: 0.04 us -> 53 us
  Pallas kernels: 0 us -> 39 us
  matrix products: 38.3 us -> 0 us
  blocking collectives: 37.2 us -> 0 us
  between operations: 13.5 us -> 0.71 us
  other arithmetic: 4.55 us -> 0.05 us
    psum x1 -> x0, waiting for transfers between devices: 226 us -> none  [local(): summed = lax.psum(partial_value, 'blk')]
    ppermute x0 -> x38, waiting for transfers between devices: none -> 60.8 us  [the longest x30 49 us: hop(): return lax.ppermute(value, ('dp', 'blk'), pairs)]
    ppermute x0 -> x38, starting transfers between devices: none -> 53 us  [the longest x30 45.3 us: hop(): return lax.ppermute(value, ('dp', 'blk'), pairs)]
    pallas_call x0 -> x37, Pallas kernels: none -> 39 us  [call(): pl.pallas_call(body, out_shape=outs, in_specs=list(specs) + [ANY] * len(a...]
    dot_general x5 -> x0, matrix products: 38.3 us -> none  [the longest x1 15.4 us: local(): jnp.einsum('enh,ehd->ned', hidden, down_weight, preferred_element_type=jn...]
    psum x1 -> x0, blocking collectives: 34.9 us -> none  [local(): mixed = lax.psum(mixed_part, 'expert')]
    reduce_scatter x1 -> x0, waiting for transfers between devices: 7.73 us -> none  [local(): lax.psum_scatter(jnp.einsum('enh,ehd->ned', hidden, down_weight, preferre...]
    another operation x3 -> x0, other arithmetic: 3.69 us -> none  [the longest x1 3.07 us: local(): partial_value = jnp.stack([gate_part, up_part])]
  transfers between devices with their start and end apart: 2 -> 38, of which waited for: 2 -> 15; matrix products, arithmetic and copies ran while one was open for 0% -> 0% of each run, Pallas kernels for 0% -> 19%
where the time goes in v2:
time: 156 us; the launch traced here: 155 us
  waiting for transfers between devices  60.8 us (39%)
  starting transfers between devices  53 us (34%)
  Pallas kernels  39 us (25%)
  local copies, waits for them, and re-layouts  1.69 us (1%)
    ppermute x30, waiting for transfers between devices, hop(): return lax.ppermute(value, ('dp', 'blk'), pairs)  49 us
    ppermute x30, starting transfers between devices, hop(): return lax.ppermute(value, ('dp', 'blk'), pairs)  45.3 us
    pallas_call x37, Pallas kernels, call(): pl.pallas_call(body, out_shape=outs, in_specs=list(specs) + [ANY] * len(a...  39 us
    ppermute x3, waiting for transfers between devices, local(): own = own + lax.ppermute(sent[step - 1], 'expert', exchange).astype(F32)  4.41 us
    ppermute x3, waiting for transfers between devices, local(): lax.ppermute(block, 'expert', [(i, i ^ step) for i in range(groups)])  4.24 us
    ppermute x3, starting transfers between devices, local(): lax.ppermute(block, 'expert', [(i, i ^ step) for i in range(groups)])  3.55 us
    ppermute x3, starting transfers between devices, local(): own = own + lax.ppermute(sent[step - 1], 'expert', exchange).astype(F32)  3.55 us
  transfers between devices with their start and end apart: 38, of which 15 were waited for; matrix products, arithmetic and copies ran while one was open for 0% of the time, Pallas kernels for 19%

profile of v2, /device:TPU:0, one launch (start us, length us, event | category | flops | bytes accessed | tf_op | source)
XLA Modules:
  0.0 155.2 jit_solution(2852421413158934794)
XLA Ops:
  0.0 1.0 copy-done
  2.6 1.2 collective-permute-done.refs_2_
  3.8 4.8 %gate_up.5 = (f32[2,2,96,768]{3,2,1,0:T(8,128)S(1)}, bf16[2,2,96,768]{3,2,1,0:T(8,128)(2,1)S(1)}) custom-call(s32[1]{0:T(128)} %bitcast.3.refs_0_, bf16[2,48,1536]{2,1,0:T(8,128)(2,1)S(1)} %pick.1.refs_1_, bf16[2,48,1536]{2,1,0:T(8,128)(2,1)S(1)} %collective-permute-done.refs_2_, bf16[2,1536,4096]{2,1,0:T(8,128)(2,1)} %refs_3_.9, bf16[2,1536,4096]{2,1,0:T(8,128)(2,1)} %refs_4_.9), custom_call_target="tpu_custom_call" | custom-call | flops 905969664 | bytes 9437184 | tf_op jit(solution)/shard_map/gate_up/pallas_call | solution.py:50
  8.6 4.8 %collective-permute-start.1 = (bf16[2,2,96,768]{3,2,1,0:T(8,128)(2,1)S(1)}, bf16[2,2,96,768]{3,2,1,0:T(8,128)(2,1)S(1)}, u32[]{:S(2)}, u32[]{:S(2)}) collective-permute-start(bf16[2,2,96,768]{3,2,1,0:T(8,128)(2,1)S(1)} %get-tuple-element.30), channel_id=1, source_target_pairs={{0,1},{19,18},{4,5},{23,22},{8,9},{27,26},{12,13},{31,30}} | collective-permute-start | bytes 1769480 | tf_op jit(solution)/shard_map/ppermute | solution.py:368
  13.4 5.1 %gate_up.6 = (f32[2,2,96,1024]{3,2,1,0:T(8,128)S(1)}, bf16[2,2,96,1024]{3,2,1,0:T(8,128)(2,1)S(1)}) custom-call(s32[1]{0:T(128)} %bitcast.3.refs_0_, bf16[2,48,1536]{2,1,0:T(8,128)(2,1)S(1)} %pick.1.refs_1_, bf16[2,48,1536]{2,1,0:T(8,128)(2,1)S(1)} %collective-permute-done.refs_2_, bf16[2,1536,4096]{2,1,0:T(8,128)(2,1)} %refs_3_.9, ...), custom_call_target="tpu_custom_call" | custom-call | flops 1207959552 | bytes 12582912 | tf_op jit(solution)/shard_map/gate_up/pallas_call | solution.py:50
  18.6 1.3 collective-permute-start.3
  19.9 0.9 collective-permute-done.1.refs_2_
  20.8 5.1 %gate_up.7 = (f32[2,2,96,1024]{3,2,1,0:T(8,128)S(1)}, bf16[2,2,96,1024]{3,2,1,0:T(8,128)(2,1)S(1)}) custom-call(s32[1]{0:T(128)} %bitcast.3.refs_0_, bf16[2,48,1536]{2,1,0:T(8,128)(2,1)S(1)} %pick.1.refs_1_, bf16[2,48,1536]{2,1,0:T(8,128)(2,1)S(1)} %collective-permute-done.refs_2_, bf16[2,1536,4096]{2,1,0:T(8,128)(2,1)} %refs_3_.9, ...), custom_call_target="tpu_custom_call" | custom-call | flops 1207959552 | bytes 12582912 | tf_op jit(solution)/shard_map/gate_up/pallas_call | solution.py:50
  25.9 4.5 %collective-permute-start.6 = (bf16[2,2,96,1024]{3,2,1,0:T(8,128)(2,1)S(1)}, bf16[2,2,96,1024]{3,2,1,0:T(8,128)(2,1)S(1)}, u32[]{:S(2)}, u32[]{:S(2)}) collective-permute-start(bf16[2,2,96,1024]{3,2,1,0:T(8,128)(2,1)S(1)} %get-tuple-element.36), channel_id=1, source_target_pairs={{0,1},{19,18},{4,5},{23,22},{8,9},{27,26},{12,13},{31,30}} | collective-permute-start | bytes 2359304 | tf_op jit(solution)/shard_map/ppermute | solution.py:368
  30.4 0.7 collective-permute-start.2
  31.2 0.7 collective-permute-start.5
  31.9 4.8 %gate_up.8 = (f32[2,2,96,768]{3,2,1,0:T(8,128)S(1)}, bf16[2,2,96,768]{3,2,1,0:T(8,128)(2,1)S(1)}) custom-call(s32[1]{0:T(128)} %bitcast.3.refs_0_, bf16[2,48,1536]{2,1,0:T(8,128)(2,1)S(1)} %pick.1.refs_1_, bf16[2,48,1536]{2,1,0:T(8,128)(2,1)S(1)} %collective-permute-done.refs_2_, bf16[2,1536,4096]{2,1,0:T(8,128)(2,1)} %refs_3_.9, ...), custom_call_target="tpu_custom_call" | custom-call | flops 905969664 | bytes 9437184 | tf_op jit(solution)/shard_map/gate_up/pallas_call | solution.py:50
  36.7 3.2 %collective-permute-done.6.refs_2_ = bf16[2,2,96,1024]{3,2,1,0:T(8,128)(2,1)S(1)} collective-permute-done((bf16[2,2,96,1024]{3,2,1,0:T(8,128)(2,1)S(1)}, bf16[2,2,96,1024]{3,2,1,0:T(8,128)(2,1)S(1)}, u32[]{:S(2)}, u32[]{:S(2)}) %collective-permute-start.6) | collective-permute-done | bytes 786464 | tf_op jit(solution)/shard_map/ppermute | solution.py:368
  39.9 0.7 collective-permute-start.10
  40.6 9.2 %collective-permute-start.4 = (bf16[2,2,96,768]{3,2,1,0:T(8,128)(2,1)S(1)}, bf16[2,2,96,768]{3,2,1,0:T(8,128)(2,1)S(1)}, u32[]{:S(2)}, u32[]{:S(2)}) collective-permute-start(bf16[2,2,96,768]{3,2,1,0:T(8,128)(2,1)S(1)} %get-tuple-element.35), channel_id=1, source_target_pairs={{0,1},{19,18},{4,5},{23,22},{8,9},{27,26},{12,13},{31,30}} | collective-permute-start | bytes 1769480 | tf_op jit(solution)/shard_map/ppermute | solution.py:368
  49.8 0.7 collective-permute-start.11
  50.5 0.7 collective-permute-start.9
  51.2 3.3 %gate_up.9 = (f32[2,2,96,512]{3,2,1,0:T(8,128)S(1)}, bf16[2,2,96,512]{3,2,1,0:T(8,128)(2,1)S(1)}) custom-call(s32[1]{0:T(128)} %bitcast.3.refs_0_, bf16[2,48,1536]{2,1,0:T(8,128)(2,1)S(1)} %pick.1.refs_1_, bf16[2,48,1536]{2,1,0:T(8,128)(2,1)S(1)} %collective-permute-done.refs_2_, bf16[2,1536,4096]{2,1,0:T(8,128)(2,1)} %refs_3_.9, ...), custom_call_target="tpu_custom_call" | custom-call | flops 603979776 | bytes 6291456 | tf_op jit(solution)/shard_map/gate_up/pallas_call | solution.py:50
  54.5 2.6 %collective-permute-done.4.refs_2_ = bf16[2,2,96,768]{3,2,1,0:T(8,128)(2,1)S(1)} collective-permute-done((bf16[2,2,96,768]{3,2,1,0:T(8,128)(2,1)S(1)}, bf16[2,2,96,768]{3,2,1,0:T(8,128)(2,1)S(1)}, u32[]{:S(2)}, u32[]{:S(2)}) %collective-permute-start.4) | collective-permute-done | bytes 589856 | tf_op jit(solution)/shard_map/ppermute | solution.py:368
  57.1 0.7 collective-permute-start.7
  57.9 0.7 collective-permute-start.17
  58.6 5.2 %collective-permute-start.8 = (bf16[2,2,96,512]{3,2,1,0:T(8,128)(2,1)S(1)}, bf16[2,2,96,512]{3,2,1,0:T(8,128)(2,1)S(1)}, u32[]{:S(2)}, u32[]{:S(2)}) collective-permute-start(bf16[2,2,96,512]{3,2,1,0:T(8,128)(2,1)S(1)} %get-tuple-element.38), channel_id=1, source_target_pairs={{0,1},{19,18},{4,5},{23,22},{8,9},{27,26},{12,13},{31,30}} | collective-permute-start | bytes 1179656 | tf_op jit(solution)/shard_map/ppermute | solution.py:368
  63.8 0.7 collective-permute-start.18
  65.1 8.1 %collective-permute-done.8.refs_2_ = bf16[2,2,96,512]{3,2,1,0:T(8,128)(2,1)S(1)} collective-permute-done((bf16[2,2,96,512]{3,2,1,0:T(8,128)(2,1)S(1)}, bf16[2,2,96,512]{3,2,1,0:T(8,128)(2,1)S(1)}, u32[]{:S(2)}, u32[]{:S(2)}) %collective-permute-start.8) | collective-permute-done | bytes 393248 | tf_op jit(solution)/shard_map/ppermute | solution.py:368
  73.9 0.7 collective-permute-start.12
  77.5 1.3 collective-permute-start.20
  80.9 1.3 collective-permute-start.25
  82.3 18.1 %collective-permute-done.20.refs_1_ = bf16[2,96,768]{2,1,0:T(8,128)(2,1)S(1)} collective-permute-done((bf16[2,96,768]{2,1,0:T(8,128)(2,1)S(1)}, bf16[2,96,768]{2,1,0:T(8,128)(2,1)S(1)}, u32[]{:S(2)}, u32[]{:S(2)}) %collective-permute-start.20) | collective-permute-done | bytes 294944 | tf_op jit(solution)/shard_map/ppermute | solution.py:368
  100.4 2.7 %down.5 = (f32[2,48,1536]{2,1,0:T(8,128)S(1)}, f32[2,48,1536]{2,1,0:T(8,128)S(1)}) custom-call(s32[1]{0:T(128)} %bitcast.3.refs_0_, bf16[2,96,768]{2,1,0:T(8,128)(2,1)S(1)} %collective-permute-done.20.refs_1_, bf16[2,96,768]{2,1,0:T(8,128)(2,1)S(1)} %pass_on.11.refs_3_.refs_2_, bf16[2,96,768]{2,1,0:T(8,128)(2,1)S(1)} %pass_on.9.refs_1_.refs_3_, ...), custom_call_target="tpu_custom_call" | custom-call | flops 452984832 | bytes 4718592 | tf_op jit(solution)/shard_map/down/pallas_call | solution.py:50
  103.8 1.3 collective-permute-start.28
  105.1 1.0 collective-permute-done.25.refs_1_
  106.1 3.1 %down.6 = (f32[2,48,1536]{2,1,0:T(8,128)S(1)}, f32[2,48,1536]{2,1,0:T(8,128)S(1)}) custom-call(s32[1]{0:T(128)} %bitcast.3.refs_0_, bf16[2,96,1024]{2,1,0:T(8,128)(2,1)S(1)} %collective-permute-done.25.refs_1_, bf16[2,96,1024]{2,1,0:T(8,128)(2,1)S(1)} %pass_on.12.refs_1_.refs_2_, bf16[2,96,1024]{2,1,0:T(8,128)(2,1)S(1)} %pass_on.10.refs_3_, ...), custom_call_target="tpu_custom_call" | custom-call | flops 603979776 | bytes 6291456 | tf_op jit(solution)/shard_map/down/pallas_call | solution.py:50
  109.3 1.3 collective-permute-start.27
  111.3 1.3 collective-permute-start.29
  112.6 15.1 %collective-permute-done.29.refs_1_ = bf16[2,96,512]{2,1,0:T(8,128)(2,1)S(1)} collective-permute-done((bf16[2,96,512]{2,1,0:T(8,128)(2,1)S(1)}, bf16[2,96,512]{2,1,0:T(8,128)(2,1)S(1)}, u32[]{:S(2)}, u32[]{:S(2)}) %collective-permute-start.29) | collective-permute-done | bytes 196640 | tf_op jit(solution)/shard_map/ppermute | solution.py:368
  127.7 2.3 %down.7 = (f32[2,48,1536]{2,1,0:T(8,128)S(1)}, f32[2,48,1536]{2,1,0:T(8,128)S(1)}) custom-call(s32[1]{0:T(128)} %bitcast.3.refs_0_, bf16[2,96,512]{2,1,0:T(8,128)(2,1)S(1)} %collective-permute-done.29.refs_1_, bf16[2,96,512]{2,1,0:T(8,128)(2,1)S(1)} %pass_on.14.refs_6_.refs_2_, bf16[2,96,512]{2,1,0:T(8,128)(2,1)S(1)} %hidden_values.8.refs_1_.refs_3_, ...), custom_call_target="tpu_custom_call" | custom-call | flops 301989888 | bytes 3145728 | tf_op jit(solution)/shard_map/down/pallas_call | solution.py:50
  130.0 3.1 %down.8 = (f32[2,48,1536]{2,1,0:T(8,128)S(1)}, f32[2,48,1536]{2,1,0:T(8,128)S(1)}) custom-call(s32[1]{0:T(128)} %bitcast.3.refs_0_, bf16[2,96,1024]{2,1,0:T(8,128)(2,1)S(1)} %collective-permute-done.28.refs_1_, bf16[2,96,1024]{2,1,0:T(8,128)(2,1)S(1)} %pass_on.16.refs_8_.refs_2_, bf16[2,96,1024]{2,1,0:T(8,128)(2,1)S(1)} %pass_on.13.refs_1_.refs_3_, ...), custom_call_target="tpu_custom_call" | custom-call | flops 603979776 | bytes 6291456 | tf_op jit(solution)/shard_map/down/pallas_call | solution.py:50
  133.1 2.7 %down.9 = (f32[2,48,1536]{2,1,0:T(8,128)S(1)}, f32[2,48,1536]{2,1,0:T(8,128)S(1)}) custom-call(s32[1]{0:T(128)} %bitcast.3.refs_0_, bf16[2,96,768]{2,1,0:T(8,128)(2,1)S(1)} %collective-permute-done.27.refs_1_, bf16[2,96,768]{2,1,0:T(8,128)(2,1)S(1)} %pass_on.17.refs_8_.refs_2_, bf16[2,96,768]{2,1,0:T(8,128)(2,1)S(1)} %pass_on.15.refs_1_.refs_3_, ...), custom_call_target="tpu_custom_call" | custom-call | flops 452984832 | bytes 4718592 | tf_op jit(solution)/shard_map/down/pallas_call | solution.py:50
  135.9 2.0 %collective-permute-done.31.refs_4_ = f32[2,48,1536]{2,1,0:T(8,128)S(1)} collective-permute-done((f32[2,48,1536]{2,1,0:T(8,128)S(1)}, f32[2,48,1536]{2,1,0:T(8,128)S(1)}, u32[]{:S(2)}, u32[]{:S(2)}) %collective-permute-start.31) | collective-permute-done | bytes 589856 | tf_op jit(solution)/shard_map/ppermute | solution.py:416
  137.9 0.7 combine.1
  138.7 2.5 %collective-permute-start.32 = (bf16[32,1536]{1,0:T(8,128)(2,1)S(1)}, bf16[32,1536]{1,0:T(8,128)(2,1)S(1)}, u32[]{:S(2)}, u32[]{:S(2)}) collective-permute-start(bf16[32,1536]{1,0:T(8,128)(2,1)S(1)} %get-tuple-element.50), channel_id=1, source_target_pairs={{0,12},{4,8},{8,4},{12,0},{1,13},{5,9},{9,5},{13,1},{2,14},{6,10},... | collective-permute-start | bytes 294920 | tf_op jit(solution)/shard_map/ppermute | solution.py:422
  142.2 2.3 %collective-permute-done.32 = bf16[32,1536]{1,0:T(8,128)(2,1)S(1)} collective-permute-done((bf16[32,1536]{1,0:T(8,128)(2,1)S(1)}, bf16[32,1536]{1,0:T(8,128)(2,1)S(1)}, u32[]{:S(2)}, u32[]{:S(2)}) %collective-permute-start.32) | collective-permute-done | bytes 98336 | tf_op jit(solution)/shard_map/ppermute | solution.py:422
  144.5 2.0 %collective-permute-done.33 = bf16[32,1536]{1,0:T(8,128)(2,1)S(1)} collective-permute-done((bf16[32,1536]{1,0:T(8,128)(2,1)S(1)}, bf16[32,1536]{1,0:T(8,128)(2,1)S(1)}, u32[]{:S(2)}, u32[]{:S(2)}) %collective-permute-start.33) | collective-permute-done | bytes 98336 | tf_op jit(solution)/shard_map/ppermute | solution.py:422
  146.7 1.8 %collective-permute-start.37 = (bf16[32,1536]{1,0:T(8,128)(2,1)S(1)}, bf16[32,1536]{1,0:T(8,128)(2,1)S(1)}, u32[]{:S(2)}, u32[]{:S(2)}) collective-permute-start(bf16[32,1536]{1,0:T(8,128)(2,1)S(1)} %add_convert_fusion.refs_1_), channel_id=1, source_target_pairs={{0,12},{4,8},{8,4},{12,0},{1,13},{5,9},{9,5},{13,1},{2,14},{6,10},... | collective-permute-start | bytes 294920 | tf_op jit(solution)/shard_map/ppermute | solution.py:426
  148.4 1.3 collective-permute-start.36
  150.2 2.8 %collective-permute-done.37.refs_4_ = bf16[32,1536]{1,0:T(8,128)(2,1)S(1)} collective-permute-done((bf16[32,1536]{1,0:T(8,128)(2,1)S(1)}, bf16[32,1536]{1,0:T(8,128)(2,1)S(1)}, u32[]{:S(2)}, u32[]{:S(2)}) %collective-permute-start.37) | collective-permute-done | bytes 98336 | tf_op jit(solution)/shard_map/ppermute | solution.py:426
  153.1 1.2 collective-permute-done.36.refs_3_
  154.5 0.8 place_blocks.1
  (74 shorter events, 11.2 us)
Async XLA Ops:
  0.0 1.0 copy-start
  1.0 0.7 copy-start.1
  2.0 1.7 %collective-permute-start = (bf16[2,48,1536]{2,1,0:T(8,128)(2,1)S(1)}, bf16[2,48,1536]{2,1,0:T(8,128)(2,1)S(1)}, u32[]{:S(2)}, u32[]{:S(2)}) collective-permute-start(bf16[2,48,1536]{2,1,0:T(8,128)(2,1)S(1)} %pick.1.refs_1_), channel_id=1, source_target_pairs={{0,16},{16,0},{1,17},{17,1},{2,18},{18,2},{3,19},{19,3},{4,20},{20... | collective-permute-start | bytes 884744 | tf_op jit(solution)/shard_map/ppermute | solution.py:372
  8.6 12.2 %collective-permute-start.1 = (bf16[2,2,96,768]{3,2,1,0:T(8,128)(2,1)S(1)}, bf16[2,2,96,768]{3,2,1,0:T(8,128)(2,1)S(1)}, u32[]{:S(2)}, u32[]{:S(2)}) collective-permute-start(bf16[2,2,96,768]{3,2,1,0:T(8,128)(2,1)S(1)} %get-tuple-element.30), channel_id=1, source_target_pairs={{0,1},{19,18},{4,5},{23,22},{8,9},{27,26},{12,13},{31,30}} | collective-permute-start | bytes 1769480 | tf_op jit(solution)/shard_map/ppermute | solution.py:368
  18.6 12.6 %collective-permute-start.3 = (bf16[2,2,96,1024]{3,2,1,0:T(8,128)(2,1)S(1)}, bf16[2,2,96,1024]{3,2,1,0:T(8,128)(2,1)S(1)}, u32[]{:S(2)}, u32[]{:S(2)}) collective-permute-start(bf16[2,2,96,1024]{3,2,1,0:T(8,128)(2,1)S(1)} %get-tuple-element.32), channel_id=1, source_target_pairs={{0,1},{19,18},{4,5},{23,22},{8,9},{27,26},{12,13},{31,30}} | collective-permute-start | bytes 2359304 | tf_op jit(solution)/shard_map/ppermute | solution.py:368
  25.9 14.0 %collective-permute-start.6 = (bf16[2,2,96,1024]{3,2,1,0:T(8,128)(2,1)S(1)}, bf16[2,2,96,1024]{3,2,1,0:T(8,128)(2,1)S(1)}, u32[]{:S(2)}, u32[]{:S(2)}) collective-permute-start(bf16[2,2,96,1024]{3,2,1,0:T(8,128)(2,1)S(1)} %get-tuple-element.36), channel_id=1, source_target_pairs={{0,1},{19,18},{4,5},{23,22},{8,9},{27,26},{12,13},{31,30}} | collective-permute-start | bytes 2359304 | tf_op jit(solution)/shard_map/ppermute | solution.py:368
  30.4 1.5 collective-permute-start.2
  31.2 19.3 %collective-permute-start.5 = (bf16[2,2,96,1024]{3,2,1,0:T(8,128)(2,1)S(1)}, bf16[2,2,96,1024]{3,2,1,0:T(8,128)(2,1)S(1)}, u32[]{:S(2)}, u32[]{:S(2)}) collective-permute-start(bf16[2,2,96,1024]{3,2,1,0:T(8,128)(2,1)S(1)} %add_to_send.10.refs_3_), channel_id=1, source_target_pairs={{1,2},{18,17},{5,6},{22,21},{9,10},{26,25},{13,14},{30,29}} | collective-permute-start | bytes 2359304 | tf_op jit(solution)/shard_map/ppermute | solution.py:368
  39.9 17.9 %collective-permute-start.10 = (bf16[2,2,96,1024]{3,2,1,0:T(8,128)(2,1)S(1)}, bf16[2,2,96,1024]{3,2,1,0:T(8,128)(2,1)S(1)}, u32[]{:S(2)}, u32[]{:S(2)}) collective-permute-start(bf16[2,2,96,1024]{3,2,1,0:T(8,128)(2,1)S(1)} %add_to_send.12.refs_3_), channel_id=1, source_target_pairs={{1,2},{18,17},{5,6},{22,21},{9,10},{26,25},{13,14},{30,29}} | collective-permute-start | bytes 2359304 | tf_op jit(solution)/shard_map/ppermute | solution.py:368
  40.6 16.5 %collective-permute-start.4 = (bf16[2,2,96,768]{3,2,1,0:T(8,128)(2,1)S(1)}, bf16[2,2,96,768]{3,2,1,0:T(8,128)(2,1)S(1)}, u32[]{:S(2)}, u32[]{:S(2)}) collective-permute-start(bf16[2,2,96,768]{3,2,1,0:T(8,128)(2,1)S(1)} %get-tuple-element.35), channel_id=1, source_target_pairs={{0,1},{19,18},{4,5},{23,22},{8,9},{27,26},{12,13},{31,30}} | collective-permute-start | bytes 1769480 | tf_op jit(solution)/shard_map/ppermute | solution.py:368
  49.8 8.0 %collective-permute-start.11 = (bf16[2,2,96,768]{3,2,1,0:T(8,128)(2,1)S(1)}, bf16[2,2,96,768]{3,2,1,0:T(8,128)(2,1)S(1)}, u32[]{:S(2)}, u32[]{:S(2)}) collective-permute-start(bf16[2,2,96,768]{3,2,1,0:T(8,128)(2,1)S(1)} %add_to_send.11.refs_5_), channel_id=1, source_target_pairs={{2,3},{17,16},{6,7},{21,20},{10,11},{25,24},{14,15},{29,28}} | collective-permute-start | bytes 1769480 | tf_op jit(solution)/shard_map/ppermute | solution.py:368
  50.5 13.2 %collective-permute-start.9 = (bf16[2,2,96,1024]{3,2,1,0:T(8,128)(2,1)S(1)}, bf16[2,2,96,1024]{3,2,1,0:T(8,128)(2,1)S(1)}, u32[]{:S(2)}, u32[]{:S(2)}) collective-permute-start(bf16[2,2,96,1024]{3,2,1,0:T(8,128)(2,1)S(1)} %add_to_send.13.refs_5_), channel_id=1, source_target_pairs={{2,3},{17,16},{6,7},{21,20},{10,11},{25,24},{14,15},{29,28}} | collective-permute-start | bytes 2359304 | tf_op jit(solution)/shard_map/ppermute | solution.py:368
  57.1 16.8 %collective-permute-start.7 = (bf16[2,2,96,768]{3,2,1,0:T(8,128)(2,1)S(1)}, bf16[2,2,96,768]{3,2,1,0:T(8,128)(2,1)S(1)}, u32[]{:S(2)}, u32[]{:S(2)}) collective-permute-start(bf16[2,2,96,768]{3,2,1,0:T(8,128)(2,1)S(1)} %add_to_send.14.refs_3_), channel_id=1, source_target_pairs={{1,2},{18,17},{5,6},{22,21},{9,10},{26,25},{13,14},{30,29}} | collective-permute-start | bytes 1769480 | tf_op jit(solution)/shard_map/ppermute | solution.py:368
  57.9 18.2 %collective-permute-start.17 = (bf16[2,2,96,1024]{3,2,1,0:T(8,128)(2,1)S(1)}, bf16[2,2,96,1024]{3,2,1,0:T(8,128)(2,1)S(1)}, u32[]{:S(2)}, u32[]{:S(2)}) collective-permute-start(bf16[2,2,96,1024]{3,2,1,0:T(8,128)(2,1)S(1)} %add_to_send.15.refs_3_), channel_id=1, source_target_pairs={{2,3},{17,16},{6,7},{21,20},{10,11},{25,24},{14,15},{29,28}} | collective-permute-start | bytes 2359304 | tf_op jit(solution)/shard_map/ppermute | solution.py:368
  58.6 14.6 %collective-permute-start.8 = (bf16[2,2,96,512]{3,2,1,0:T(8,128)(2,1)S(1)}, bf16[2,2,96,512]{3,2,1,0:T(8,128)(2,1)S(1)}, u32[]{:S(2)}, u32[]{:S(2)}) collective-permute-start(bf16[2,2,96,512]{3,2,1,0:T(8,128)(2,1)S(1)} %get-tuple-element.38), channel_id=1, source_target_pairs={{0,1},{19,18},{4,5},{23,22},{8,9},{27,26},{12,13},{31,30}} | collective-permute-start | bytes 1179656 | tf_op jit(solution)/shard_map/ppermute | solution.py:368
  63.8 11.6 %collective-permute-start.18 = (bf16[2,96,1024]{2,1,0:T(8,128)(2,1)S(1)}, bf16[2,96,1024]{2,1,0:T(8,128)(2,1)S(1)}, u32[]{:S(2)}, u32[]{:S(2)}) collective-permute-start(bf16[2,96,1024]{2,1,0:T(8,128)(2,1)S(1)} %hidden_values.6.refs_3_.refs_4_), channel_id=1, source_target_pairs={{3,2},{16,17},{7,6},{20,21},{11,10},{24,25},{15,14},{28,29}} | collective-permute-start | bytes 1179656 | tf_op jit(solution)/shard_map/ppermute | solution.py:368
  64.5 10.2 %collective-permute-start.13 = (bf16[2,96,768]{2,1,0:T(8,128)(2,1)S(1)}, bf16[2,96,768]{2,1,0:T(8,128)(2,1)S(1)}, u32[]{:S(2)}, u32[]{:S(2)}) collective-permute-start(bf16[2,96,768]{2,1,0:T(8,128)(2,1)S(1)} %hidden_values.5.refs_3_.refs_4_), channel_id=1, source_target_pairs={{3,2},{16,17},{7,6},{20,21},{11,10},{24,25},{15,14},{28,29}} | collective-permute-start | bytes 884744 | tf_op jit(solution)/shard_map/ppermute | solution.py:368
  73.2 3.6 %collective-permute-start.16 = (bf16[2,2,96,512]{3,2,1,0:T(8,128)(2,1)S(1)}, bf16[2,2,96,512]{3,2,1,0:T(8,128)(2,1)S(1)}, u32[]{:S(2)}, u32[]{:S(2)}) collective-permute-start(bf16[2,2,96,512]{3,2,1,0:T(8,128)(2,1)S(1)} %round_to_send.1.refs_3_), channel_id=1, source_target_pairs={{3,2},{16,17},{7,6},{20,21},{11,10},{24,25},{15,14},{28,29}} | collective-permute-start | bytes 1179656 | tf_op jit(solution)/shard_map/ppermute | solution.py:368
  73.9 4.9 %collective-permute-start.12 = (bf16[2,2,96,768]{3,2,1,0:T(8,128)(2,1)S(1)}, bf16[2,2,96,768]{3,2,1,0:T(8,128)(2,1)S(1)}, u32[]{:S(2)}, u32[]{:S(2)}) collective-permute-start(bf16[2,2,96,768]{3,2,1,0:T(8,128)(2,1)S(1)} %add_to_send.17.refs_1_), channel_id=1, source_target_pairs={{2,3},{17,16},{6,7},{21,20},{10,11},{25,24},{14,15},{29,28}} | collective-permute-start | bytes 1769480 | tf_op jit(solution)/shard_map/ppermute | solution.py:368
  74.6 2.8 %collective-permute-start.15 = (bf16[2,2,96,512]{3,2,1,0:T(8,128)(2,1)S(1)}, bf16[2,2,96,512]{3,2,1,0:T(8,128)(2,1)S(1)}, u32[]{:S(2)}, u32[]{:S(2)}) collective-permute-start(bf16[2,2,96,512]{3,2,1,0:T(8,128)(2,1)S(1)} %add_to_send.16.refs_2_), channel_id=1, source_target_pairs={{1,2},{18,17},{5,6},{22,21},{9,10},{26,25},{13,14},{30,29}} | collective-permute-start | bytes 1179656 | tf_op jit(solution)/shard_map/ppermute | solution.py:368
  75.3 4.2 %collective-permute-start.23 = (bf16[2,96,1024]{2,1,0:T(8,128)(2,1)S(1)}, bf16[2,96,1024]{2,1,0:T(8,128)(2,1)S(1)}, u32[]{:S(2)}, u32[]{:S(2)}) collective-permute-start(bf16[2,96,1024]{2,1,0:T(8,128)(2,1)S(1)} %pass_on.10.refs_3_), channel_id=1, source_target_pairs={{2,1},{17,18},{6,5},{21,22},{10,9},{25,26},{14,13},{29,30}} | collective-permute-start | bytes 1179656 | tf_op jit(solution)/shard_map/ppermute | solution.py:368
  76.1 3.5 %collective-permute-start.22 = (bf16[2,96,1024]{2,1,0:T(8,128)(2,1)S(1)}, bf16[2,96,1024]{2,1,0:T(8,128)(2,1)S(1)}, u32[]{:S(2)}, u32[]{:S(2)}) collective-permute-start(bf16[2,96,1024]{2,1,0:T(8,128)(2,1)S(1)} %hidden_values.7.refs_4_), channel_id=1, source_target_pairs={{3,2},{16,17},{7,6},{20,21},{11,10},{24,25},{15,14},{28,29}} | collective-permute-start | bytes 1179656 | tf_op jit(solution)/shard_map/ppermute | solution.py:368
  76.8 0.7 collective-permute-start.14
  77.5 22.9 %collective-permute-start.20 = (bf16[2,96,768]{2,1,0:T(8,128)(2,1)S(1)}, bf16[2,96,768]{2,1,0:T(8,128)(2,1)S(1)}, u32[]{:S(2)}, u32[]{:S(2)}) collective-permute-start(bf16[2,96,768]{2,1,0:T(8,128)(2,1)S(1)} %pass_on.11.refs_3_.refs_2_), channel_id=1, source_target_pairs={{1,0},{18,19},{5,4},{22,23},{9,8},{26,27},{13,12},{30,31}} | collective-permute-start | bytes 884744 | tf_op jit(solution)/shard_map/ppermute | solution.py:368
  78.8 24.3 %collective-permute-start.19 = (bf16[2,96,768]{2,1,0:T(8,128)(2,1)S(1)}, bf16[2,96,768]{2,1,0:T(8,128)(2,1)S(1)}, u32[]{:S(2)}, u32[]{:S(2)}) collective-permute-start(bf16[2,96,768]{2,1,0:T(8,128)(2,1)S(1)} %hidden_values.9.refs_1_.refs_4_), channel_id=1, source_target_pairs={{3,2},{16,17},{7,6},{20,21},{11,10},{24,25},{15,14},{28,29}} | collective-permute-start | bytes 884744 | tf_op jit(solution)/shard_map/ppermute | solution.py:368
  79.6 24.2 %collective-permute-start.26 = (bf16[2,96,1024]{2,1,0:T(8,128)(2,1)S(1)}, bf16[2,96,1024]{2,1,0:T(8,128)(2,1)S(1)}, u32[]{:S(2)}, u32[]{:S(2)}) collective-permute-start(bf16[2,96,1024]{2,1,0:T(8,128)(2,1)S(1)} %pass_on.13.refs_1_.refs_3_), channel_id=1, source_target_pairs={{2,1},{17,18},{6,5},{21,22},{10,9},{25,26},{14,13},{29,30}} | collective-permute-start | bytes 1179656 | tf_op jit(solution)/shard_map/ppermute | solution.py:368
  80.3 2.0 %collective-permute-start.21 = (bf16[2,96,512]{2,1,0:T(8,128)(2,1)S(1)}, bf16[2,96,512]{2,1,0:T(8,128)(2,1)S(1)}, u32[]{:S(2)}, u32[]{:S(2)}) collective-permute-start(bf16[2,96,512]{2,1,0:T(8,128)(2,1)S(1)} %hidden_values.8.refs_1_.refs_3_), channel_id=1, source_target_pairs={{2,1},{17,18},{6,5},{21,22},{10,9},{25,26},{14,13},{29,30}} | collective-permute-start | bytes 589832 | tf_op jit(solution)/shard_map/ppermute | solution.py:368
  80.9 25.2 %collective-permute-start.25 = (bf16[2,96,1024]{2,1,0:T(8,128)(2,1)S(1)}, bf16[2,96,1024]{2,1,0:T(8,128)(2,1)S(1)}, u32[]{:S(2)}, u32[]{:S(2)}) collective-permute-start(bf16[2,96,1024]{2,1,0:T(8,128)(2,1)S(1)} %pass_on.12.refs_1_.refs_2_), channel_id=1, source_target_pairs={{1,0},{18,19},{5,4},{22,23},{9,8},{26,27},{13,12},{30,31}} | collective-permute-start | bytes 1179656 | tf_op jit(solution)/shard_map/ppermute | solution.py:368
  103.1 6.2 %collective-permute-start.24 = (bf16[2,96,768]{2,1,0:T(8,128)(2,1)S(1)}, bf16[2,96,768]{2,1,0:T(8,128)(2,1)S(1)}, u32[]{:S(2)}, u32[]{:S(2)}) collective-permute-start(bf16[2,96,768]{2,1,0:T(8,128)(2,1)S(1)} %pass_on.15.refs_1_.refs_3_), channel_id=1, source_target_pairs={{2,1},{17,18},{6,5},{21,22},{10,9},{25,26},{14,13},{29,30}} | collective-permute-start | bytes 884744 | tf_op jit(solution)/shard_map/ppermute | solution.py:368
  103.8 26.1 %collective-permute-start.28 = (bf16[2,96,1024]{2,1,0:T(8,128)(2,1)S(1)}, bf16[2,96,1024]{2,1,0:T(8,128)(2,1)S(1)}, u32[]{:S(2)}, u32[]{:S(2)}) collective-permute-start(bf16[2,96,1024]{2,1,0:T(8,128)(2,1)S(1)} %pass_on.16.refs_8_.refs_2_), channel_id=1, source_target_pairs={{1,0},{18,19},{5,4},{22,23},{9,8},{26,27},{13,12},{30,31}} | collective-permute-start | bytes 1179656 | tf_op jit(solution)/shard_map/ppermute | solution.py:368
  109.3 23.8 %collective-permute-start.27 = (bf16[2,96,768]{2,1,0:T(8,128)(2,1)S(1)}, bf16[2,96,768]{2,1,0:T(8,128)(2,1)S(1)}, u32[]{:S(2)}, u32[]{:S(2)}) collective-permute-start(bf16[2,96,768]{2,1,0:T(8,128)(2,1)S(1)} %pass_on.17.refs_8_.refs_2_), channel_id=1, source_target_pairs={{1,0},{18,19},{5,4},{22,23},{9,8},{26,27},{13,12},{30,31}} | collective-permute-start | bytes 884744 | tf_op jit(solution)/shard_map/ppermute | solution.py:368
  110.6 2.0 %collective-permute-start.30 = (bf16[2,96,512]{2,1,0:T(8,128)(2,1)S(1)}, bf16[2,96,512]{2,1,0:T(8,128)(2,1)S(1)}, u32[]{:S(2)}, u32[]{:S(2)}) collective-permute-start(bf16[2,96,512]{2,1,0:T(8,128)(2,1)S(1)} %hidden_values.8.refs_1_.refs_3_), channel_id=1, source_target_pairs={{2,3},{17,16},{6,7},{21,20},{10,11},{25,24},{14,15},{29,28}} | collective-permute-start | bytes 589832 | tf_op jit(solution)/shard_map/ppermute | solution.py:368
  111.3 16.4 %collective-permute-start.29 = (bf16[2,96,512]{2,1,0:T(8,128)(2,1)S(1)}, bf16[2,96,512]{2,1,0:T(8,128)(2,1)S(1)}, u32[]{:S(2)}, u32[]{:S(2)}) collective-permute-start(bf16[2,96,512]{2,1,0:T(8,128)(2,1)S(1)} %pass_on.14.refs_6_.refs_2_), channel_id=1, source_target_pairs={{1,0},{18,19},{5,4},{22,23},{9,8},{26,27},{13,12},{30,31}} | collective-permute-start | bytes 589832 | tf_op jit(solution)/shard_map/ppermute | solution.py:368
  133.1 4.8 %copy-start.2 = (s32[128,2]{0,1:T(2,128)S(1)}, s32[128,2]{0,1:T(2,128)}, u32[]{:S(2)}) copy-start(s32[128,2]{0,1:T(2,128)} %param.7) | copy-start | bytes 3076
  133.1 4.8 %copy-start.3 = (f32[128,2]{0,1:T(2,128)S(1)}, f32[128,2]{0,1:T(2,128)}, u32[]{:S(2)}) copy-start(f32[128,2]{0,1:T(2,128)} %param.8) | copy-start | bytes 3076
  135.8 2.1 %collective-permute-start.31 = (f32[2,48,1536]{2,1,0:T(8,128)S(1)}, f32[2,48,1536]{2,1,0:T(8,128)S(1)}, u32[]{:S(2)}, u32[]{:S(2)}) collective-permute-start(f32[2,48,1536]{2,1,0:T(8,128)S(1)} %get-tuple-element.48), channel_id=1, source_target_pairs={{0,16},{16,0},{1,17},{17,1},{2,18},{18,2},{3,19},{19,3},{4,20},{20... | collective-permute-start | bytes 1769480 | tf_op jit(solution)/shard_map/ppermute | solution.py:416
  138.7 5.9 %collective-permute-start.32 = (bf16[32,1536]{1,0:T(8,128)(2,1)S(1)}, bf16[32,1536]{1,0:T(8,128)(2,1)S(1)}, u32[]{:S(2)}, u32[]{:S(2)}) collective-permute-start(bf16[32,1536]{1,0:T(8,128)(2,1)S(1)} %get-tuple-element.50), channel_id=1, source_target_pairs={{0,12},{4,8},{8,4},{12,0},{1,13},{5,9},{9,5},{13,1},{2,14},{6,10},... | collective-permute-start | bytes 294920 | tf_op jit(solution)/shard_map/ppermute | solution.py:422
  141.2 5.4 %collective-permute-start.33 = (bf16[32,1536]{1,0:T(8,128)(2,1)S(1)}, bf16[32,1536]{1,0:T(8,128)(2,1)S(1)}, u32[]{:S(2)}, u32[]{:S(2)}) collective-permute-start(bf16[32,1536]{1,0:T(8,128)(2,1)S(1)} %get-tuple-element.51), channel_id=1, source_target_pairs={{0,8},{4,12},{8,0},{12,4},{1,9},{5,13},{9,1},{13,5},{2,10},{6,14},... | collective-permute-start | bytes 294920 | tf_op jit(solution)/shard_map/ppermute | solution.py:422
  141.7 4.9 %collective-permute-start.34 = (bf16[32,1536]{1,0:T(8,128)(2,1)S(1)}, bf16[32,1536]{1,0:T(8,128)(2,1)S(1)}, u32[]{:S(2)}, u32[]{:S(2)}) collective-permute-start(bf16[32,1536]{1,0:T(8,128)(2,1)S(1)} %get-tuple-element.52), channel_id=1, source_target_pairs={{0,4},{4,0},{8,12},{12,8},{1,5},{5,1},{9,13},{13,9},{2,6},{6,2},{1... | collective-permute-start | bytes 294920 | tf_op jit(solution)/shard_map/ppermute | solution.py:422
  146.7 6.4 %collective-permute-start.37 = (bf16[32,1536]{1,0:T(8,128)(2,1)S(1)}, bf16[32,1536]{1,0:T(8,128)(2,1)S(1)}, u32[]{:S(2)}, u32[]{:S(2)}) collective-permute-start(bf16[32,1536]{1,0:T(8,128)(2,1)S(1)} %add_convert_fusion.refs_1_), channel_id=1, source_target_pairs={{0,12},{4,8},{8,4},{12,0},{1,13},{5,9},{9,5},{13,1},{2,14},{6,10},... | collective-permute-start | bytes 294920 | tf_op jit(solution)/shard_map/ppermute | solution.py:426
  148.4 5.8 %collective-permute-start.36 = (bf16[32,1536]{1,0:T(8,128)(2,1)S(1)}, bf16[32,1536]{1,0:T(8,128)(2,1)S(1)}, u32[]{:S(2)}, u32[]{:S(2)}) collective-permute-start(bf16[32,1536]{1,0:T(8,128)(2,1)S(1)} %add_convert_fusion.refs_1_), channel_id=1, source_target_pairs={{0,8},{4,12},{8,0},{12,4},{1,9},{5,13},{9,1},{13,5},{2,10},{6,14},... | collective-permute-start | bytes 294920 | tf_op jit(solution)/shard_map/ppermute | solution.py:426
  149.7 4.7 %collective-permute-start.35 = (bf16[32,1536]{1,0:T(8,128)(2,1)S(1)}, bf16[32,1536]{1,0:T(8,128)(2,1)S(1)}, u32[]{:S(2)}, u32[]{:S(2)}) collective-permute-start(bf16[32,1536]{1,0:T(8,128)(2,1)S(1)} %add_convert_fusion.refs_1_), channel_id=1, source_target_pairs={{0,4},{4,0},{8,12},{12,8},{1,5},{5,1},{9,13},{13,9},{2,6},{6,2},{1... | collective-permute-start | bytes 294920 | tf_op jit(solution)/shard_map/ppermute | solution.py:426

commit v3 on v2

--- a/solution.py
+++ b/solution.py
@@ -11,7 +11,7 @@
 F32, BF16 = jnp.float32, jnp.bfloat16
 MIB = 1024 * 1024
 
-CHUNKS = ((3, "end"), (4, "end"), (4, "end"), (3, "end"), (2, "inner"))
+CHUNKS = ((3, "end"), (3, "end"), (3, "end"), (3, "inner"), (2, "inner"), (2, "inner"))
 
 ROUTES = {
     "end": {
@@ -20,19 +20,20 @@
     },
     "inner": {
         "m0": (0, 1, None), "mb": (3, 2, None), "m1": (1, 2, "m0"),
-        "a0": (2, 1, None), "a1": (2, 3, None), "a2": (1, 0, "a0"),
+        "a0": (2, 1, None), "a1": (2, 3, None), "a2": (2, 0, None),
     },
 }
 OWNER = {"end": (3, ("m2",)), "inner": (2, ("m1", "mb"))}
 HELD = {"end": ("a2", "a1", "a0", None), "inner": ("a2", "a0", None, "a1")}
 
 ORDER = (
-    ("g", 0), ("m0", 0), ("g", 1), ("m0", 1), ("m1", 0), ("g", 2), ("m0", 2), ("m1", 1),
-    ("m2", 0), ("g", 3), ("m0", 3), ("m1", 2), ("m2", 1), ("g", 4), ("m0", 4), ("m1", 3),
-    ("h", 0), ("a0", 0), ("m2", 2), ("h", 1), ("a0", 1), ("m1", 4), ("mb", 4), ("m2", 3),
-    ("a1", 0), ("a1", 1), ("h", 2), ("a0", 2), ("h", 4), ("a0", 4), ("a2", 0), ("a1", 4),
-    ("h", 3), ("a0", 3), ("a2", 1), ("a1", 2), ("a2", 4), ("d", 0), ("a1", 3), ("a2", 2),
-    ("d", 1), ("a2", 3), ("d", 4), ("d", 2), ("d", 3),
+    ("g", 0), ("m0", 0), ("g", 2), ("m0", 2), ("g", 1), ("m0", 1), ("m1", 0), ("g", 3),
+    ("m0", 3), ("m1", 2), ("g", 4), ("m0", 4), ("m1", 1), ("m2", 0), ("mb", 3), ("m1", 3),
+    ("m2", 2), ("mb", 4), ("g", 5), ("m0", 5), ("m2", 1), ("h", 0), ("m1", 4), ("h", 3),
+    ("a0", 0), ("a0", 3), ("h", 2), ("a0", 2), ("m1", 5), ("mb", 5), ("a1", 0), ("h", 4),
+    ("a1", 3), ("a2", 3), ("a2", 4), ("a1", 2), ("h", 1), ("a0", 1), ("h", 5), ("a1", 5),
+    ("a1", 4), ("a2", 0), ("a1", 1), ("a2", 2), ("a2", 5), ("a0", 5), ("a0", 4), ("a2", 1),
+    ("d", 3), ("d", 0), ("d", 5), ("d", 2), ("d", 4), ("d", 1),
 )
 
 SMEM = pl.BlockSpec(memory_space=pltpu.SMEM)
@@ -41,7 +42,7 @@
 HBM = pl.BlockSpec(memory_space=pltpu.HBM)
 
 
-def call(kernel, name, outs, operands, specs, after, scratch=(), aliases=None, limit=42, cost=(0, 0)):
+def call(kernel, name, outs, operands, specs, after, scratch=(), aliases=None, limit=6):
     count = len(operands)
 
     def body(*refs):
@@ -54,7 +55,6 @@
         out_specs=jax.tree.map(lambda _: VMEM, outs) if aliases is None else ANY,
         scratch_shapes=list(scratch),
         input_output_aliases=aliases or {},
-        cost_estimate=pl.CostEstimate(flops=cost[0], bytes_accessed=cost[1], transcendentals=0),
         compiler_params=pltpu.CompilerParams(vmem_limit_bytes=limit * MIB),
         name=name,
     )(*operands, *after)
@@ -160,8 +160,7 @@
         [SMEM] + [VMEM] * len(rows) + [HBM, HBM],
         after,
         [pltpu.VMEM((slots, block, width), BF16), pltpu.SemaphoreType.DMA((slots,))],
-        limit=42,
-        cost=(4 * local_count * count * depth * width, 4 * local_count * depth * width),
+        limit=30,
     )
 
 
@@ -224,20 +223,7 @@
         held_refs, weight_ref = refs[:places], refs[places]
         total_refs = refs[places + 1 : places + 1 + len(totals)]
         out_refs = refs[places + 1 + len(totals) :][: len(row_counts)]
-        hidden, weights, sems = refs[-3:]
-        copies = []
-        for e in range(local_count):
-            for k in range(pieces):
-                at = e * pieces + k
-                copies.append(
-                    pltpu.make_async_copy(
-                        weight_ref.at[e, pl.ds(start + k * block, block), :],
-                        weights.at[at],
-                        sems.at[at],
-                    )
-                )
-        for copy in copies:
-            copy.start()
+        hidden = refs[-1]
         for i in range(places):
 
             @pl.when(place_ref[0] == i)
@@ -247,10 +233,9 @@
         for e in range(local_count):
             product = None
             for k in range(pieces):
-                copies[e * pieces + k].wait()
                 part = jnp.dot(
                     hidden[e, :, k * block : (k + 1) * block],
-                    weights[e * pieces + k],
+                    weight_ref[e, start + k * block : start + (k + 1) * block, :],
                     preferred_element_type=F32,
                 )
                 product = part if product is None else product + part
@@ -267,25 +252,21 @@
         "down",
         shapes,
         operands,
-        [SMEM] + [VMEM] * places + [HBM] + [VMEM] * len(totals),
+        [SMEM] + [VMEM] * (places + 1 + len(totals)),
         after,
         [
             pltpu.VMEM(held[0].shape, BF16),
-            pltpu.VMEM((local_count * pieces, block, features), BF16),
-            pltpu.SemaphoreType.DMA((local_count * pieces,)),
         ],
-        limit=42,
-        cost=(2 * local_count * count * features * width, 2 * local_count * features * width),
-    )
-
-
-def combine(group, ids, weights, sums, groups):
+        limit=6 + 2 * local_count * count * features * 4 // MIB,
+    )
+
+
+def combine(group, ids, weights, sums):
     local_count, _, features = sums[0].shape
     tokens = ids.shape[1]
-    block = tokens // groups
 
     def kernel(group_ref, ids_ref, weights_ref, *refs):
-        sum_refs, own_ref, sent = refs[: len(sums)], refs[len(sums)], refs[len(sums) + 1 :]
+        sum_refs, out_ref = refs[:-1], refs[-1]
         hit, named = slot_hits(ids_ref[...], group_ref[0], local_count)
         scale = sum(
             jnp.where(named[k], weights_ref[k : k + 1, :], 0.0) for k in range(len(named))
@@ -301,53 +282,38 @@
         rows_low = (rows - rows_high.astype(F32)).astype(BF16)
 
         def product(a, b):
-            return lax.dot_general(
-                a, b, (((0,), (0,)), ((), ())), preferred_element_type=F32
-            )
+            return lax.dot_general(a, b, (((0,), (0,)), ((), ())), preferred_element_type=F32)
 
         mixed = (
             product(scale_high, rows_high)
             + product(scale_high, rows_low)
             + product(scale_low, rows_high)
         )
-        for place in range(groups):
-            piece = mixed[place * block : (place + 1) * block]
-            step = group_ref[0] ^ place
-
-            @pl.when(step == 0)
-            def _():
-                own_ref[...] = piece
-
-            for other in range(1, groups):
-
-                @pl.when(step == other)
-                def _():
-                    sent[other - 1][...] = piece.astype(BF16)
+        out_ref[...] = mixed.astype(BF16)
 
     return call(
         kernel,
         "combine",
-        [jax.ShapeDtypeStruct((block, features), F32)]
-        + [jax.ShapeDtypeStruct((block, features), BF16)] * (groups - 1),
+        jax.ShapeDtypeStruct((tokens, features), BF16),
         [group, ids, weights, *sums],
         [SMEM] + [VMEM] * (2 + len(sums)),
         [],
     )
 
 
-def place_blocks(group, pieces):
-    block, features = pieces[0].shape
-
-    def kernel(group_ref, *refs):
-        out_ref = refs[-1]
-        for step, piece_ref in enumerate(refs[:-1]):
-            start = pl.multiple_of((group_ref[0] ^ step) * block, block)
-            out_ref[pl.ds(start, block), :] = piece_ref[...]
-
-    shape = jax.ShapeDtypeStruct((block * len(pieces), features), BF16)
-    return call(
-        kernel, "place_blocks", shape, [group, *pieces], [SMEM] + [VMEM] * len(pieces), []
-    )
+def sum_blocks(parts):
+    groups = parts.shape[0]
+
+    def kernel(parts_ref, out_ref):
+        total = parts_ref[0].astype(F32)
+        for i in range(1, groups):
+            total = total + parts_ref[i].astype(F32)
+        total = total.astype(BF16)
+        for i in range(groups):
+            out_ref[i] = total
+
+    shape = jax.ShapeDtypeStruct(parts.shape, BF16)
+    return call(kernel, "sum_blocks", shape, [parts], [VMEM], [])
 
 
 def local(mesh_shape, tokens, expert_ids, route_weights, gate_weight, up_weight, down_weight):
@@ -416,15 +382,10 @@
         sums = [totals[0], lax.ppermute(totals[1], "dp", swap)]
     else:
         sums = [lax.psum_scatter(totals[0], "dp", scatter_dimension=1, tiled=True)]
-    own, *sent = combine(group, ids, choice_weights, sums, groups)
-    for step in range(groups - 1, 0, -1):
-        exchange = [(i, i ^ step) for i in range(groups)]
-        own = own + lax.ppermute(sent[step - 1], "expert", exchange).astype(F32)
-    block = own.astype(BF16)
-    pieces = [block]
-    for step in range(1, groups):
-        pieces.append(lax.ppermute(block, "expert", [(i, i ^ step) for i in range(groups)]))
-    return place_blocks(group, pieces)
+    mixed = combine(group, ids, choice_weights, sums)
+    parts = mixed.reshape(groups, mixed.shape[0] // groups, mixed.shape[1])
+    parts = lax.all_to_all(parts, "expert", 0, 0)
+    return lax.all_to_all(sum_blocks(parts), "expert", 0, 0).reshape(mixed.shape)
 
 
 def solution(mesh):

time: 156 us -> 135 us (0.87)
  waiting for transfers between devices: 60.8 us -> 33.1 us
  blocking collectives: 0 us -> 20 us
  starting transfers between devices: 53 us -> 43.5 us
  Pallas kernels: 39 us -> 32.9 us
  local copies, waits for them, and re-layouts: 1.69 us -> 3.49 us
    all_to_all x0 -> x2, blocking collectives: none -> 20 us  [the longest x1 11.2 us: local(): parts = lax.all_to_all(parts, 'expert', 0, 0)]
    ppermute x30 -> x36, waiting for transfers between devices: 49 us -> 30.2 us  [hop(): return lax.ppermute(value, ('dp', 'blk'), pairs)]
    ppermute x6 -> x0, waiting for transfers between devices: 8.64 us -> none  [the longest x3 4.41 us: local(): own = own + lax.ppermute(sent[step - 1], 'expert', exchange).astype(F32)]
    ppermute x6 -> x0, starting transfers between devices: 7.11 us -> none  [the longest x3 3.55 us: local(): lax.ppermute(block, 'expert', [(i, i ^ step) for i in range(groups)])]
    pallas_call x37 -> x39, Pallas kernels: 39 us -> 32.9 us  [call(): pl.pallas_call(body, out_shape=outs, in_specs=list(specs) + [ANY] * len(a...]
    ppermute x30 -> x36, starting transfers between devices: 45.3 us -> 41 us  [hop(): return lax.ppermute(value, ('dp', 'blk'), pairs)]
    ppermute x1, starting transfers between devices: 0.07 us -> 1.91 us  [local(): sums = [totals[0], lax.ppermute(totals[1], 'dp', swap)]]
    unnamed x8 -> x25, local copies, waits for them, and re-layouts: 1.69 us -> 3.49 us
  transfers between devices with their start and end apart: 38 -> 38, of which waited for: 15 -> 8; matrix products, arithmetic and copies ran while one was open for 0% -> 0% of each run, Pallas kernels for 19% -> 20%
where the time goes in v3:
time: 135 us; the launch traced here: 134 us
  starting transfers between devices  43.5 us (32%)
  waiting for transfers between devices  33.1 us (25%)
  Pallas kernels  32.9 us (24%)
  blocking collectives  20 us (15%)
  local copies, waits for them, and re-layouts  3.49 us (3%)
    ppermute x36, starting transfers between devices, hop(): return lax.ppermute(value, ('dp', 'blk'), pairs)  41 us
    pallas_call x39, Pallas kernels, call(): pl.pallas_call(body, out_shape=outs, in_specs=list(specs) + [ANY] * len(a...  32.9 us
    ppermute x36, waiting for transfers between devices, hop(): return lax.ppermute(value, ('dp', 'blk'), pairs)  30.2 us
    all_to_all x1, blocking collectives, local(): parts = lax.all_to_all(parts, 'expert', 0, 0)  11.2 us
    all_to_all x1, blocking collectives, local(): lax.all_to_all(sum_blocks(parts), 'expert', 0, 0).reshape(mixed.shape)  8.85 us
    unnamed x25, local copies, waits for them, and re-layouts  3.49 us
  transfers between devices with their start and end apart: 38, of which 8 were waited for; matrix products, arithmetic and copies ran while one was open for 0% of the time, Pallas kernels for 20%

profile of v3, /device:TPU:0, one launch (start us, length us, event | category | flops | bytes accessed | tf_op | source)
XLA Modules:
  0.0 133.9 jit_solution(14281477339334595009)
XLA Ops:
  0.0 1.0 copy-done
  2.6 1.2 collective-permute-done.refs_2_
  3.8 4.8 %gate_up.6 = (f32[2,2,96,768]{3,2,1,0:T(8,128)S(1)}, bf16[2,2,96,768]{3,2,1,0:T(8,128)(2,1)S(1)}) custom-call(s32[1]{0:T(128)} %bitcast.3.refs_0_, bf16[2,48,1536]{2,1,0:T(8,128)(2,1)S(1)} %pick.1.refs_1_, bf16[2,48,1536]{2,1,0:T(8,128)(2,1)S(1)} %collective-permute-done.refs_2_, bf16[2,1536,4096]{2,1,0:T(8,128)(2,1)} %refs_3_.11, ...), custom_call_target="tpu_custom_call" | custom-call | tf_op jit(solution)/shard_map/gate_up/pallas_call | solution.py:51
  8.6 4.8 %collective-permute-start.3 = (bf16[2,2,96,768]{3,2,1,0:T(8,128)(2,1)S(1)}, bf16[2,2,96,768]{3,2,1,0:T(8,128)(2,1)S(1)}, u32[]{:S(2)}, u32[]{:S(2)}) collective-permute-start(bf16[2,2,96,768]{3,2,1,0:T(8,128)(2,1)S(1)} %get-tuple-element.34), channel_id=1, source_target_pairs={{0,1},{19,18},{4,5},{23,22},{8,9},{27,26},{12,13},{31,30}} | collective-permute-start | bytes 1769480 | tf_op jit(solution)/shard_map/ppermute | solution.py:334
  13.4 4.8 %gate_up.7 = (f32[2,2,96,768]{3,2,1,0:T(8,128)S(1)}, bf16[2,2,96,768]{3,2,1,0:T(8,128)(2,1)S(1)}) custom-call(s32[1]{0:T(128)} %bitcast.3.refs_0_, bf16[2,48,1536]{2,1,0:T(8,128)(2,1)S(1)} %pick.1.refs_1_, bf16[2,48,1536]{2,1,0:T(8,128)(2,1)S(1)} %collective-permute-done.refs_2_, bf16[2,1536,4096]{2,1,0:T(8,128)(2,1)} %refs_3_.11, ...), custom_call_target="tpu_custom_call" | custom-call | tf_op jit(solution)/shard_map/gate_up/pallas_call | solution.py:51
  18.2 1.3 collective-permute-start.2
  19.6 4.8 %gate_up.8 = (f32[2,2,96,768]{3,2,1,0:T(8,128)S(1)}, bf16[2,2,96,768]{3,2,1,0:T(8,128)(2,1)S(1)}) custom-call(s32[1]{0:T(128)} %bitcast.3.refs_0_, bf16[2,48,1536]{2,1,0:T(8,128)(2,1)S(1)} %pick.1.refs_1_, bf16[2,48,1536]{2,1,0:T(8,128)(2,1)S(1)} %collective-permute-done.refs_2_, bf16[2,1536,4096]{2,1,0:T(8,128)(2,1)} %refs_3_.11, ...), custom_call_target="tpu_custom_call" | custom-call | tf_op jit(solution)/shard_map/gate_up/pallas_call | solution.py:51
  24.4 1.3 collective-permute-start.1
  25.7 0.7 collective-permute-start.7
  26.4 4.8 %gate_up.9 = (f32[2,2,96,768]{3,2,1,0:T(8,128)S(1)}, bf16[2,2,96,768]{3,2,1,0:T(8,128)(2,1)S(1)}) custom-call(s32[1]{0:T(128)} %bitcast.3.refs_0_, bf16[2,48,1536]{2,1,0:T(8,128)(2,1)S(1)} %pick.1.refs_1_, bf16[2,48,1536]{2,1,0:T(8,128)(2,1)S(1)} %collective-permute-done.refs_2_, bf16[2,1536,4096]{2,1,0:T(8,128)(2,1)} %refs_3_.11, ...), custom_call_target="tpu_custom_call" | custom-call | tf_op jit(solution)/shard_map/gate_up/pallas_call | solution.py:51
  31.2 2.1 %collective-permute-start.6 = (bf16[2,2,96,768]{3,2,1,0:T(8,128)(2,1)S(1)}, bf16[2,2,96,768]{3,2,1,0:T(8,128)(2,1)S(1)}, u32[]{:S(2)}, u32[]{:S(2)}) collective-permute-start(bf16[2,2,96,768]{3,2,1,0:T(8,128)(2,1)S(1)} %get-tuple-element.37), channel_id=1, source_target_pairs={{0,1},{19,18},{4,5},{23,22},{8,9},{27,26},{12,13},{31,30}} | collective-permute-start | bytes 1769480 | tf_op jit(solution)/shard_map/ppermute | solution.py:334
  33.4 0.7 collective-permute-start.5
  34.1 3.2 %gate_up.10 = (f32[2,2,96,512]{3,2,1,0:T(8,128)S(1)}, bf16[2,2,96,512]{3,2,1,0:T(8,128)(2,1)S(1)}) custom-call(s32[1]{0:T(128)} %bitcast.3.refs_0_, bf16[2,48,1536]{2,1,0:T(8,128)(2,1)S(1)} %pick.1.refs_1_, bf16[2,48,1536]{2,1,0:T(8,128)(2,1)S(1)} %collective-permute-done.refs_2_, bf16[2,1536,4096]{2,1,0:T(8,128)(2,1)} %refs_3_.11, ...), custom_call_target="tpu_custom_call" | custom-call | tf_op jit(solution)/shard_map/gate_up/pallas_call | solution.py:51
  37.3 2.0 %collective-permute-start.12 = (bf16[2,2,96,512]{3,2,1,0:T(8,128)(2,1)S(1)}, bf16[2,2,96,512]{3,2,1,0:T(8,128)(2,1)S(1)}, u32[]{:S(2)}, u32[]{:S(2)}) collective-permute-start(bf16[2,2,96,512]{3,2,1,0:T(8,128)(2,1)S(1)} %get-tuple-element.39), channel_id=1, source_target_pairs={{0,1},{19,18},{4,5},{23,22},{8,9},{27,26},{12,13},{31,30}} | collective-permute-start | bytes 1179656 | tf_op jit(solution)/shard_map/ppermute | solution.py:334
  39.4 0.7 collective-permute-start.4
  40.1 0.7 collective-permute-start.13
  40.9 0.7 collective-permute-start.10
  41.6 0.7 collective-permute-start.11
  42.5 2.5 %collective-permute-done.12.refs_2_ = bf16[2,2,96,512]{3,2,1,0:T(8,128)(2,1)S(1)} collective-permute-done((bf16[2,2,96,512]{3,2,1,0:T(8,128)(2,1)S(1)}, bf16[2,2,96,512]{3,2,1,0:T(8,128)(2,1)S(1)}, u32[]{:S(2)}, u32[]{:S(2)}) %collective-permute-start.12) | collective-permute-done | bytes 393248 | tf_op jit(solution)/shard_map/ppermute | solution.py:334
  45.0 0.8 copy-done.1
  45.7 0.7 collective-permute-start.9
  46.5 4.1 %gate_up.11 = (f32[2,2,96,512]{3,2,1,0:T(8,128)S(1)}, bf16[2,2,96,512]{3,2,1,0:T(8,128)(2,1)}) custom-call(s32[1]{0:T(128)} %bitcast.3.refs_0_, bf16[2,48,1536]{2,1,0:T(8,128)(2,1)S(1)} %pick.1.refs_1_, bf16[2,48,1536]{2,1,0:T(8,128)(2,1)S(1)} %collective-permute-done.refs_2_, bf16[2,1536,4096]{2,1,0:T(8,128)(2,1)} %refs_3_.11, ...), custom_call_target="tpu_custom_call" | custom-call | tf_op jit(solution)/shard_map/gate_up/pallas_call | solution.py:51
  50.6 4.7 %collective-permute-start.18 = (bf16[2,2,96,512]{3,2,1,0:T(8,128)(2,1)}, bf16[2,2,96,512]{3,2,1,0:T(8,128)(2,1)S(1)}, u32[]{:S(2)}, u32[]{:S(2)}) collective-permute-start(bf16[2,2,96,512]{3,2,1,0:T(8,128)(2,1)} %get-tuple-element.40), channel_id=1, source_target_pairs={{0,1},{19,18},{4,5},{23,22},{8,9},{27,26},{12,13},{31,30}} | collective-permute-start | bytes 1179656 | tf_op jit(solution)/shard_map/ppermute | solution.py:334
  55.3 0.7 collective-permute-start.16
  56.0 0.8 collective-permute-start.8
  57.2 0.8 collective-permute-start.17
  58.7 6.3 %collective-permute-done.18.refs_2_ = bf16[2,2,96,512]{3,2,1,0:T(8,128)(2,1)S(1)} collective-permute-done((bf16[2,2,96,512]{3,2,1,0:T(8,128)(2,1)}, bf16[2,2,96,512]{3,2,1,0:T(8,128)(2,1)S(1)}, u32[]{:S(2)}, u32[]{:S(2)}) %collective-permute-start.18) | collective-permute-done | bytes 393248 | tf_op jit(solution)/shard_map/ppermute | solution.py:334
  65.8 0.8 collective-permute-start.22
  66.6 0.8 collective-permute-start.21
  68.9 1.3 collective-permute-start.34
  73.1 11.8 %collective-permute-done.34.refs_1_ = bf16[2,96,768]{2,1,0:T(8,128)(2,1)S(1)} collective-permute-done((bf16[2,96,768]{2,1,0:T(8,128)(2,1)S(1)}, bf16[2,96,768]{2,1,0:T(8,128)(2,1)S(1)}, u32[]{:S(2)}, u32[]{:S(2)}) %collective-permute-start.34) | collective-permute-done | bytes 294944 | tf_op jit(solution)/shard_map/ppermute | solution.py:334
  84.9 1.3 collective-permute-start.33
  86.2 1.3 collective-permute-start.30
  88.9 1.3 collective-permute-start.29
  90.2 6.3 %collective-permute-done.30.refs_1_ = bf16[2,96,512]{2,1,0:T(8,128)(2,1)S(1)} collective-permute-done((bf16[2,96,512]{2,1,0:T(8,128)(2,1)S(1)}, bf16[2,96,512]{2,1,0:T(8,128)(2,1)S(1)}, u32[]{:S(2)}, u32[]{:S(2)}) %collective-permute-start.30) | collective-permute-done | bytes 196640 | tf_op jit(solution)/shard_map/ppermute | solution.py:334
  96.5 1.3 collective-permute-start.25
  97.7 1.3 collective-permute-start.26
  100.5 0.9 down.6
  101.4 0.9 down.7
  103.1 0.9 down.9
  104.0 2.3 %collective-permute-done.26.refs_1_ = bf16[2,96,512]{2,1,0:T(8,128)(2,1)S(1)} collective-permute-done((bf16[2,96,512]{2,1,0:T(8,128)(2,1)S(1)}, bf16[2,96,512]{2,1,0:T(8,128)(2,1)S(1)}, u32[]{:S(2)}, u32[]{:S(2)}) %collective-permute-start.26) | collective-permute-done | bytes 196640 | tf_op jit(solution)/shard_map/ppermute | solution.py:334
  107.0 0.9 collective-permute-done.25.refs_1_
  108.0 0.9 down.11
  108.9 1.9 %collective-permute-start.37 = (f32[2,48,1536]{2,1,0:T(8,128)S(1)}, f32[2,48,1536]{2,1,0:T(8,128)S(1)}, u32[]{:S(2)}, u32[]{:S(2)}) collective-permute-start(f32[2,48,1536]{2,1,0:T(8,128)S(1)} %get-tuple-element.52), channel_id=1, source_target_pairs={{0,16},{16,0},{1,17},{17,1},{2,18},{18,2},{3,19},{19,3},{4,20},{20... | collective-permute-start | bytes 1769480 | tf_op jit(solution)/shard_map/ppermute | solution.py:382
  110.8 1.6 %collective-permute-done.37.refs_4_ = f32[2,48,1536]{2,1,0:T(8,128)S(1)} collective-permute-done((f32[2,48,1536]{2,1,0:T(8,128)S(1)}, f32[2,48,1536]{2,1,0:T(8,128)S(1)}, u32[]{:S(2)}, u32[]{:S(2)}) %collective-permute-start.37) | collective-permute-done | bytes 589856 | tf_op jit(solution)/shard_map/ppermute | solution.py:382
  113.1 11.2 %all_to_all.10.refs_0_ = bf16[4,32,1536]{2,1,0:T(8,128)(2,1)S(1)} all-to-all(bf16[4,32,1536]{2,1,0:T(8,128)(2,1)S(1)} %bitcast.8), channel_id=1, replica_groups=mesh['dp'=2,'expert'=4,'blk'=4] {'expert'}, dimensions={0} | all-to-all | bytes 786432 | tf_op jit(solution)/shard_map/all_to_all | solution.py:387
  124.3 8.8 %all_to_all.11 = bf16[4,32,1536]{2,1,0:T(8,128)(2,1)S(1)} all-to-all(bf16[4,32,1536]{2,1,0:T(8,128)(2,1)S(1)} %sum_blocks.1), channel_id=1, replica_groups=mesh['dp'=2,'expert'=4,'blk'=4] {'expert'}, dimensions={0} | all-to-all | bytes 786432 | tf_op jit(solution)/shard_map/all_to_all | solution.py:388
  133.2 0.7 copy.20
  (95 shorter events, 12.5 us)
Async XLA Ops:
  0.0 1.0 copy-start
  2.0 1.7 %collective-permute-start = (bf16[2,48,1536]{2,1,0:T(8,128)(2,1)S(1)}, bf16[2,48,1536]{2,1,0:T(8,128)(2,1)S(1)}, u32[]{:S(2)}, u32[]{:S(2)}) collective-permute-start(bf16[2,48,1536]{2,1,0:T(8,128)(2,1)S(1)} %pick.1.refs_1_), channel_id=1, source_target_pairs={{0,16},{16,0},{1,17},{17,1},{2,18},{18,2},{3,19},{19,3},{4,20},{20... | collective-permute-start | bytes 884744 | tf_op jit(solution)/shard_map/ppermute | solution.py:338
  8.6 17.1 %collective-permute-start.3 = (bf16[2,2,96,768]{3,2,1,0:T(8,128)(2,1)S(1)}, bf16[2,2,96,768]{3,2,1,0:T(8,128)(2,1)S(1)}, u32[]{:S(2)}, u32[]{:S(2)}) collective-permute-start(bf16[2,2,96,768]{3,2,1,0:T(8,128)(2,1)S(1)} %get-tuple-element.34), channel_id=1, source_target_pairs={{0,1},{19,18},{4,5},{23,22},{8,9},{27,26},{12,13},{31,30}} | collective-permute-start | bytes 1769480 | tf_op jit(solution)/shard_map/ppermute | solution.py:334
  18.2 15.2 %collective-permute-start.2 = (bf16[2,2,96,768]{3,2,1,0:T(8,128)(2,1)S(1)}, bf16[2,2,96,768]{3,2,1,0:T(8,128)(2,1)S(1)}, u32[]{:S(2)}, u32[]{:S(2)}) collective-permute-start(bf16[2,2,96,768]{3,2,1,0:T(8,128)(2,1)S(1)} %get-tuple-element.33), channel_id=1, source_target_pairs={{0,1},{19,18},{4,5},{23,22},{8,9},{27,26},{12,13},{31,30}} | collective-permute-start | bytes 1769480 | tf_op jit(solution)/shard_map/ppermute | solution.py:334
  24.4 15.0 %collective-permute-start.1 = (bf16[2,2,96,768]{3,2,1,0:T(8,128)(2,1)S(1)}, bf16[2,2,96,768]{3,2,1,0:T(8,128)(2,1)S(1)}, u32[]{:S(2)}, u32[]{:S(2)}) collective-permute-start(bf16[2,2,96,768]{3,2,1,0:T(8,128)(2,1)S(1)} %get-tuple-element.32), channel_id=1, source_target_pairs={{0,1},{19,18},{4,5},{23,22},{8,9},{27,26},{12,13},{31,30}} | collective-permute-start | bytes 1769480 | tf_op jit(solution)/shard_map/ppermute | solution.py:334
  25.7 14.4 %collective-permute-start.7 = (bf16[2,2,96,768]{3,2,1,0:T(8,128)(2,1)S(1)}, bf16[2,2,96,768]{3,2,1,0:T(8,128)(2,1)S(1)}, u32[]{:S(2)}, u32[]{:S(2)}) collective-permute-start(bf16[2,2,96,768]{3,2,1,0:T(8,128)(2,1)S(1)} %add_to_send.9.refs_5_), channel_id=1, source_target_pairs={{1,2},{18,17},{5,6},{22,21},{9,10},{26,25},{13,14},{30,29}} | collective-permute-start | bytes 1769480 | tf_op jit(solution)/shard_map/ppermute | solution.py:334
  31.2 9.6 %collective-permute-start.6 = (bf16[2,2,96,768]{3,2,1,0:T(8,128)(2,1)S(1)}, bf16[2,2,96,768]{3,2,1,0:T(8,128)(2,1)S(1)}, u32[]{:S(2)}, u32[]{:S(2)}) collective-permute-start(bf16[2,2,96,768]{3,2,1,0:T(8,128)(2,1)S(1)} %get-tuple-element.37), channel_id=1, source_target_pairs={{0,1},{19,18},{4,5},{23,22},{8,9},{27,26},{12,13},{31,30}} | collective-permute-start | bytes 1769480 | tf_op jit(solution)/shard_map/ppermute | solution.py:334
  33.4 8.2 %collective-permute-start.5 = (bf16[2,2,96,768]{3,2,1,0:T(8,128)(2,1)S(1)}, bf16[2,2,96,768]{3,2,1,0:T(8,128)(2,1)S(1)}, u32[]{:S(2)}, u32[]{:S(2)}) collective-permute-start(bf16[2,2,96,768]{3,2,1,0:T(8,128)(2,1)S(1)} %add_to_send.10.refs_5_), channel_id=1, source_target_pairs={{1,2},{18,17},{5,6},{22,21},{9,10},{26,25},{13,14},{30,29}} | collective-permute-start | bytes 1769480 | tf_op jit(solution)/shard_map/ppermute | solution.py:334
  37.3 7.6 %collective-permute-start.12 = (bf16[2,2,96,512]{3,2,1,0:T(8,128)(2,1)S(1)}, bf16[2,2,96,512]{3,2,1,0:T(8,128)(2,1)S(1)}, u32[]{:S(2)}, u32[]{:S(2)}) collective-permute-start(bf16[2,2,96,512]{3,2,1,0:T(8,128)(2,1)S(1)} %get-tuple-element.39), channel_id=1, source_target_pairs={{0,1},{19,18},{4,5},{23,22},{8,9},{27,26},{12,13},{31,30}} | collective-permute-start | bytes 1179656 | tf_op jit(solution)/shard_map/ppermute | solution.py:334
  39.4 11.2 %collective-permute-start.4 = (bf16[2,2,96,768]{3,2,1,0:T(8,128)(2,1)S(1)}, bf16[2,2,96,768]{3,2,1,0:T(8,128)(2,1)S(1)}, u32[]{:S(2)}, u32[]{:S(2)}) collective-permute-start(bf16[2,2,96,768]{3,2,1,0:T(8,128)(2,1)S(1)} %add_to_send.11.refs_3_), channel_id=1, source_target_pairs={{1,2},{18,17},{5,6},{22,21},{9,10},{26,25},{13,14},{30,29}} | collective-permute-start | bytes 1769480 | tf_op jit(solution)/shard_map/ppermute | solution.py:334
  40.1 15.2 %collective-permute-start.13 = (bf16[2,2,96,768]{3,2,1,0:T(8,128)(2,1)S(1)}, bf16[2,2,96,768]{3,2,1,0:T(8,128)(2,1)S(1)}, u32[]{:S(2)}, u32[]{:S(2)}) collective-permute-start(bf16[2,2,96,768]{3,2,1,0:T(8,128)(2,1)S(1)} %add_to_send.12.refs_2_), channel_id=1, source_target_pairs={{2,3},{17,16},{6,7},{21,20},{10,11},{25,24},{14,15},{29,28}} | collective-permute-start | bytes 1769480 | tf_op jit(solution)/shard_map/ppermute | solution.py:334
  40.9 15.2 %collective-permute-start.10 = (bf16[2,2,96,768]{3,2,1,0:T(8,128)(2,1)S(1)}, bf16[2,2,96,768]{3,2,1,0:T(8,128)(2,1)S(1)}, u32[]{:S(2)}, u32[]{:S(2)}) collective-permute-start(bf16[2,2,96,768]{3,2,1,0:T(8,128)(2,1)S(1)} %add_to_send.13.refs_3_), channel_id=1, source_target_pairs={{1,2},{18,17},{5,6},{22,21},{9,10},{26,25},{13,14},{30,29}} | collective-permute-start | bytes 1769480 | tf_op jit(solution)/shard_map/ppermute | solution.py:334
  41.6 15.6 %collective-permute-start.11 = (bf16[2,2,96,768]{3,2,1,0:T(8,128)(2,1)S(1)}, bf16[2,2,96,768]{3,2,1,0:T(8,128)(2,1)S(1)}, u32[]{:S(2)}, u32[]{:S(2)}) collective-permute-start(bf16[2,2,96,768]{3,2,1,0:T(8,128)(2,1)S(1)} %round_to_send.3.refs_3_), channel_id=1, source_target_pairs={{3,2},{16,17},{7,6},{20,21},{11,10},{24,25},{15,14},{28,29}} | collective-permute-start | bytes 1769480 | tf_op jit(solution)/shard_map/ppermute | solution.py:334
  45.7 12.3 %collective-permute-start.9 = (bf16[2,2,96,768]{3,2,1,0:T(8,128)(2,1)S(1)}, bf16[2,2,96,768]{3,2,1,0:T(8,128)(2,1)S(1)}, u32[]{:S(2)}, u32[]{:S(2)}) collective-permute-start(bf16[2,2,96,768]{3,2,1,0:T(8,128)(2,1)S(1)} %add_to_send.14.refs_2_), channel_id=1, source_target_pairs={{2,3},{17,16},{6,7},{21,20},{10,11},{25,24},{14,15},{29,28}} | collective-permute-start | bytes 1769480 | tf_op jit(solution)/shard_map/ppermute | solution.py:334
  46.4 54.0 %slice-start = ((s8[25165824]{0:T(1024)(128)(4,1)}), s8[4194304]{0:T(1024)(128)(4,1)S(1)}, s32[]{:S(2)}) async-start(s8[25165824]{0:T(1024)(128)(4,1)} %bitcast.6), calls=%async_computation.2 | async-start | bytes 8388608
  46.4 54.0 %slice-start.1 = ((s8[25165824]{0:T(1024)(128)(4,1)}), s8[4194304]{0:T(1024)(128)(4,1)S(1)}, s32[]{:S(2)}) async-start(s8[25165824]{0:T(1024)(128)(4,1)} %bitcast.6), calls=%async_computation.3 | async-start | bytes 8388608
  46.4 54.0 %slice-start.2 = ((s8[25165824]{0:T(1024)(128)(4,1)}), s8[4194304]{0:T(1024)(128)(4,1)S(1)}, s32[]{:S(2)}) async-start(s8[25165824]{0:T(1024)(128)(4,1)} %bitcast.6), calls=%async_computation.4 | async-start | bytes 8388608
  46.5 54.0 %slice-start.3 = ((s8[25165824]{0:T(1024)(128)(4,1)}), s8[4194304]{0:T(1024)(128)(4,1)S(1)}, s32[]{:S(2)}) async-start(s8[25165824]{0:T(1024)(128)(4,1)} %bitcast.6), calls=%async_computation.5 | async-start | bytes 8388608
  50.6 14.5 %collective-permute-start.18 = (bf16[2,2,96,512]{3,2,1,0:T(8,128)(2,1)}, bf16[2,2,96,512]{3,2,1,0:T(8,128)(2,1)S(1)}, u32[]{:S(2)}, u32[]{:S(2)}) collective-permute-start(bf16[2,2,96,512]{3,2,1,0:T(8,128)(2,1)} %get-tuple-element.40), channel_id=1, source_target_pairs={{0,1},{19,18},{4,5},{23,22},{8,9},{27,26},{12,13},{31,30}} | collective-permute-start | bytes 1179656 | tf_op jit(solution)/shard_map/ppermute | solution.py:334
  55.3 10.5 %collective-permute-start.16 = (bf16[2,2,96,512]{3,2,1,0:T(8,128)(2,1)S(1)}, bf16[2,2,96,512]{3,2,1,0:T(8,128)(2,1)S(1)}, u32[]{:S(2)}, u32[]{:S(2)}) collective-permute-start(bf16[2,2,96,512]{3,2,1,0:T(8,128)(2,1)S(1)} %round_to_send.4.refs_5_), channel_id=1, source_target_pairs={{3,2},{16,17},{7,6},{20,21},{11,10},{24,25},{15,14},{28,29}} | collective-permute-start | bytes 1179656 | tf_op jit(solution)/shard_map/ppermute | solution.py:334
  56.0 44.5 %slice-start.4 = ((s8[25165824]{0:T(1024)(128)(4,1)}), s8[4194304]{0:T(1024)(128)(4,1)S(1)}, s32[]{:S(2)}) async-start(s8[25165824]{0:T(1024)(128)(4,1)} %bitcast.6), calls=%async_computation.6 | async-start | bytes 8388608
  56.0 1.1 copy-start.2
  56.0 12.2 %collective-permute-start.8 = (bf16[2,2,96,768]{3,2,1,0:T(8,128)(2,1)S(1)}, bf16[2,2,96,768]{3,2,1,0:T(8,128)(2,1)S(1)}, u32[]{:S(2)}, u32[]{:S(2)}) collective-permute-start(bf16[2,2,96,768]{3,2,1,0:T(8,128)(2,1)S(1)} %add_to_send.15.refs_3_), channel_id=1, source_target_pairs={{2,3},{17,16},{6,7},{21,20},{10,11},{25,24},{14,15},{29,28}} | collective-permute-start | bytes 1769480 | tf_op jit(solution)/shard_map/ppermute | solution.py:334
  57.2 9.5 %collective-permute-start.17 = (bf16[2,96,768]{2,1,0:T(8,128)(2,1)S(1)}, bf16[2,96,768]{2,1,0:T(8,128)(2,1)S(1)}, u32[]{:S(2)}, u32[]{:S(2)}) collective-permute-start(bf16[2,96,768]{2,1,0:T(8,128)(2,1)S(1)} %hidden_values.6.refs_3_.refs_4_), channel_id=1, source_target_pairs={{3,2},{16,17},{7,6},{20,21},{11,10},{24,25},{15,14},{28,29}} | collective-permute-start | bytes 884744 | tf_op jit(solution)/shard_map/ppermute | solution.py:334
  58.0 9.5 %collective-permute-start.15 = (bf16[2,2,96,512]{3,2,1,0:T(8,128)(2,1)S(1)}, bf16[2,2,96,512]{3,2,1,0:T(8,128)(2,1)S(1)}, u32[]{:S(2)}, u32[]{:S(2)}) collective-permute-start(bf16[2,2,96,512]{3,2,1,0:T(8,128)(2,1)S(1)} %add_to_send.16.refs_4_), channel_id=1, source_target_pairs={{1,2},{18,17},{5,6},{22,21},{9,10},{26,25},{13,14},{30,29}} | collective-permute-start | bytes 1179656 | tf_op jit(solution)/shard_map/ppermute | solution.py:334
  65.1 3.1 %collective-permute-start.14 = (bf16[2,96,768]{2,1,0:T(8,128)(2,1)S(1)}, bf16[2,96,768]{2,1,0:T(8,128)(2,1)S(1)}, u32[]{:S(2)}, u32[]{:S(2)}) collective-permute-start(bf16[2,96,768]{2,1,0:T(8,128)(2,1)S(1)} %hidden_values.8.refs_3_.refs_4_), channel_id=1, source_target_pairs={{3,2},{16,17},{7,6},{20,21},{11,10},{24,25},{15,14},{28,29}} | collective-permute-start | bytes 884744 | tf_op jit(solution)/shard_map/ppermute | solution.py:334
  65.8 34.7 %slice-start.5 = ((s8[25165824]{0:T(1024)(128)(4,1)}), s8[4194304]{0:T(1024)(128)(4,1)S(1)}, s32[]{:S(2)}) async-start(s8[25165824]{0:T(1024)(128)(4,1)} %bitcast.6), calls=%async_computation.7 | async-start | bytes 8388608
  65.8 4.4 %collective-permute-start.22 = (bf16[2,2,96,512]{3,2,1,0:T(8,128)(2,1)S(1)}, bf16[2,2,96,512]{3,2,1,0:T(8,128)(2,1)S(1)}, u32[]{:S(2)}, u32[]{:S(2)}) collective-permute-start(bf16[2,2,96,512]{3,2,1,0:T(8,128)(2,1)S(1)} %round_to_send.5.refs_1_), channel_id=1, source_target_pairs={{3,2},{16,17},{7,6},{20,21},{11,10},{24,25},{15,14},{28,29}} | collective-permute-start | bytes 1179656 | tf_op jit(solution)/shard_map/ppermute | solution.py:334
  66.6 4.3 %collective-permute-start.21 = (bf16[2,2,96,512]{3,2,1,0:T(8,128)(2,1)S(1)}, bf16[2,2,96,512]{3,2,1,0:T(8,128)(2,1)S(1)}, u32[]{:S(2)}, u32[]{:S(2)}) collective-permute-start(bf16[2,2,96,512]{3,2,1,0:T(8,128)(2,1)S(1)} %add_to_send.17.refs_2_), channel_id=1, source_target_pairs={{1,2},{18,17},{5,6},{22,21},{9,10},{26,25},{13,14},{30,29}} | collective-permute-start | bytes 1179656 | tf_op jit(solution)/shard_map/ppermute | solution.py:334
  67.5 4.1 %collective-permute-start.20 = (bf16[2,96,768]{2,1,0:T(8,128)(2,1)S(1)}, bf16[2,96,768]{2,1,0:T(8,128)(2,1)S(1)}, u32[]{:S(2)}, u32[]{:S(2)}) collective-permute-start(bf16[2,96,768]{2,1,0:T(8,128)(2,1)S(1)} %pass_on.6.refs_4_.refs_3_), channel_id=1, source_target_pairs={{2,1},{17,18},{6,5},{21,22},{10,9},{25,26},{14,13},{29,30}} | collective-permute-start | bytes 884744 | tf_op jit(solution)/shard_map/ppermute | solution.py:334
  68.2 4.1 %collective-permute-start.19 = (bf16[2,96,768]{2,1,0:T(8,128)(2,1)S(1)}, bf16[2,96,768]{2,1,0:T(8,128)(2,1)S(1)}, u32[]{:S(2)}, u32[]{:S(2)}) collective-permute-start(bf16[2,96,768]{2,1,0:T(8,128)(2,1)S(1)} %hidden_values.10.refs_4_), channel_id=1, source_target_pairs={{3,2},{16,17},{7,6},{20,21},{11,10},{24,25},{15,14},{28,29}} | collective-permute-start | bytes 884744 | tf_op jit(solution)/shard_map/ppermute | solution.py:334
  68.9 15.9 %collective-permute-start.34 = (bf16[2,96,768]{2,1,0:T(8,128)(2,1)S(1)}, bf16[2,96,768]{2,1,0:T(8,128)(2,1)S(1)}, u32[]{:S(2)}, u32[]{:S(2)}) collective-permute-start(bf16[2,96,768]{2,1,0:T(8,128)(2,1)S(1)} %hidden_values.7.refs_3_), channel_id=1, source_target_pairs={{2,0},{17,19},{6,4},{21,23},{10,8},{25,27},{14,12},{29,31}} | collective-permute-start | bytes 884744 | tf_op jit(solution)/shard_map/ppermute | solution.py:334
  70.2 15.9 %collective-permute-start.35 = (bf16[2,96,768]{2,1,0:T(8,128)(2,1)S(1)}, bf16[2,96,768]{2,1,0:T(8,128)(2,1)S(1)}, u32[]{:S(2)}, u32[]{:S(2)}) collective-permute-start(bf16[2,96,768]{2,1,0:T(8,128)(2,1)S(1)} %hidden_values.7.refs_3_), channel_id=1, source_target_pairs={{2,1},{17,18},{6,5},{21,22},{10,9},{25,26},{14,13},{29,30}} | collective-permute-start | bytes 884744 | tf_op jit(solution)/shard_map/ppermute | solution.py:334
  70.9 16.5 %collective-permute-start.36 = (bf16[2,96,768]{2,1,0:T(8,128)(2,1)S(1)}, bf16[2,96,768]{2,1,0:T(8,128)(2,1)S(1)}, u32[]{:S(2)}, u32[]{:S(2)}) collective-permute-start(bf16[2,96,768]{2,1,0:T(8,128)(2,1)S(1)} %hidden_values.7.refs_3_), channel_id=1, source_target_pairs={{2,3},{17,16},{6,7},{21,20},{10,11},{25,24},{14,15},{29,28}} | collective-permute-start | bytes 884744 | tf_op jit(solution)/shard_map/ppermute | solution.py:334
  71.6 16.5 %collective-permute-start.24 = (bf16[2,96,768]{2,1,0:T(8,128)(2,1)S(1)}, bf16[2,96,768]{2,1,0:T(8,128)(2,1)S(1)}, u32[]{:S(2)}, u32[]{:S(2)}) collective-permute-start(bf16[2,96,768]{2,1,0:T(8,128)(2,1)S(1)} %pass_on.7.refs_3_), channel_id=1, source_target_pairs={{2,1},{17,18},{6,5},{21,22},{10,9},{25,26},{14,13},{29,30}} | collective-permute-start | bytes 884744 | tf_op jit(solution)/shard_map/ppermute | solution.py:334
  72.4 16.5 %collective-permute-start.23 = (bf16[2,96,768]{2,1,0:T(8,128)(2,1)S(1)}, bf16[2,96,768]{2,1,0:T(8,128)(2,1)S(1)}, u32[]{:S(2)}, u32[]{:S(2)}) collective-permute-start(bf16[2,96,768]{2,1,0:T(8,128)(2,1)S(1)} %pass_on.9.refs_1_.refs_3_), channel_id=1, source_target_pairs={{2,1},{17,18},{6,5},{21,22},{10,9},{25,26},{14,13},{29,30}} | collective-permute-start | bytes 884744 | tf_op jit(solution)/shard_map/ppermute | solution.py:334
  84.9 14.9 %collective-permute-start.33 = (bf16[2,96,768]{2,1,0:T(8,128)(2,1)S(1)}, bf16[2,96,768]{2,1,0:T(8,128)(2,1)S(1)}, u32[]{:S(2)}, u32[]{:S(2)}) collective-permute-start(bf16[2,96,768]{2,1,0:T(8,128)(2,1)S(1)} %pass_on.8.refs_1_.refs_2_), channel_id=1, source_target_pairs={{1,0},{18,19},{5,4},{22,23},{9,8},{26,27},{13,12},{30,31}} | collective-permute-start | bytes 884744 | tf_op jit(solution)/shard_map/ppermute | solution.py:334
  86.2 10.3 %collective-permute-start.30 = (bf16[2,96,512]{2,1,0:T(8,128)(2,1)S(1)}, bf16[2,96,512]{2,1,0:T(8,128)(2,1)S(1)}, u32[]{:S(2)}, u32[]{:S(2)}) collective-permute-start(bf16[2,96,512]{2,1,0:T(8,128)(2,1)S(1)} %hidden_values.11.refs_1_.refs_3_), channel_id=1, source_target_pairs={{2,0},{17,19},{6,4},{21,23},{10,8},{25,27},{14,12},{29,31}} | collective-permute-start | bytes 589832 | tf_op jit(solution)/shard_map/ppermute | solution.py:334
  87.5 10.3 %collective-permute-start.31 = (bf16[2,96,512]{2,1,0:T(8,128)(2,1)S(1)}, bf16[2,96,512]{2,1,0:T(8,128)(2,1)S(1)}, u32[]{:S(2)}, u32[]{:S(2)}) collective-permute-start(bf16[2,96,512]{2,1,0:T(8,128)(2,1)S(1)} %hidden_values.11.refs_1_.refs_3_), channel_id=1, source_target_pairs={{2,1},{17,18},{6,5},{21,22},{10,9},{25,26},{14,13},{29,30}} | collective-permute-start | bytes 589832 | tf_op jit(solution)/shard_map/ppermute | solution.py:334
  88.2 10.9 %collective-permute-start.32 = (bf16[2,96,512]{2,1,0:T(8,128)(2,1)S(1)}, bf16[2,96,512]{2,1,0:T(8,128)(2,1)S(1)}, u32[]{:S(2)}, u32[]{:S(2)}) collective-permute-start(bf16[2,96,512]{2,1,0:T(8,128)(2,1)S(1)} %hidden_values.11.refs_1_.refs_3_), channel_id=1, source_target_pairs={{2,3},{17,16},{6,7},{21,20},{10,11},{25,24},{14,15},{29,28}} | collective-permute-start | bytes 589832 | tf_op jit(solution)/shard_map/ppermute | solution.py:334
  88.9 14.2 %collective-permute-start.29 = (bf16[2,96,768]{2,1,0:T(8,128)(2,1)S(1)}, bf16[2,96,768]{2,1,0:T(8,128)(2,1)S(1)}, u32[]{:S(2)}, u32[]{:S(2)}) collective-permute-start(bf16[2,96,768]{2,1,0:T(8,128)(2,1)S(1)} %pass_on.10.refs_1_.refs_2_), channel_id=1, source_target_pairs={{1,0},{18,19},{5,4},{22,23},{9,8},{26,27},{13,12},{30,31}} | collective-permute-start | bytes 884744 | tf_op jit(solution)/shard_map/ppermute | solution.py:334
  96.5 11.5 %collective-permute-start.25 = (bf16[2,96,768]{2,1,0:T(8,128)(2,1)S(1)}, bf16[2,96,768]{2,1,0:T(8,128)(2,1)S(1)}, u32[]{:S(2)}, u32[]{:S(2)}) collective-permute-start(bf16[2,96,768]{2,1,0:T(8,128)(2,1)S(1)} %pass_on.11.refs_6_.refs_2_), channel_id=1, source_target_pairs={{1,0},{18,19},{5,4},{22,23},{9,8},{26,27},{13,12},{30,31}} | collective-permute-start | bytes 884744 | tf_op jit(solution)/shard_map/ppermute | solution.py:334
  97.7 8.6 %collective-permute-start.26 = (bf16[2,96,512]{2,1,0:T(8,128)(2,1)S(1)}, bf16[2,96,512]{2,1,0:T(8,128)(2,1)S(1)}, u32[]{:S(2)}, u32[]{:S(2)}) collective-permute-start(bf16[2,96,512]{2,1,0:T(8,128)(2,1)S(1)} %hidden_values.9.refs_1_.refs_3_), channel_id=1, source_target_pairs={{2,0},{17,19},{6,4},{21,23},{10,8},{25,27},{14,12},{29,31}} | collective-permute-start | bytes 589832 | tf_op jit(solution)/shard_map/ppermute | solution.py:334
  99.1 7.3 %collective-permute-start.27 = (bf16[2,96,512]{2,1,0:T(8,128)(2,1)S(1)}, bf16[2,96,512]{2,1,0:T(8,128)(2,1)S(1)}, u32[]{:S(2)}, u32[]{:S(2)}) collective-permute-start(bf16[2,96,512]{2,1,0:T(8,128)(2,1)S(1)} %hidden_values.9.refs_1_.refs_3_), channel_id=1, source_target_pairs={{2,1},{17,18},{6,5},{21,22},{10,9},{25,26},{14,13},{29,30}} | collective-permute-start | bytes 589832 | tf_op jit(solution)/shard_map/ppermute | solution.py:334
  99.8 6.6 %collective-permute-start.28 = (bf16[2,96,512]{2,1,0:T(8,128)(2,1)S(1)}, bf16[2,96,512]{2,1,0:T(8,128)(2,1)S(1)}, u32[]{:S(2)}, u32[]{:S(2)}) collective-permute-start(bf16[2,96,512]{2,1,0:T(8,128)(2,1)S(1)} %hidden_values.9.refs_1_.refs_3_), channel_id=1, source_target_pairs={{2,3},{17,16},{6,7},{21,20},{10,11},{25,24},{14,15},{29,28}} | collective-permute-start | bytes 589832 | tf_op jit(solution)/shard_map/ppermute | solution.py:334
  107.9 4.5 %copy-start.4 = (s32[128,2]{0,1:T(2,128)S(1)}, s32[128,2]{0,1:T(2,128)}, u32[]{:S(2)}) copy-start(s32[128,2]{0,1:T(2,128)} %param.7) | copy-start | bytes 3076
  108.0 4.5 %copy-start.5 = (f32[128,2]{0,1:T(2,128)S(1)}, f32[128,2]{0,1:T(2,128)}, u32[]{:S(2)}) copy-start(f32[128,2]{0,1:T(2,128)} %param.8) | copy-start | bytes 3076
  108.9 3.5 %collective-permute-start.37 = (f32[2,48,1536]{2,1,0:T(8,128)S(1)}, f32[2,48,1536]{2,1,0:T(8,128)S(1)}, u32[]{:S(2)}, u32[]{:S(2)}) collective-permute-start(f32[2,48,1536]{2,1,0:T(8,128)S(1)} %get-tuple-element.52), channel_id=1, source_target_pairs={{0,16},{16,0},{1,17},{17,1},{2,18},{18,2},{3,19},{19,3},{4,20},{20... | collective-permute-start | bytes 1769480 | tf_op jit(solution)/shard_map/ppermute | solution.py:382
  (2 other events, 1.4 us)

commit v4 on v2

v4 whole, which is shorter than its diff:
```python
import functools

import jax
import jax.numpy as jnp
from jax import lax
from jax.experimental import pallas as pl
from jax.experimental.pallas import tpu as pltpu
from jax.sharding import PartitionSpec as P

CAP = 48
F32, BF16 = jnp.float32, jnp.bfloat16
MIB = 1024 * 1024

SHARES = (2, 4, 4, 4, 2)
GROUPS = {0: (0, 1), 2: (2,), 3: (3,), 4: (4,)}

ORDER = (
    ("g", 1), ("h1", 1), ("g", 2), ("g", 0), ("h1", 0), ("h2", 1), ("h1", 2), ("g", 3),
    ("h2", 0), ("h1", 3), ("h3", 1), ("h2", 2), ("g", 4), ("h3", 0), ("h2", 3), ("h1", 4),
    ("h3", 2), ("s", 0), ("b1", 0), ("h3", 3), ("h2", 4), ("s", 2), ("b1", 2), ("b2", 0),
    ("h3", 4), ("s", 3), ("b1", 3), ("b2", 2), ("s", 4), ("b3", 0), ("b1", 4), ("b2", 3),
    ("b3", 2), ("b2", 4), ("b3", 3), ("d", 2), ("b3", 4), ("d", 0), ("d", 3), ("d", 4),
)

SMEM = pl.BlockSpec(memory_space=pltpu.SMEM)
VMEM = pl.BlockSpec(memory_space=pltpu.VMEM)
ANY = pl.BlockSpec(memory_space=pl.ANY)
HBM = pl.BlockSpec(memory_space=pltpu.HBM)


def call(kernel, name, outs, operands, specs, after, scratch=(), aliases=None, limit=6):
    count = len(operands)

    def body(*refs):
        kernel(*refs[:count], *refs[count + len(after) :])

    return pl.pallas_call(
        body,
        out_shape=outs,
        in_specs=list(specs) + [ANY] * len(after),
        out_specs=jax.tree.map(lambda _: VMEM, outs) if aliases is None else ANY,
        scratch_shapes=list(scratch),
        input_output_aliases=aliases or {},
        compiler_params=pltpu.CompilerParams(vmem_limit_bytes=limit * MIB),
        name=name,
    )(*operands, *after)


def chunk_widths(half):
    widths, start = [], 0
    for share in SHARES:
        width = min(max(128, share * half // 16 // 128 * 128), half - start)
        if width:
            widths.append(width)
        start += width
    widths[-1] += half - start
    return widths


def slot_hits(ids, group, local_count):
    tokens, lanes = ids.shape[1], local_count * CAP
    slot = lax.broadcasted_iota(jnp.int32, (lanes, tokens), 0)
    expert = jnp.full((lanes, tokens), group * local_count, jnp.int32)
    for step in range(1, local_count):
        passed = (slot >= CAP).astype(jnp.int32) if step == 1 else passed_next
        expert = expert + passed
        slot = slot - CAP * passed
        passed_next = (slot >= CAP).astype(jnp.int32)
    named = [ids[k : k + 1, :] == expert for k in range(ids.shape[0])]
    member = functools.reduce(jnp.logical_or, named)
    earlier = lax.broadcasted_iota(jnp.int32, (tokens, tokens), 0) < lax.broadcasted_iota(
        jnp.int32, (tokens, tokens), 1
    )
    position = jnp.dot(
        member.astype(F32).astype(BF16),
        earlier.astype(F32).astype(BF16),
        preferred_element_type=F32,
    )
    return member & (position.astype(jnp.int32) == slot), named


def pick(group, ids, tokens, local_count):
    def kernel(group_ref, ids_ref, tokens_ref, out_ref):
        hit, _ = slot_hits(ids_ref[...], group_ref[0], local_count)
        rows = jnp.dot(
            hit.astype(F32).astype(BF16), tokens_ref[...], preferred_element_type=F32
        ).astype(BF16)
        for e in range(local_count):
            out_ref[e] = rows[e * CAP : (e + 1) * CAP]

    shape = jax.ShapeDtypeStruct((local_count, CAP, tokens.shape[1]), BF16)
    return call(kernel, "pick", shape, [group, ids, tokens], [SMEM, VMEM, VMEM], [])


def gate_up(place, rows, weights, start, width, after):
    local_count, _, depth = rows[0].shape
    count = sum(part.shape[1] for part in rows)
    half = weights[0].shape[2] // 2
    pieces = 2
    block = depth // pieces

    def kernel(place_ref, *refs):
        row_refs, weight_refs = refs[: len(rows)], refs[len(rows) : len(rows) + 2]
        far_ref, short_ref, near_ref, held, sems = refs[len(rows) + 2 :]
        copies = {}
        for part in range(2):
            side = (1 - place_ref[1]) if part == 0 else place_ref[1]
            column = pl.multiple_of(side * half + start, 128)
            for e in range(local_count):
                for i in range(2):
                    at = (part * local_count + e) * 2 + i
                    for k in range(pieces):
                        copies[at, k] = pltpu.make_async_copy(
                            weight_refs[i].at[e, pl.ds(k * block, block), pl.ds(column, width)],
                            held.at[at, pl.ds(k * block, block), :],
                            sems.at[at * pieces + k],
                        )
                        copies[at, k].start()
        for part, full_ref in enumerate((far_ref, near_ref)):
            for e in range(local_count):
                x = jnp.concatenate([ref[e] for ref in row_refs], axis=0)
                for i in range(2):
                    at = (part * local_count + e) * 2 + i
                    for k in range(pieces):
                        copies[at, k].wait()
                    full_ref[i, e] = jnp.dot(x, held[at], preferred_element_type=F32)
                    if part == 0:

                        @pl.when(place_ref[0] == 1)
                        def _():
                            short_ref[i, e] = full_ref[i, e].astype(BF16)

    shape = (2, local_count, count, width)
    slots = 4 * local_count
    return call(
        kernel,
        "gate_up",
        [jax.ShapeDtypeStruct(shape, kind) for kind in (F32, BF16, F32)],
        [place, *rows, *weights],
        [SMEM] + [VMEM] * len(rows) + [HBM, HBM],
        after,
        [pltpu.VMEM((slots, depth, width), BF16), pltpu.SemaphoreType.DMA((slots * pieces,))],
        limit=30,
    )


def add_to_send(place, full, got, after):
    def kernel(place_ref, full_ref, got_ref, out_ref):
        @pl.when(place_ref[0] == 0)
        def _():
            for e in range(full_ref.shape[1]):
                for i in range(2):
                    out_ref[i, e] = (full_ref[i, e] + got_ref[i, e].astype(F32)).astype(BF16)

    shape = jax.ShapeDtypeStruct(full.shape, BF16)
    return call(kernel, "add_to_send", shape, [place, full, got], [SMEM, VMEM, VMEM], after)


def hidden_values(place, full, got, after):
    widths = [part.shape[3] for part in full]

    def kernel(place_ref, *refs):
        out_ref = refs[-1]

        @pl.when(place_ref[0] == 1)
        def _():
            start = 0
            for c, width in enumerate(widths):
                full_ref, got_ref = refs[c], refs[len(widths) + c]
                for e in range(out_ref.shape[0]):
                    gate = full_ref[0, e] + got_ref[0, e].astype(F32)
                    up = full_ref[1, e] + got_ref[1, e].astype(F32)
                    value = gate / (1.0 + jnp.exp(-gate)) * up
                    out_ref[e, :, start : start + width] = value.astype(BF16)
                start += width

    shape = jax.ShapeDtypeStruct(full[0].shape[1:3] + (sum(widths),), BF16)
    specs = [SMEM] + [VMEM] * (2 * len(widths))
    return call(kernel, "hidden_values", shape, [place, *full, *got], specs, after)


def pass_on(value, after):
    def kernel(value_ref, out_ref):
        del value_ref, out_ref

    shape = jax.ShapeDtypeStruct(value.shape, value.dtype)
    return call(kernel, "pass_on", shape, [value], [ANY], after, aliases={0: 0})


def down(place, held, down_weight, starts, widths, totals, row_counts, after):
    local_count, count, width = held[0].shape
    features = down_weight.shape[2]
    half = down_weight.shape[1] // 2

    def kernel(place_ref, *refs):
        held_refs, weight_ref = refs[:4], refs[4]
        total_refs = refs[5 : 5 + len(totals)]
        out_refs, hidden = refs[5 + len(totals) : -1], refs[-1]
        for part in range(2):
            for kind in range(2):

                @pl.when(place_ref[0] == 1 - kind)
                def _():
                    hidden[part] = held_refs[part * 2 + kind][...]

        for e in range(local_count):
            product = None
            for part in range(2):
                side = place_ref[1] if part == 0 else (1 - place_ref[1])
                column = 0
                for start, size in zip(starts, widths):
                    row = pl.multiple_of(side * half + start, 128)
                    value = jnp.dot(
                        hidden[part, e, :, column : column + size],
                        weight_ref[e, pl.ds(row, size), :],
                        preferred_element_type=F32,
                    )
                    product = value if product is None else product + value
                    column += size
            first = 0
            for i, rows in enumerate(row_counts):
                value = product[first : first + rows]
                out_refs[i][e] = total_refs[i][e] + value if totals else value
                first += rows

    return call(
        kernel,
        "down",
        [jax.ShapeDtypeStruct((local_count, rows, features), F32) for rows in row_counts],
        [place, *held, down_weight, *totals],
        [SMEM] + [VMEM] * (5 + len(totals)),
        after,
        [pltpu.VMEM((2,) + held[0].shape, BF16)],
        limit=6 + 2 * local_count * count * features * 4 // MIB,
    )


def combine(group, ids, weights, sums, groups):
    local_count, _, features = sums[0].shape
    tokens = ids.shape[1]
    block = tokens // groups

    def kernel(group_ref, ids_ref, weights_ref, *refs):
        sum_refs, own_ref, sent = refs[: len(sums)], refs[len(sums)], refs[len(sums) + 1 :]
        hit, named = slot_hits(ids_ref[...], group_ref[0], local_count)
        scale = sum(
            jnp.where(named[k], weights_ref[k : k + 1, :], 0.0) for k in range(len(named))
        )
        scale = jnp.where(hit, scale, 0.0)
        scale_high = scale.astype(BF16)
        scale_low = (scale - scale_high.astype(F32)).astype(BF16)
        rows = jnp.concatenate(
            [functools.reduce(jnp.add, [ref[e] for ref in sum_refs]) for e in range(local_count)],
            axis=0,
        )
        rows_high = rows.astype(BF16)
        rows_low = (rows - rows_high.astype(F32)).astype(BF16)

        def product(a, b):
            return lax.dot_general(
                a, b, (((0,), (0,)), ((), ())), preferred_element_type=F32
            )

        mixed = (
            product(scale_high, rows_high)
            + product(scale_high, rows_low)
            + product(scale_low, rows_high)
        )
        for place in range(groups):
            piece = mixed[place * block : (place + 1) * block]
            step = group_ref[0] ^ place

            @pl.when(step == 0)
            def _():
                own_ref[...] = piece

            for other in range(1, groups):

                @pl.when(step == other)
                def _():
                    sent[other - 1][...] = piece.astype(BF16)

    return call(
        kernel,
        "combine",
        [jax.ShapeDtypeStruct((block, features), F32)]
        + [jax.ShapeDtypeStruct((block, features), BF16)] * (groups - 1),
        [group, ids, weights, *sums],
        [SMEM] + [VMEM] * (2 + len(sums)),
        [],
    )


def place_blocks(group, pieces):
    block, features = pieces[0].shape

    def kernel(group_ref, *refs):
        out_ref = refs[-1]
        for step, piece_ref in enumerate(refs[:-1]):
            start = pl.multiple_of((group_ref[0] ^ step) * block, block)
            out_ref[pl.ds(start, block), :] = piece_ref[...]

    shape = jax.ShapeDtypeStruct((block * len(pieces), features), BF16)
    return call(
        kernel, "place_blocks", shape, [group, *pieces], [SMEM] + [VMEM] * len(pieces), []
    )


def local(mesh_shape, tokens, expert_ids, route_weights, gate_weight, up_weight, down_weight):
    shards, groups, line = mesh_shape["dp"], mesh_shape["expert"], mesh_shape["blk"]
    local_count, _, hidden_count = gate_weight.shape
    group = lax.axis_index("expert").astype(jnp.int32).reshape(1)
    line_at = lax.axis_index("blk")
    at_end = (line_at == 0) | (line_at == line - 1)
    near = line_at >= line // 2
    place = jnp.stack([at_end, near]).astype(jnp.int32)
    ids, choice_weights = expert_ids.T, route_weights.T
    swap = [(0, 1), (1, 0)]
    hops = {"1": [(0, 1), (3, 2)], "2": [(0, 0), (1, 2), (2, 1), (3, 3)], "3": [(1, 0), (2, 3)]}

    rows = pick(group, ids, tokens, local_count)
    if shards == 2:
        rows = [rows, lax.ppermute(rows, "dp", swap)]
    else:
        rows = [lax.all_gather(rows, "dp", axis=1, tiled=True)]
    row_counts = [part.shape[1] for part in rows]

    widths = chunk_widths(hidden_count // 2)
    starts = [sum(widths[:c]) for c in range(len(widths))]
    far, short, near_part, values, got, totals, after = {}, {}, {}, {}, {}, [], []
    for name, c in ORDER:
        if c >= len(widths):
            continue
        group_of = [q for q in GROUPS.get(c, ()) if q < len(widths)]
        if name == "g":
            far[c], short[c], near_part[c] = gate_up(
                place, rows, (gate_weight, up_weight), starts[c], widths[c], after
            )
            after = [far[c]]
        elif name == "s":
            values[c] = hidden_values(
                place, [near_part[q] for q in group_of], [got["h3", q] for q in group_of], after
            )
            after = [values[c]]
        elif name == "d":
            totals = down(
                place,
                [values[c], got["b1", c], got["b3", c], got["b2", c]],
                down_weight,
                [starts[q] for q in group_of],
                [widths[q] for q in group_of],
                totals,
                row_counts,
                after,
            )
            after = [totals[0]]
        else:
            if name == "h1":
                sent = short[c]
            elif name == "b1":
                sent = values[c]
            else:
                before = (name[0] + str(int(name[1]) - 1), c)
                if name[0] == "h":
                    full = far[c] if name == "h2" else near_part[c]
                    sent = add_to_send(place, full, got[before], after)
                else:
                    sent = got[before] = pass_on(got[before], after)
                after = [sent]
            got[name, c] = lax.ppermute(sent, "blk", hops[name[1]])

    if shards == 2:
        sums = [totals[0], lax.ppermute(totals[1], "dp", swap)]
    else:
        sums = [lax.psum_scatter(totals[0], "dp", scatter_dimension=1, tiled=True)]
    own, *sent = combine(group, ids, choice_weights, sums, groups)
    for step in range(groups - 1, 0, -1):
        exchange = [(i, i ^ step) for i in range(groups)]
        own = own + lax.ppermute(sent[step - 1], "expert", exchange).astype(F32)
    block = own.astype(BF16)
    pieces = [block]
    for step in range(1, groups):
        pieces.append(lax.ppermute(block, "expert", [(i, i ^ step) for i in range(groups)]))
    return place_blocks(group, pieces)


def solution(mesh):
    placed = (
        P("dp", "blk"),
        P("dp", None),
        P("dp", None),
        P("expert", "blk", "dp"),
        P("expert", "blk", "dp"),
        P("expert", "dp", "blk"),
    )
    return jax.shard_map(
        functools.partial(local, dict(mesh.shape)),
        mesh=mesh,
        in_specs=placed,
        out_specs=P("dp", "blk"),
        check_vma=False,
    )
```

time: 156 us -> 145 us (0.929)
  waiting for transfers between devices: 60.8 us -> 29.8 us
  starting transfers between devices: 53 us -> 67.9 us
  Pallas kernels: 39 us -> 44.5 us
    ppermute x30 -> x27, waiting for transfers between devices: 49 us -> 17.7 us  [local(): got[name, c] = lax.ppermute(sent, 'blk', hops[name[1]])]
    ppermute x30 -> x27, starting transfers between devices: 45.3 us -> 60.2 us  [local(): got[name, c] = lax.ppermute(sent, 'blk', hops[name[1]])]
    pallas_call x37 -> x34, Pallas kernels: 39 us -> 44.5 us  [call(): pl.pallas_call(body, out_shape=outs, in_specs=list(specs) + [ANY] * len(a...]
  transfers between devices with their start and end apart: 38 -> 35, of which waited for: 15 -> 14; matrix products, arithmetic and copies ran while one was open for 0% -> 0% of each run, Pallas kernels for 19% -> 24%
where the time goes in v4:
time: 145 us
  starting transfers between devices  67.9 us (47%)
  Pallas kernels  44.5 us (31%)
  waiting for transfers between devices  29.8 us (21%)
  local copies, waits for them, and re-layouts  1.72 us (1%)
    ppermute x27, starting transfers between devices, local(): got[name, c] = lax.ppermute(sent, 'blk', hops[name[1]])  60.2 us
    pallas_call x34, Pallas kernels, call(): pl.pallas_call(body, out_shape=outs, in_specs=list(specs) + [ANY] * len(a...  44.5 us
    ppermute x27, waiting for transfers between devices, local(): got[name, c] = lax.ppermute(sent, 'blk', hops[name[1]])  17.7 us
    ppermute x3, waiting for transfers between devices, local(): lax.ppermute(block, 'expert', [(i, i ^ step) for i in range(groups)])  4.61 us
    ppermute x3, waiting for transfers between devices, local(): own = own + lax.ppermute(sent[step - 1], 'expert', exchange).astype(F32)  4.41 us
    ppermute x3, starting transfers between devices, local(): own = own + lax.ppermute(sent[step - 1], 'expert', exchange).astype(F32)  3.55 us
    ppermute x3, starting transfers between devices, local(): lax.ppermute(block, 'expert', [(i, i ^ step) for i in range(groups)])  3.55 us
  transfers between devices with their start and end apart: 35, of which 14 were waited for; matrix products, arithmetic and copies ran while one was open for 0% of the time, Pallas kernels for 24%

profile of v4, /device:TPU:0, one launch (start us, length us, event | category | flops | bytes accessed | tf_op | source)
XLA Modules:
  0.0 144.8 jit_solution(18371308766487929988)
XLA Ops:
  0.0 1.0 copy-done
  2.6 1.1 collective-permute-done.refs_2_
  3.8 5.7 %gate_up.5 = (f32[2,2,96,512]{3,2,1,0:T(8,128)S(1)}, bf16[2,2,96,512]{3,2,1,0:T(8,128)(2,1)S(1)}, f32[2,2,96,512]{3,2,1,0:T(8,128)S(1)}) custom-call(s32[2]{0:T(128)S(1)} %add_convert_fusion.1.refs_0_, bf16[2,48,1536]{2,1,0:T(8,128)(2,1)S(1)} %pick.1.refs_1_, bf16[2,48,1536]{2,1,0:T(8,128)(2,1)S(1)} %collective-permute-done.refs_2_, ...), custom_call_target="tpu_custom_call" | custom-call | tf_op jit(solution)/shard_map/gate_up/pallas_call | solution.py:37
  9.5 4.9 %collective-permute-start.2 = (bf16[2,2,96,512]{3,2,1,0:T(8,128)(2,1)S(1)}, bf16[2,2,96,512]{3,2,1,0:T(8,128)(2,1)S(1)}, u32[]{:S(2)}, u32[]{:S(2)}) collective-permute-start(bf16[2,2,96,512]{3,2,1,0:T(8,128)(2,1)S(1)} %get-tuple-element.36), channel_id=1, source_target_pairs={{0,1},{3,2},{4,5},{7,6},{8,9},{11,10},{12,13},{15,14},{16,17},{19,... | collective-permute-start | bytes 1179656 | tf_op jit(solution)/shard_map/ppermute | solution.py:370
  14.4 5.8 %gate_up.6 = (f32[2,2,96,512]{3,2,1,0:T(8,128)S(1)}, bf16[2,2,96,512]{3,2,1,0:T(8,128)(2,1)S(1)}, f32[2,2,96,512]{3,2,1,0:T(8,128)S(1)}) custom-call(s32[2]{0:T(128)S(1)} %add_convert_fusion.1.refs_0_, bf16[2,48,1536]{2,1,0:T(8,128)(2,1)S(1)} %pick.1.refs_1_, bf16[2,48,1536]{2,1,0:T(8,128)(2,1)S(1)} %collective-permute-done.refs_2_, ...), custom_call_target="tpu_custom_call" | custom-call | tf_op jit(solution)/shard_map/gate_up/pallas_call | solution.py:37
  20.2 4.7 %gate_up.7 = (f32[2,2,96,256]{3,2,1,0:T(8,128)S(1)}, bf16[2,2,96,256]{3,2,1,0:T(8,128)(2,1)S(1)}, f32[2,2,96,256]{3,2,1,0:T(8,128)S(1)}) custom-call(s32[2]{0:T(128)S(1)} %add_convert_fusion.1.refs_0_, bf16[2,48,1536]{2,1,0:T(8,128)(2,1)S(1)} %pick.1.refs_1_, bf16[2,48,1536]{2,1,0:T(8,128)(2,1)S(1)} %collective-permute-done.refs_2_, ...), custom_call_target="tpu_custom_call" | custom-call | tf_op jit(solution)/shard_map/gate_up/pallas_call | solution.py:37
  26.1 5.5 %collective-permute-start.1 = (bf16[2,2,96,512]{3,2,1,0:T(8,128)(2,1)S(1)}, bf16[2,2,96,512]{3,2,1,0:T(8,128)(2,1)S(1)}, u32[]{:S(2)}, u32[]{:S(2)}) collective-permute-start(bf16[2,2,96,512]{3,2,1,0:T(8,128)(2,1)S(1)} %get-tuple-element.34), channel_id=1, source_target_pairs={{0,1},{3,2},{4,5},{7,6},{8,9},{11,10},{12,13},{15,14},{16,17},{19,... | collective-permute-start | bytes 1179656 | tf_op jit(solution)/shard_map/ppermute | solution.py:370
  31.6 1.3 collective-permute-start.4
  32.9 5.8 %gate_up.8 = (f32[2,2,96,512]{3,2,1,0:T(8,128)S(1)}, bf16[2,2,96,512]{3,2,1,0:T(8,128)(2,1)S(1)}, f32[2,2,96,512]{3,2,1,0:T(8,128)S(1)}) custom-call(s32[2]{0:T(128)S(1)} %add_convert_fusion.1.refs_0_, bf16[2,48,1536]{2,1,0:T(8,128)(2,1)S(1)} %pick.1.refs_1_, bf16[2,48,1536]{2,1,0:T(8,128)(2,1)S(1)} %collective-permute-done.refs_2_, ...), custom_call_target="tpu_custom_call" | custom-call | tf_op jit(solution)/shard_map/gate_up/pallas_call | solution.py:37
  38.6 1.3 collective-permute-start.6
  40.0 5.3 %collective-permute-done.4.refs_2_ = bf16[2,2,96,256]{3,2,1,0:T(8,128)(2,1)S(1)} collective-permute-done((bf16[2,2,96,256]{3,2,1,0:T(8,128)(2,1)S(1)}, bf16[2,2,96,256]{3,2,1,0:T(8,128)(2,1)S(1)}, u32[]{:S(2)}, u32[]{:S(2)}) %collective-permute-start.4) | collective-permute-done | bytes 196640 | tf_op jit(solution)/shard_map/ppermute | solution.py:370
  47.7 0.8 collective-permute-start.11
  48.6 1.6 %collective-permute-start.10 = (bf16[2,2,96,512]{3,2,1,0:T(8,128)(2,1)S(1)}, bf16[2,2,96,512]{3,2,1,0:T(8,128)(2,1)S(1)}, u32[]{:S(2)}, u32[]{:S(2)}) collective-permute-start(bf16[2,2,96,512]{3,2,1,0:T(8,128)(2,1)S(1)} %add_to_send.12.refs_3_), channel_id=1, source_target_pairs={{1,0},{2,3},{5,4},{6,7},{9,8},{10,11},{13,12},{14,15},{17,16},{18,... | collective-permute-start | bytes 1179656 | tf_op jit(solution)/shard_map/ppermute | solution.py:370
  50.1 5.5 %gate_up.9 = (f32[2,2,96,256]{3,2,1,0:T(8,128)S(1)}, bf16[2,2,96,256]{3,2,1,0:T(8,128)(2,1)S(1)}, f32[2,2,96,256]{3,2,1,0:T(8,128)S(1)}) custom-call(s32[2]{0:T(128)S(1)} %add_convert_fusion.1.refs_0_, bf16[2,48,1536]{2,1,0:T(8,128)(2,1)S(1)} %pick.1.refs_1_, bf16[2,48,1536]{2,1,0:T(8,128)(2,1)S(1)} %collective-permute-done.refs_2_, ...), custom_call_target="tpu_custom_call" | custom-call | tf_op jit(solution)/shard_map/gate_up/pallas_call | solution.py:37
  57.4 1.3 collective-permute-start.9
  59.3 1.3 collective-permute-start.14
  60.6 11.1 %collective-permute-start.5 = (bf16[2,2,96,256]{3,2,1,0:T(8,128)(2,1)S(1)}, bf16[2,2,96,256]{3,2,1,0:T(8,128)(2,1)S(1)}, u32[]{:S(2)}, u32[]{:S(2)}) collective-permute-start(bf16[2,2,96,256]{3,2,1,0:T(8,128)(2,1)S(1)} %get-tuple-element.42), channel_id=1, source_target_pairs={{0,1},{3,2},{4,5},{7,6},{8,9},{11,10},{12,13},{15,14},{16,17},{19,... | collective-permute-start | bytes 589832 | tf_op jit(solution)/shard_map/ppermute | solution.py:370
  72.4 0.8 hidden_values.4.refs_3_.refs_1_
  73.1 1.3 collective-permute-start.13
  75.0 1.4 collective-permute-start.17
  77.7 1.3 collective-permute-done.14.refs_2_
  79.8 5.4 %collective-permute-start.16 = (bf16[2,96,512]{2,1,0:T(8,128)(2,1)S(1)}, bf16[2,96,512]{2,1,0:T(8,128)(2,1)S(1)}, u32[]{:S(2)}, u32[]{:S(2)}) collective-permute-start(bf16[2,96,512]{2,1,0:T(8,128)(2,1)S(1)} %hidden_values.5.refs_1_), channel_id=1, source_target_pairs={{0,1},{3,2},{4,5},{7,6},{8,9},{11,10},{12,13},{15,14},{16,17},{19,... | collective-permute-start | bytes 589832 | tf_op jit(solution)/shard_map/ppermute | solution.py:370
  86.4 1.3 collective-permute-start.15
  87.8 0.7 hidden_values.6.refs_1_
  88.5 4.4 %collective-permute-start.20 = (bf16[2,96,512]{2,1,0:T(8,128)(2,1)S(1)}, bf16[2,96,512]{2,1,0:T(8,128)(2,1)S(1)}, u32[]{:S(2)}, u32[]{:S(2)}) collective-permute-start(bf16[2,96,512]{2,1,0:T(8,128)(2,1)S(1)} %hidden_values.6.refs_1_), channel_id=1, source_target_pairs={{0,1},{3,2},{4,5},{7,6},{8,9},{11,10},{12,13},{15,14},{16,17},{19,... | collective-permute-start | bytes 589832 | tf_op jit(solution)/shard_map/ppermute | solution.py:370
  94.7 1.4 collective-permute-done.20.refs_0_
  96.7 6.6 %collective-permute-start.18 = (bf16[2,96,256]{2,1,0:T(8,128)(2,1)S(1)}, bf16[2,96,256]{2,1,0:T(8,128)(2,1)S(1)}, u32[]{:S(2)}, u32[]{:S(2)}) collective-permute-start(bf16[2,96,256]{2,1,0:T(8,128)(2,1)S(1)} %hidden_values.7.refs_1_), channel_id=1, source_target_pairs={{0,1},{3,2},{4,5},{7,6},{8,9},{11,10},{12,13},{15,14},{16,17},{19,... | collective-permute-start | bytes 294920 | tf_op jit(solution)/shard_map/ppermute | solution.py:370
  103.4 1.3 collective-permute-start.27
  104.7 1.5 %collective-permute-start.23 = (bf16[2,96,512]{2,1,0:T(8,128)(2,1)S(1)}, bf16[2,96,512]{2,1,0:T(8,128)(2,1)S(1)}, u32[]{:S(2)}, u32[]{:S(2)}) collective-permute-start(bf16[2,96,512]{2,1,0:T(8,128)(2,1)S(1)} %pass_on.12.refs_1_.refs_4_), channel_id=1, source_target_pairs={{1,0},{2,3},{5,4},{6,7},{9,8},{10,11},{13,12},{14,15},{17,16},{18,... | collective-permute-start | bytes 589832 | tf_op jit(solution)/shard_map/ppermute | solution.py:370
  106.2 1.3 collective-permute-start.26
  108.2 7.3 %collective-permute-done.23.refs_3_ = bf16[2,96,512]{2,1,0:T(8,128)(2,1)S(1)} collective-permute-done((bf16[2,96,512]{2,1,0:T(8,128)(2,1)S(1)}, bf16[2,96,512]{2,1,0:T(8,128)(2,1)S(1)}, u32[]{:S(2)}, u32[]{:S(2)}) %collective-permute-start.23) | collective-permute-done | bytes 196640 | tf_op jit(solution)/shard_map/ppermute | solution.py:370
  115.5 1.7 %down.4 = (f32[2,48,1536]{2,1,0:T(8,128)S(1)}, f32[2,48,1536]{2,1,0:T(8,128)S(1)}) custom-call(s32[2]{0:T(128)S(1)} %add_convert_fusion.1.refs_0_, bf16[2,96,512]{2,1,0:T(8,128)(2,1)S(1)} %hidden_values.5.refs_1_, bf16[2,96,512]{2,1,0:T(8,128)(2,1)S(1)} %pass_on.9.refs_3_.refs_2_, bf16[2,96,512]{2,1,0:T(8,128)(2,1)S(1)} %collective-permute-done.23.refs_3_, ...), custom_call_target="tpu_custom_call" | custom-call | tf_op jit(solution)/shard_map/down/pallas_call | solution.py:37
  117.3 1.3 collective-permute-start.25
  118.6 2.3 %down.5 = (f32[2,48,1536]{2,1,0:T(8,128)S(1)}, f32[2,48,1536]{2,1,0:T(8,128)S(1)}) custom-call(s32[2]{0:T(128)S(1)} %add_convert_fusion.1.refs_0_, bf16[2,96,768]{2,1,0:T(8,128)(2,1)S(1)} %hidden_values.4.refs_3_.refs_1_, bf16[2,96,768]{2,1,0:T(8,128)(2,1)S(1)} %pass_on.8.refs_3_.refs_2_, bf16[2,96,768]{2,1,0:T(8,128)(2,1)S(1)} %collective-permute-done.27.refs_3_, ...), custom_call_target="tpu_custom_call" | custom-call | tf_op jit(solution)/shard_map/down/pallas_call | solution.py:37
  120.9 1.7 %down.6 = (f32[2,48,1536]{2,1,0:T(8,128)S(1)}, f32[2,48,1536]{2,1,0:T(8,128)S(1)}) custom-call(s32[2]{0:T(128)S(1)} %add_convert_fusion.1.refs_0_, bf16[2,96,512]{2,1,0:T(8,128)(2,1)S(1)} %hidden_values.6.refs_1_, bf16[2,96,512]{2,1,0:T(8,128)(2,1)S(1)} %pass_on.11.refs_1_.refs_2_, bf16[2,96,512]{2,1,0:T(8,128)(2,1)S(1)} %collective-permute-done.26.refs_3_, ...), custom_call_target="tpu_custom_call" | custom-call | tf_op jit(solution)/shard_map/down/pallas_call | solution.py:37
  122.6 1.2 collective-permute-done.25.refs_3_
  123.8 1.2 down.7
  125.1 2.0 %collective-permute-done.28.refs_4_ = f32[2,48,1536]{2,1,0:T(8,128)S(1)} collective-permute-done((f32[2,48,1536]{2,1,0:T(8,128)S(1)}, f32[2,48,1536]{2,1,0:T(8,128)S(1)}, u32[]{:S(2)}, u32[]{:S(2)}) %collective-permute-start.28) | collective-permute-done | bytes 589856 | tf_op jit(solution)/shard_map/ppermute | solution.py:373
  127.1 0.7 combine.1
  127.8 2.5 %collective-permute-start.29 = (bf16[32,1536]{1,0:T(8,128)(2,1)S(1)}, bf16[32,1536]{1,0:T(8,128)(2,1)S(1)}, u32[]{:S(2)}, u32[]{:S(2)}) collective-permute-start(bf16[32,1536]{1,0:T(8,128)(2,1)S(1)} %get-tuple-element.56), channel_id=1, source_target_pairs={{0,12},{4,8},{8,4},{12,0},{1,13},{5,9},{9,5},{13,1},{2,14},{6,10},... | collective-permute-start | bytes 294920 | tf_op jit(solution)/shard_map/ppermute | solution.py:379
  131.4 2.3 %collective-permute-done.29 = bf16[32,1536]{1,0:T(8,128)(2,1)S(1)} collective-permute-done((bf16[32,1536]{1,0:T(8,128)(2,1)S(1)}, bf16[32,1536]{1,0:T(8,128)(2,1)S(1)}, u32[]{:S(2)}, u32[]{:S(2)}) %collective-permute-start.29) | collective-permute-done | bytes 98336 | tf_op jit(solution)/shard_map/ppermute | solution.py:379
  133.7 2.0 %collective-permute-done.30 = bf16[32,1536]{1,0:T(8,128)(2,1)S(1)} collective-permute-done((bf16[32,1536]{1,0:T(8,128)(2,1)S(1)}, bf16[32,1536]{1,0:T(8,128)(2,1)S(1)}, u32[]{:S(2)}, u32[]{:S(2)}) %collective-permute-start.30) | collective-permute-done | bytes 98336 | tf_op jit(solution)/shard_map/ppermute | solution.py:379
  135.8 1.6 %collective-permute-start.32 = (bf16[32,1536]{1,0:T(8,128)(2,1)S(1)}, bf16[32,1536]{1,0:T(8,128)(2,1)S(1)}, u32[]{:S(2)}, u32[]{:S(2)}) collective-permute-start(bf16[32,1536]{1,0:T(8,128)(2,1)S(1)} %add_convert_fusion.refs_1_), channel_id=1, source_target_pairs={{0,4},{4,0},{8,12},{12,8},{1,5},{5,1},{9,13},{13,9},{2,6},{6,2},{1... | collective-permute-start | bytes 294920 | tf_op jit(solution)/shard_map/ppermute | solution.py:383
  137.5 0.7 collective-permute-start.33
  138.2 1.2 collective-permute-start.34
  139.4 1.1 collective-permute-done.32.refs_2_
  140.5 3.5 %collective-permute-done.33.refs_3_ = bf16[32,1536]{1,0:T(8,128)(2,1)S(1)} collective-permute-done((bf16[32,1536]{1,0:T(8,128)(2,1)S(1)}, bf16[32,1536]{1,0:T(8,128)(2,1)S(1)}, u32[]{:S(2)}, u32[]{:S(2)}) %collective-permute-start.33) | collective-permute-done | bytes 98336 | tf_op jit(solution)/shard_map/ppermute | solution.py:383
  144.0 0.8 place_blocks.1
  (79 shorter events, 16.3 us)
Async XLA Ops:
  0.0 1.0 copy-start
  1.0 0.7 copy-start.1
  2.0 1.7 %collective-permute-start = (bf16[2,48,1536]{2,1,0:T(8,128)(2,1)S(1)}, bf16[2,48,1536]{2,1,0:T(8,128)(2,1)S(1)}, u32[]{:S(2)}, u32[]{:S(2)}) collective-permute-start(bf16[2,48,1536]{2,1,0:T(8,128)(2,1)S(1)} %pick.1.refs_1_), channel_id=1, source_target_pairs={{0,16},{16,0},{1,17},{17,1},{2,18},{18,2},{3,19},{19,3},{4,20},{20... | collective-permute-start | bytes 884744 | tf_op jit(solution)/shard_map/ppermute | solution.py:323
  9.5 15.3 %collective-permute-start.2 = (bf16[2,2,96,512]{3,2,1,0:T(8,128)(2,1)S(1)}, bf16[2,2,96,512]{3,2,1,0:T(8,128)(2,1)S(1)}, u32[]{:S(2)}, u32[]{:S(2)}) collective-permute-start(bf16[2,2,96,512]{3,2,1,0:T(8,128)(2,1)S(1)} %get-tuple-element.36), channel_id=1, source_target_pairs={{0,1},{3,2},{4,5},{7,6},{8,9},{11,10},{12,13},{15,14},{16,17},{19,... | collective-permute-start | bytes 1179656 | tf_op jit(solution)/shard_map/ppermute | solution.py:370
  25.4 21.1 %collective-permute-start.3 = (bf16[2,2,96,512]{3,2,1,0:T(8,128)(2,1)S(1)}, bf16[2,2,96,512]{3,2,1,0:T(8,128)(2,1)S(1)}, u32[]{:S(2)}, u32[]{:S(2)}) collective-permute-start(bf16[2,2,96,512]{3,2,1,0:T(8,128)(2,1)S(1)} %add_to_send.10.refs_5_), channel_id=1, source_target_pairs={{0,0},{1,2},{2,1},{3,3},{4,4},{5,6},{6,5},{7,7},{8,8},{9,10},{10,9... | collective-permute-start | bytes 1179656 | tf_op jit(solution)/shard_map/ppermute | solution.py:370
  26.1 21.0 %collective-permute-start.1 = (bf16[2,2,96,512]{3,2,1,0:T(8,128)(2,1)S(1)}, bf16[2,2,96,512]{3,2,1,0:T(8,128)(2,1)S(1)}, u32[]{:S(2)}, u32[]{:S(2)}) collective-permute-start(bf16[2,2,96,512]{3,2,1,0:T(8,128)(2,1)S(1)} %get-tuple-element.34), channel_id=1, source_target_pairs={{0,1},{3,2},{4,5},{7,6},{8,9},{11,10},{12,13},{15,14},{16,17},{19,... | collective-permute-start | bytes 1179656 | tf_op jit(solution)/shard_map/ppermute | solution.py:370
  31.6 13.7 %collective-permute-start.4 = (bf16[2,2,96,256]{3,2,1,0:T(8,128)(2,1)S(1)}, bf16[2,2,96,256]{3,2,1,0:T(8,128)(2,1)S(1)}, u32[]{:S(2)}, u32[]{:S(2)}) collective-permute-start(bf16[2,2,96,256]{3,2,1,0:T(8,128)(2,1)S(1)} %get-tuple-element.38), channel_id=1, source_target_pairs={{0,1},{3,2},{4,5},{7,6},{8,9},{11,10},{12,13},{15,14},{16,17},{19,... | collective-permute-start | bytes 589832 | tf_op jit(solution)/shard_map/ppermute | solution.py:370
  38.6 17.5 %collective-permute-start.6 = (bf16[2,2,96,512]{3,2,1,0:T(8,128)(2,1)S(1)}, bf16[2,2,96,512]{3,2,1,0:T(8,128)(2,1)S(1)}, u32[]{:S(2)}, u32[]{:S(2)}) collective-permute-start(bf16[2,2,96,512]{3,2,1,0:T(8,128)(2,1)S(1)} %get-tuple-element.44), channel_id=1, source_target_pairs={{0,1},{3,2},{4,5},{7,6},{8,9},{11,10},{12,13},{15,14},{16,17},{19,... | collective-permute-start | bytes 1179656 | tf_op jit(solution)/shard_map/ppermute | solution.py:370
  45.9 9.7 %collective-permute-start.7 = (bf16[2,2,96,256]{3,2,1,0:T(8,128)(2,1)S(1)}, bf16[2,2,96,256]{3,2,1,0:T(8,128)(2,1)S(1)}, u32[]{:S(2)}, u32[]{:S(2)}) collective-permute-start(bf16[2,2,96,256]{3,2,1,0:T(8,128)(2,1)S(1)} %add_to_send.11.refs_3_), channel_id=1, source_target_pairs={{0,0},{1,2},{2,1},{3,3},{4,4},{5,6},{6,5},{7,7},{8,8},{9,10},{10,9... | collective-permute-start | bytes 589832 | tf_op jit(solution)/shard_map/ppermute | solution.py:370
  47.7 67.8 %slice-start = ((s8[25165824]{0:T(1024)(128)(4,1)}), s8[4194304]{0:T(1024)(128)(4,1)S(1)}, s32[]{:S(2)}) async-start(s8[25165824]{0:T(1024)(128)(4,1)} %bitcast.5), calls=%async_computation | async-start | bytes 8388608
  47.7 67.8 %slice-start.1 = ((s8[25165824]{0:T(1024)(128)(4,1)}), s8[4194304]{0:T(1024)(128)(4,1)S(1)}, s32[]{:S(2)}) async-start(s8[25165824]{0:T(1024)(128)(4,1)} %bitcast.5), calls=%async_computation.1 | async-start | bytes 8388608
  47.7 67.8 %slice-start.2 = ((s8[25165824]{0:T(1024)(128)(4,1)}), s8[4194304]{0:T(1024)(128)(4,1)S(1)}, s32[]{:S(2)}) async-start(s8[25165824]{0:T(1024)(128)(4,1)} %bitcast.5), calls=%async_computation.2 | async-start | bytes 8388608
  47.7 67.8 %slice-start.3 = ((s8[25165824]{0:T(1024)(128)(4,1)}), s8[4194304]{0:T(1024)(128)(4,1)S(1)}, s32[]{:S(2)}) async-start(s8[25165824]{0:T(1024)(128)(4,1)} %bitcast.5), calls=%async_computation.3 | async-start | bytes 8388608
  47.7 67.8 %slice-start.4 = ((s8[25165824]{0:T(1024)(128)(4,1)}), s8[4194304]{0:T(1024)(128)(4,1)S(1)}, s32[]{:S(2)}) async-start(s8[25165824]{0:T(1024)(128)(4,1)} %bitcast.5), calls=%async_computation.4 | async-start | bytes 8388608
  47.7 11.0 %collective-permute-start.11 = (bf16[2,2,96,512]{3,2,1,0:T(8,128)(2,1)S(1)}, bf16[2,2,96,512]{3,2,1,0:T(8,128)(2,1)S(1)}, u32[]{:S(2)}, u32[]{:S(2)}) collective-permute-start(bf16[2,2,96,512]{3,2,1,0:T(8,128)(2,1)S(1)} %add_to_send.13.refs_5_), channel_id=1, source_target_pairs={{0,0},{1,2},{2,1},{3,3},{4,4},{5,6},{6,5},{7,7},{8,8},{9,10},{10,9... | collective-permute-start | bytes 1179656 | tf_op jit(solution)/shard_map/ppermute | solution.py:370
  48.6 23.8 %collective-permute-start.10 = (bf16[2,2,96,512]{3,2,1,0:T(8,128)(2,1)S(1)}, bf16[2,2,96,512]{3,2,1,0:T(8,128)(2,1)S(1)}, u32[]{:S(2)}, u32[]{:S(2)}) collective-permute-start(bf16[2,2,96,512]{3,2,1,0:T(8,128)(2,1)S(1)} %add_to_send.12.refs_3_), channel_id=1, source_target_pairs={{1,0},{2,3},{5,4},{6,7},{9,8},{10,11},{13,12},{14,15},{17,16},{18,... | collective-permute-start | bytes 1179656 | tf_op jit(solution)/shard_map/ppermute | solution.py:370
  56.7 17.7 %collective-permute-start.8 = (bf16[2,2,96,512]{3,2,1,0:T(8,128)(2,1)S(1)}, bf16[2,2,96,512]{3,2,1,0:T(8,128)(2,1)S(1)}, u32[]{:S(2)}, u32[]{:S(2)}) collective-permute-start(bf16[2,2,96,512]{3,2,1,0:T(8,128)(2,1)S(1)} %add_to_send.15.refs_3_), channel_id=1, source_target_pairs={{0,0},{1,2},{2,1},{3,3},{4,4},{5,6},{6,5},{7,7},{8,8},{9,10},{10,9... | collective-permute-start | bytes 1179656 | tf_op jit(solution)/shard_map/ppermute | solution.py:370
  57.4 14.9 %collective-permute-start.9 = (bf16[2,2,96,256]{3,2,1,0:T(8,128)(2,1)S(1)}, bf16[2,2,96,256]{3,2,1,0:T(8,128)(2,1)S(1)}, u32[]{:S(2)}, u32[]{:S(2)}) collective-permute-start(bf16[2,2,96,256]{3,2,1,0:T(8,128)(2,1)S(1)} %add_to_send.14.refs_3_), channel_id=1, source_target_pairs={{1,0},{2,3},{5,4},{6,7},{9,8},{10,11},{13,12},{14,15},{17,16},{18,... | collective-permute-start | bytes 589832 | tf_op jit(solution)/shard_map/ppermute | solution.py:370
  59.3 19.8 %collective-permute-start.14 = (bf16[2,2,96,512]{3,2,1,0:T(8,128)(2,1)S(1)}, bf16[2,2,96,512]{3,2,1,0:T(8,128)(2,1)S(1)}, u32[]{:S(2)}, u32[]{:S(2)}) collective-permute-start(bf16[2,2,96,512]{3,2,1,0:T(8,128)(2,1)S(1)} %add_to_send.16.refs_5_), channel_id=1, source_target_pairs={{1,0},{2,3},{5,4},{6,7},{9,8},{10,11},{13,12},{14,15},{17,16},{18,... | collective-permute-start | bytes 1179656 | tf_op jit(solution)/shard_map/ppermute | solution.py:370
  60.6 15.9 %collective-permute-start.5 = (bf16[2,2,96,256]{3,2,1,0:T(8,128)(2,1)S(1)}, bf16[2,2,96,256]{3,2,1,0:T(8,128)(2,1)S(1)}, u32[]{:S(2)}, u32[]{:S(2)}) collective-permute-start(bf16[2,2,96,256]{3,2,1,0:T(8,128)(2,1)S(1)} %get-tuple-element.42), channel_id=1, source_target_pairs={{0,1},{3,2},{4,5},{7,6},{8,9},{11,10},{12,13},{15,14},{16,17},{19,... | collective-permute-start | bytes 589832 | tf_op jit(solution)/shard_map/ppermute | solution.py:370
  73.1 12.0 %collective-permute-start.13 = (bf16[2,96,768]{2,1,0:T(8,128)(2,1)S(1)}, bf16[2,96,768]{2,1,0:T(8,128)(2,1)S(1)}, u32[]{:S(2)}, u32[]{:S(2)}) collective-permute-start(bf16[2,96,768]{2,1,0:T(8,128)(2,1)S(1)} %hidden_values.4.refs_3_.refs_1_), channel_id=1, source_target_pairs={{0,1},{3,2},{4,5},{7,6},{8,9},{11,10},{12,13},{15,14},{16,17},{19,... | collective-permute-start | bytes 884744 | tf_op jit(solution)/shard_map/ppermute | solution.py:370
  74.5 41.0 %slice-start.5 = ((s8[25165824]{0:T(1024)(128)(4,1)}), s8[4194304]{0:T(1024)(128)(4,1)S(1)}, s32[]{:S(2)}) async-start(s8[25165824]{0:T(1024)(128)(4,1)} %bitcast.5), calls=%async_computation.5 | async-start | bytes 8388608
  75.0 12.7 %collective-permute-start.17 = (bf16[2,2,96,512]{3,2,1,0:T(8,128)(2,1)S(1)}, bf16[2,2,96,512]{3,2,1,0:T(8,128)(2,1)S(1)}, u32[]{:S(2)}, u32[]{:S(2)}) collective-permute-start(bf16[2,2,96,512]{3,2,1,0:T(8,128)(2,1)S(1)} %add_to_send.17.refs_3_), channel_id=1, source_target_pairs={{1,0},{2,3},{5,4},{6,7},{9,8},{10,11},{13,12},{14,15},{17,16},{18,... | collective-permute-start | bytes 1179656 | tf_op jit(solution)/shard_map/ppermute | solution.py:370
  77.0 8.8 %collective-permute-start.12 = (bf16[2,2,96,256]{3,2,1,0:T(8,128)(2,1)S(1)}, bf16[2,2,96,256]{3,2,1,0:T(8,128)(2,1)S(1)}, u32[]{:S(2)}, u32[]{:S(2)}) collective-permute-start(bf16[2,2,96,256]{3,2,1,0:T(8,128)(2,1)S(1)} %add_to_send.18.refs_3_), channel_id=1, source_target_pairs={{0,0},{1,2},{2,1},{3,3},{4,4},{5,6},{6,5},{7,7},{8,8},{9,10},{10,9... | collective-permute-start | bytes 589832 | tf_op jit(solution)/shard_map/ppermute | solution.py:370
  79.8 13.1 %collective-permute-start.16 = (bf16[2,96,512]{2,1,0:T(8,128)(2,1)S(1)}, bf16[2,96,512]{2,1,0:T(8,128)(2,1)S(1)}, u32[]{:S(2)}, u32[]{:S(2)}) collective-permute-start(bf16[2,96,512]{2,1,0:T(8,128)(2,1)S(1)} %hidden_values.5.refs_1_), channel_id=1, source_target_pairs={{0,1},{3,2},{4,5},{7,6},{8,9},{11,10},{12,13},{15,14},{16,17},{19,... | collective-permute-start | bytes 589832 | tf_op jit(solution)/shard_map/ppermute | solution.py:370
  85.2 9.5 %collective-permute-start.21 = (bf16[2,96,768]{2,1,0:T(8,128)(2,1)S(1)}, bf16[2,96,768]{2,1,0:T(8,128)(2,1)S(1)}, u32[]{:S(2)}, u32[]{:S(2)}) collective-permute-start(bf16[2,96,768]{2,1,0:T(8,128)(2,1)S(1)} %pass_on.8.refs_3_.refs_2_), channel_id=1, source_target_pairs={{0,0},{1,2},{2,1},{3,3},{4,4},{5,6},{6,5},{7,7},{8,8},{9,10},{10,9... | collective-permute-start | bytes 884744 | tf_op jit(solution)/shard_map/ppermute | solution.py:370
  86.4 7.6 %collective-permute-start.15 = (bf16[2,2,96,256]{3,2,1,0:T(8,128)(2,1)S(1)}, bf16[2,2,96,256]{3,2,1,0:T(8,128)(2,1)S(1)}, u32[]{:S(2)}, u32[]{:S(2)}) collective-permute-start(bf16[2,2,96,256]{3,2,1,0:T(8,128)(2,1)S(1)} %add_to_send.19.refs_3_), channel_id=1, source_target_pairs={{1,0},{2,3},{5,4},{6,7},{9,8},{10,11},{13,12},{14,15},{17,16},{18,... | collective-permute-start | bytes 589832 | tf_op jit(solution)/shard_map/ppermute | solution.py:370
  88.5 7.6 %collective-permute-start.20 = (bf16[2,96,512]{2,1,0:T(8,128)(2,1)S(1)}, bf16[2,96,512]{2,1,0:T(8,128)(2,1)S(1)}, u32[]{:S(2)}, u32[]{:S(2)}) collective-permute-start(bf16[2,96,512]{2,1,0:T(8,128)(2,1)S(1)} %hidden_values.6.refs_1_), channel_id=1, source_target_pairs={{0,1},{3,2},{4,5},{7,6},{8,9},{11,10},{12,13},{15,14},{16,17},{19,... | collective-permute-start | bytes 589832 | tf_op jit(solution)/shard_map/ppermute | solution.py:370
  92.9 11.8 %collective-permute-start.19 = (bf16[2,96,512]{2,1,0:T(8,128)(2,1)S(1)}, bf16[2,96,512]{2,1,0:T(8,128)(2,1)S(1)}, u32[]{:S(2)}, u32[]{:S(2)}) collective-permute-start(bf16[2,96,512]{2,1,0:T(8,128)(2,1)S(1)} %pass_on.9.refs_3_.refs_2_), channel_id=1, source_target_pairs={{0,0},{1,2},{2,1},{3,3},{4,4},{5,6},{6,5},{7,7},{8,8},{9,10},{10,9... | collective-permute-start | bytes 589832 | tf_op jit(solution)/shard_map/ppermute | solution.py:370
  96.0 10.1 %collective-permute-start.24 = (bf16[2,96,512]{2,1,0:T(8,128)(2,1)S(1)}, bf16[2,96,512]{2,1,0:T(8,128)(2,1)S(1)}, u32[]{:S(2)}, u32[]{:S(2)}) collective-permute-start(bf16[2,96,512]{2,1,0:T(8,128)(2,1)S(1)} %pass_on.11.refs_1_.refs_2_), channel_id=1, source_target_pairs={{0,0},{1,2},{2,1},{3,3},{4,4},{5,6},{6,5},{7,7},{8,8},{9,10},{10,9... | collective-permute-start | bytes 589832 | tf_op jit(solution)/shard_map/ppermute | solution.py:370
  96.7 9.4 %collective-permute-start.18 = (bf16[2,96,256]{2,1,0:T(8,128)(2,1)S(1)}, bf16[2,96,256]{2,1,0:T(8,128)(2,1)S(1)}, u32[]{:S(2)}, u32[]{:S(2)}) collective-permute-start(bf16[2,96,256]{2,1,0:T(8,128)(2,1)S(1)} %hidden_values.7.refs_1_), channel_id=1, source_target_pairs={{0,1},{3,2},{4,5},{7,6},{8,9},{11,10},{12,13},{15,14},{16,17},{19,... | collective-permute-start | bytes 294920 | tf_op jit(solution)/shard_map/ppermute | solution.py:370
  103.4 15.2 %collective-permute-start.27 = (bf16[2,96,768]{2,1,0:T(8,128)(2,1)S(1)}, bf16[2,96,768]{2,1,0:T(8,128)(2,1)S(1)}, u32[]{:S(2)}, u32[]{:S(2)}) collective-permute-start(bf16[2,96,768]{2,1,0:T(8,128)(2,1)S(1)} %pass_on.10.refs_1_.refs_4_), channel_id=1, source_target_pairs={{1,0},{2,3},{5,4},{6,7},{9,8},{10,11},{13,12},{14,15},{17,16},{18,... | collective-permute-start | bytes 884744 | tf_op jit(solution)/shard_map/ppermute | solution.py:370
  104.7 10.8 %collective-permute-start.23 = (bf16[2,96,512]{2,1,0:T(8,128)(2,1)S(1)}, bf16[2,96,512]{2,1,0:T(8,128)(2,1)S(1)}, u32[]{:S(2)}, u32[]{:S(2)}) collective-permute-start(bf16[2,96,512]{2,1,0:T(8,128)(2,1)S(1)} %pass_on.12.refs_1_.refs_4_), channel_id=1, source_target_pairs={{1,0},{2,3},{5,4},{6,7},{9,8},{10,11},{13,12},{14,15},{17,16},{18,... | collective-permute-start | bytes 589832 | tf_op jit(solution)/shard_map/ppermute | solution.py:370
  106.2 14.6 %collective-permute-start.26 = (bf16[2,96,512]{2,1,0:T(8,128)(2,1)S(1)}, bf16[2,96,512]{2,1,0:T(8,128)(2,1)S(1)}, u32[]{:S(2)}, u32[]{:S(2)}) collective-permute-start(bf16[2,96,512]{2,1,0:T(8,128)(2,1)S(1)} %pass_on.14.refs_6_.refs_4_), channel_id=1, source_target_pairs={{1,0},{2,3},{5,4},{6,7},{9,8},{10,11},{13,12},{14,15},{17,16},{18,... | collective-permute-start | bytes 589832 | tf_op jit(solution)/shard_map/ppermute | solution.py:370
  107.5 9.8 %collective-permute-start.22 = (bf16[2,96,256]{2,1,0:T(8,128)(2,1)S(1)}, bf16[2,96,256]{2,1,0:T(8,128)(2,1)S(1)}, u32[]{:S(2)}, u32[]{:S(2)}) collective-permute-start(bf16[2,96,256]{2,1,0:T(8,128)(2,1)S(1)} %pass_on.13.refs_1_.refs_2_), channel_id=1, source_target_pairs={{0,0},{1,2},{2,1},{3,3},{4,4},{5,6},{6,5},{7,7},{8,8},{9,10},{10,9... | collective-permute-start | bytes 294920 | tf_op jit(solution)/shard_map/ppermute | solution.py:370
  117.3 6.5 %collective-permute-start.25 = (bf16[2,96,256]{2,1,0:T(8,128)(2,1)S(1)}, bf16[2,96,256]{2,1,0:T(8,128)(2,1)S(1)}, u32[]{:S(2)}, u32[]{:S(2)}) collective-permute-start(bf16[2,96,256]{2,1,0:T(8,128)(2,1)S(1)} %pass_on.15.refs_8_.refs_4_), channel_id=1, source_target_pairs={{1,0},{2,3},{5,4},{6,7},{9,8},{10,11},{13,12},{14,15},{17,16},{18,... | collective-permute-start | bytes 294920 | tf_op jit(solution)/shard_map/ppermute | solution.py:370
  120.8 6.2 %copy-start.2 = (s32[128,2]{0,1:T(2,128)S(1)}, s32[128,2]{0,1:T(2,128)}, u32[]{:S(2)}) copy-start(s32[128,2]{0,1:T(2,128)} %param.7) | copy-start | bytes 3076
  120.9 6.2 %copy-start.3 = (f32[128,2]{0,1:T(2,128)S(1)}, f32[128,2]{0,1:T(2,128)}, u32[]{:S(2)}) copy-start(f32[128,2]{0,1:T(2,128)} %param.8) | copy-start | bytes 3076
  125.0 2.1 %collective-permute-start.28 = (f32[2,48,1536]{2,1,0:T(8,128)S(1)}, f32[2,48,1536]{2,1,0:T(8,128)S(1)}, u32[]{:S(2)}, u32[]{:S(2)}) collective-permute-start(f32[2,48,1536]{2,1,0:T(8,128)S(1)} %get-tuple-element.54), channel_id=1, source_target_pairs={{0,16},{16,0},{1,17},{17,1},{2,18},{18,2},{3,19},{19,3},{4,20},{20... | collective-permute-start | bytes 1769480 | tf_op jit(solution)/shard_map/ppermute | solution.py:373
  127.8 5.9 %collective-permute-start.29 = (bf16[32,1536]{1,0:T(8,128)(2,1)S(1)}, bf16[32,1536]{1,0:T(8,128)(2,1)S(1)}, u32[]{:S(2)}, u32[]{:S(2)}) collective-permute-start(bf16[32,1536]{1,0:T(8,128)(2,1)S(1)} %get-tuple-element.56), channel_id=1, source_target_pairs={{0,12},{4,8},{8,4},{12,0},{1,13},{5,9},{9,5},{13,1},{2,14},{6,10},... | collective-permute-start | bytes 294920 | tf_op jit(solution)/shard_map/ppermute | solution.py:379
  130.3 5.4 %collective-permute-start.30 = (bf16[32,1536]{1,0:T(8,128)(2,1)S(1)}, bf16[32,1536]{1,0:T(8,128)(2,1)S(1)}, u32[]{:S(2)}, u32[]{:S(2)}) collective-permute-start(bf16[32,1536]{1,0:T(8,128)(2,1)S(1)} %get-tuple-element.57), channel_id=1, source_target_pairs={{0,8},{4,12},{8,0},{12,4},{1,9},{5,13},{9,1},{13,5},{2,10},{6,14},... | collective-permute-start | bytes 294920 | tf_op jit(solution)/shard_map/ppermute | solution.py:379
  130.9 4.9 %collective-permute-start.31 = (bf16[32,1536]{1,0:T(8,128)(2,1)S(1)}, bf16[32,1536]{1,0:T(8,128)(2,1)S(1)}, u32[]{:S(2)}, u32[]{:S(2)}) collective-permute-start(bf16[32,1536]{1,0:T(8,128)(2,1)S(1)} %get-tuple-element.58), channel_id=1, source_target_pairs={{0,4},{4,0},{8,12},{12,8},{1,5},{5,1},{9,13},{13,9},{2,6},{6,2},{1... | collective-permute-start | bytes 294920 | tf_op jit(solution)/shard_map/ppermute | solution.py:379
  135.8 4.7 %collective-permute-start.32 = (bf16[32,1536]{1,0:T(8,128)(2,1)S(1)}, bf16[32,1536]{1,0:T(8,128)(2,1)S(1)}, u32[]{:S(2)}, u32[]{:S(2)}) collective-permute-start(bf16[32,1536]{1,0:T(8,128)(2,1)S(1)} %add_convert_fusion.refs_1_), channel_id=1, source_target_pairs={{0,4},{4,0},{8,12},{12,8},{1,5},{5,1},{9,13},{13,9},{2,6},{6,2},{1... | collective-permute-start | bytes 294920 | tf_op jit(solution)/shard_map/ppermute | solution.py:383
  137.5 6.6 %collective-permute-start.33 = (bf16[32,1536]{1,0:T(8,128)(2,1)S(1)}, bf16[32,1536]{1,0:T(8,128)(2,1)S(1)}, u32[]{:S(2)}, u32[]{:S(2)}) collective-permute-start(bf16[32,1536]{1,0:T(8,128)(2,1)S(1)} %add_convert_fusion.refs_1_), channel_id=1, source_target_pairs={{0,8},{4,12},{8,0},{12,4},{1,9},{5,13},{9,1},{13,5},{2,10},{6,14},... | collective-permute-start | bytes 294920 | tf_op jit(solution)/shard_map/ppermute | solution.py:383
  138.2 5.9 %collective-permute-start.34 = (bf16[32,1536]{1,0:T(8,128)(2,1)S(1)}, bf16[32,1536]{1,0:T(8,128)(2,1)S(1)}, u32[]{:S(2)}, u32[]{:S(2)}) collective-permute-start(bf16[32,1536]{1,0:T(8,128)(2,1)S(1)} %add_convert_fusion.refs_1_), channel_id=1, source_target_pairs={{0,12},{4,8},{8,4},{12,0},{1,13},{5,9},{9,5},{13,1},{2,14},{6,10},... | collective-permute-start | bytes 294920 | tf_op jit(solution)/shard_map/ppermute | solution.py:383

commit v5 on v2

--- a/solution.py
+++ b/solution.py
@@ -11,7 +11,7 @@
 F32, BF16 = jnp.float32, jnp.bfloat16
 MIB = 1024 * 1024
 
-CHUNKS = ((3, "end"), (4, "end"), (4, "end"), (3, "end"), (2, "inner"))
+CHUNKS = ((2, "end"), (4, "end"), (4, "end"), (4, "inner"), (2, "direct"))
 
 ROUTES = {
     "end": {
@@ -22,17 +22,25 @@
         "m0": (0, 1, None), "mb": (3, 2, None), "m1": (1, 2, "m0"),
         "a0": (2, 1, None), "a1": (2, 3, None), "a2": (1, 0, "a0"),
     },
+    "direct": {
+        "m0": (0, 1, None), "mb": (3, 2, None), "m1": (1, 2, "m0"),
+        "a0": (2, 1, None), "a1": (2, 3, None), "a2": (2, 0, None),
+    },
 }
-OWNER = {"end": (3, ("m2",)), "inner": (2, ("m1", "mb"))}
-HELD = {"end": ("a2", "a1", "a0", None), "inner": ("a2", "a0", None, "a1")}
+OWNER = {"end": (3, ("m2",)), "inner": (2, ("m1", "mb")), "direct": (2, ("m1", "mb"))}
+HELD = {
+    "end": ("a2", "a1", "a0", None),
+    "inner": ("a2", "a0", None, "a1"),
+    "direct": ("a2", "a0", None, "a1"),
+}
 
 ORDER = (
-    ("g", 0), ("m0", 0), ("g", 1), ("m0", 1), ("m1", 0), ("g", 2), ("m0", 2), ("m1", 1),
-    ("m2", 0), ("g", 3), ("m0", 3), ("m1", 2), ("m2", 1), ("g", 4), ("m0", 4), ("m1", 3),
-    ("h", 0), ("a0", 0), ("m2", 2), ("h", 1), ("a0", 1), ("m1", 4), ("mb", 4), ("m2", 3),
-    ("a1", 0), ("a1", 1), ("h", 2), ("a0", 2), ("h", 4), ("a0", 4), ("a2", 0), ("a1", 4),
-    ("h", 3), ("a0", 3), ("a2", 1), ("a1", 2), ("a2", 4), ("d", 0), ("a1", 3), ("a2", 2),
-    ("d", 1), ("a2", 3), ("d", 4), ("d", 2), ("d", 3),
+    ("g", 0), ("m0", 0), ("g", 2), ("m0", 2), ("m1", 0), ("g", 1), ("m2", 0), ("h", 0),
+    ("m0", 1), ("m1", 2), ("a0", 0), ("g", 3), ("m0", 3), ("m1", 1), ("m2", 2), ("mb", 3),
+    ("a1", 0), ("g", 4), ("m1", 3), ("a2", 0), ("h", 2), ("m0", 4), ("m2", 1), ("d", 0),
+    ("m1", 4), ("a0", 2), ("h", 3), ("a0", 3), ("a1", 3), ("h", 1), ("a0", 1), ("a1", 2),
+    ("a2", 3), ("a1", 1), ("a2", 2), ("d", 3), ("mb", 4), ("a2", 1), ("h", 4), ("a0", 4),
+    ("a2", 4), ("a1", 4), ("d", 2), ("d", 1), ("d", 4),
 )
 
 SMEM = pl.BlockSpec(memory_space=pltpu.SMEM)
@@ -41,7 +49,7 @@
 HBM = pl.BlockSpec(memory_space=pltpu.HBM)
 
 
-def call(kernel, name, outs, operands, specs, after, scratch=(), aliases=None, limit=42, cost=(0, 0)):
+def call(kernel, name, outs, operands, specs, after, scratch=(), aliases=None, limit=6):
     count = len(operands)
 
     def body(*refs):
@@ -54,7 +62,6 @@
         out_specs=jax.tree.map(lambda _: VMEM, outs) if aliases is None else ANY,
         scratch_shapes=list(scratch),
         input_output_aliases=aliases or {},
-        cost_estimate=pl.CostEstimate(flops=cost[0], bytes_accessed=cost[1], transcendentals=0),
         compiler_params=pltpu.CompilerParams(vmem_limit_bytes=limit * MIB),
         name=name,
     )(*operands, *after)
@@ -117,41 +124,31 @@
     block = depth // pieces
 
     def kernel(place_ref, *refs):
-        row_refs = refs[: len(rows)]
-        weight_refs, full_ref, short_ref, held, sems = refs[len(rows) : len(rows) + 2], *refs[len(rows) + 2 :]
-        copies = []
-        for e in range(local_count):
-            for i in range(2):
-                for k in range(pieces):
-                    at = (e * 2 + i) * pieces + k
-                    copies.append(
-                        pltpu.make_async_copy(
-                            weight_refs[i].at[e, pl.ds(k * block, block), pl.ds(start, width)],
-                            held.at[at],
-                            sems.at[at],
-                        )
-                    )
-        for copy in copies:
-            copy.start()
+        row_refs, weight_refs = refs[: len(rows)], refs[len(rows) : len(rows) + 2]
+        full_ref, short_ref, held, sems = refs[len(rows) + 2 :]
+        copies = {}
+        for at in range(2 * local_count):
+            for k in range(pieces):
+                copies[at, k] = pltpu.make_async_copy(
+                    weight_refs[at % 2].at[at // 2, pl.ds(k * block, block), pl.ds(start, width)],
+                    held.at[at, pl.ds(k * block, block), :],
+                    sems.at[at * pieces + k],
+                )
+                copies[at, k].start()
         for e in range(local_count):
             x = jnp.concatenate([ref[e] for ref in row_refs], axis=0)
             for i in range(2):
-                total = None
+                at = e * 2 + i
                 for k in range(pieces):
-                    at = (e * 2 + i) * pieces + k
-                    copies[at].wait()
-                    part = jnp.dot(
-                        x[:, k * block : (k + 1) * block], held[at], preferred_element_type=F32
-                    )
-                    total = part if total is None else total + part
-                full_ref[i, e] = total
+                    copies[at, k].wait()
+                full_ref[i, e] = jnp.dot(x, held[at], preferred_element_type=F32)
 
                 @pl.when(place_ref[0] == 0)
                 def _():
-                    short_ref[i, e] = total.astype(BF16)
+                    short_ref[i, e] = full_ref[i, e].astype(BF16)
 
     shape = (2, local_count, count, width)
-    slots = 2 * local_count * pieces
+    slots = 2 * local_count
     return call(
         kernel,
         "gate_up",
@@ -159,9 +156,8 @@
         [place, *rows, *weights],
         [SMEM] + [VMEM] * len(rows) + [HBM, HBM],
         after,
-        [pltpu.VMEM((slots, block, width), BF16), pltpu.SemaphoreType.DMA((slots,))],
-        limit=42,
-        cost=(4 * local_count * count * depth * width, 4 * local_count * depth * width),
+        [pltpu.VMEM((slots, depth, width), BF16), pltpu.SemaphoreType.DMA((slots * pieces,))],
+        limit=30,
     )
 
 
@@ -224,20 +220,7 @@
         held_refs, weight_ref = refs[:places], refs[places]
         total_refs = refs[places + 1 : places + 1 + len(totals)]
         out_refs = refs[places + 1 + len(totals) :][: len(row_counts)]
-        hidden, weights, sems = refs[-3:]
-        copies = []
-        for e in range(local_count):
-            for k in range(pieces):
-                at = e * pieces + k
-                copies.append(
-                    pltpu.make_async_copy(
-                        weight_ref.at[e, pl.ds(start + k * block, block), :],
-                        weights.at[at],
-                        sems.at[at],
-                    )
-                )
-        for copy in copies:
-            copy.start()
+        hidden = refs[-1]
         for i in range(places):
 
             @pl.when(place_ref[0] == i)
@@ -247,10 +230,9 @@
         for e in range(local_count):
             product = None
             for k in range(pieces):
-                copies[e * pieces + k].wait()
                 part = jnp.dot(
                     hidden[e, :, k * block : (k + 1) * block],
-                    weights[e * pieces + k],
+                    weight_ref[e, start + k * block : start + (k + 1) * block, :],
                     preferred_element_type=F32,
                 )
                 product = part if product is None else product + part
@@ -267,15 +249,12 @@
         "down",
         shapes,
         operands,
-        [SMEM] + [VMEM] * places + [HBM] + [VMEM] * len(totals),
+        [SMEM] + [VMEM] * (places + 1 + len(totals)),
         after,
         [
             pltpu.VMEM(held[0].shape, BF16),
-            pltpu.VMEM((local_count * pieces, block, features), BF16),
-            pltpu.SemaphoreType.DMA((local_count * pieces,)),
         ],
-        limit=42,
-        cost=(2 * local_count * count * features * width, 2 * local_count * features * width),
+        limit=6 + 2 * local_count * count * features * 4 // MIB,
     )
 
 

time: 156 us -> 145 us (0.929)
  waiting for transfers between devices: 60.8 us -> 44.6 us
  starting transfers between devices: 53 us -> 59.9 us
  Pallas kernels: 39 us -> 34.8 us
  local copies, waits for them, and re-layouts: 1.69 us -> 4.55 us
    ppermute x30, waiting for transfers between devices: 49 us -> 32.8 us  [hop(): return lax.ppermute(value, ('dp', 'blk'), pairs)]
    ppermute x30, starting transfers between devices: 45.3 us -> 52.2 us  [hop(): return lax.ppermute(value, ('dp', 'blk'), pairs)]
    pallas_call x37 -> x35, Pallas kernels: 39 us -> 34.8 us  [call(): pl.pallas_call(body, out_shape=outs, in_specs=list(specs) + [ANY] * len(a...]
    unnamed x8 -> x24, local copies, waits for them, and re-layouts: 1.69 us -> 4.55 us
  transfers between devices with their start and end apart: 38 -> 38, of which waited for: 15 -> 15; matrix products, arithmetic and copies ran while one was open for 0% -> 0% of each run, Pallas kernels for 19% -> 20%
where the time goes in v5:
time: 145 us
  starting transfers between devices  59.9 us (41%)
  waiting for transfers between devices  44.6 us (31%)
  Pallas kernels  34.8 us (24%)
  local copies, waits for them, and re-layouts  4.55 us (3%)
    ppermute x30, starting transfers between devices, hop(): return lax.ppermute(value, ('dp', 'blk'), pairs)  52.2 us
    pallas_call x35, Pallas kernels, call(): pl.pallas_call(body, out_shape=outs, in_specs=list(specs) + [ANY] * len(a...  34.8 us
    ppermute x30, waiting for transfers between devices, hop(): return lax.ppermute(value, ('dp', 'blk'), pairs)  32.8 us
    unnamed x24, local copies, waits for them, and re-layouts  4.55 us
    ppermute x3, waiting for transfers between devices, local(): own = own + lax.ppermute(sent[step - 1], 'expert', exchange).astype(F32)  4.43 us
    ppermute x3, waiting for transfers between devices, local(): lax.ppermute(block, 'expert', [(i, i ^ step) for i in range(groups)])  4.24 us
    ppermute x3, starting transfers between devices, local(): lax.ppermute(block, 'expert', [(i, i ^ step) for i in range(groups)])  3.55 us
    ppermute x3, starting transfers between devices, local(): own = own + lax.ppermute(sent[step - 1], 'expert', exchange).astype(F32)  3.55 us
  transfers between devices with their start and end apart: 38, of which 15 were waited for; matrix products, arithmetic and copies ran while one was open for 0% of the time, Pallas kernels for 20%

profile of v5, /device:TPU:0, one launch (start us, length us, event | category | flops | bytes accessed | tf_op | source)
XLA Modules:
  0.0 144.6 jit_solution(8630591604572256230)
XLA Ops:
  0.0 1.0 copy-done.2
  2.6 1.2 collective-permute-done.refs_2_
  3.8 3.3 %gate_up.5 = (f32[2,2,96,512]{3,2,1,0:T(8,128)S(1)}, bf16[2,2,96,512]{3,2,1,0:T(8,128)(2,1)S(1)}) custom-call(s32[1]{0:T(128)} %bitcast.3.refs_0_, bf16[2,48,1536]{2,1,0:T(8,128)(2,1)S(1)} %pick.1.refs_1_, bf16[2,48,1536]{2,1,0:T(8,128)(2,1)S(1)} %collective-permute-done.refs_2_, bf16[2,1536,4096]{2,1,0:T(8,128)(2,1)} %refs_3_.9, bf16[2,1536,4096]{2,1,0:T(8,128)(2,1)} %refs_4_.9), custom_call_target="tpu_custom_call" | custom-call | tf_op jit(solution)/shard_map/gate_up/pallas_call | solution.py:58
  7.1 4.9 %collective-permute-start.1 = (bf16[2,2,96,512]{3,2,1,0:T(8,128)(2,1)S(1)}, bf16[2,2,96,512]{3,2,1,0:T(8,128)(2,1)S(1)}, u32[]{:S(2)}, u32[]{:S(2)}) collective-permute-start(bf16[2,2,96,512]{3,2,1,0:T(8,128)(2,1)S(1)} %get-tuple-element.30), channel_id=1, source_target_pairs={{0,1},{19,18},{4,5},{23,22},{8,9},{27,26},{12,13},{31,30}} | collective-permute-start | bytes 1179656 | tf_op jit(solution)/shard_map/ppermute | solution.py:347
  12.0 5.4 %gate_up.6 = (f32[2,2,96,1024]{3,2,1,0:T(8,128)S(1)}, bf16[2,2,96,1024]{3,2,1,0:T(8,128)(2,1)S(1)}) custom-call(s32[1]{0:T(128)} %bitcast.3.refs_0_, bf16[2,48,1536]{2,1,0:T(8,128)(2,1)S(1)} %pick.1.refs_1_, bf16[2,48,1536]{2,1,0:T(8,128)(2,1)S(1)} %collective-permute-done.refs_2_, bf16[2,1536,4096]{2,1,0:T(8,128)(2,1)} %refs_3_.9, ...), custom_call_target="tpu_custom_call" | custom-call | tf_op jit(solution)/shard_map/gate_up/pallas_call | solution.py:58
  18.1 5.0 %collective-permute-start.5 = (bf16[2,2,96,1024]{3,2,1,0:T(8,128)(2,1)S(1)}, bf16[2,2,96,1024]{3,2,1,0:T(8,128)(2,1)S(1)}, u32[]{:S(2)}, u32[]{:S(2)}) collective-permute-start(bf16[2,2,96,1024]{3,2,1,0:T(8,128)(2,1)S(1)} %get-tuple-element.33), channel_id=1, source_target_pairs={{0,1},{19,18},{4,5},{23,22},{8,9},{27,26},{12,13},{31,30}} | collective-permute-start | bytes 2359304 | tf_op jit(solution)/shard_map/ppermute | solution.py:347
  23.1 5.4 %gate_up.7 = (f32[2,2,96,1024]{3,2,1,0:T(8,128)S(1)}, bf16[2,2,96,1024]{3,2,1,0:T(8,128)(2,1)S(1)}) custom-call(s32[1]{0:T(128)} %bitcast.3.refs_0_, bf16[2,48,1536]{2,1,0:T(8,128)(2,1)S(1)} %pick.1.refs_1_, bf16[2,48,1536]{2,1,0:T(8,128)(2,1)S(1)} %collective-permute-done.refs_2_, bf16[2,1536,4096]{2,1,0:T(8,128)(2,1)} %refs_3_.9, ...), custom_call_target="tpu_custom_call" | custom-call | tf_op jit(solution)/shard_map/gate_up/pallas_call | solution.py:58
  29.2 1.3 collective-permute-start.7
  30.6 1.9 %collective-permute-done.5.refs_2_ = bf16[2,2,96,1024]{3,2,1,0:T(8,128)(2,1)S(1)} collective-permute-done((bf16[2,2,96,1024]{3,2,1,0:T(8,128)(2,1)S(1)}, bf16[2,2,96,1024]{3,2,1,0:T(8,128)(2,1)S(1)}, u32[]{:S(2)}, u32[]{:S(2)}) %collective-permute-start.5) | collective-permute-done | bytes 786464 | tf_op jit(solution)/shard_map/ppermute | solution.py:347
  33.2 5.4 %gate_up.8 = (f32[2,2,96,1024]{3,2,1,0:T(8,128)S(1)}, bf16[2,2,96,1024]{3,2,1,0:T(8,128)(2,1)S(1)}) custom-call(s32[1]{0:T(128)} %bitcast.3.refs_0_, bf16[2,48,1536]{2,1,0:T(8,128)(2,1)S(1)} %pick.1.refs_1_, bf16[2,48,1536]{2,1,0:T(8,128)(2,1)S(1)} %collective-permute-done.refs_2_, bf16[2,1536,4096]{2,1,0:T(8,128)(2,1)} %refs_3_.9, ...), custom_call_target="tpu_custom_call" | custom-call | tf_op jit(solution)/shard_map/gate_up/pallas_call | solution.py:58
  38.6 6.2 %collective-permute-start.10 = (bf16[2,2,96,1024]{3,2,1,0:T(8,128)(2,1)S(1)}, bf16[2,2,96,1024]{3,2,1,0:T(8,128)(2,1)S(1)}, u32[]{:S(2)}, u32[]{:S(2)}) collective-permute-start(bf16[2,2,96,1024]{3,2,1,0:T(8,128)(2,1)S(1)} %get-tuple-element.38), channel_id=1, source_target_pairs={{0,1},{19,18},{4,5},{23,22},{8,9},{27,26},{12,13},{31,30}} | collective-permute-start | bytes 2359304 | tf_op jit(solution)/shard_map/ppermute | solution.py:347
  44.8 1.5 %collective-permute-start.13 = (bf16[2,2,96,1024]{3,2,1,0:T(8,128)(2,1)S(1)}, bf16[2,2,96,1024]{3,2,1,0:T(8,128)(2,1)}, u32[]{:S(2)}, u32[]{:S(2)}) collective-permute-start(bf16[2,2,96,1024]{3,2,1,0:T(8,128)(2,1)S(1)} %add_to_send.12.refs_2_), channel_id=1, source_target_pairs={{2,3},{17,16},{6,7},{21,20},{10,11},{25,24},{14,15},{29,28}} | collective-permute-start | bytes 2359304 | tf_op jit(solution)/shard_map/ppermute | solution.py:347
  46.4 1.5 %collective-permute-start.12 = (bf16[2,2,96,1024]{3,2,1,0:T(8,128)(2,1)S(1)}, bf16[2,2,96,1024]{3,2,1,0:T(8,128)(2,1)}, u32[]{:S(2)}, u32[]{:S(2)}) collective-permute-start(bf16[2,2,96,1024]{3,2,1,0:T(8,128)(2,1)S(1)} %add_to_send.11.refs_3_), channel_id=1, source_target_pairs={{1,2},{18,17},{5,6},{22,21},{9,10},{26,25},{13,14},{30,29}} | collective-permute-start | bytes 2359304 | tf_op jit(solution)/shard_map/ppermute | solution.py:347
  48.6 0.9 round_to_send.2.refs_1_
  49.5 1.5 %collective-permute-start.16 = (bf16[2,2,96,1024]{3,2,1,0:T(8,128)(2,1)}, bf16[2,2,96,1024]{3,2,1,0:T(8,128)(2,1)}, u32[]{:S(2)}, u32[]{:S(2)}) collective-permute-start(bf16[2,2,96,1024]{3,2,1,0:T(8,128)(2,1)} %round_to_send.2.refs_1_), channel_id=1, source_target_pairs={{3,2},{16,17},{7,6},{20,21},{11,10},{24,25},{15,14},{28,29}} | collective-permute-start | bytes 2359304 | tf_op jit(solution)/shard_map/ppermute | solution.py:347
  51.1 0.8 collective-permute-start.9
  51.9 3.7 %gate_up.9 = (f32[2,2,96,512]{3,2,1,0:T(8,128)S(1)}, bf16[2,2,96,512]{3,2,1,0:T(8,128)(2,1)S(1)}) custom-call(s32[1]{0:T(128)} %bitcast.3.refs_0_, bf16[2,48,1536]{2,1,0:T(8,128)(2,1)S(1)} %pick.1.refs_1_, bf16[2,48,1536]{2,1,0:T(8,128)(2,1)S(1)} %collective-permute-done.refs_2_, bf16[2,1536,4096]{2,1,0:T(8,128)(2,1)} %refs_3_.9, ...), custom_call_target="tpu_custom_call" | custom-call | tf_op jit(solution)/shard_map/gate_up/pallas_call | solution.py:58
  55.7 1.5 %collective-permute-done.10.refs_2_ = bf16[2,2,96,1024]{3,2,1,0:T(8,128)(2,1)S(1)} collective-permute-done((bf16[2,2,96,1024]{3,2,1,0:T(8,128)(2,1)S(1)}, bf16[2,2,96,1024]{3,2,1,0:T(8,128)(2,1)S(1)}, u32[]{:S(2)}, u32[]{:S(2)}) %collective-permute-start.10) | collective-permute-done | bytes 786464 | tf_op jit(solution)/shard_map/ppermute | solution.py:347
  57.2 0.9 copy-done
  58.1 2.0 %copy-done.1 = bf16[2,2,96,1024]{3,2,1,0:T(8,128)(2,1)S(1)} copy-done((bf16[2,2,96,1024]{3,2,1,0:T(8,128)(2,1)S(1)}, bf16[2,2,96,1024]{3,2,1,0:T(8,128)(2,1)}, u32[]{:S(2)}) %copy-start.1) | copy-done | bytes 786456
  60.0 0.8 collective-permute-start.15
  60.9 1.5 %hidden_values.6.refs_3_.refs_4_ = bf16[2,96,1024]{2,1,0:T(8,128)(2,1)S(1)} custom-call(s32[1]{0:T(128)} %bitcast.3.refs_0_, f32[2,2,96,1024]{3,2,1,0:T(8,128)S(1)} %get-tuple-element.31.refs_3_.refs_1_, bf16[2,2,96,1024]{3,2,1,0:T(8,128)(2,1)} %collective-permute-done.13.refs_2_, bf16[2,96,512]{2,1,0:T(8,128)(2,1)S(1)} %pass_on.8.refs_3_.refs_2_), custom_call_target="tpu_custom_call" | custom-call | tf_op jit(solution)/shard_map/hidden_values/pallas_call | solution.py:58
  62.4 1.1 add_to_send.14.refs_6_
  64.2 12.0 %collective-permute-start.8 = (bf16[2,2,96,512]{3,2,1,0:T(8,128)(2,1)S(1)}, bf16[2,2,96,512]{3,2,1,0:T(8,128)(2,1)S(1)}, u32[]{:S(2)}, u32[]{:S(2)}) collective-permute-start(bf16[2,2,96,512]{3,2,1,0:T(8,128)(2,1)S(1)} %get-tuple-element.37), channel_id=1, source_target_pairs={{0,1},{19,18},{4,5},{23,22},{8,9},{27,26},{12,13},{31,30}} | collective-permute-start | bytes 1179656 | tf_op jit(solution)/shard_map/ppermute | solution.py:347
  76.2 1.3 collective-permute-start.11
  77.5 6.3 %collective-permute-done.11.refs_1_ = bf16[2,96,512]{2,1,0:T(8,128)(2,1)S(1)} collective-permute-done((bf16[2,96,512]{2,1,0:T(8,128)(2,1)S(1)}, bf16[2,96,512]{2,1,0:T(8,128)(2,1)S(1)}, u32[]{:S(2)}, u32[]{:S(2)}) %collective-permute-start.11) | collective-permute-done | bytes 196640 | tf_op jit(solution)/shard_map/ppermute | solution.py:347
  85.2 1.1 hidden_values.7.refs_3_
  89.2 1.3 collective-permute-start.20
  91.9 12.2 %collective-permute-done.20.refs_1_ = bf16[2,96,1024]{2,1,0:T(8,128)(2,1)S(1)} collective-permute-done((bf16[2,96,1024]{2,1,0:T(8,128)(2,1)S(1)}, bf16[2,96,1024]{2,1,0:T(8,128)(2,1)S(1)}, u32[]{:S(2)}, u32[]{:S(2)}) %collective-permute-start.20) | collective-permute-done | bytes 393248 | tf_op jit(solution)/shard_map/ppermute | solution.py:347
  104.1 1.2 down.6
  106.0 1.3 collective-permute-start.30
  107.4 1.3 collective-permute-start.29
  110.1 1.3 collective-permute-start.26
  111.4 6.4 %collective-permute-done.30.refs_1_ = bf16[2,96,1024]{2,1,0:T(8,128)(2,1)S(1)} collective-permute-done((bf16[2,96,1024]{2,1,0:T(8,128)(2,1)S(1)}, bf16[2,96,1024]{2,1,0:T(8,128)(2,1)S(1)}, u32[]{:S(2)}, u32[]{:S(2)}) %collective-permute-start.30) | collective-permute-done | bytes 393248 | tf_op jit(solution)/shard_map/ppermute | solution.py:347
  117.8 1.2 down.7
  119.0 3.0 %collective-permute-done.29.refs_1_ = bf16[2,96,1024]{2,1,0:T(8,128)(2,1)S(1)} collective-permute-done((bf16[2,96,1024]{2,1,0:T(8,128)(2,1)S(1)}, bf16[2,96,1024]{2,1,0:T(8,128)(2,1)S(1)}, u32[]{:S(2)}, u32[]{:S(2)}) %collective-permute-start.29) | collective-permute-done | bytes 393248 | tf_op jit(solution)/shard_map/ppermute | solution.py:347
  122.0 1.2 down.8
  123.2 1.3 collective-permute-done.26.refs_1_
  125.3 2.0 %collective-permute-done.31.refs_4_ = f32[2,48,1536]{2,1,0:T(8,128)S(1)} collective-permute-done((f32[2,48,1536]{2,1,0:T(8,128)S(1)}, f32[2,48,1536]{2,1,0:T(8,128)S(1)}, u32[]{:S(2)}, u32[]{:S(2)}) %collective-permute-start.31) | collective-permute-done | bytes 589856 | tf_op jit(solution)/shard_map/ppermute | solution.py:395
  127.3 0.7 combine.1
  128.0 2.5 %collective-permute-start.32 = (bf16[32,1536]{1,0:T(8,128)(2,1)S(1)}, bf16[32,1536]{1,0:T(8,128)(2,1)S(1)}, u32[]{:S(2)}, u32[]{:S(2)}) collective-permute-start(bf16[32,1536]{1,0:T(8,128)(2,1)S(1)} %get-tuple-element.50), channel_id=1, source_target_pairs={{0,12},{4,8},{8,4},{12,0},{1,13},{5,9},{9,5},{13,1},{2,14},{6,10},... | collective-permute-start | bytes 294920 | tf_op jit(solution)/shard_map/ppermute | solution.py:401
  131.6 2.3 %collective-permute-done.32 = bf16[32,1536]{1,0:T(8,128)(2,1)S(1)} collective-permute-done((bf16[32,1536]{1,0:T(8,128)(2,1)S(1)}, bf16[32,1536]{1,0:T(8,128)(2,1)S(1)}, u32[]{:S(2)}, u32[]{:S(2)}) %collective-permute-start.32) | collective-permute-done | bytes 98336 | tf_op jit(solution)/shard_map/ppermute | solution.py:401
  133.9 2.0 %collective-permute-done.33 = bf16[32,1536]{1,0:T(8,128)(2,1)S(1)} collective-permute-done((bf16[32,1536]{1,0:T(8,128)(2,1)S(1)}, bf16[32,1536]{1,0:T(8,128)(2,1)S(1)}, u32[]{:S(2)}, u32[]{:S(2)}) %collective-permute-start.33) | collective-permute-done | bytes 98336 | tf_op jit(solution)/shard_map/ppermute | solution.py:401
  136.1 1.7 %collective-permute-start.37 = (bf16[32,1536]{1,0:T(8,128)(2,1)S(1)}, bf16[32,1536]{1,0:T(8,128)(2,1)S(1)}, u32[]{:S(2)}, u32[]{:S(2)}) collective-permute-start(bf16[32,1536]{1,0:T(8,128)(2,1)S(1)} %add_convert_fusion.refs_1_), channel_id=1, source_target_pairs={{0,12},{4,8},{8,4},{12,0},{1,13},{5,9},{9,5},{13,1},{2,14},{6,10},... | collective-permute-start | bytes 294920 | tf_op jit(solution)/shard_map/ppermute | solution.py:405
  137.8 1.3 collective-permute-start.36
  139.6 2.8 %collective-permute-done.37.refs_4_ = bf16[32,1536]{1,0:T(8,128)(2,1)S(1)} collective-permute-done((bf16[32,1536]{1,0:T(8,128)(2,1)S(1)}, bf16[32,1536]{1,0:T(8,128)(2,1)S(1)}, u32[]{:S(2)}, u32[]{:S(2)}) %collective-permute-start.37) | collective-permute-done | bytes 98336 | tf_op jit(solution)/shard_map/ppermute | solution.py:405
  142.5 1.1 collective-permute-done.36.refs_3_
  143.9 0.8 place_blocks.1
  (89 shorter events, 15.3 us)
Async XLA Ops:
  0.0 1.0 copy-start.2
  2.0 1.7 %collective-permute-start = (bf16[2,48,1536]{2,1,0:T(8,128)(2,1)S(1)}, bf16[2,48,1536]{2,1,0:T(8,128)(2,1)S(1)}, u32[]{:S(2)}, u32[]{:S(2)}) collective-permute-start(bf16[2,48,1536]{2,1,0:T(8,128)(2,1)S(1)} %pick.1.refs_1_), channel_id=1, source_target_pairs={{0,16},{16,0},{1,17},{17,1},{2,18},{18,2},{3,19},{19,3},{4,20},{20... | collective-permute-start | bytes 884744 | tf_op jit(solution)/shard_map/ppermute | solution.py:351
  7.1 10.3 %collective-permute-start.1 = (bf16[2,2,96,512]{3,2,1,0:T(8,128)(2,1)S(1)}, bf16[2,2,96,512]{3,2,1,0:T(8,128)(2,1)S(1)}, u32[]{:S(2)}, u32[]{:S(2)}) collective-permute-start(bf16[2,2,96,512]{3,2,1,0:T(8,128)(2,1)S(1)} %get-tuple-element.30), channel_id=1, source_target_pairs={{0,1},{19,18},{4,5},{23,22},{8,9},{27,26},{12,13},{31,30}} | collective-permute-start | bytes 1179656 | tf_op jit(solution)/shard_map/ppermute | solution.py:347
  17.4 11.1 %collective-permute-start.2 = (bf16[2,2,96,512]{3,2,1,0:T(8,128)(2,1)S(1)}, bf16[2,2,96,512]{3,2,1,0:T(8,128)(2,1)S(1)}, u32[]{:S(2)}, u32[]{:S(2)}) collective-permute-start(bf16[2,2,96,512]{3,2,1,0:T(8,128)(2,1)S(1)} %add_to_send.8.refs_5_), channel_id=1, source_target_pairs={{1,2},{18,17},{5,6},{22,21},{9,10},{26,25},{13,14},{30,29}} | collective-permute-start | bytes 1179656 | tf_op jit(solution)/shard_map/ppermute | solution.py:347
  18.1 14.4 %collective-permute-start.5 = (bf16[2,2,96,1024]{3,2,1,0:T(8,128)(2,1)S(1)}, bf16[2,2,96,1024]{3,2,1,0:T(8,128)(2,1)S(1)}, u32[]{:S(2)}, u32[]{:S(2)}) collective-permute-start(bf16[2,2,96,1024]{3,2,1,0:T(8,128)(2,1)S(1)} %get-tuple-element.33), channel_id=1, source_target_pairs={{0,1},{19,18},{4,5},{23,22},{8,9},{27,26},{12,13},{31,30}} | collective-permute-start | bytes 2359304 | tf_op jit(solution)/shard_map/ppermute | solution.py:347
  28.5 2.0 %collective-permute-start.3 = (bf16[2,2,96,512]{3,2,1,0:T(8,128)(2,1)S(1)}, bf16[2,2,96,512]{3,2,1,0:T(8,128)(2,1)S(1)}, u32[]{:S(2)}, u32[]{:S(2)}) collective-permute-start(bf16[2,2,96,512]{3,2,1,0:T(8,128)(2,1)S(1)} %add_to_send.9.refs_3_), channel_id=1, source_target_pairs={{2,3},{17,16},{6,7},{21,20},{10,11},{25,24},{14,15},{29,28}} | collective-permute-start | bytes 1179656 | tf_op jit(solution)/shard_map/ppermute | solution.py:347
  29.2 15.6 %collective-permute-start.7 = (bf16[2,2,96,1024]{3,2,1,0:T(8,128)(2,1)S(1)}, bf16[2,2,96,1024]{3,2,1,0:T(8,128)(2,1)S(1)}, u32[]{:S(2)}, u32[]{:S(2)}) collective-permute-start(bf16[2,2,96,1024]{3,2,1,0:T(8,128)(2,1)S(1)} %get-tuple-element.35), channel_id=1, source_target_pairs={{0,1},{19,18},{4,5},{23,22},{8,9},{27,26},{12,13},{31,30}} | collective-permute-start | bytes 2359304 | tf_op jit(solution)/shard_map/ppermute | solution.py:347
  32.5 12.3 %collective-permute-start.6 = (bf16[2,2,96,1024]{3,2,1,0:T(8,128)(2,1)S(1)}, bf16[2,2,96,1024]{3,2,1,0:T(8,128)(2,1)S(1)}, u32[]{:S(2)}, u32[]{:S(2)}) collective-permute-start(bf16[2,2,96,1024]{3,2,1,0:T(8,128)(2,1)S(1)} %add_to_send.10.refs_5_), channel_id=1, source_target_pairs={{1,2},{18,17},{5,6},{22,21},{9,10},{26,25},{13,14},{30,29}} | collective-permute-start | bytes 2359304 | tf_op jit(solution)/shard_map/ppermute | solution.py:347
  38.6 18.6 %collective-permute-start.10 = (bf16[2,2,96,1024]{3,2,1,0:T(8,128)(2,1)S(1)}, bf16[2,2,96,1024]{3,2,1,0:T(8,128)(2,1)S(1)}, u32[]{:S(2)}, u32[]{:S(2)}) collective-permute-start(bf16[2,2,96,1024]{3,2,1,0:T(8,128)(2,1)S(1)} %get-tuple-element.38), channel_id=1, source_target_pairs={{0,1},{19,18},{4,5},{23,22},{8,9},{27,26},{12,13},{31,30}} | collective-permute-start | bytes 2359304 | tf_op jit(solution)/shard_map/ppermute | solution.py:347
  44.8 16.1 %collective-permute-start.13 = (bf16[2,2,96,1024]{3,2,1,0:T(8,128)(2,1)S(1)}, bf16[2,2,96,1024]{3,2,1,0:T(8,128)(2,1)}, u32[]{:S(2)}, u32[]{:S(2)}) collective-permute-start(bf16[2,2,96,1024]{3,2,1,0:T(8,128)(2,1)S(1)} %add_to_send.12.refs_2_), channel_id=1, source_target_pairs={{2,3},{17,16},{6,7},{21,20},{10,11},{25,24},{14,15},{29,28}} | collective-permute-start | bytes 2359304 | tf_op jit(solution)/shard_map/ppermute | solution.py:347
  46.4 16.0 %collective-permute-start.12 = (bf16[2,2,96,1024]{3,2,1,0:T(8,128)(2,1)S(1)}, bf16[2,2,96,1024]{3,2,1,0:T(8,128)(2,1)}, u32[]{:S(2)}, u32[]{:S(2)}) collective-permute-start(bf16[2,2,96,1024]{3,2,1,0:T(8,128)(2,1)S(1)} %add_to_send.11.refs_3_), channel_id=1, source_target_pairs={{1,2},{18,17},{5,6},{22,21},{9,10},{26,25},{13,14},{30,29}} | collective-permute-start | bytes 2359304 | tf_op jit(solution)/shard_map/ppermute | solution.py:347
  47.9 3.1 %collective-permute-start.4 = (bf16[2,96,512]{2,1,0:T(8,128)(2,1)S(1)}, bf16[2,96,512]{2,1,0:T(8,128)(2,1)S(1)}, u32[]{:S(2)}, u32[]{:S(2)}) collective-permute-start(bf16[2,96,512]{2,1,0:T(8,128)(2,1)S(1)} %hidden_values.5.refs_3_.refs_4_), channel_id=1, source_target_pairs={{3,2},{16,17},{7,6},{20,21},{11,10},{24,25},{15,14},{28,29}} | collective-permute-start | bytes 589832 | tf_op jit(solution)/shard_map/ppermute | solution.py:347
  49.5 35.7 %collective-permute-start.16 = (bf16[2,2,96,1024]{3,2,1,0:T(8,128)(2,1)}, bf16[2,2,96,1024]{3,2,1,0:T(8,128)(2,1)}, u32[]{:S(2)}, u32[]{:S(2)}) collective-permute-start(bf16[2,2,96,1024]{3,2,1,0:T(8,128)(2,1)} %round_to_send.2.refs_1_), channel_id=1, source_target_pairs={{3,2},{16,17},{7,6},{20,21},{11,10},{24,25},{15,14},{28,29}} | collective-permute-start | bytes 2359304 | tf_op jit(solution)/shard_map/ppermute | solution.py:347
  51.1 33.3 %slice-start = ((s8[25165824]{0:T(1024)(128)(4,1)}), s8[4194304]{0:T(1024)(128)(4,1)S(1)}, s32[]{:S(2)}) async-start(s8[25165824]{0:T(1024)(128)(4,1)} %bitcast.4), calls=%async_computation | async-start | bytes 8388608
  51.1 33.3 %slice-start.1 = ((s8[25165824]{0:T(1024)(128)(4,1)}), s8[4194304]{0:T(1024)(128)(4,1)S(1)}, s32[]{:S(2)}) async-start(s8[25165824]{0:T(1024)(128)(4,1)} %bitcast.4), calls=%async_computation.1 | async-start | bytes 8388608
  51.1 33.4 %slice-start.2 = ((s8[25165824]{0:T(1024)(128)(4,1)}), s8[4194304]{0:T(1024)(128)(4,1)S(1)}, s32[]{:S(2)}) async-start(s8[25165824]{0:T(1024)(128)(4,1)} %bitcast.4), calls=%async_computation.2 | async-start | bytes 8388608
  51.1 33.4 %slice-start.3 = ((s8[25165824]{0:T(1024)(128)(4,1)}), s8[4194304]{0:T(1024)(128)(4,1)S(1)}, s32[]{:S(2)}) async-start(s8[25165824]{0:T(1024)(128)(4,1)} %bitcast.4), calls=%async_computation.3 | async-start | bytes 8388608
  51.1 33.4 %slice-start.4 = ((s8[25165824]{0:T(1024)(128)(4,1)}), s8[4194304]{0:T(1024)(128)(4,1)S(1)}, s32[]{:S(2)}) async-start(s8[25165824]{0:T(1024)(128)(4,1)} %bitcast.4), calls=%async_computation.4 | async-start | bytes 8388608
  51.1 9.8 %collective-permute-start.9 = (bf16[2,96,512]{2,1,0:T(8,128)(2,1)S(1)}, bf16[2,96,512]{2,1,0:T(8,128)(2,1)S(1)}, u32[]{:S(2)}, u32[]{:S(2)}) collective-permute-start(bf16[2,96,512]{2,1,0:T(8,128)(2,1)S(1)} %pass_on.7.refs_5_.refs_3_), channel_id=1, source_target_pairs={{2,1},{17,18},{6,5},{21,22},{10,9},{25,26},{14,13},{29,30}} | collective-permute-start | bytes 589832 | tf_op jit(solution)/shard_map/ppermute | solution.py:347
  58.1 2.0 %copy-start.1 = (bf16[2,2,96,1024]{3,2,1,0:T(8,128)(2,1)S(1)}, bf16[2,2,96,1024]{3,2,1,0:T(8,128)(2,1)}, u32[]{:S(2)}) copy-start(bf16[2,2,96,1024]{3,2,1,0:T(8,128)(2,1)} %copy-done) | copy-start | bytes 2359300
  60.0 24.4 %slice-start.5 = ((s8[25165824]{0:T(1024)(128)(4,1)}), s8[4194304]{0:T(1024)(128)(4,1)S(1)}, s32[]{:S(2)}) async-start(s8[25165824]{0:T(1024)(128)(4,1)} %bitcast.4), calls=%async_computation.5 | async-start | bytes 8388608
  60.0 25.2 %collective-permute-start.15 = (bf16[2,2,96,1024]{3,2,1,0:T(8,128)(2,1)S(1)}, bf16[2,2,96,1024]{3,2,1,0:T(8,128)(2,1)S(1)}, u32[]{:S(2)}, u32[]{:S(2)}) collective-permute-start(bf16[2,2,96,1024]{3,2,1,0:T(8,128)(2,1)S(1)} %add_to_send.13.refs_1_), channel_id=1, source_target_pairs={{1,2},{18,17},{5,6},{22,21},{9,10},{26,25},{13,14},{30,29}} | collective-permute-start | bytes 2359304 | tf_op jit(solution)/shard_map/ppermute | solution.py:347
  63.5 23.5 %collective-permute-start.19 = (bf16[2,2,96,1024]{3,2,1,0:T(8,128)(2,1)S(1)}, bf16[2,2,96,1024]{3,2,1,0:T(8,128)(2,1)S(1)}, u32[]{:S(2)}, u32[]{:S(2)}) collective-permute-start(bf16[2,2,96,1024]{3,2,1,0:T(8,128)(2,1)S(1)} %add_to_send.14.refs_6_), channel_id=1, source_target_pairs={{2,3},{17,16},{6,7},{21,20},{10,11},{25,24},{14,15},{29,28}} | collective-permute-start | bytes 2359304 | tf_op jit(solution)/shard_map/ppermute | solution.py:347
  64.2 21.0 %collective-permute-start.8 = (bf16[2,2,96,512]{3,2,1,0:T(8,128)(2,1)S(1)}, bf16[2,2,96,512]{3,2,1,0:T(8,128)(2,1)S(1)}, u32[]{:S(2)}, u32[]{:S(2)}) collective-permute-start(bf16[2,2,96,512]{3,2,1,0:T(8,128)(2,1)S(1)} %get-tuple-element.37), channel_id=1, source_target_pairs={{0,1},{19,18},{4,5},{23,22},{8,9},{27,26},{12,13},{31,30}} | collective-permute-start | bytes 1179656 | tf_op jit(solution)/shard_map/ppermute | solution.py:347
  76.2 7.6 %collective-permute-start.11 = (bf16[2,96,512]{2,1,0:T(8,128)(2,1)S(1)}, bf16[2,96,512]{2,1,0:T(8,128)(2,1)S(1)}, u32[]{:S(2)}, u32[]{:S(2)}) collective-permute-start(bf16[2,96,512]{2,1,0:T(8,128)(2,1)S(1)} %pass_on.8.refs_3_.refs_2_), channel_id=1, source_target_pairs={{1,0},{18,19},{5,4},{22,23},{9,8},{26,27},{13,12},{30,31}} | collective-permute-start | bytes 589832 | tf_op jit(solution)/shard_map/ppermute | solution.py:347
  83.7 4.7 %collective-permute-start.18 = (bf16[2,96,1024]{2,1,0:T(8,128)(2,1)S(1)}, bf16[2,96,1024]{2,1,0:T(8,128)(2,1)S(1)}, u32[]{:S(2)}, u32[]{:S(2)}) collective-permute-start(bf16[2,96,1024]{2,1,0:T(8,128)(2,1)S(1)} %hidden_values.6.refs_3_.refs_4_), channel_id=1, source_target_pairs={{3,2},{16,17},{7,6},{20,21},{11,10},{24,25},{15,14},{28,29}} | collective-permute-start | bytes 1179656 | tf_op jit(solution)/shard_map/ppermute | solution.py:347
  86.3 2.8 %collective-permute-start.17 = (bf16[2,96,1024]{2,1,0:T(8,128)(2,1)S(1)}, bf16[2,96,1024]{2,1,0:T(8,128)(2,1)S(1)}, u32[]{:S(2)}, u32[]{:S(2)}) collective-permute-start(bf16[2,96,1024]{2,1,0:T(8,128)(2,1)S(1)} %hidden_values.7.refs_3_), channel_id=1, source_target_pairs={{2,1},{17,18},{6,5},{21,22},{10,9},{25,26},{14,13},{29,30}} | collective-permute-start | bytes 1179656 | tf_op jit(solution)/shard_map/ppermute | solution.py:347
  87.1 3.4 %collective-permute-start.23 = (bf16[2,96,1024]{2,1,0:T(8,128)(2,1)S(1)}, bf16[2,96,1024]{2,1,0:T(8,128)(2,1)S(1)}, u32[]{:S(2)}, u32[]{:S(2)}) collective-permute-start(bf16[2,96,1024]{2,1,0:T(8,128)(2,1)S(1)} %hidden_values.8.refs_1_.refs_4_), channel_id=1, source_target_pairs={{3,2},{16,17},{7,6},{20,21},{11,10},{24,25},{15,14},{28,29}} | collective-permute-start | bytes 1179656 | tf_op jit(solution)/shard_map/ppermute | solution.py:347
  87.8 4.2 %collective-permute-start.21 = (bf16[2,96,1024]{2,1,0:T(8,128)(2,1)S(1)}, bf16[2,96,1024]{2,1,0:T(8,128)(2,1)S(1)}, u32[]{:S(2)}, u32[]{:S(2)}) collective-permute-start(bf16[2,96,1024]{2,1,0:T(8,128)(2,1)S(1)} %hidden_values.7.refs_3_), channel_id=1, source_target_pairs={{2,3},{17,16},{6,7},{21,20},{10,11},{25,24},{14,15},{29,28}} | collective-permute-start | bytes 1179656 | tf_op jit(solution)/shard_map/ppermute | solution.py:347
  88.5 3.4 %collective-permute-start.22 = (bf16[2,96,1024]{2,1,0:T(8,128)(2,1)S(1)}, bf16[2,96,1024]{2,1,0:T(8,128)(2,1)S(1)}, u32[]{:S(2)}, u32[]{:S(2)}) collective-permute-start(bf16[2,96,1024]{2,1,0:T(8,128)(2,1)S(1)} %pass_on.9.refs_1_.refs_3_), channel_id=1, source_target_pairs={{2,1},{17,18},{6,5},{21,22},{10,9},{25,26},{14,13},{29,30}} | collective-permute-start | bytes 1179656 | tf_op jit(solution)/shard_map/ppermute | solution.py:347
  89.2 15.0 %collective-permute-start.20 = (bf16[2,96,1024]{2,1,0:T(8,128)(2,1)S(1)}, bf16[2,96,1024]{2,1,0:T(8,128)(2,1)S(1)}, u32[]{:S(2)}, u32[]{:S(2)}) collective-permute-start(bf16[2,96,1024]{2,1,0:T(8,128)(2,1)S(1)} %pass_on.10.refs_1_.refs_2_), channel_id=1, source_target_pairs={{1,0},{18,19},{5,4},{22,23},{9,8},{26,27},{13,12},{30,31}} | collective-permute-start | bytes 1179656 | tf_op jit(solution)/shard_map/ppermute | solution.py:347
  90.5 16.8 %collective-permute-start.25 = (bf16[2,96,1024]{2,1,0:T(8,128)(2,1)S(1)}, bf16[2,96,1024]{2,1,0:T(8,128)(2,1)S(1)}, u32[]{:S(2)}, u32[]{:S(2)}) collective-permute-start(bf16[2,96,1024]{2,1,0:T(8,128)(2,1)S(1)} %pass_on.11.refs_1_.refs_3_), channel_id=1, source_target_pairs={{2,1},{17,18},{6,5},{21,22},{10,9},{25,26},{14,13},{29,30}} | collective-permute-start | bytes 1179656 | tf_op jit(solution)/shard_map/ppermute | solution.py:347
  91.2 17.5 %collective-permute-start.14 = (bf16[2,2,96,512]{3,2,1,0:T(8,128)(2,1)S(1)}, bf16[2,2,96,512]{3,2,1,0:T(8,128)(2,1)S(1)}, u32[]{:S(2)}, u32[]{:S(2)}) collective-permute-start(bf16[2,2,96,512]{3,2,1,0:T(8,128)(2,1)S(1)} %add_to_send.15.refs_4_), channel_id=1, source_target_pairs={{1,2},{18,17},{5,6},{22,21},{9,10},{26,25},{13,14},{30,29}} | collective-permute-start | bytes 1179656 | tf_op jit(solution)/shard_map/ppermute | solution.py:347
  105.3 3.3 %collective-permute-start.24 = (bf16[2,2,96,512]{3,2,1,0:T(8,128)(2,1)S(1)}, bf16[2,2,96,512]{3,2,1,0:T(8,128)(2,1)S(1)}, u32[]{:S(2)}, u32[]{:S(2)}) collective-permute-start(bf16[2,2,96,512]{3,2,1,0:T(8,128)(2,1)S(1)} %round_to_send.3.refs_1_), channel_id=1, source_target_pairs={{3,2},{16,17},{7,6},{20,21},{11,10},{24,25},{15,14},{28,29}} | collective-permute-start | bytes 1179656 | tf_op jit(solution)/shard_map/ppermute | solution.py:347
  106.0 11.8 %collective-permute-start.30 = (bf16[2,96,1024]{2,1,0:T(8,128)(2,1)S(1)}, bf16[2,96,1024]{2,1,0:T(8,128)(2,1)S(1)}, u32[]{:S(2)}, u32[]{:S(2)}) collective-permute-start(bf16[2,96,1024]{2,1,0:T(8,128)(2,1)S(1)} %pass_on.12.refs_8_.refs_2_), channel_id=1, source_target_pairs={{1,0},{18,19},{5,4},{22,23},{9,8},{26,27},{13,12},{30,31}} | collective-permute-start | bytes 1179656 | tf_op jit(solution)/shard_map/ppermute | solution.py:347
  107.4 14.7 %collective-permute-start.29 = (bf16[2,96,1024]{2,1,0:T(8,128)(2,1)S(1)}, bf16[2,96,1024]{2,1,0:T(8,128)(2,1)S(1)}, u32[]{:S(2)}, u32[]{:S(2)}) collective-permute-start(bf16[2,96,1024]{2,1,0:T(8,128)(2,1)S(1)} %pass_on.13.refs_4_.refs_2_), channel_id=1, source_target_pairs={{1,0},{18,19},{5,4},{22,23},{9,8},{26,27},{13,12},{30,31}} | collective-permute-start | bytes 1179656 | tf_op jit(solution)/shard_map/ppermute | solution.py:347
  108.7 14.5 %collective-permute-start.28 = (bf16[2,96,512]{2,1,0:T(8,128)(2,1)S(1)}, bf16[2,96,512]{2,1,0:T(8,128)(2,1)S(1)}, u32[]{:S(2)}, u32[]{:S(2)}) collective-permute-start(bf16[2,96,512]{2,1,0:T(8,128)(2,1)S(1)} %hidden_values.9.refs_8_.refs_3_), channel_id=1, source_target_pairs={{2,3},{17,16},{6,7},{21,20},{10,11},{25,24},{14,15},{29,28}} | collective-permute-start | bytes 589832 | tf_op jit(solution)/shard_map/ppermute | solution.py:347
  109.4 13.9 %collective-permute-start.27 = (bf16[2,96,512]{2,1,0:T(8,128)(2,1)S(1)}, bf16[2,96,512]{2,1,0:T(8,128)(2,1)S(1)}, u32[]{:S(2)}, u32[]{:S(2)}) collective-permute-start(bf16[2,96,512]{2,1,0:T(8,128)(2,1)S(1)} %hidden_values.9.refs_8_.refs_3_), channel_id=1, source_target_pairs={{2,1},{17,18},{6,5},{21,22},{10,9},{25,26},{14,13},{29,30}} | collective-permute-start | bytes 589832 | tf_op jit(solution)/shard_map/ppermute | solution.py:347
  110.1 14.5 %collective-permute-start.26 = (bf16[2,96,512]{2,1,0:T(8,128)(2,1)S(1)}, bf16[2,96,512]{2,1,0:T(8,128)(2,1)S(1)}, u32[]{:S(2)}, u32[]{:S(2)}) collective-permute-start(bf16[2,96,512]{2,1,0:T(8,128)(2,1)S(1)} %hidden_values.9.refs_8_.refs_3_), channel_id=1, source_target_pairs={{2,0},{17,19},{6,4},{21,23},{10,8},{25,27},{14,12},{29,31}} | collective-permute-start | bytes 589832 | tf_op jit(solution)/shard_map/ppermute | solution.py:347
  122.0 5.3 %copy-start.4 = (s32[128,2]{0,1:T(2,128)S(1)}, s32[128,2]{0,1:T(2,128)}, u32[]{:S(2)}) copy-start(s32[128,2]{0,1:T(2,128)} %param.7) | copy-start | bytes 3076
  122.0 5.3 %copy-start.5 = (f32[128,2]{0,1:T(2,128)S(1)}, f32[128,2]{0,1:T(2,128)}, u32[]{:S(2)}) copy-start(f32[128,2]{0,1:T(2,128)} %param.8) | copy-start | bytes 3076
  125.2 2.1 %collective-permute-start.31 = (f32[2,48,1536]{2,1,0:T(8,128)S(1)}, f32[2,48,1536]{2,1,0:T(8,128)S(1)}, u32[]{:S(2)}, u32[]{:S(2)}) collective-permute-start(f32[2,48,1536]{2,1,0:T(8,128)S(1)} %get-tuple-element.48), channel_id=1, source_target_pairs={{0,16},{16,0},{1,17},{17,1},{2,18},{18,2},{3,19},{19,3},{4,20},{20... | collective-permute-start | bytes 1769480 | tf_op jit(solution)/shard_map/ppermute | solution.py:395
  128.0 5.9 %collective-permute-start.32 = (bf16[32,1536]{1,0:T(8,128)(2,1)S(1)}, bf16[32,1536]{1,0:T(8,128)(2,1)S(1)}, u32[]{:S(2)}, u32[]{:S(2)}) collective-permute-start(bf16[32,1536]{1,0:T(8,128)(2,1)S(1)} %get-tuple-element.50), channel_id=1, source_target_pairs={{0,12},{4,8},{8,4},{12,0},{1,13},{5,9},{9,5},{13,1},{2,14},{6,10},... | collective-permute-start | bytes 294920 | tf_op jit(solution)/shard_map/ppermute | solution.py:401
  130.6 5.4 %collective-permute-start.33 = (bf16[32,1536]{1,0:T(8,128)(2,1)S(1)}, bf16[32,1536]{1,0:T(8,128)(2,1)S(1)}, u32[]{:S(2)}, u32[]{:S(2)}) collective-permute-start(bf16[32,1536]{1,0:T(8,128)(2,1)S(1)} %get-tuple-element.51), channel_id=1, source_target_pairs={{0,8},{4,12},{8,0},{12,4},{1,9},{5,13},{9,1},{13,5},{2,10},{6,14},... | collective-permute-start | bytes 294920 | tf_op jit(solution)/shard_map/ppermute | solution.py:401
  131.1 5.0 %collective-permute-start.34 = (bf16[32,1536]{1,0:T(8,128)(2,1)S(1)}, bf16[32,1536]{1,0:T(8,128)(2,1)S(1)}, u32[]{:S(2)}, u32[]{:S(2)}) collective-permute-start(bf16[32,1536]{1,0:T(8,128)(2,1)S(1)} %get-tuple-element.52), channel_id=1, source_target_pairs={{0,4},{4,0},{8,12},{12,8},{1,5},{5,1},{9,13},{13,9},{2,6},{6,2},{1... | collective-permute-start | bytes 294920 | tf_op jit(solution)/shard_map/ppermute | solution.py:401
  136.1 6.4 %collective-permute-start.37 = (bf16[32,1536]{1,0:T(8,128)(2,1)S(1)}, bf16[32,1536]{1,0:T(8,128)(2,1)S(1)}, u32[]{:S(2)}, u32[]{:S(2)}) collective-permute-start(bf16[32,1536]{1,0:T(8,128)(2,1)S(1)} %add_convert_fusion.refs_1_), channel_id=1, source_target_pairs={{0,12},{4,8},{8,4},{12,0},{1,13},{5,9},{9,5},{13,1},{2,14},{6,10},... | collective-permute-start | bytes 294920 | tf_op jit(solution)/shard_map/ppermute | solution.py:405
  137.8 5.8 %collective-permute-start.36 = (bf16[32,1536]{1,0:T(8,128)(2,1)S(1)}, bf16[32,1536]{1,0:T(8,128)(2,1)S(1)}, u32[]{:S(2)}, u32[]{:S(2)}) collective-permute-start(bf16[32,1536]{1,0:T(8,128)(2,1)S(1)} %add_convert_fusion.refs_1_), channel_id=1, source_target_pairs={{0,8},{4,12},{8,0},{12,4},{1,9},{5,13},{9,1},{13,5},{2,10},{6,14},... | collective-permute-start | bytes 294920 | tf_op jit(solution)/shard_map/ppermute | solution.py:405
  139.1 4.7 %collective-permute-start.35 = (bf16[32,1536]{1,0:T(8,128)(2,1)S(1)}, bf16[32,1536]{1,0:T(8,128)(2,1)S(1)}, u32[]{:S(2)}, u32[]{:S(2)}) collective-permute-start(bf16[32,1536]{1,0:T(8,128)(2,1)S(1)} %add_convert_fusion.refs_1_), channel_id=1, source_target_pairs={{0,4},{4,0},{8,12},{12,8},{1,5},{5,1},{9,13},{13,9},{2,6},{6,2},{1... | collective-permute-start | bytes 294920 | tf_op jit(solution)/shard_map/ppermute | solution.py:405
  (2 other events, 1.6 us)

commit v6 on v5

--- a/solution.py
+++ b/solution.py
@@ -11,36 +11,30 @@
 F32, BF16 = jnp.float32, jnp.bfloat16
 MIB = 1024 * 1024
 
-CHUNKS = ((2, "end"), (4, "end"), (4, "end"), (4, "inner"), (2, "direct"))
-
-ROUTES = {
-    "end": {
-        "m0": (0, 1, None), "m1": (1, 2, "m0"), "m2": (2, 3, "m1"),
-        "a0": (3, 2, None), "a1": (2, 1, "a0"), "a2": (1, 0, "a1"),
-    },
-    "inner": {
-        "m0": (0, 1, None), "mb": (3, 2, None), "m1": (1, 2, "m0"),
-        "a0": (2, 1, None), "a1": (2, 3, None), "a2": (1, 0, "a0"),
-    },
-    "direct": {
-        "m0": (0, 1, None), "mb": (3, 2, None), "m1": (1, 2, "m0"),
-        "a0": (2, 1, None), "a1": (2, 3, None), "a2": (2, 0, None),
-    },
+CHUNKS = ((3, "end"), (3, "end"), (3, "end"), (3, "end"), (2, "inner"), (2, "inner"))
+GROUPS = {0: ((0,), "relay"), 1: ((1,), "relay"), 2: ((2,), "relay"), 3: ((3,), "relay"), 4: ((4,), "relay"), 5: ((5,), "relay")}
+
+SUMS = {
+    "end": {"m0": (0, 1, None), "m1": (1, 2, "m0"), "m2": (2, 3, "m1")},
+    "inner": {"m0": (0, 1, None), "mb": (3, 2, None), "m1": (1, 2, "m0")},
 }
-OWNER = {"end": (3, ("m2",)), "inner": (2, ("m1", "mb")), "direct": (2, ("m1", "mb"))}
-HELD = {
-    "end": ("a2", "a1", "a0", None),
-    "inner": ("a2", "a0", None, "a1"),
-    "direct": ("a2", "a0", None, "a1"),
+BACK = {
+    ("end", "relay"): {"a0": (3, 2, None), "a1": (2, 1, "a0"), "a2": (1, 0, "a1")},
+    ("end", "direct"): {"a0": (3, 2, None), "a1": (3, 1, None), "a2": (3, 0, None)},
+    ("inner", "relay"): {"a0": (2, 1, None), "a1": (2, 3, None), "a2": (1, 0, "a0")},
+    ("inner", "direct"): {"a0": (2, 1, None), "a1": (2, 3, None), "a2": (2, 0, None)},
 }
+OWNER = {"end": (3, ("m2",)), "inner": (2, ("m1", "mb"))}
+HELD = {"end": ("a2", "a1", "a0", None), "inner": ("a2", "a0", None, "a1")}
 
 ORDER = (
-    ("g", 0), ("m0", 0), ("g", 2), ("m0", 2), ("m1", 0), ("g", 1), ("m2", 0), ("h", 0),
-    ("m0", 1), ("m1", 2), ("a0", 0), ("g", 3), ("m0", 3), ("m1", 1), ("m2", 2), ("mb", 3),
-    ("a1", 0), ("g", 4), ("m1", 3), ("a2", 0), ("h", 2), ("m0", 4), ("m2", 1), ("d", 0),
-    ("m1", 4), ("a0", 2), ("h", 3), ("a0", 3), ("a1", 3), ("h", 1), ("a0", 1), ("a1", 2),
-    ("a2", 3), ("a1", 1), ("a2", 2), ("d", 3), ("mb", 4), ("a2", 1), ("h", 4), ("a0", 4),
-    ("a2", 4), ("a1", 4), ("d", 2), ("d", 1), ("d", 4),
+    ("g", 0), ("m0", 0), ("g", 4), ("m0", 4), ("g", 2), ("m0", 2), ("m1", 0), ("g", 1),
+    ("m0", 1), ("g", 3), ("m0", 3), ("m1", 2), ("mb", 4), ("m2", 0), ("g", 5), ("m0", 5),
+    ("m1", 1), ("m2", 2), ("h", 0), ("a0", 0), ("m1", 3), ("m1", 4), ("m2", 1), ("h", 2),
+    ("a1", 0), ("m2", 3), ("a0", 2), ("m1", 5), ("a1", 2), ("a2", 0), ("h", 1), ("h", 4),
+    ("a2", 2), ("a0", 4), ("a0", 1), ("a1", 1), ("a2", 4), ("h", 3), ("d", 0), ("a1", 4),
+    ("mb", 5), ("a2", 1), ("d", 2), ("a0", 3), ("a1", 3), ("d", 1), ("h", 5), ("a2", 3),
+    ("d", 4), ("a0", 5), ("a1", 5), ("a2", 5), ("d", 3), ("d", 5),
 )
 
 SMEM = pl.BlockSpec(memory_space=pltpu.SMEM)
@@ -184,21 +178,28 @@
 
 
 def hidden_values(place, at, full, got, after):
-    def kernel(place_ref, full_ref, *refs):
-        got_refs, out_ref = refs[:-1], refs[-1]
+    widths = [part.shape[3] for part in full]
+    flat = [value for values in got for value in values]
+    arrivals = len(got[0])
+
+    def kernel(place_ref, *refs):
+        out_ref, got_refs = refs[-1], refs[len(widths) : -1]
 
         @pl.when(place_ref[0] == at)
         def _():
-            for e in range(full_ref.shape[1]):
-                gate, up = full_ref[0, e], full_ref[1, e]
-                for ref in got_refs:
-                    gate, up = gate + ref[0, e].astype(F32), up + ref[1, e].astype(F32)
-                out_ref[e] = (gate / (1.0 + jnp.exp(-gate)) * up).astype(BF16)
-
-    shape = jax.ShapeDtypeStruct(full.shape[1:], BF16)
-    return call(
-        kernel, "hidden_values", shape, [place, full, *got], [SMEM] + [VMEM] * (1 + len(got)), after
-    )
+            start = 0
+            for c, width in enumerate(widths):
+                for e in range(out_ref.shape[0]):
+                    gate, up = refs[c][0, e], refs[c][1, e]
+                    for ref in got_refs[c * arrivals : (c + 1) * arrivals]:
+                        gate, up = gate + ref[0, e].astype(F32), up + ref[1, e].astype(F32)
+                    value = gate / (1.0 + jnp.exp(-gate)) * up
+                    out_ref[e, :, start : start + width] = value.astype(BF16)
+                start += width
+
+    shape = jax.ShapeDtypeStruct(full[0].shape[1:3] + (sum(widths),), BF16)
+    specs = [SMEM] + [VMEM] * (len(full) + len(flat))
+    return call(kernel, "hidden_values", shape, [place, *full, *flat], specs, after)
 
 
 def pass_on(value, after):
@@ -209,18 +210,15 @@
     return call(kernel, "pass_on", shape, [value], [ANY], after, aliases={0: 0})
 
 
-def down(place, held, down_weight, start, totals, row_counts, after):
-    local_count, count, width = held[0].shape
+def down(place, held, down_weight, starts, widths, totals, row_counts, after):
+    local_count, count, _ = held[0].shape
     features = down_weight.shape[2]
-    block = 256 if width % 256 == 0 else 128
-    pieces = width // block
     places = len(held)
 
     def kernel(place_ref, *refs):
         held_refs, weight_ref = refs[:places], refs[places]
         total_refs = refs[places + 1 : places + 1 + len(totals)]
-        out_refs = refs[places + 1 + len(totals) :][: len(row_counts)]
-        hidden = refs[-1]
+        out_refs, hidden = refs[places + 1 + len(totals) : -1], refs[-1]
         for i in range(places):
 
             @pl.when(place_ref[0] == i)
@@ -228,32 +226,29 @@
                 hidden[...] = held_refs[i][...]
 
         for e in range(local_count):
-            product = None
-            for k in range(pieces):
-                part = jnp.dot(
-                    hidden[e, :, k * block : (k + 1) * block],
-                    weight_ref[e, start + k * block : start + (k + 1) * block, :],
+            product, column = None, 0
+            for start, width in zip(starts, widths):
+                value = jnp.dot(
+                    hidden[e, :, column : column + width],
+                    weight_ref[e, start : start + width, :],
                     preferred_element_type=F32,
                 )
-                product = part if product is None else product + part
+                product = value if product is None else product + value
+                column += width
             first = 0
             for i, rows in enumerate(row_counts):
                 value = product[first : first + rows]
                 out_refs[i][e] = total_refs[i][e] + value if totals else value
                 first += rows
 
-    shapes = [jax.ShapeDtypeStruct((local_count, rows, features), F32) for rows in row_counts]
-    operands = [place, *held, down_weight, *totals]
     return call(
         kernel,
         "down",
-        shapes,
-        operands,
+        [jax.ShapeDtypeStruct((local_count, rows, features), F32) for rows in row_counts],
+        [place, *held, down_weight, *totals],
         [SMEM] + [VMEM] * (places + 1 + len(totals)),
         after,
-        [
-            pltpu.VMEM(held[0].shape, BF16),
-        ],
+        [pltpu.VMEM(held[0].shape, BF16)],
         limit=6 + 2 * local_count * count * features * 4 // MIB,
     )
 
@@ -360,21 +355,32 @@
         if c >= len(widths):
             continue
         kind = CHUNKS[c][1]
-        route = ROUTES[kind]
         owner, summed_by = OWNER[kind]
+        chunks, way = GROUPS.get(c, ((), ""))
+        chunks = [q for q in chunks if q < len(widths)]
         if name == "g":
             full[c], short[c] = gate_up(
                 place, rows, (gate_weight, up_weight), starts[c], widths[c], after
             )
             after = [full[c]]
         elif name == "h":
-            values[c] = hidden_values(place, owner, full[c], [got[c, m] for m in summed_by], after)
+            arrived = [[got[m, q] for m in summed_by] for q in chunks]
+            values[c] = hidden_values(place, owner, [full[q] for q in chunks], arrived, after)
             after = [values[c]]
         elif name == "d":
-            held = [values[c] if m is None else got[c, m] for m in HELD[kind]]
-            totals = down(place, held, down_weight, starts[c], totals, row_counts, after)
+            totals = down(
+                place,
+                [values[c] if m is None else got[m, c] for m in HELD[kind]],
+                down_weight,
+                [starts[q] for q in chunks],
+                [widths[q] for q in chunks],
+                totals,
+                row_counts,
+                after,
+            )
             after = [totals[0]]
         else:
+            route = SUMS[kind] if name[0] == "m" else BACK[kind, way]
             source, target, needed = route[name]
             if name == "m0":
                 sent = short[c]
@@ -382,14 +388,14 @@
                 sent = round_to_send(place, source, full[c], after)
                 after = [sent]
             elif name[0] == "m":
-                sent = add_to_send(place, source, full[c], got[c, needed], after)
+                sent = add_to_send(place, source, full[c], got[needed, c], after)
                 after = [sent]
             elif needed is None:
                 sent = values[c]
             else:
-                sent = got[c, needed] = pass_on(got[c, needed], after)
+                sent = got[needed, c] = pass_on(got[needed, c], after)
                 after = [sent]
-            got[c, name] = hop(sent, source, target)
+            got[name, c] = hop(sent, source, target)
 
     if shards == 2:
         sums = [totals[0], lax.ppermute(totals[1], "dp", swap)]

time: 145 us -> 137 us (0.945)
  starting transfers between devices: 59.9 us -> 51.1 us
  waiting for transfers between devices: 44.6 us -> 50.5 us
  Pallas kernels: 34.8 us -> 31.7 us
  local copies, waits for them, and re-layouts: 4.55 us -> 1.72 us
    ppermute x30 -> x36, starting transfers between devices: 52.2 us -> 43.4 us  [hop(): return lax.ppermute(value, ('dp', 'blk'), pairs)]
    ppermute x30 -> x36, waiting for transfers between devices: 32.8 us -> 38.5 us  [hop(): return lax.ppermute(value, ('dp', 'blk'), pairs)]
    pallas_call x35 -> x43, Pallas kernels: 34.8 us -> 31.7 us  [call(): pl.pallas_call(body, out_shape=outs, in_specs=list(specs) + [ANY] * len(a...]
    unnamed x24 -> x20, local copies, waits for them, and re-layouts: 4.55 us -> 1.72 us
  transfers between devices with their start and end apart: 38 -> 44, of which waited for: 15 -> 16; matrix products, arithmetic and copies ran while one was open for 0% -> 0% of each run, Pallas kernels for 20% -> 18%
where the time goes in v6:
time: 137 us; the launch traced here: 136 us
  starting transfers between devices  51.1 us (37%)
  waiting for transfers between devices  50.5 us (37%)
  Pallas kernels  31.7 us (23%)
  local copies, waits for them, and re-layouts  1.72 us (1%)
    ppermute x36, starting transfers between devices, hop(): return lax.ppermute(value, ('dp', 'blk'), pairs)  43.4 us
    ppermute x36, waiting for transfers between devices, hop(): return lax.ppermute(value, ('dp', 'blk'), pairs)  38.5 us
    pallas_call x43, Pallas kernels, call(): pl.pallas_call(body, out_shape=outs, in_specs=list(specs) + [ANY] * len(a...  31.7 us
    ppermute x3, waiting for transfers between devices, local(): own = own + lax.ppermute(sent[step - 1], 'expert', exchange).astype(F32)  5.06 us
    ppermute x3, waiting for transfers between devices, local(): lax.ppermute(block, 'expert', [(i, i ^ step) for i in range(groups)])  3.77 us
    ppermute x3, starting transfers between devices, local(): own = own + lax.ppermute(sent[step - 1], 'expert', exchange).astype(F32)  3.55 us
    ppermute x3, starting transfers between devices, local(): lax.ppermute(block, 'expert', [(i, i ^ step) for i in range(groups)])  3.55 us
  transfers between devices with their start and end apart: 44, of which 16 were waited for; matrix products, arithmetic and copies ran while one was open for 0% of the time, Pallas kernels for 18%

profile of v6, /device:TPU:0, one launch (start us, length us, event | category | flops | bytes accessed | tf_op | source)
XLA Modules:
  0.0 135.9 jit_solution(11397865060410091472)
XLA Ops:
  0.0 1.0 copy-done
  2.6 1.2 collective-permute-done.refs_2_
  3.8 4.4 %gate_up.6 = (f32[2,2,96,768]{3,2,1,0:T(8,128)S(1)}, bf16[2,2,96,768]{3,2,1,0:T(8,128)(2,1)S(1)}) custom-call(s32[1]{0:T(128)} %bitcast.3.refs_0_, bf16[2,48,1536]{2,1,0:T(8,128)(2,1)S(1)} %pick.1.refs_1_, bf16[2,48,1536]{2,1,0:T(8,128)(2,1)S(1)} %collective-permute-done.refs_2_, bf16[2,1536,4096]{2,1,0:T(8,128)(2,1)} %refs_3_.11, ...), custom_call_target="tpu_custom_call" | custom-call | tf_op jit(solution)/shard_map/gate_up/pallas_call | solution.py:52
  8.2 4.9 %collective-permute-start.1 = (bf16[2,2,96,768]{3,2,1,0:T(8,128)(2,1)S(1)}, bf16[2,2,96,768]{3,2,1,0:T(8,128)(2,1)S(1)}, u32[]{:S(2)}, u32[]{:S(2)}) collective-permute-start(bf16[2,2,96,768]{3,2,1,0:T(8,128)(2,1)S(1)} %get-tuple-element.34), channel_id=1, source_target_pairs={{0,1},{19,18},{4,5},{23,22},{8,9},{27,26},{12,13},{31,30}} | collective-permute-start | bytes 1769480 | tf_op jit(solution)/shard_map/ppermute | solution.py:342
  13.1 3.3 %gate_up.7 = (f32[2,2,96,512]{3,2,1,0:T(8,128)S(1)}, bf16[2,2,96,512]{3,2,1,0:T(8,128)(2,1)S(1)}) custom-call(s32[1]{0:T(128)} %bitcast.3.refs_0_, bf16[2,48,1536]{2,1,0:T(8,128)(2,1)S(1)} %pick.1.refs_1_, bf16[2,48,1536]{2,1,0:T(8,128)(2,1)S(1)} %collective-permute-done.refs_2_, bf16[2,1536,4096]{2,1,0:T(8,128)(2,1)} %refs_3_.11, ...), custom_call_target="tpu_custom_call" | custom-call | tf_op jit(solution)/shard_map/gate_up/pallas_call | solution.py:52
  16.4 4.4 %gate_up.8 = (f32[2,2,96,768]{3,2,1,0:T(8,128)S(1)}, bf16[2,2,96,768]{3,2,1,0:T(8,128)(2,1)S(1)}) custom-call(s32[1]{0:T(128)} %bitcast.3.refs_0_, bf16[2,48,1536]{2,1,0:T(8,128)(2,1)S(1)} %pick.1.refs_1_, bf16[2,48,1536]{2,1,0:T(8,128)(2,1)S(1)} %collective-permute-done.refs_2_, bf16[2,1536,4096]{2,1,0:T(8,128)(2,1)} %refs_3_.11, ...), custom_call_target="tpu_custom_call" | custom-call | tf_op jit(solution)/shard_map/gate_up/pallas_call | solution.py:52
  20.9 1.3 collective-permute-start.3
  23.0 4.4 %gate_up.9 = (f32[2,2,96,768]{3,2,1,0:T(8,128)S(1)}, bf16[2,2,96,768]{3,2,1,0:T(8,128)(2,1)S(1)}) custom-call(s32[1]{0:T(128)} %bitcast.3.refs_0_, bf16[2,48,1536]{2,1,0:T(8,128)(2,1)S(1)} %pick.1.refs_1_, bf16[2,48,1536]{2,1,0:T(8,128)(2,1)S(1)} %collective-permute-done.refs_2_, bf16[2,1536,4096]{2,1,0:T(8,128)(2,1)} %refs_3_.11, ...), custom_call_target="tpu_custom_call" | custom-call | tf_op jit(solution)/shard_map/gate_up/pallas_call | solution.py:52
  27.4 3.3 %collective-permute-start.8 = (bf16[2,2,96,768]{3,2,1,0:T(8,128)(2,1)S(1)}, bf16[2,2,96,768]{3,2,1,0:T(8,128)(2,1)S(1)}, u32[]{:S(2)}, u32[]{:S(2)}) collective-permute-start(bf16[2,2,96,768]{3,2,1,0:T(8,128)(2,1)S(1)} %get-tuple-element.43), channel_id=1, source_target_pairs={{0,1},{19,18},{4,5},{23,22},{8,9},{27,26},{12,13},{31,30}} | collective-permute-start | bytes 1769480 | tf_op jit(solution)/shard_map/ppermute | solution.py:342
  30.8 4.4 %gate_up.10 = (f32[2,2,96,768]{3,2,1,0:T(8,128)S(1)}, bf16[2,2,96,768]{3,2,1,0:T(8,128)(2,1)S(1)}) custom-call(s32[1]{0:T(128)} %bitcast.3.refs_0_, bf16[2,48,1536]{2,1,0:T(8,128)(2,1)S(1)} %pick.1.refs_1_, bf16[2,48,1536]{2,1,0:T(8,128)(2,1)S(1)} %collective-permute-done.refs_2_, bf16[2,1536,4096]{2,1,0:T(8,128)(2,1)} %refs_3_.11, ...), custom_call_target="tpu_custom_call" | custom-call | tf_op jit(solution)/shard_map/gate_up/pallas_call | solution.py:52
  36.7 2.0 %collective-permute-start.5 = (bf16[2,2,96,768]{3,2,1,0:T(8,128)(2,1)S(1)}, bf16[2,2,96,768]{3,2,1,0:T(8,128)(2,1)S(1)}, u32[]{:S(2)}, u32[]{:S(2)}) collective-permute-start(bf16[2,2,96,768]{3,2,1,0:T(8,128)(2,1)S(1)} %get-tuple-element.42), channel_id=1, source_target_pairs={{0,1},{19,18},{4,5},{23,22},{8,9},{27,26},{12,13},{31,30}} | collective-permute-start | bytes 1769480 | tf_op jit(solution)/shard_map/ppermute | solution.py:342
  38.7 3.5 %gate_up.11 = (f32[2,2,96,512]{3,2,1,0:T(8,128)S(1)}, bf16[2,2,96,512]{3,2,1,0:T(8,128)(2,1)S(1)}) custom-call(s32[1]{0:T(128)} %bitcast.3.refs_0_, bf16[2,48,1536]{2,1,0:T(8,128)(2,1)S(1)} %pick.1.refs_1_, bf16[2,48,1536]{2,1,0:T(8,128)(2,1)S(1)} %collective-permute-done.refs_2_, bf16[2,1536,4096]{2,1,0:T(8,128)(2,1)} %refs_3_.11, ...), custom_call_target="tpu_custom_call" | custom-call | tf_op jit(solution)/shard_map/gate_up/pallas_call | solution.py:52
  42.3 0.8 collective-permute-start.12
  43.1 0.8 collective-permute-start.11
  44.0 2.5 %collective-permute-start.13 = (bf16[2,2,96,512]{3,2,1,0:T(8,128)(2,1)S(1)}, bf16[2,2,96,512]{3,2,1,0:T(8,128)(2,1)S(1)}, u32[]{:S(2)}, u32[]{:S(2)}) collective-permute-start(bf16[2,2,96,512]{3,2,1,0:T(8,128)(2,1)S(1)} %get-tuple-element.44), channel_id=1, source_target_pairs={{0,1},{19,18},{4,5},{23,22},{8,9},{27,26},{12,13},{31,30}} | collective-permute-start | bytes 1179656 | tf_op jit(solution)/shard_map/ppermute | solution.py:342
  46.6 0.8 collective-permute-start.9
  48.1 5.8 %collective-permute-done.13.refs_2_ = bf16[2,2,96,512]{3,2,1,0:T(8,128)(2,1)S(1)} collective-permute-done((bf16[2,2,96,512]{3,2,1,0:T(8,128)(2,1)S(1)}, bf16[2,2,96,512]{3,2,1,0:T(8,128)(2,1)S(1)}, u32[]{:S(2)}, u32[]{:S(2)}) %collective-permute-start.13) | collective-permute-done | bytes 393248 | tf_op jit(solution)/shard_map/ppermute | solution.py:342
  53.9 4.4 %collective-permute-start.4 = (bf16[2,2,96,512]{3,2,1,0:T(8,128)(2,1)S(1)}, bf16[2,2,96,512]{3,2,1,0:T(8,128)(2,1)S(1)}, u32[]{:S(2)}, u32[]{:S(2)}) collective-permute-start(bf16[2,2,96,512]{3,2,1,0:T(8,128)(2,1)S(1)} %get-tuple-element.41), channel_id=1, source_target_pairs={{0,1},{19,18},{4,5},{23,22},{8,9},{27,26},{12,13},{31,30}} | collective-permute-start | bytes 1179656 | tf_op jit(solution)/shard_map/ppermute | solution.py:342
  59.1 0.9 collective-permute-start.16
  60.0 0.8 collective-permute-start.15
  60.8 5.2 %collective-permute-done.4.refs_2_ = bf16[2,2,96,512]{3,2,1,0:T(8,128)(2,1)S(1)} collective-permute-done((bf16[2,2,96,512]{3,2,1,0:T(8,128)(2,1)S(1)}, bf16[2,2,96,512]{3,2,1,0:T(8,128)(2,1)S(1)}, u32[]{:S(2)}, u32[]{:S(2)}) %collective-permute-start.4) | collective-permute-done | bytes 393248 | tf_op jit(solution)/shard_map/ppermute | solution.py:342
  70.3 1.3 collective-permute-start.17
  72.4 1.3 collective-permute-start.28
  75.1 9.5 %collective-permute-done.17.refs_1_ = bf16[2,96,768]{2,1,0:T(8,128)(2,1)S(1)} collective-permute-done((bf16[2,96,768]{2,1,0:T(8,128)(2,1)S(1)}, bf16[2,96,768]{2,1,0:T(8,128)(2,1)S(1)}, u32[]{:S(2)}, u32[]{:S(2)}) %collective-permute-start.17) | collective-permute-done | bytes 294944 | tf_op jit(solution)/shard_map/ppermute | solution.py:342
  84.6 0.9 down.6
  86.3 1.3 collective-permute-start.27
  87.7 0.9 down.7
  90.0 8.2 %collective-permute-done.27.refs_1_ = bf16[2,96,768]{2,1,0:T(8,128)(2,1)S(1)} collective-permute-done((bf16[2,96,768]{2,1,0:T(8,128)(2,1)S(1)}, bf16[2,96,768]{2,1,0:T(8,128)(2,1)S(1)}, u32[]{:S(2)}, u32[]{:S(2)}) %collective-permute-start.27) | collective-permute-done | bytes 294944 | tf_op jit(solution)/shard_map/ppermute | solution.py:342
  98.3 1.3 collective-permute-start.31
  99.6 0.9 down.8
  101.2 1.3 collective-permute-start.36
  103.2 2.6 %collective-permute-done.31.refs_1_ = bf16[2,96,512]{2,1,0:T(8,128)(2,1)S(1)} collective-permute-done((bf16[2,96,512]{2,1,0:T(8,128)(2,1)S(1)}, bf16[2,96,512]{2,1,0:T(8,128)(2,1)S(1)}, u32[]{:S(2)}, u32[]{:S(2)}) %collective-permute-start.31) | collective-permute-done | bytes 196640 | tf_op jit(solution)/shard_map/ppermute | solution.py:342
  106.5 1.3 collective-permute-start.34
  107.8 2.7 %collective-permute-done.36.refs_1_ = bf16[2,96,768]{2,1,0:T(8,128)(2,1)S(1)} collective-permute-done((bf16[2,96,768]{2,1,0:T(8,128)(2,1)S(1)}, bf16[2,96,768]{2,1,0:T(8,128)(2,1)S(1)}, u32[]{:S(2)}, u32[]{:S(2)}) %collective-permute-start.36) | collective-permute-done | bytes 294944 | tf_op jit(solution)/shard_map/ppermute | solution.py:342
  110.5 0.9 down.10
  111.4 4.3 %collective-permute-done.34.refs_1_ = bf16[2,96,512]{2,1,0:T(8,128)(2,1)S(1)} collective-permute-done((bf16[2,96,512]{2,1,0:T(8,128)(2,1)S(1)}, bf16[2,96,512]{2,1,0:T(8,128)(2,1)S(1)}, u32[]{:S(2)}, u32[]{:S(2)}) %collective-permute-start.34) | collective-permute-done | bytes 196640 | tf_op jit(solution)/shard_map/ppermute | solution.py:342
  116.4 2.0 %collective-permute-done.37.refs_4_ = f32[2,48,1536]{2,1,0:T(8,128)S(1)} collective-permute-done((f32[2,48,1536]{2,1,0:T(8,128)S(1)}, f32[2,48,1536]{2,1,0:T(8,128)S(1)}, u32[]{:S(2)}, u32[]{:S(2)}) %collective-permute-start.37) | collective-permute-done | bytes 589856 | tf_op jit(solution)/shard_map/ppermute | solution.py:401
  119.2 1.6 %collective-permute-start.40 = (bf16[32,1536]{1,0:T(8,128)(2,1)S(1)}, bf16[32,1536]{1,0:T(8,128)(2,1)S(1)}, u32[]{:S(2)}, u32[]{:S(2)}) collective-permute-start(bf16[32,1536]{1,0:T(8,128)(2,1)S(1)} %get-tuple-element.60), channel_id=1, source_target_pairs={{0,4},{4,0},{8,12},{12,8},{1,5},{5,1},{9,13},{13,9},{2,6},{6,2},{1... | collective-permute-start | bytes 294920 | tf_op jit(solution)/shard_map/ppermute | solution.py:407
  120.7 1.5 %collective-permute-start.39 = (bf16[32,1536]{1,0:T(8,128)(2,1)S(1)}, bf16[32,1536]{1,0:T(8,128)(2,1)S(1)}, u32[]{:S(2)}, u32[]{:S(2)}) collective-permute-start(bf16[32,1536]{1,0:T(8,128)(2,1)S(1)} %get-tuple-element.59), channel_id=1, source_target_pairs={{0,8},{4,12},{8,0},{12,4},{1,9},{5,13},{9,1},{13,5},{2,10},{6,14},... | collective-permute-start | bytes 294920 | tf_op jit(solution)/shard_map/ppermute | solution.py:407
  122.7 1.3 collective-permute-done.40
  124.1 2.4 %collective-permute-done.39 = bf16[32,1536]{1,0:T(8,128)(2,1)S(1)} collective-permute-done((bf16[32,1536]{1,0:T(8,128)(2,1)S(1)}, bf16[32,1536]{1,0:T(8,128)(2,1)S(1)}, u32[]{:S(2)}, u32[]{:S(2)}) %collective-permute-start.39) | collective-permute-done | bytes 98336 | tf_op jit(solution)/shard_map/ppermute | solution.py:407
  126.5 1.3 collective-permute-done.38
  127.8 0.9 collective-permute-start.41
  128.8 0.9 collective-permute-start.42
  129.6 1.7 %collective-permute-start.43 = (bf16[32,1536]{1,0:T(8,128)(2,1)S(1)}, bf16[32,1536]{1,0:T(8,128)(2,1)S(1)}, u32[]{:S(2)}, u32[]{:S(2)}) collective-permute-start(bf16[32,1536]{1,0:T(8,128)(2,1)S(1)} %add_convert_fusion.refs_1_), channel_id=1, source_target_pairs={{0,12},{4,8},{8,4},{12,0},{1,13},{5,9},{9,5},{13,1},{2,14},{6,10},... | collective-permute-start | bytes 294920 | tf_op jit(solution)/shard_map/ppermute | solution.py:411
  131.4 2.1 %collective-permute-done.41.refs_2_ = bf16[32,1536]{1,0:T(8,128)(2,1)S(1)} collective-permute-done((bf16[32,1536]{1,0:T(8,128)(2,1)S(1)}, bf16[32,1536]{1,0:T(8,128)(2,1)S(1)}, u32[]{:S(2)}, u32[]{:S(2)}) %collective-permute-start.41) | collective-permute-done | bytes 98336 | tf_op jit(solution)/shard_map/ppermute | solution.py:411
  133.8 1.3 collective-permute-done.43.refs_4_
  135.2 0.8 place_blocks.1
  (105 shorter events, 18.0 us)
Async XLA Ops:
  2.0 1.7 %collective-permute-start = (bf16[2,48,1536]{2,1,0:T(8,128)(2,1)S(1)}, bf16[2,48,1536]{2,1,0:T(8,128)(2,1)S(1)}, u32[]{:S(2)}, u32[]{:S(2)}) collective-permute-start(bf16[2,48,1536]{2,1,0:T(8,128)(2,1)S(1)} %pick.1.refs_1_), channel_id=1, source_target_pairs={{0,16},{16,0},{1,17},{17,1},{2,18},{18,2},{3,19},{19,3},{4,20},{20... | collective-permute-start | bytes 884744 | tf_op jit(solution)/shard_map/ppermute | solution.py:346
  8.2 14.0 %collective-permute-start.1 = (bf16[2,2,96,768]{3,2,1,0:T(8,128)(2,1)S(1)}, bf16[2,2,96,768]{3,2,1,0:T(8,128)(2,1)S(1)}, u32[]{:S(2)}, u32[]{:S(2)}) collective-permute-start(bf16[2,2,96,768]{3,2,1,0:T(8,128)(2,1)S(1)} %get-tuple-element.34), channel_id=1, source_target_pairs={{0,1},{19,18},{4,5},{23,22},{8,9},{27,26},{12,13},{31,30}} | collective-permute-start | bytes 1769480 | tf_op jit(solution)/shard_map/ppermute | solution.py:342
  20.9 14.3 %collective-permute-start.3 = (bf16[2,2,96,768]{3,2,1,0:T(8,128)(2,1)S(1)}, bf16[2,2,96,768]{3,2,1,0:T(8,128)(2,1)S(1)}, u32[]{:S(2)}, u32[]{:S(2)}) collective-permute-start(bf16[2,2,96,768]{3,2,1,0:T(8,128)(2,1)S(1)} %get-tuple-element.37), channel_id=1, source_target_pairs={{0,1},{19,18},{4,5},{23,22},{8,9},{27,26},{12,13},{31,30}} | collective-permute-start | bytes 1769480 | tf_op jit(solution)/shard_map/ppermute | solution.py:342
  22.3 13.7 %collective-permute-start.2 = (bf16[2,2,96,768]{3,2,1,0:T(8,128)(2,1)S(1)}, bf16[2,2,96,768]{3,2,1,0:T(8,128)(2,1)S(1)}, u32[]{:S(2)}, u32[]{:S(2)}) collective-permute-start(bf16[2,2,96,768]{3,2,1,0:T(8,128)(2,1)S(1)} %add_to_send.10.refs_5_), channel_id=1, source_target_pairs={{1,2},{18,17},{5,6},{22,21},{9,10},{26,25},{13,14},{30,29}} | collective-permute-start | bytes 1769480 | tf_op jit(solution)/shard_map/ppermute | solution.py:342
  27.4 14.8 %collective-permute-start.8 = (bf16[2,2,96,768]{3,2,1,0:T(8,128)(2,1)S(1)}, bf16[2,2,96,768]{3,2,1,0:T(8,128)(2,1)S(1)}, u32[]{:S(2)}, u32[]{:S(2)}) collective-permute-start(bf16[2,2,96,768]{3,2,1,0:T(8,128)(2,1)S(1)} %get-tuple-element.43), channel_id=1, source_target_pairs={{0,1},{19,18},{4,5},{23,22},{8,9},{27,26},{12,13},{31,30}} | collective-permute-start | bytes 1769480 | tf_op jit(solution)/shard_map/ppermute | solution.py:342
  35.2 7.9 %collective-permute-start.7 = (bf16[2,2,96,768]{3,2,1,0:T(8,128)(2,1)S(1)}, bf16[2,2,96,768]{3,2,1,0:T(8,128)(2,1)S(1)}, u32[]{:S(2)}, u32[]{:S(2)}) collective-permute-start(bf16[2,2,96,768]{3,2,1,0:T(8,128)(2,1)S(1)} %add_to_send.11.refs_2_), channel_id=1, source_target_pairs={{1,2},{18,17},{5,6},{22,21},{9,10},{26,25},{13,14},{30,29}} | collective-permute-start | bytes 1769480 | tf_op jit(solution)/shard_map/ppermute | solution.py:342
  36.0 10.5 %collective-permute-start.6 = (bf16[2,2,96,768]{3,2,1,0:T(8,128)(2,1)S(1)}, bf16[2,2,96,768]{3,2,1,0:T(8,128)(2,1)S(1)}, u32[]{:S(2)}, u32[]{:S(2)}) collective-permute-start(bf16[2,2,96,768]{3,2,1,0:T(8,128)(2,1)S(1)} %add_to_send.12.refs_5_), channel_id=1, source_target_pairs={{2,3},{17,16},{6,7},{21,20},{10,11},{25,24},{14,15},{29,28}} | collective-permute-start | bytes 1769480 | tf_op jit(solution)/shard_map/ppermute | solution.py:342
  36.7 9.9 %collective-permute-start.5 = (bf16[2,2,96,768]{3,2,1,0:T(8,128)(2,1)S(1)}, bf16[2,2,96,768]{3,2,1,0:T(8,128)(2,1)S(1)}, u32[]{:S(2)}, u32[]{:S(2)}) collective-permute-start(bf16[2,2,96,768]{3,2,1,0:T(8,128)(2,1)S(1)} %get-tuple-element.42), channel_id=1, source_target_pairs={{0,1},{19,18},{4,5},{23,22},{8,9},{27,26},{12,13},{31,30}} | collective-permute-start | bytes 1769480 | tf_op jit(solution)/shard_map/ppermute | solution.py:342
  38.7 45.9 %slice-start = ((s8[25165824]{0:T(1024)(128)(4,1)}), s8[4194304]{0:T(1024)(128)(4,1)S(1)}, s32[]{:S(2)}) async-start(s8[25165824]{0:T(1024)(128)(4,1)} %bitcast.4), calls=%async_computation | async-start | bytes 8388608
  38.7 45.9 %slice-start.1 = ((s8[25165824]{0:T(1024)(128)(4,1)}), s8[4194304]{0:T(1024)(128)(4,1)S(1)}, s32[]{:S(2)}) async-start(s8[25165824]{0:T(1024)(128)(4,1)} %bitcast.4), calls=%async_computation.1 | async-start | bytes 8388608
  38.7 45.9 %slice-start.2 = ((s8[25165824]{0:T(1024)(128)(4,1)}), s8[4194304]{0:T(1024)(128)(4,1)S(1)}, s32[]{:S(2)}) async-start(s8[25165824]{0:T(1024)(128)(4,1)} %bitcast.4), calls=%async_computation.2 | async-start | bytes 8388608
  38.7 45.9 %slice-start.3 = ((s8[25165824]{0:T(1024)(128)(4,1)}), s8[4194304]{0:T(1024)(128)(4,1)S(1)}, s32[]{:S(2)}) async-start(s8[25165824]{0:T(1024)(128)(4,1)} %bitcast.4), calls=%async_computation.3 | async-start | bytes 8388608
  42.3 16.1 %collective-permute-start.12 = (bf16[2,2,96,768]{3,2,1,0:T(8,128)(2,1)S(1)}, bf16[2,2,96,768]{3,2,1,0:T(8,128)(2,1)S(1)}, u32[]{:S(2)}, u32[]{:S(2)}) collective-permute-start(bf16[2,2,96,768]{3,2,1,0:T(8,128)(2,1)S(1)} %add_to_send.13.refs_3_), channel_id=1, source_target_pairs={{1,2},{18,17},{5,6},{22,21},{9,10},{26,25},{13,14},{30,29}} | collective-permute-start | bytes 1769480 | tf_op jit(solution)/shard_map/ppermute | solution.py:342
  43.1 16.0 %collective-permute-start.11 = (bf16[2,2,96,768]{3,2,1,0:T(8,128)(2,1)S(1)}, bf16[2,2,96,768]{3,2,1,0:T(8,128)(2,1)S(1)}, u32[]{:S(2)}, u32[]{:S(2)}) collective-permute-start(bf16[2,2,96,768]{3,2,1,0:T(8,128)(2,1)S(1)} %add_to_send.14.refs_3_), channel_id=1, source_target_pairs={{2,3},{17,16},{6,7},{21,20},{10,11},{25,24},{14,15},{29,28}} | collective-permute-start | bytes 1769480 | tf_op jit(solution)/shard_map/ppermute | solution.py:342
  44.0 9.9 %collective-permute-start.13 = (bf16[2,2,96,512]{3,2,1,0:T(8,128)(2,1)S(1)}, bf16[2,2,96,512]{3,2,1,0:T(8,128)(2,1)S(1)}, u32[]{:S(2)}, u32[]{:S(2)}) collective-permute-start(bf16[2,2,96,512]{3,2,1,0:T(8,128)(2,1)S(1)} %get-tuple-element.44), channel_id=1, source_target_pairs={{0,1},{19,18},{4,5},{23,22},{8,9},{27,26},{12,13},{31,30}} | collective-permute-start | bytes 1179656 | tf_op jit(solution)/shard_map/ppermute | solution.py:342
  46.6 20.1 %collective-permute-start.9 = (bf16[2,2,96,768]{3,2,1,0:T(8,128)(2,1)S(1)}, bf16[2,2,96,768]{3,2,1,0:T(8,128)(2,1)S(1)}, u32[]{:S(2)}, u32[]{:S(2)}) collective-permute-start(bf16[2,2,96,768]{3,2,1,0:T(8,128)(2,1)S(1)} %add_to_send.15.refs_3_), channel_id=1, source_target_pairs={{1,2},{18,17},{5,6},{22,21},{9,10},{26,25},{13,14},{30,29}} | collective-permute-start | bytes 1769480 | tf_op jit(solution)/shard_map/ppermute | solution.py:342
  47.4 12.6 %collective-permute-start.10 = (bf16[2,96,768]{2,1,0:T(8,128)(2,1)S(1)}, bf16[2,96,768]{2,1,0:T(8,128)(2,1)S(1)}, u32[]{:S(2)}, u32[]{:S(2)}) collective-permute-start(bf16[2,96,768]{2,1,0:T(8,128)(2,1)S(1)} %hidden_values.6.refs_3_.refs_4_), channel_id=1, source_target_pairs={{3,2},{16,17},{7,6},{20,21},{11,10},{24,25},{15,14},{28,29}} | collective-permute-start | bytes 884744 | tf_op jit(solution)/shard_map/ppermute | solution.py:342
  53.9 12.1 %collective-permute-start.4 = (bf16[2,2,96,512]{3,2,1,0:T(8,128)(2,1)S(1)}, bf16[2,2,96,512]{3,2,1,0:T(8,128)(2,1)S(1)}, u32[]{:S(2)}, u32[]{:S(2)}) collective-permute-start(bf16[2,2,96,512]{3,2,1,0:T(8,128)(2,1)S(1)} %get-tuple-element.41), channel_id=1, source_target_pairs={{0,1},{19,18},{4,5},{23,22},{8,9},{27,26},{12,13},{31,30}} | collective-permute-start | bytes 1179656 | tf_op jit(solution)/shard_map/ppermute | solution.py:342
  58.4 10.5 %collective-permute-start.21 = (bf16[2,2,96,768]{3,2,1,0:T(8,128)(2,1)S(1)}, bf16[2,2,96,768]{3,2,1,0:T(8,128)(2,1)S(1)}, u32[]{:S(2)}, u32[]{:S(2)}) collective-permute-start(bf16[2,2,96,768]{3,2,1,0:T(8,128)(2,1)S(1)} %add_to_send.17.refs_3_), channel_id=1, source_target_pairs={{2,3},{17,16},{6,7},{21,20},{10,11},{25,24},{14,15},{29,28}} | collective-permute-start | bytes 1769480 | tf_op jit(solution)/shard_map/ppermute | solution.py:342
  59.1 8.3 %collective-permute-start.16 = (bf16[2,96,768]{2,1,0:T(8,128)(2,1)S(1)}, bf16[2,96,768]{2,1,0:T(8,128)(2,1)S(1)}, u32[]{:S(2)}, u32[]{:S(2)}) collective-permute-start(bf16[2,96,768]{2,1,0:T(8,128)(2,1)S(1)} %hidden_values.7.refs_1_.refs_4_), channel_id=1, source_target_pairs={{3,2},{16,17},{7,6},{20,21},{11,10},{24,25},{15,14},{28,29}} | collective-permute-start | bytes 884744 | tf_op jit(solution)/shard_map/ppermute | solution.py:342
  60.0 8.2 %collective-permute-start.15 = (bf16[2,96,768]{2,1,0:T(8,128)(2,1)S(1)}, bf16[2,96,768]{2,1,0:T(8,128)(2,1)S(1)}, u32[]{:S(2)}, u32[]{:S(2)}) collective-permute-start(bf16[2,96,768]{2,1,0:T(8,128)(2,1)S(1)} %pass_on.10.refs_3_), channel_id=1, source_target_pairs={{2,1},{17,18},{6,5},{21,22},{10,9},{25,26},{14,13},{29,30}} | collective-permute-start | bytes 884744 | tf_op jit(solution)/shard_map/ppermute | solution.py:342
  66.0 3.6 %collective-permute-start.20 = (bf16[2,2,96,512]{3,2,1,0:T(8,128)(2,1)S(1)}, bf16[2,2,96,512]{3,2,1,0:T(8,128)(2,1)S(1)}, u32[]{:S(2)}, u32[]{:S(2)}) collective-permute-start(bf16[2,2,96,512]{3,2,1,0:T(8,128)(2,1)S(1)} %round_to_send.2.refs_3_), channel_id=1, source_target_pairs={{3,2},{16,17},{7,6},{20,21},{11,10},{24,25},{15,14},{28,29}} | collective-permute-start | bytes 1179656 | tf_op jit(solution)/shard_map/ppermute | solution.py:342
  66.7 2.9 %collective-permute-start.19 = (bf16[2,2,96,512]{3,2,1,0:T(8,128)(2,1)S(1)}, bf16[2,2,96,512]{3,2,1,0:T(8,128)(2,1)S(1)}, u32[]{:S(2)}, u32[]{:S(2)}) collective-permute-start(bf16[2,2,96,512]{3,2,1,0:T(8,128)(2,1)S(1)} %add_to_send.16.refs_3_), channel_id=1, source_target_pairs={{1,2},{18,17},{5,6},{22,21},{9,10},{26,25},{13,14},{30,29}} | collective-permute-start | bytes 1179656 | tf_op jit(solution)/shard_map/ppermute | solution.py:342
  67.5 6.2 %collective-permute-start.18 = (bf16[2,2,96,768]{3,2,1,0:T(8,128)(2,1)S(1)}, bf16[2,2,96,768]{3,2,1,0:T(8,128)(2,1)S(1)}, u32[]{:S(2)}, u32[]{:S(2)}) collective-permute-start(bf16[2,2,96,768]{3,2,1,0:T(8,128)(2,1)S(1)} %add_to_send.18.refs_3_), channel_id=1, source_target_pairs={{2,3},{17,16},{6,7},{21,20},{10,11},{25,24},{14,15},{29,28}} | collective-permute-start | bytes 1769480 | tf_op jit(solution)/shard_map/ppermute | solution.py:342
  68.2 3.4 %collective-permute-start.24 = (bf16[2,96,768]{2,1,0:T(8,128)(2,1)S(1)}, bf16[2,96,768]{2,1,0:T(8,128)(2,1)S(1)}, u32[]{:S(2)}, u32[]{:S(2)}) collective-permute-start(bf16[2,96,768]{2,1,0:T(8,128)(2,1)S(1)} %pass_on.11.refs_1_.refs_3_), channel_id=1, source_target_pairs={{2,1},{17,18},{6,5},{21,22},{10,9},{25,26},{14,13},{29,30}} | collective-permute-start | bytes 884744 | tf_op jit(solution)/shard_map/ppermute | solution.py:342
  68.9 2.7 %collective-permute-start.23 = (bf16[2,96,768]{2,1,0:T(8,128)(2,1)S(1)}, bf16[2,96,768]{2,1,0:T(8,128)(2,1)S(1)}, u32[]{:S(2)}, u32[]{:S(2)}) collective-permute-start(bf16[2,96,768]{2,1,0:T(8,128)(2,1)S(1)} %hidden_values.8.refs_4_), channel_id=1, source_target_pairs={{3,2},{16,17},{7,6},{20,21},{11,10},{24,25},{15,14},{28,29}} | collective-permute-start | bytes 884744 | tf_op jit(solution)/shard_map/ppermute | solution.py:342
  69.7 4.0 %collective-permute-start.22 = (bf16[2,96,512]{2,1,0:T(8,128)(2,1)S(1)}, bf16[2,96,512]{2,1,0:T(8,128)(2,1)S(1)}, u32[]{:S(2)}, u32[]{:S(2)}) collective-permute-start(bf16[2,96,512]{2,1,0:T(8,128)(2,1)S(1)} %hidden_values.9.refs_1_.refs_3_), channel_id=1, source_target_pairs={{2,1},{17,18},{6,5},{21,22},{10,9},{25,26},{14,13},{29,30}} | collective-permute-start | bytes 589832 | tf_op jit(solution)/shard_map/ppermute | solution.py:342
  70.3 14.2 %collective-permute-start.17 = (bf16[2,96,768]{2,1,0:T(8,128)(2,1)S(1)}, bf16[2,96,768]{2,1,0:T(8,128)(2,1)S(1)}, u32[]{:S(2)}, u32[]{:S(2)}) collective-permute-start(bf16[2,96,768]{2,1,0:T(8,128)(2,1)S(1)} %pass_on.12.refs_3_.refs_2_), channel_id=1, source_target_pairs={{1,0},{18,19},{5,4},{22,23},{9,8},{26,27},{13,12},{30,31}} | collective-permute-start | bytes 884744 | tf_op jit(solution)/shard_map/ppermute | solution.py:342
  71.7 14.6 %collective-permute-start.26 = (bf16[2,96,768]{2,1,0:T(8,128)(2,1)S(1)}, bf16[2,96,768]{2,1,0:T(8,128)(2,1)S(1)}, u32[]{:S(2)}, u32[]{:S(2)}) collective-permute-start(bf16[2,96,768]{2,1,0:T(8,128)(2,1)S(1)} %pass_on.14.refs_1_.refs_3_), channel_id=1, source_target_pairs={{2,1},{17,18},{6,5},{21,22},{10,9},{25,26},{14,13},{29,30}} | collective-permute-start | bytes 884744 | tf_op jit(solution)/shard_map/ppermute | solution.py:342
  72.4 15.4 %collective-permute-start.28 = (bf16[2,96,768]{2,1,0:T(8,128)(2,1)S(1)}, bf16[2,96,768]{2,1,0:T(8,128)(2,1)S(1)}, u32[]{:S(2)}, u32[]{:S(2)}) collective-permute-start(bf16[2,96,768]{2,1,0:T(8,128)(2,1)S(1)} %pass_on.13.refs_1_.refs_2_), channel_id=1, source_target_pairs={{1,0},{18,19},{5,4},{22,23},{9,8},{26,27},{13,12},{30,31}} | collective-permute-start | bytes 884744 | tf_op jit(solution)/shard_map/ppermute | solution.py:342
  73.7 15.0 %collective-permute-start.29 = (bf16[2,96,768]{2,1,0:T(8,128)(2,1)S(1)}, bf16[2,96,768]{2,1,0:T(8,128)(2,1)S(1)}, u32[]{:S(2)}, u32[]{:S(2)}) collective-permute-start(bf16[2,96,768]{2,1,0:T(8,128)(2,1)S(1)} %hidden_values.10.refs_6_.refs_4_), channel_id=1, source_target_pairs={{3,2},{16,17},{7,6},{20,21},{11,10},{24,25},{15,14},{28,29}} | collective-permute-start | bytes 884744 | tf_op jit(solution)/shard_map/ppermute | solution.py:342
  74.4 26.1 %collective-permute-start.14 = (bf16[2,2,96,512]{3,2,1,0:T(8,128)(2,1)S(1)}, bf16[2,2,96,512]{3,2,1,0:T(8,128)(2,1)S(1)}, u32[]{:S(2)}, u32[]{:S(2)}) collective-permute-start(bf16[2,2,96,512]{3,2,1,0:T(8,128)(2,1)S(1)} %add_to_send.19.refs_1_), channel_id=1, source_target_pairs={{1,2},{18,17},{5,6},{22,21},{9,10},{26,25},{13,14},{30,29}} | collective-permute-start | bytes 1179656 | tf_op jit(solution)/shard_map/ppermute | solution.py:342
  85.6 14.9 %collective-permute-start.25 = (bf16[2,2,96,512]{3,2,1,0:T(8,128)(2,1)S(1)}, bf16[2,2,96,512]{3,2,1,0:T(8,128)(2,1)S(1)}, u32[]{:S(2)}, u32[]{:S(2)}) collective-permute-start(bf16[2,2,96,512]{3,2,1,0:T(8,128)(2,1)S(1)} %round_to_send.3.refs_1_), channel_id=1, source_target_pairs={{3,2},{16,17},{7,6},{20,21},{11,10},{24,25},{15,14},{28,29}} | collective-permute-start | bytes 1179656 | tf_op jit(solution)/shard_map/ppermute | solution.py:342
  86.3 12.0 %collective-permute-start.27 = (bf16[2,96,768]{2,1,0:T(8,128)(2,1)S(1)}, bf16[2,96,768]{2,1,0:T(8,128)(2,1)S(1)}, u32[]{:S(2)}, u32[]{:S(2)}) collective-permute-start(bf16[2,96,768]{2,1,0:T(8,128)(2,1)S(1)} %pass_on.16.refs_8_.refs_2_), channel_id=1, source_target_pairs={{1,0},{18,19},{5,4},{22,23},{9,8},{26,27},{13,12},{30,31}} | collective-permute-start | bytes 884744 | tf_op jit(solution)/shard_map/ppermute | solution.py:342
  88.7 12.5 %collective-permute-start.33 = (bf16[2,96,768]{2,1,0:T(8,128)(2,1)S(1)}, bf16[2,96,768]{2,1,0:T(8,128)(2,1)S(1)}, u32[]{:S(2)}, u32[]{:S(2)}) collective-permute-start(bf16[2,96,768]{2,1,0:T(8,128)(2,1)S(1)} %pass_on.17.refs_8_.refs_3_), channel_id=1, source_target_pairs={{2,1},{17,18},{6,5},{21,22},{10,9},{25,26},{14,13},{29,30}} | collective-permute-start | bytes 884744 | tf_op jit(solution)/shard_map/ppermute | solution.py:342
  89.4 13.8 %collective-permute-start.32 = (bf16[2,96,512]{2,1,0:T(8,128)(2,1)S(1)}, bf16[2,96,512]{2,1,0:T(8,128)(2,1)S(1)}, u32[]{:S(2)}, u32[]{:S(2)}) collective-permute-start(bf16[2,96,512]{2,1,0:T(8,128)(2,1)S(1)} %hidden_values.9.refs_1_.refs_3_), channel_id=1, source_target_pairs={{2,3},{17,16},{6,7},{21,20},{10,11},{25,24},{14,15},{29,28}} | collective-permute-start | bytes 589832 | tf_op jit(solution)/shard_map/ppermute | solution.py:342
  98.3 7.6 %collective-permute-start.31 = (bf16[2,96,512]{2,1,0:T(8,128)(2,1)S(1)}, bf16[2,96,512]{2,1,0:T(8,128)(2,1)S(1)}, u32[]{:S(2)}, u32[]{:S(2)}) collective-permute-start(bf16[2,96,512]{2,1,0:T(8,128)(2,1)S(1)} %pass_on.15.refs_3_.refs_2_), channel_id=1, source_target_pairs={{1,0},{18,19},{5,4},{22,23},{9,8},{26,27},{13,12},{30,31}} | collective-permute-start | bytes 589832 | tf_op jit(solution)/shard_map/ppermute | solution.py:342
  100.5 6.0 %collective-permute-start.30 = (bf16[2,96,512]{2,1,0:T(8,128)(2,1)S(1)}, bf16[2,96,512]{2,1,0:T(8,128)(2,1)S(1)}, u32[]{:S(2)}, u32[]{:S(2)}) collective-permute-start(bf16[2,96,512]{2,1,0:T(8,128)(2,1)S(1)} %hidden_values.11.refs_1_.refs_3_), channel_id=1, source_target_pairs={{2,1},{17,18},{6,5},{21,22},{10,9},{25,26},{14,13},{29,30}} | collective-permute-start | bytes 589832 | tf_op jit(solution)/shard_map/ppermute | solution.py:342
  101.2 9.2 %collective-permute-start.36 = (bf16[2,96,768]{2,1,0:T(8,128)(2,1)S(1)}, bf16[2,96,768]{2,1,0:T(8,128)(2,1)S(1)}, u32[]{:S(2)}, u32[]{:S(2)}) collective-permute-start(bf16[2,96,768]{2,1,0:T(8,128)(2,1)S(1)} %pass_on.18.refs_8_.refs_2_), channel_id=1, source_target_pairs={{1,0},{18,19},{5,4},{22,23},{9,8},{26,27},{13,12},{30,31}} | collective-permute-start | bytes 884744 | tf_op jit(solution)/shard_map/ppermute | solution.py:342
  102.5 8.9 %collective-permute-start.35 = (bf16[2,96,512]{2,1,0:T(8,128)(2,1)S(1)}, bf16[2,96,512]{2,1,0:T(8,128)(2,1)S(1)}, u32[]{:S(2)}, u32[]{:S(2)}) collective-permute-start(bf16[2,96,512]{2,1,0:T(8,128)(2,1)S(1)} %hidden_values.11.refs_1_.refs_3_), channel_id=1, source_target_pairs={{2,3},{17,16},{6,7},{21,20},{10,11},{25,24},{14,15},{29,28}} | collective-permute-start | bytes 589832 | tf_op jit(solution)/shard_map/ppermute | solution.py:342
  106.5 9.1 %collective-permute-start.34 = (bf16[2,96,512]{2,1,0:T(8,128)(2,1)S(1)}, bf16[2,96,512]{2,1,0:T(8,128)(2,1)S(1)}, u32[]{:S(2)}, u32[]{:S(2)}) collective-permute-start(bf16[2,96,512]{2,1,0:T(8,128)(2,1)S(1)} %pass_on.19.refs_8_.refs_2_), channel_id=1, source_target_pairs={{1,0},{18,19},{5,4},{22,23},{9,8},{26,27},{13,12},{30,31}} | collective-permute-start | bytes 589832 | tf_op jit(solution)/shard_map/ppermute | solution.py:342
  116.3 2.1 %collective-permute-start.37 = (f32[2,48,1536]{2,1,0:T(8,128)S(1)}, f32[2,48,1536]{2,1,0:T(8,128)S(1)}, u32[]{:S(2)}, u32[]{:S(2)}) collective-permute-start(f32[2,48,1536]{2,1,0:T(8,128)S(1)} %get-tuple-element.56), channel_id=1, source_target_pairs={{0,16},{16,0},{1,17},{17,1},{2,18},{18,2},{3,19},{19,3},{4,20},{20... | collective-permute-start | bytes 1769480 | tf_op jit(solution)/shard_map/ppermute | solution.py:401
  119.2 4.9 %collective-permute-start.40 = (bf16[32,1536]{1,0:T(8,128)(2,1)S(1)}, bf16[32,1536]{1,0:T(8,128)(2,1)S(1)}, u32[]{:S(2)}, u32[]{:S(2)}) collective-permute-start(bf16[32,1536]{1,0:T(8,128)(2,1)S(1)} %get-tuple-element.60), channel_id=1, source_target_pairs={{0,4},{4,0},{8,12},{12,8},{1,5},{5,1},{9,13},{13,9},{2,6},{6,2},{1... | collective-permute-start | bytes 294920 | tf_op jit(solution)/shard_map/ppermute | solution.py:407
  120.7 5.8 %collective-permute-start.39 = (bf16[32,1536]{1,0:T(8,128)(2,1)S(1)}, bf16[32,1536]{1,0:T(8,128)(2,1)S(1)}, u32[]{:S(2)}, u32[]{:S(2)}) collective-permute-start(bf16[32,1536]{1,0:T(8,128)(2,1)S(1)} %get-tuple-element.59), channel_id=1, source_target_pairs={{0,8},{4,12},{8,0},{12,4},{1,9},{5,13},{9,1},{13,5},{2,10},{6,14},... | collective-permute-start | bytes 294920 | tf_op jit(solution)/shard_map/ppermute | solution.py:407
  122.3 5.5 %collective-permute-start.38 = (bf16[32,1536]{1,0:T(8,128)(2,1)S(1)}, bf16[32,1536]{1,0:T(8,128)(2,1)S(1)}, u32[]{:S(2)}, u32[]{:S(2)}) collective-permute-start(bf16[32,1536]{1,0:T(8,128)(2,1)S(1)} %get-tuple-element.58), channel_id=1, source_target_pairs={{0,12},{4,8},{8,4},{12,0},{1,13},{5,9},{9,5},{13,1},{2,14},{6,10},... | collective-permute-start | bytes 294920 | tf_op jit(solution)/shard_map/ppermute | solution.py:407
  127.8 5.6 %collective-permute-start.41 = (bf16[32,1536]{1,0:T(8,128)(2,1)S(1)}, bf16[32,1536]{1,0:T(8,128)(2,1)S(1)}, u32[]{:S(2)}, u32[]{:S(2)}) collective-permute-start(bf16[32,1536]{1,0:T(8,128)(2,1)S(1)} %add_convert_fusion.refs_1_), channel_id=1, source_target_pairs={{0,4},{4,0},{8,12},{12,8},{1,5},{5,1},{9,13},{13,9},{2,6},{6,2},{1... | collective-permute-start | bytes 294920 | tf_op jit(solution)/shard_map/ppermute | solution.py:411
  128.8 5.0 %collective-permute-start.42 = (bf16[32,1536]{1,0:T(8,128)(2,1)S(1)}, bf16[32,1536]{1,0:T(8,128)(2,1)S(1)}, u32[]{:S(2)}, u32[]{:S(2)}) collective-permute-start(bf16[32,1536]{1,0:T(8,128)(2,1)S(1)} %add_convert_fusion.refs_1_), channel_id=1, source_target_pairs={{0,8},{4,12},{8,0},{12,4},{1,9},{5,13},{9,1},{13,5},{2,10},{6,14},... | collective-permute-start | bytes 294920 | tf_op jit(solution)/shard_map/ppermute | solution.py:411
  129.6 5.5 %collective-permute-start.43 = (bf16[32,1536]{1,0:T(8,128)(2,1)S(1)}, bf16[32,1536]{1,0:T(8,128)(2,1)S(1)}, u32[]{:S(2)}, u32[]{:S(2)}) collective-permute-start(bf16[32,1536]{1,0:T(8,128)(2,1)S(1)} %add_convert_fusion.refs_1_), channel_id=1, source_target_pairs={{0,12},{4,8},{8,4},{12,0},{1,13},{5,9},{9,5},{13,1},{2,14},{6,10},... | collective-permute-start | bytes 294920 | tf_op jit(solution)/shard_map/ppermute | solution.py:411
  (6 other events, 72.5 us)

commit v7 on v5

--- a/solution.py
+++ b/solution.py
@@ -11,7 +11,7 @@
 F32, BF16 = jnp.float32, jnp.bfloat16
 MIB = 1024 * 1024
 
-CHUNKS = ((2, "end"), (4, "end"), (4, "end"), (4, "inner"), (2, "direct"))
+CHUNKS = ((3, "end"), (3, "end"), (3, "end"), (3, "inner"), (2, "inner"), (2, "inner"))
 
 ROUTES = {
     "end": {
@@ -20,27 +20,20 @@
     },
     "inner": {
         "m0": (0, 1, None), "mb": (3, 2, None), "m1": (1, 2, "m0"),
-        "a0": (2, 1, None), "a1": (2, 3, None), "a2": (1, 0, "a0"),
-    },
-    "direct": {
-        "m0": (0, 1, None), "mb": (3, 2, None), "m1": (1, 2, "m0"),
         "a0": (2, 1, None), "a1": (2, 3, None), "a2": (2, 0, None),
     },
 }
-OWNER = {"end": (3, ("m2",)), "inner": (2, ("m1", "mb")), "direct": (2, ("m1", "mb"))}
-HELD = {
-    "end": ("a2", "a1", "a0", None),
-    "inner": ("a2", "a0", None, "a1"),
-    "direct": ("a2", "a0", None, "a1"),
-}
+OWNER = {"end": (3, ("m2",)), "inner": (2, ("m1", "mb"))}
+HELD = {"end": ("a2", "a1", "a0", None), "inner": ("a2", "a0", None, "a1")}
 
 ORDER = (
-    ("g", 0), ("m0", 0), ("g", 2), ("m0", 2), ("m1", 0), ("g", 1), ("m2", 0), ("h", 0),
-    ("m0", 1), ("m1", 2), ("a0", 0), ("g", 3), ("m0", 3), ("m1", 1), ("m2", 2), ("mb", 3),
-    ("a1", 0), ("g", 4), ("m1", 3), ("a2", 0), ("h", 2), ("m0", 4), ("m2", 1), ("d", 0),
-    ("m1", 4), ("a0", 2), ("h", 3), ("a0", 3), ("a1", 3), ("h", 1), ("a0", 1), ("a1", 2),
-    ("a2", 3), ("a1", 1), ("a2", 2), ("d", 3), ("mb", 4), ("a2", 1), ("h", 4), ("a0", 4),
-    ("a2", 4), ("a1", 4), ("d", 2), ("d", 1), ("d", 4),
+    ("g", 0), ("m0", 0), ("g", 2), ("m0", 2), ("g", 1), ("m0", 1), ("m1", 0), ("g", 3),
+    ("m0", 3), ("m1", 2), ("g", 4), ("m0", 4), ("m1", 1), ("m2", 0), ("mb", 3), ("m1", 3),
+    ("m2", 2), ("mb", 4), ("g", 5), ("m0", 5), ("m2", 1), ("h", 0), ("m1", 4), ("h", 3),
+    ("a0", 0), ("a0", 3), ("h", 2), ("a0", 2), ("m1", 5), ("mb", 5), ("a1", 0), ("h", 4),
+    ("a1", 3), ("a2", 3), ("a2", 4), ("a1", 2), ("h", 1), ("a0", 1), ("h", 5), ("a1", 5),
+    ("a1", 4), ("a2", 0), ("a1", 1), ("a2", 2), ("a2", 5), ("a0", 5), ("a0", 4), ("a2", 1),
+    ("d", 3), ("d", 0), ("d", 5), ("d", 2), ("d", 4), ("d", 1),
 )
 
 SMEM = pl.BlockSpec(memory_space=pltpu.SMEM)

time: 145 us -> 130 us (0.90)
  starting transfers between devices: 59.9 us -> 50.9 us
  waiting for transfers between devices: 44.6 us -> 42 us
  Pallas kernels: 34.8 us -> 32.5 us
  local copies, waits for them, and re-layouts: 4.55 us -> 2.75 us
    ppermute x30 -> x36, starting transfers between devices: 52.2 us -> 41.3 us  [hop(): return lax.ppermute(value, ('dp', 'blk'), pairs)]
    ppermute x30 -> x36, waiting for transfers between devices: 32.8 us -> 29.9 us  [hop(): return lax.ppermute(value, ('dp', 'blk'), pairs)]
    pallas_call x35 -> x39, Pallas kernels: 34.8 us -> 32.5 us  [call(): pl.pallas_call(body, out_shape=outs, in_specs=list(specs) + [ANY] * len(a...]
    ppermute x1, starting transfers between devices: 0.07 us -> 1.91 us  [local(): sums = [totals[0], lax.ppermute(totals[1], 'dp', swap)]]
    unnamed x24, local copies, waits for them, and re-layouts: 4.55 us -> 2.75 us
  transfers between devices with their start and end apart: 38 -> 44, of which waited for: 15 -> 13; matrix products, arithmetic and copies ran while one was open for 0% -> 0% of each run, Pallas kernels for 20% -> 20%
where the time goes in v7:
time: 130 us; the launch traced here: 129 us
  starting transfers between devices  50.9 us (39%)
  waiting for transfers between devices  42 us (32%)
  Pallas kernels  32.5 us (25%)
  local copies, waits for them, and re-layouts  2.75 us (2%)
    ppermute x36, starting transfers between devices, hop(): return lax.ppermute(value, ('dp', 'blk'), pairs)  41.3 us
    pallas_call x39, Pallas kernels, call(): pl.pallas_call(body, out_shape=outs, in_specs=list(specs) + [ANY] * len(a...  32.5 us
    ppermute x36, waiting for transfers between devices, hop(): return lax.ppermute(value, ('dp', 'blk'), pairs)  29.9 us
    ppermute x3, waiting for transfers between devices, local(): own = own + lax.ppermute(sent[step - 1], 'expert', exchange).astype(F32)  4.64 us
    ppermute x3, waiting for transfers between devices, local(): lax.ppermute(block, 'expert', [(i, i ^ step) for i in range(groups)])  4.62 us
    ppermute x3, starting transfers between devices, local(): own = own + lax.ppermute(sent[step - 1], 'expert', exchange).astype(F32)  3.57 us
    ppermute x3, starting transfers between devices, local(): lax.ppermute(block, 'expert', [(i, i ^ step) for i in range(groups)])  3.55 us
    unnamed x24, local copies, waits for them, and re-layouts  2.75 us
  transfers between devices with their start and end apart: 44, of which 13 were waited for; matrix products, arithmetic and copies ran while one was open for 0% of the time, Pallas kernels for 20%

profile of v7, /device:TPU:0, one launch (start us, length us, event | category | flops | bytes accessed | tf_op | source)
XLA Modules:
  0.0 129.0 jit_solution(5163767478792924886)
XLA Ops:
  0.0 1.0 copy-done
  2.6 1.2 collective-permute-done.refs_2_
  3.8 4.4 %gate_up.6 = (f32[2,2,96,768]{3,2,1,0:T(8,128)S(1)}, bf16[2,2,96,768]{3,2,1,0:T(8,128)(2,1)S(1)}) custom-call(s32[1]{0:T(128)} %bitcast.3.refs_0_, bf16[2,48,1536]{2,1,0:T(8,128)(2,1)S(1)} %pick.1.refs_1_, bf16[2,48,1536]{2,1,0:T(8,128)(2,1)S(1)} %collective-permute-done.refs_2_, bf16[2,1536,4096]{2,1,0:T(8,128)(2,1)} %refs_3_.11, ...), custom_call_target="tpu_custom_call" | custom-call | tf_op jit(solution)/shard_map/gate_up/pallas_call | solution.py:51
  8.2 4.9 %collective-permute-start.3 = (bf16[2,2,96,768]{3,2,1,0:T(8,128)(2,1)S(1)}, bf16[2,2,96,768]{3,2,1,0:T(8,128)(2,1)S(1)}, u32[]{:S(2)}, u32[]{:S(2)}) collective-permute-start(bf16[2,2,96,768]{3,2,1,0:T(8,128)(2,1)S(1)} %get-tuple-element.38), channel_id=1, source_target_pairs={{0,1},{19,18},{4,5},{23,22},{8,9},{27,26},{12,13},{31,30}} | collective-permute-start | bytes 1769480 | tf_op jit(solution)/shard_map/ppermute | solution.py:340
  13.1 4.5 %gate_up.7 = (f32[2,2,96,768]{3,2,1,0:T(8,128)S(1)}, bf16[2,2,96,768]{3,2,1,0:T(8,128)(2,1)S(1)}) custom-call(s32[1]{0:T(128)} %bitcast.3.refs_0_, bf16[2,48,1536]{2,1,0:T(8,128)(2,1)S(1)} %pick.1.refs_1_, bf16[2,48,1536]{2,1,0:T(8,128)(2,1)S(1)} %collective-permute-done.refs_2_, bf16[2,1536,4096]{2,1,0:T(8,128)(2,1)} %refs_3_.11, ...), custom_call_target="tpu_custom_call" | custom-call | tf_op jit(solution)/shard_map/gate_up/pallas_call | solution.py:51
  17.6 1.3 %collective-permute-start.2 = (bf16[2,2,96,768]{3,2,1,0:T(8,128)(2,1)S(1)}, bf16[2,2,96,768]{3,2,1,0:T(8,128)(2,1)S(1)}, u32[]{:S(2)}, u32[]{:S(2)}) collective-permute-start(bf16[2,2,96,768]{3,2,1,0:T(8,128)(2,1)S(1)} %get-tuple-element.37), channel_id=1, source_target_pairs={{0,1},{19,18},{4,5},{23,22},{8,9},{27,26},{12,13},{31,30}} | collective-permute-start | bytes 1769480 | tf_op jit(solution)/shard_map/ppermute | solution.py:340
  18.9 4.4 %gate_up.8 = (f32[2,2,96,768]{3,2,1,0:T(8,128)S(1)}, bf16[2,2,96,768]{3,2,1,0:T(8,128)(2,1)S(1)}) custom-call(s32[1]{0:T(128)} %bitcast.3.refs_0_, bf16[2,48,1536]{2,1,0:T(8,128)(2,1)S(1)} %pick.1.refs_1_, bf16[2,48,1536]{2,1,0:T(8,128)(2,1)S(1)} %collective-permute-done.refs_2_, bf16[2,1536,4096]{2,1,0:T(8,128)(2,1)} %refs_3_.11, ...), custom_call_target="tpu_custom_call" | custom-call | tf_op jit(solution)/shard_map/gate_up/pallas_call | solution.py:51
  23.3 1.3 %collective-permute-start.1 = (bf16[2,2,96,768]{3,2,1,0:T(8,128)(2,1)S(1)}, bf16[2,2,96,768]{3,2,1,0:T(8,128)(2,1)S(1)}, u32[]{:S(2)}, u32[]{:S(2)}) collective-permute-start(bf16[2,2,96,768]{3,2,1,0:T(8,128)(2,1)S(1)} %get-tuple-element.36), channel_id=1, source_target_pairs={{0,1},{19,18},{4,5},{23,22},{8,9},{27,26},{12,13},{31,30}} | collective-permute-start | bytes 1769480 | tf_op jit(solution)/shard_map/ppermute | solution.py:340
  25.4 4.4 %gate_up.9 = (f32[2,2,96,768]{3,2,1,0:T(8,128)S(1)}, bf16[2,2,96,768]{3,2,1,0:T(8,128)(2,1)S(1)}) custom-call(s32[1]{0:T(128)} %bitcast.3.refs_0_, bf16[2,48,1536]{2,1,0:T(8,128)(2,1)S(1)} %pick.1.refs_1_, bf16[2,48,1536]{2,1,0:T(8,128)(2,1)S(1)} %collective-permute-done.refs_2_, bf16[2,1536,4096]{2,1,0:T(8,128)(2,1)} %refs_3_.11, ...), custom_call_target="tpu_custom_call" | custom-call | tf_op jit(solution)/shard_map/gate_up/pallas_call | solution.py:51
  29.9 2.2 %collective-permute-start.6 = (bf16[2,2,96,768]{3,2,1,0:T(8,128)(2,1)S(1)}, bf16[2,2,96,768]{3,2,1,0:T(8,128)(2,1)S(1)}, u32[]{:S(2)}, u32[]{:S(2)}) collective-permute-start(bf16[2,2,96,768]{3,2,1,0:T(8,128)(2,1)S(1)} %get-tuple-element.41), channel_id=1, source_target_pairs={{0,1},{19,18},{4,5},{23,22},{8,9},{27,26},{12,13},{31,30}} | collective-permute-start | bytes 1769480 | tf_op jit(solution)/shard_map/ppermute | solution.py:340
  32.8 3.3 %gate_up.10 = (f32[2,2,96,512]{3,2,1,0:T(8,128)S(1)}, bf16[2,2,96,512]{3,2,1,0:T(8,128)(2,1)S(1)}) custom-call(s32[1]{0:T(128)} %bitcast.3.refs_0_, bf16[2,48,1536]{2,1,0:T(8,128)(2,1)S(1)} %pick.1.refs_1_, bf16[2,48,1536]{2,1,0:T(8,128)(2,1)S(1)} %collective-permute-done.refs_2_, bf16[2,1536,4096]{2,1,0:T(8,128)(2,1)} %refs_3_.11, ...), custom_call_target="tpu_custom_call" | custom-call | tf_op jit(solution)/shard_map/gate_up/pallas_call | solution.py:51
  36.2 2.0 %collective-permute-start.12 = (bf16[2,2,96,512]{3,2,1,0:T(8,128)(2,1)S(1)}, bf16[2,2,96,512]{3,2,1,0:T(8,128)(2,1)S(1)}, u32[]{:S(2)}, u32[]{:S(2)}) collective-permute-start(bf16[2,2,96,512]{3,2,1,0:T(8,128)(2,1)S(1)} %get-tuple-element.43), channel_id=1, source_target_pairs={{0,1},{19,18},{4,5},{23,22},{8,9},{27,26},{12,13},{31,30}} | collective-permute-start | bytes 1179656 | tf_op jit(solution)/shard_map/ppermute | solution.py:340
  41.1 2.5 %collective-permute-done.12.refs_2_ = bf16[2,2,96,512]{3,2,1,0:T(8,128)(2,1)S(1)} collective-permute-done((bf16[2,2,96,512]{3,2,1,0:T(8,128)(2,1)S(1)}, bf16[2,2,96,512]{3,2,1,0:T(8,128)(2,1)S(1)}, u32[]{:S(2)}, u32[]{:S(2)}) %collective-permute-start.12) | collective-permute-done | bytes 393248 | tf_op jit(solution)/shard_map/ppermute | solution.py:340
  43.7 0.8 copy-done.1
  45.2 4.2 %gate_up.11 = (f32[2,2,96,512]{3,2,1,0:T(8,128)S(1)}, bf16[2,2,96,512]{3,2,1,0:T(8,128)(2,1)}) custom-call(s32[1]{0:T(128)} %bitcast.3.refs_0_, bf16[2,48,1536]{2,1,0:T(8,128)(2,1)S(1)} %pick.1.refs_1_, bf16[2,48,1536]{2,1,0:T(8,128)(2,1)S(1)} %collective-permute-done.refs_2_, bf16[2,1536,4096]{2,1,0:T(8,128)(2,1)} %refs_3_.11, ...), custom_call_target="tpu_custom_call" | custom-call | tf_op jit(solution)/shard_map/gate_up/pallas_call | solution.py:51
  49.4 4.7 %collective-permute-start.18 = (bf16[2,2,96,512]{3,2,1,0:T(8,128)(2,1)}, bf16[2,2,96,512]{3,2,1,0:T(8,128)(2,1)S(1)}, u32[]{:S(2)}, u32[]{:S(2)}) collective-permute-start(bf16[2,2,96,512]{3,2,1,0:T(8,128)(2,1)} %get-tuple-element.44), channel_id=1, source_target_pairs={{0,1},{19,18},{4,5},{23,22},{8,9},{27,26},{12,13},{31,30}} | collective-permute-start | bytes 1179656 | tf_op jit(solution)/shard_map/ppermute | solution.py:340
  54.9 0.8 collective-permute-start.8
  56.0 0.8 collective-permute-start.17
  56.8 0.9 collective-permute-start.15
  57.7 6.2 %collective-permute-done.18.refs_2_ = bf16[2,2,96,512]{3,2,1,0:T(8,128)(2,1)S(1)} collective-permute-done((bf16[2,2,96,512]{3,2,1,0:T(8,128)(2,1)}, bf16[2,2,96,512]{3,2,1,0:T(8,128)(2,1)S(1)}, u32[]{:S(2)}, u32[]{:S(2)}) %collective-permute-start.18) | collective-permute-done | bytes 393248 | tf_op jit(solution)/shard_map/ppermute | solution.py:340
  64.6 0.8 collective-permute-start.22
  65.5 0.8 collective-permute-start.21
  67.8 1.3 %collective-permute-start.34 = (bf16[2,96,768]{2,1,0:T(8,128)(2,1)S(1)}, bf16[2,96,768]{2,1,0:T(8,128)(2,1)S(1)}, u32[]{:S(2)}, u32[]{:S(2)}) collective-permute-start(bf16[2,96,768]{2,1,0:T(8,128)(2,1)S(1)} %hidden_values.7.refs_3_), channel_id=1, source_target_pairs={{2,0},{17,19},{6,4},{21,23},{10,8},{25,27},{14,12},{29,31}} | collective-permute-start | bytes 884744 | tf_op jit(solution)/shard_map/ppermute | solution.py:340
  71.9 11.6 %collective-permute-done.34.refs_1_ = bf16[2,96,768]{2,1,0:T(8,128)(2,1)S(1)} collective-permute-done((bf16[2,96,768]{2,1,0:T(8,128)(2,1)S(1)}, bf16[2,96,768]{2,1,0:T(8,128)(2,1)S(1)}, u32[]{:S(2)}, u32[]{:S(2)}) %collective-permute-start.34) | collective-permute-done | bytes 294944 | tf_op jit(solution)/shard_map/ppermute | solution.py:340
  83.5 1.3 collective-permute-start.33
  84.8 1.3 %collective-permute-start.30 = (bf16[2,96,512]{2,1,0:T(8,128)(2,1)S(1)}, bf16[2,96,512]{2,1,0:T(8,128)(2,1)S(1)}, u32[]{:S(2)}, u32[]{:S(2)}) collective-permute-start(bf16[2,96,512]{2,1,0:T(8,128)(2,1)S(1)} %hidden_values.11.refs_1_.refs_3_), channel_id=1, source_target_pairs={{2,0},{17,19},{6,4},{21,23},{10,8},{25,27},{14,12},{29,31}} | collective-permute-start | bytes 589832 | tf_op jit(solution)/shard_map/ppermute | solution.py:340
  87.5 1.3 %collective-permute-start.29 = (bf16[2,96,768]{2,1,0:T(8,128)(2,1)S(1)}, bf16[2,96,768]{2,1,0:T(8,128)(2,1)S(1)}, u32[]{:S(2)}, u32[]{:S(2)}) collective-permute-start(bf16[2,96,768]{2,1,0:T(8,128)(2,1)S(1)} %pass_on.10.refs_1_.refs_2_), channel_id=1, source_target_pairs={{1,0},{18,19},{5,4},{22,23},{9,8},{26,27},{13,12},{30,31}} | collective-permute-start | bytes 884744 | tf_op jit(solution)/shard_map/ppermute | solution.py:340
  88.8 6.3 %collective-permute-done.30.refs_1_ = bf16[2,96,512]{2,1,0:T(8,128)(2,1)S(1)} collective-permute-done((bf16[2,96,512]{2,1,0:T(8,128)(2,1)S(1)}, bf16[2,96,512]{2,1,0:T(8,128)(2,1)S(1)}, u32[]{:S(2)}, u32[]{:S(2)}) %collective-permute-start.30) | collective-permute-done | bytes 196640 | tf_op jit(solution)/shard_map/ppermute | solution.py:340
  95.1 1.3 collective-permute-start.25
  96.4 1.3 %collective-permute-start.26 = (bf16[2,96,512]{2,1,0:T(8,128)(2,1)S(1)}, bf16[2,96,512]{2,1,0:T(8,128)(2,1)S(1)}, u32[]{:S(2)}, u32[]{:S(2)}) collective-permute-start(bf16[2,96,512]{2,1,0:T(8,128)(2,1)S(1)} %hidden_values.9.refs_1_.refs_3_), channel_id=1, source_target_pairs={{2,0},{17,19},{6,4},{21,23},{10,8},{25,27},{14,12},{29,31}} | collective-permute-start | bytes 589832 | tf_op jit(solution)/shard_map/ppermute | solution.py:340
  99.1 0.9 down.6
  100.1 0.9 down.7
  101.7 0.9 down.9
  102.6 2.3 %collective-permute-done.26.refs_1_ = bf16[2,96,512]{2,1,0:T(8,128)(2,1)S(1)} collective-permute-done((bf16[2,96,512]{2,1,0:T(8,128)(2,1)S(1)}, bf16[2,96,512]{2,1,0:T(8,128)(2,1)S(1)}, u32[]{:S(2)}, u32[]{:S(2)}) %collective-permute-start.26) | collective-permute-done | bytes 196640 | tf_op jit(solution)/shard_map/ppermute | solution.py:340
  105.7 0.9 collective-permute-done.25.refs_1_
  106.6 0.9 down.11
  107.5 1.9 %collective-permute-start.37 = (f32[2,48,1536]{2,1,0:T(8,128)S(1)}, f32[2,48,1536]{2,1,0:T(8,128)S(1)}, u32[]{:S(2)}, u32[]{:S(2)}) collective-permute-start(f32[2,48,1536]{2,1,0:T(8,128)S(1)} %get-tuple-element.56), channel_id=1, source_target_pairs={{0,16},{16,0},{1,17},{17,1},{2,18},{18,2},{3,19},{19,3},{4,20},{20... | collective-permute-start | bytes 1769480 | tf_op jit(solution)/shard_map/ppermute | solution.py:388
  109.4 1.6 %collective-permute-done.37.refs_4_ = f32[2,48,1536]{2,1,0:T(8,128)S(1)} collective-permute-done((f32[2,48,1536]{2,1,0:T(8,128)S(1)}, f32[2,48,1536]{2,1,0:T(8,128)S(1)}, u32[]{:S(2)}, u32[]{:S(2)}) %collective-permute-start.37) | collective-permute-done | bytes 589856 | tf_op jit(solution)/shard_map/ppermute | solution.py:388
  111.1 0.7 combine.1
  111.8 2.5 %collective-permute-start.38 = (bf16[32,1536]{1,0:T(8,128)(2,1)S(1)}, bf16[32,1536]{1,0:T(8,128)(2,1)S(1)}, u32[]{:S(2)}, u32[]{:S(2)}) collective-permute-start(bf16[32,1536]{1,0:T(8,128)(2,1)S(1)} %get-tuple-element.58), channel_id=1, source_target_pairs={{0,12},{4,8},{8,4},{12,0},{1,13},{5,9},{9,5},{13,1},{2,14},{6,10},... | collective-permute-start | bytes 294920 | tf_op jit(solution)/shard_map/ppermute | solution.py:394
  115.4 2.6 %collective-permute-done.38 = bf16[32,1536]{1,0:T(8,128)(2,1)S(1)} collective-permute-done((bf16[32,1536]{1,0:T(8,128)(2,1)S(1)}, bf16[32,1536]{1,0:T(8,128)(2,1)S(1)}, u32[]{:S(2)}, u32[]{:S(2)}) %collective-permute-start.38) | collective-permute-done | bytes 98336 | tf_op jit(solution)/shard_map/ppermute | solution.py:394
  118.0 2.0 %collective-permute-done.39 = bf16[32,1536]{1,0:T(8,128)(2,1)S(1)} collective-permute-done((bf16[32,1536]{1,0:T(8,128)(2,1)S(1)}, bf16[32,1536]{1,0:T(8,128)(2,1)S(1)}, u32[]{:S(2)}, u32[]{:S(2)}) %collective-permute-start.39) | collective-permute-done | bytes 98336 | tf_op jit(solution)/shard_map/ppermute | solution.py:394
  120.1 1.6 %collective-permute-start.41 = (bf16[32,1536]{1,0:T(8,128)(2,1)S(1)}, bf16[32,1536]{1,0:T(8,128)(2,1)S(1)}, u32[]{:S(2)}, u32[]{:S(2)}) collective-permute-start(bf16[32,1536]{1,0:T(8,128)(2,1)S(1)} %add_convert_fusion.refs_1_), channel_id=1, source_target_pairs={{0,4},{4,0},{8,12},{12,8},{1,5},{5,1},{9,13},{13,9},{2,6},{6,2},{1... | collective-permute-start | bytes 294920 | tf_op jit(solution)/shard_map/ppermute | solution.py:398
  121.7 0.7 collective-permute-start.42
  122.4 1.2 collective-permute-start.43
  123.6 1.2 collective-permute-done.41.refs_2_
  124.8 3.4 %collective-permute-done.42.refs_3_ = bf16[32,1536]{1,0:T(8,128)(2,1)S(1)} collective-permute-done((bf16[32,1536]{1,0:T(8,128)(2,1)S(1)}, bf16[32,1536]{1,0:T(8,128)(2,1)S(1)}, u32[]{:S(2)}, u32[]{:S(2)}) %collective-permute-start.42) | collective-permute-done | bytes 98336 | tf_op jit(solution)/shard_map/ppermute | solution.py:398
  128.3 0.8 place_blocks.1
  (105 shorter events, 17.6 us)
Async XLA Ops:
  2.0 1.7 %collective-permute-start = (bf16[2,48,1536]{2,1,0:T(8,128)(2,1)S(1)}, bf16[2,48,1536]{2,1,0:T(8,128)(2,1)S(1)}, u32[]{:S(2)}, u32[]{:S(2)}) collective-permute-start(bf16[2,48,1536]{2,1,0:T(8,128)(2,1)S(1)} %pick.1.refs_1_), channel_id=1, source_target_pairs={{0,16},{16,0},{1,17},{17,1},{2,18},{18,2},{3,19},{19,3},{4,20},{20... | collective-permute-start | bytes 884744 | tf_op jit(solution)/shard_map/ppermute | solution.py:344
  8.2 16.5 %collective-permute-start.3 = (bf16[2,2,96,768]{3,2,1,0:T(8,128)(2,1)S(1)}, bf16[2,2,96,768]{3,2,1,0:T(8,128)(2,1)S(1)}, u32[]{:S(2)}, u32[]{:S(2)}) collective-permute-start(bf16[2,2,96,768]{3,2,1,0:T(8,128)(2,1)S(1)} %get-tuple-element.38), channel_id=1, source_target_pairs={{0,1},{19,18},{4,5},{23,22},{8,9},{27,26},{12,13},{31,30}} | collective-permute-start | bytes 1769480 | tf_op jit(solution)/shard_map/ppermute | solution.py:340
  17.6 14.5 %collective-permute-start.2 = (bf16[2,2,96,768]{3,2,1,0:T(8,128)(2,1)S(1)}, bf16[2,2,96,768]{3,2,1,0:T(8,128)(2,1)S(1)}, u32[]{:S(2)}, u32[]{:S(2)}) collective-permute-start(bf16[2,2,96,768]{3,2,1,0:T(8,128)(2,1)S(1)} %get-tuple-element.37), channel_id=1, source_target_pairs={{0,1},{19,18},{4,5},{23,22},{8,9},{27,26},{12,13},{31,30}} | collective-permute-start | bytes 1769480 | tf_op jit(solution)/shard_map/ppermute | solution.py:340
  23.3 14.8 %collective-permute-start.1 = (bf16[2,2,96,768]{3,2,1,0:T(8,128)(2,1)S(1)}, bf16[2,2,96,768]{3,2,1,0:T(8,128)(2,1)S(1)}, u32[]{:S(2)}, u32[]{:S(2)}) collective-permute-start(bf16[2,2,96,768]{3,2,1,0:T(8,128)(2,1)S(1)} %get-tuple-element.36), channel_id=1, source_target_pairs={{0,1},{19,18},{4,5},{23,22},{8,9},{27,26},{12,13},{31,30}} | collective-permute-start | bytes 1769480 | tf_op jit(solution)/shard_map/ppermute | solution.py:340
  24.7 14.2 %collective-permute-start.7 = (bf16[2,2,96,768]{3,2,1,0:T(8,128)(2,1)S(1)}, bf16[2,2,96,768]{3,2,1,0:T(8,128)(2,1)S(1)}, u32[]{:S(2)}, u32[]{:S(2)}) collective-permute-start(bf16[2,2,96,768]{3,2,1,0:T(8,128)(2,1)S(1)} %add_to_send.9.refs_5_), channel_id=1, source_target_pairs={{1,2},{18,17},{5,6},{22,21},{9,10},{26,25},{13,14},{30,29}} | collective-permute-start | bytes 1769480 | tf_op jit(solution)/shard_map/ppermute | solution.py:340
  29.9 9.8 %collective-permute-start.6 = (bf16[2,2,96,768]{3,2,1,0:T(8,128)(2,1)S(1)}, bf16[2,2,96,768]{3,2,1,0:T(8,128)(2,1)S(1)}, u32[]{:S(2)}, u32[]{:S(2)}) collective-permute-start(bf16[2,2,96,768]{3,2,1,0:T(8,128)(2,1)S(1)} %get-tuple-element.41), channel_id=1, source_target_pairs={{0,1},{19,18},{4,5},{23,22},{8,9},{27,26},{12,13},{31,30}} | collective-permute-start | bytes 1769480 | tf_op jit(solution)/shard_map/ppermute | solution.py:340
  32.1 8.3 %collective-permute-start.5 = (bf16[2,2,96,768]{3,2,1,0:T(8,128)(2,1)S(1)}, bf16[2,2,96,768]{3,2,1,0:T(8,128)(2,1)S(1)}, u32[]{:S(2)}, u32[]{:S(2)}) collective-permute-start(bf16[2,2,96,768]{3,2,1,0:T(8,128)(2,1)S(1)} %add_to_send.10.refs_5_), channel_id=1, source_target_pairs={{1,2},{18,17},{5,6},{22,21},{9,10},{26,25},{13,14},{30,29}} | collective-permute-start | bytes 1769480 | tf_op jit(solution)/shard_map/ppermute | solution.py:340
  36.2 7.5 %collective-permute-start.12 = (bf16[2,2,96,512]{3,2,1,0:T(8,128)(2,1)S(1)}, bf16[2,2,96,512]{3,2,1,0:T(8,128)(2,1)S(1)}, u32[]{:S(2)}, u32[]{:S(2)}) collective-permute-start(bf16[2,2,96,512]{3,2,1,0:T(8,128)(2,1)S(1)} %get-tuple-element.43), channel_id=1, source_target_pairs={{0,1},{19,18},{4,5},{23,22},{8,9},{27,26},{12,13},{31,30}} | collective-permute-start | bytes 1179656 | tf_op jit(solution)/shard_map/ppermute | solution.py:340
  38.2 11.2 %collective-permute-start.4 = (bf16[2,2,96,768]{3,2,1,0:T(8,128)(2,1)S(1)}, bf16[2,2,96,768]{3,2,1,0:T(8,128)(2,1)S(1)}, u32[]{:S(2)}, u32[]{:S(2)}) collective-permute-start(bf16[2,2,96,768]{3,2,1,0:T(8,128)(2,1)S(1)} %add_to_send.11.refs_3_), channel_id=1, source_target_pairs={{1,2},{18,17},{5,6},{22,21},{9,10},{26,25},{13,14},{30,29}} | collective-permute-start | bytes 1769480 | tf_op jit(solution)/shard_map/ppermute | solution.py:340
  38.9 15.2 %collective-permute-start.13 = (bf16[2,2,96,768]{3,2,1,0:T(8,128)(2,1)S(1)}, bf16[2,2,96,768]{3,2,1,0:T(8,128)(2,1)S(1)}, u32[]{:S(2)}, u32[]{:S(2)}) collective-permute-start(bf16[2,2,96,768]{3,2,1,0:T(8,128)(2,1)S(1)} %add_to_send.12.refs_2_), channel_id=1, source_target_pairs={{2,3},{17,16},{6,7},{21,20},{10,11},{25,24},{14,15},{29,28}} | collective-permute-start | bytes 1769480 | tf_op jit(solution)/shard_map/ppermute | solution.py:340
  39.7 15.2 %collective-permute-start.10 = (bf16[2,2,96,768]{3,2,1,0:T(8,128)(2,1)S(1)}, bf16[2,2,96,768]{3,2,1,0:T(8,128)(2,1)S(1)}, u32[]{:S(2)}, u32[]{:S(2)}) collective-permute-start(bf16[2,2,96,768]{3,2,1,0:T(8,128)(2,1)S(1)} %add_to_send.13.refs_3_), channel_id=1, source_target_pairs={{1,2},{18,17},{5,6},{22,21},{9,10},{26,25},{13,14},{30,29}} | collective-permute-start | bytes 1769480 | tf_op jit(solution)/shard_map/ppermute | solution.py:340
  40.4 15.6 %collective-permute-start.11 = (bf16[2,2,96,768]{3,2,1,0:T(8,128)(2,1)S(1)}, bf16[2,2,96,768]{3,2,1,0:T(8,128)(2,1)S(1)}, u32[]{:S(2)}, u32[]{:S(2)}) collective-permute-start(bf16[2,2,96,768]{3,2,1,0:T(8,128)(2,1)S(1)} %round_to_send.3.refs_3_), channel_id=1, source_target_pairs={{3,2},{16,17},{7,6},{20,21},{11,10},{24,25},{15,14},{28,29}} | collective-permute-start | bytes 1769480 | tf_op jit(solution)/shard_map/ppermute | solution.py:340
  44.4 12.4 %collective-permute-start.9 = (bf16[2,2,96,768]{3,2,1,0:T(8,128)(2,1)S(1)}, bf16[2,2,96,768]{3,2,1,0:T(8,128)(2,1)S(1)}, u32[]{:S(2)}, u32[]{:S(2)}) collective-permute-start(bf16[2,2,96,768]{3,2,1,0:T(8,128)(2,1)S(1)} %add_to_send.14.refs_2_), channel_id=1, source_target_pairs={{2,3},{17,16},{6,7},{21,20},{10,11},{25,24},{14,15},{29,28}} | collective-permute-start | bytes 1769480 | tf_op jit(solution)/shard_map/ppermute | solution.py:340
  45.1 53.9 %slice-start = ((s8[25165824]{0:T(1024)(128)(4,1)}), s8[4194304]{0:T(1024)(128)(4,1)S(1)}, s32[]{:S(2)}) async-start(s8[25165824]{0:T(1024)(128)(4,1)} %bitcast.4), calls=%async_computation | async-start | bytes 8388608
  45.1 53.9 %slice-start.1 = ((s8[25165824]{0:T(1024)(128)(4,1)}), s8[4194304]{0:T(1024)(128)(4,1)S(1)}, s32[]{:S(2)}) async-start(s8[25165824]{0:T(1024)(128)(4,1)} %bitcast.4), calls=%async_computation.1 | async-start | bytes 8388608
  45.2 53.9 %slice-start.2 = ((s8[25165824]{0:T(1024)(128)(4,1)}), s8[4194304]{0:T(1024)(128)(4,1)S(1)}, s32[]{:S(2)}) async-start(s8[25165824]{0:T(1024)(128)(4,1)} %bitcast.4), calls=%async_computation.2 | async-start | bytes 8388608
  45.2 53.9 %slice-start.3 = ((s8[25165824]{0:T(1024)(128)(4,1)}), s8[4194304]{0:T(1024)(128)(4,1)S(1)}, s32[]{:S(2)}) async-start(s8[25165824]{0:T(1024)(128)(4,1)} %bitcast.4), calls=%async_computation.3 | async-start | bytes 8388608
  49.4 14.5 %collective-permute-start.18 = (bf16[2,2,96,512]{3,2,1,0:T(8,128)(2,1)}, bf16[2,2,96,512]{3,2,1,0:T(8,128)(2,1)S(1)}, u32[]{:S(2)}, u32[]{:S(2)}) collective-permute-start(bf16[2,2,96,512]{3,2,1,0:T(8,128)(2,1)} %get-tuple-element.44), channel_id=1, source_target_pairs={{0,1},{19,18},{4,5},{23,22},{8,9},{27,26},{12,13},{31,30}} | collective-permute-start | bytes 1179656 | tf_op jit(solution)/shard_map/ppermute | solution.py:340
  54.1 10.5 %collective-permute-start.16 = (bf16[2,2,96,512]{3,2,1,0:T(8,128)(2,1)S(1)}, bf16[2,2,96,512]{3,2,1,0:T(8,128)(2,1)S(1)}, u32[]{:S(2)}, u32[]{:S(2)}) collective-permute-start(bf16[2,2,96,512]{3,2,1,0:T(8,128)(2,1)S(1)} %round_to_send.4.refs_5_), channel_id=1, source_target_pairs={{3,2},{16,17},{7,6},{20,21},{11,10},{24,25},{15,14},{28,29}} | collective-permute-start | bytes 1179656 | tf_op jit(solution)/shard_map/ppermute | solution.py:340
  54.9 12.2 %collective-permute-start.8 = (bf16[2,2,96,768]{3,2,1,0:T(8,128)(2,1)S(1)}, bf16[2,2,96,768]{3,2,1,0:T(8,128)(2,1)S(1)}, u32[]{:S(2)}, u32[]{:S(2)}) collective-permute-start(bf16[2,2,96,768]{3,2,1,0:T(8,128)(2,1)S(1)} %add_to_send.15.refs_3_), channel_id=1, source_target_pairs={{2,3},{17,16},{6,7},{21,20},{10,11},{25,24},{14,15},{29,28}} | collective-permute-start | bytes 1769480 | tf_op jit(solution)/shard_map/ppermute | solution.py:340
  56.0 9.5 %collective-permute-start.17 = (bf16[2,96,768]{2,1,0:T(8,128)(2,1)S(1)}, bf16[2,96,768]{2,1,0:T(8,128)(2,1)S(1)}, u32[]{:S(2)}, u32[]{:S(2)}) collective-permute-start(bf16[2,96,768]{2,1,0:T(8,128)(2,1)S(1)} %hidden_values.6.refs_3_.refs_4_), channel_id=1, source_target_pairs={{3,2},{16,17},{7,6},{20,21},{11,10},{24,25},{15,14},{28,29}} | collective-permute-start | bytes 884744 | tf_op jit(solution)/shard_map/ppermute | solution.py:340
  56.8 9.5 %collective-permute-start.15 = (bf16[2,2,96,512]{3,2,1,0:T(8,128)(2,1)S(1)}, bf16[2,2,96,512]{3,2,1,0:T(8,128)(2,1)S(1)}, u32[]{:S(2)}, u32[]{:S(2)}) collective-permute-start(bf16[2,2,96,512]{3,2,1,0:T(8,128)(2,1)S(1)} %add_to_send.16.refs_4_), channel_id=1, source_target_pairs={{1,2},{18,17},{5,6},{22,21},{9,10},{26,25},{13,14},{30,29}} | collective-permute-start | bytes 1179656 | tf_op jit(solution)/shard_map/ppermute | solution.py:340
  63.9 3.1 %collective-permute-start.14 = (bf16[2,96,768]{2,1,0:T(8,128)(2,1)S(1)}, bf16[2,96,768]{2,1,0:T(8,128)(2,1)S(1)}, u32[]{:S(2)}, u32[]{:S(2)}) collective-permute-start(bf16[2,96,768]{2,1,0:T(8,128)(2,1)S(1)} %hidden_values.8.refs_3_.refs_4_), channel_id=1, source_target_pairs={{3,2},{16,17},{7,6},{20,21},{11,10},{24,25},{15,14},{28,29}} | collective-permute-start | bytes 884744 | tf_op jit(solution)/shard_map/ppermute | solution.py:340
  64.6 4.4 %collective-permute-start.22 = (bf16[2,2,96,512]{3,2,1,0:T(8,128)(2,1)S(1)}, bf16[2,2,96,512]{3,2,1,0:T(8,128)(2,1)S(1)}, u32[]{:S(2)}, u32[]{:S(2)}) collective-permute-start(bf16[2,2,96,512]{3,2,1,0:T(8,128)(2,1)S(1)} %round_to_send.5.refs_1_), channel_id=1, source_target_pairs={{3,2},{16,17},{7,6},{20,21},{11,10},{24,25},{15,14},{28,29}} | collective-permute-start | bytes 1179656 | tf_op jit(solution)/shard_map/ppermute | solution.py:340
  65.5 4.3 %collective-permute-start.21 = (bf16[2,2,96,512]{3,2,1,0:T(8,128)(2,1)S(1)}, bf16[2,2,96,512]{3,2,1,0:T(8,128)(2,1)S(1)}, u32[]{:S(2)}, u32[]{:S(2)}) collective-permute-start(bf16[2,2,96,512]{3,2,1,0:T(8,128)(2,1)S(1)} %add_to_send.17.refs_2_), channel_id=1, source_target_pairs={{1,2},{18,17},{5,6},{22,21},{9,10},{26,25},{13,14},{30,29}} | collective-permute-start | bytes 1179656 | tf_op jit(solution)/shard_map/ppermute | solution.py:340
  66.3 4.1 %collective-permute-start.20 = (bf16[2,96,768]{2,1,0:T(8,128)(2,1)S(1)}, bf16[2,96,768]{2,1,0:T(8,128)(2,1)S(1)}, u32[]{:S(2)}, u32[]{:S(2)}) collective-permute-start(bf16[2,96,768]{2,1,0:T(8,128)(2,1)S(1)} %pass_on.6.refs_4_.refs_3_), channel_id=1, source_target_pairs={{2,1},{17,18},{6,5},{21,22},{10,9},{25,26},{14,13},{29,30}} | collective-permute-start | bytes 884744 | tf_op jit(solution)/shard_map/ppermute | solution.py:340
  67.1 4.1 %collective-permute-start.19 = (bf16[2,96,768]{2,1,0:T(8,128)(2,1)S(1)}, bf16[2,96,768]{2,1,0:T(8,128)(2,1)S(1)}, u32[]{:S(2)}, u32[]{:S(2)}) collective-permute-start(bf16[2,96,768]{2,1,0:T(8,128)(2,1)S(1)} %hidden_values.10.refs_4_), channel_id=1, source_target_pairs={{3,2},{16,17},{7,6},{20,21},{11,10},{24,25},{15,14},{28,29}} | collective-permute-start | bytes 884744 | tf_op jit(solution)/shard_map/ppermute | solution.py:340
  67.8 15.7 %collective-permute-start.34 = (bf16[2,96,768]{2,1,0:T(8,128)(2,1)S(1)}, bf16[2,96,768]{2,1,0:T(8,128)(2,1)S(1)}, u32[]{:S(2)}, u32[]{:S(2)}) collective-permute-start(bf16[2,96,768]{2,1,0:T(8,128)(2,1)S(1)} %hidden_values.7.refs_3_), channel_id=1, source_target_pairs={{2,0},{17,19},{6,4},{21,23},{10,8},{25,27},{14,12},{29,31}} | collective-permute-start | bytes 884744 | tf_op jit(solution)/shard_map/ppermute | solution.py:340
  69.1 15.7 %collective-permute-start.35 = (bf16[2,96,768]{2,1,0:T(8,128)(2,1)S(1)}, bf16[2,96,768]{2,1,0:T(8,128)(2,1)S(1)}, u32[]{:S(2)}, u32[]{:S(2)}) collective-permute-start(bf16[2,96,768]{2,1,0:T(8,128)(2,1)S(1)} %hidden_values.7.refs_3_), channel_id=1, source_target_pairs={{2,1},{17,18},{6,5},{21,22},{10,9},{25,26},{14,13},{29,30}} | collective-permute-start | bytes 884744 | tf_op jit(solution)/shard_map/ppermute | solution.py:340
  69.8 16.3 %collective-permute-start.36 = (bf16[2,96,768]{2,1,0:T(8,128)(2,1)S(1)}, bf16[2,96,768]{2,1,0:T(8,128)(2,1)S(1)}, u32[]{:S(2)}, u32[]{:S(2)}) collective-permute-start(bf16[2,96,768]{2,1,0:T(8,128)(2,1)S(1)} %hidden_values.7.refs_3_), channel_id=1, source_target_pairs={{2,3},{17,16},{6,7},{21,20},{10,11},{25,24},{14,15},{29,28}} | collective-permute-start | bytes 884744 | tf_op jit(solution)/shard_map/ppermute | solution.py:340
  70.5 16.3 %collective-permute-start.24 = (bf16[2,96,768]{2,1,0:T(8,128)(2,1)S(1)}, bf16[2,96,768]{2,1,0:T(8,128)(2,1)S(1)}, u32[]{:S(2)}, u32[]{:S(2)}) collective-permute-start(bf16[2,96,768]{2,1,0:T(8,128)(2,1)S(1)} %pass_on.7.refs_3_), channel_id=1, source_target_pairs={{2,1},{17,18},{6,5},{21,22},{10,9},{25,26},{14,13},{29,30}} | collective-permute-start | bytes 884744 | tf_op jit(solution)/shard_map/ppermute | solution.py:340
  71.2 16.3 %collective-permute-start.23 = (bf16[2,96,768]{2,1,0:T(8,128)(2,1)S(1)}, bf16[2,96,768]{2,1,0:T(8,128)(2,1)S(1)}, u32[]{:S(2)}, u32[]{:S(2)}) collective-permute-start(bf16[2,96,768]{2,1,0:T(8,128)(2,1)S(1)} %pass_on.9.refs_1_.refs_3_), channel_id=1, source_target_pairs={{2,1},{17,18},{6,5},{21,22},{10,9},{25,26},{14,13},{29,30}} | collective-permute-start | bytes 884744 | tf_op jit(solution)/shard_map/ppermute | solution.py:340
  83.5 14.9 %collective-permute-start.33 = (bf16[2,96,768]{2,1,0:T(8,128)(2,1)S(1)}, bf16[2,96,768]{2,1,0:T(8,128)(2,1)S(1)}, u32[]{:S(2)}, u32[]{:S(2)}) collective-permute-start(bf16[2,96,768]{2,1,0:T(8,128)(2,1)S(1)} %pass_on.8.refs_1_.refs_2_), channel_id=1, source_target_pairs={{1,0},{18,19},{5,4},{22,23},{9,8},{26,27},{13,12},{30,31}} | collective-permute-start | bytes 884744 | tf_op jit(solution)/shard_map/ppermute | solution.py:340
  84.8 10.3 %collective-permute-start.30 = (bf16[2,96,512]{2,1,0:T(8,128)(2,1)S(1)}, bf16[2,96,512]{2,1,0:T(8,128)(2,1)S(1)}, u32[]{:S(2)}, u32[]{:S(2)}) collective-permute-start(bf16[2,96,512]{2,1,0:T(8,128)(2,1)S(1)} %hidden_values.11.refs_1_.refs_3_), channel_id=1, source_target_pairs={{2,0},{17,19},{6,4},{21,23},{10,8},{25,27},{14,12},{29,31}} | collective-permute-start | bytes 589832 | tf_op jit(solution)/shard_map/ppermute | solution.py:340
  86.1 10.3 %collective-permute-start.31 = (bf16[2,96,512]{2,1,0:T(8,128)(2,1)S(1)}, bf16[2,96,512]{2,1,0:T(8,128)(2,1)S(1)}, u32[]{:S(2)}, u32[]{:S(2)}) collective-permute-start(bf16[2,96,512]{2,1,0:T(8,128)(2,1)S(1)} %hidden_values.11.refs_1_.refs_3_), channel_id=1, source_target_pairs={{2,1},{17,18},{6,5},{21,22},{10,9},{25,26},{14,13},{29,30}} | collective-permute-start | bytes 589832 | tf_op jit(solution)/shard_map/ppermute | solution.py:340
  86.8 10.9 %collective-permute-start.32 = (bf16[2,96,512]{2,1,0:T(8,128)(2,1)S(1)}, bf16[2,96,512]{2,1,0:T(8,128)(2,1)S(1)}, u32[]{:S(2)}, u32[]{:S(2)}) collective-permute-start(bf16[2,96,512]{2,1,0:T(8,128)(2,1)S(1)} %hidden_values.11.refs_1_.refs_3_), channel_id=1, source_target_pairs={{2,3},{17,16},{6,7},{21,20},{10,11},{25,24},{14,15},{29,28}} | collective-permute-start | bytes 589832 | tf_op jit(solution)/shard_map/ppermute | solution.py:340
  87.5 14.2 %collective-permute-start.29 = (bf16[2,96,768]{2,1,0:T(8,128)(2,1)S(1)}, bf16[2,96,768]{2,1,0:T(8,128)(2,1)S(1)}, u32[]{:S(2)}, u32[]{:S(2)}) collective-permute-start(bf16[2,96,768]{2,1,0:T(8,128)(2,1)S(1)} %pass_on.10.refs_1_.refs_2_), channel_id=1, source_target_pairs={{1,0},{18,19},{5,4},{22,23},{9,8},{26,27},{13,12},{30,31}} | collective-permute-start | bytes 884744 | tf_op jit(solution)/shard_map/ppermute | solution.py:340
  95.1 11.5 %collective-permute-start.25 = (bf16[2,96,768]{2,1,0:T(8,128)(2,1)S(1)}, bf16[2,96,768]{2,1,0:T(8,128)(2,1)S(1)}, u32[]{:S(2)}, u32[]{:S(2)}) collective-permute-start(bf16[2,96,768]{2,1,0:T(8,128)(2,1)S(1)} %pass_on.11.refs_6_.refs_2_), channel_id=1, source_target_pairs={{1,0},{18,19},{5,4},{22,23},{9,8},{26,27},{13,12},{30,31}} | collective-permute-start | bytes 884744 | tf_op jit(solution)/shard_map/ppermute | solution.py:340
  96.4 8.6 %collective-permute-start.26 = (bf16[2,96,512]{2,1,0:T(8,128)(2,1)S(1)}, bf16[2,96,512]{2,1,0:T(8,128)(2,1)S(1)}, u32[]{:S(2)}, u32[]{:S(2)}) collective-permute-start(bf16[2,96,512]{2,1,0:T(8,128)(2,1)S(1)} %hidden_values.9.refs_1_.refs_3_), channel_id=1, source_target_pairs={{2,0},{17,19},{6,4},{21,23},{10,8},{25,27},{14,12},{29,31}} | collective-permute-start | bytes 589832 | tf_op jit(solution)/shard_map/ppermute | solution.py:340
  97.7 7.3 %collective-permute-start.27 = (bf16[2,96,512]{2,1,0:T(8,128)(2,1)S(1)}, bf16[2,96,512]{2,1,0:T(8,128)(2,1)S(1)}, u32[]{:S(2)}, u32[]{:S(2)}) collective-permute-start(bf16[2,96,512]{2,1,0:T(8,128)(2,1)S(1)} %hidden_values.9.refs_1_.refs_3_), channel_id=1, source_target_pairs={{2,1},{17,18},{6,5},{21,22},{10,9},{25,26},{14,13},{29,30}} | collective-permute-start | bytes 589832 | tf_op jit(solution)/shard_map/ppermute | solution.py:340
  98.4 6.6 %collective-permute-start.28 = (bf16[2,96,512]{2,1,0:T(8,128)(2,1)S(1)}, bf16[2,96,512]{2,1,0:T(8,128)(2,1)S(1)}, u32[]{:S(2)}, u32[]{:S(2)}) collective-permute-start(bf16[2,96,512]{2,1,0:T(8,128)(2,1)S(1)} %hidden_values.9.refs_1_.refs_3_), channel_id=1, source_target_pairs={{2,3},{17,16},{6,7},{21,20},{10,11},{25,24},{14,15},{29,28}} | collective-permute-start | bytes 589832 | tf_op jit(solution)/shard_map/ppermute | solution.py:340
  107.5 3.5 %collective-permute-start.37 = (f32[2,48,1536]{2,1,0:T(8,128)S(1)}, f32[2,48,1536]{2,1,0:T(8,128)S(1)}, u32[]{:S(2)}, u32[]{:S(2)}) collective-permute-start(f32[2,48,1536]{2,1,0:T(8,128)S(1)} %get-tuple-element.56), channel_id=1, source_target_pairs={{0,16},{16,0},{1,17},{17,1},{2,18},{18,2},{3,19},{19,3},{4,20},{20... | collective-permute-start | bytes 1769480 | tf_op jit(solution)/shard_map/ppermute | solution.py:388
  111.8 6.1 %collective-permute-start.38 = (bf16[32,1536]{1,0:T(8,128)(2,1)S(1)}, bf16[32,1536]{1,0:T(8,128)(2,1)S(1)}, u32[]{:S(2)}, u32[]{:S(2)}) collective-permute-start(bf16[32,1536]{1,0:T(8,128)(2,1)S(1)} %get-tuple-element.58), channel_id=1, source_target_pairs={{0,12},{4,8},{8,4},{12,0},{1,13},{5,9},{9,5},{13,1},{2,14},{6,10},... | collective-permute-start | bytes 294920 | tf_op jit(solution)/shard_map/ppermute | solution.py:394
  114.4 5.6 %collective-permute-start.39 = (bf16[32,1536]{1,0:T(8,128)(2,1)S(1)}, bf16[32,1536]{1,0:T(8,128)(2,1)S(1)}, u32[]{:S(2)}, u32[]{:S(2)}) collective-permute-start(bf16[32,1536]{1,0:T(8,128)(2,1)S(1)} %get-tuple-element.59), channel_id=1, source_target_pairs={{0,8},{4,12},{8,0},{12,4},{1,9},{5,13},{9,1},{13,5},{2,10},{6,14},... | collective-permute-start | bytes 294920 | tf_op jit(solution)/shard_map/ppermute | solution.py:394
  114.9 5.2 %collective-permute-start.40 = (bf16[32,1536]{1,0:T(8,128)(2,1)S(1)}, bf16[32,1536]{1,0:T(8,128)(2,1)S(1)}, u32[]{:S(2)}, u32[]{:S(2)}) collective-permute-start(bf16[32,1536]{1,0:T(8,128)(2,1)S(1)} %get-tuple-element.60), channel_id=1, source_target_pairs={{0,4},{4,0},{8,12},{12,8},{1,5},{5,1},{9,13},{13,9},{2,6},{6,2},{1... | collective-permute-start | bytes 294920 | tf_op jit(solution)/shard_map/ppermute | solution.py:394
  120.1 4.7 %collective-permute-start.41 = (bf16[32,1536]{1,0:T(8,128)(2,1)S(1)}, bf16[32,1536]{1,0:T(8,128)(2,1)S(1)}, u32[]{:S(2)}, u32[]{:S(2)}) collective-permute-start(bf16[32,1536]{1,0:T(8,128)(2,1)S(1)} %add_convert_fusion.refs_1_), channel_id=1, source_target_pairs={{0,4},{4,0},{8,12},{12,8},{1,5},{5,1},{9,13},{13,9},{2,6},{6,2},{1... | collective-permute-start | bytes 294920 | tf_op jit(solution)/shard_map/ppermute | solution.py:398
  121.7 6.6 %collective-permute-start.42 = (bf16[32,1536]{1,0:T(8,128)(2,1)S(1)}, bf16[32,1536]{1,0:T(8,128)(2,1)S(1)}, u32[]{:S(2)}, u32[]{:S(2)}) collective-permute-start(bf16[32,1536]{1,0:T(8,128)(2,1)S(1)} %add_convert_fusion.refs_1_), channel_id=1, source_target_pairs={{0,8},{4,12},{8,0},{12,4},{1,9},{5,13},{9,1},{13,5},{2,10},{6,14},... | collective-permute-start | bytes 294920 | tf_op jit(solution)/shard_map/ppermute | solution.py:398
  122.4 5.9 %collective-permute-start.43 = (bf16[32,1536]{1,0:T(8,128)(2,1)S(1)}, bf16[32,1536]{1,0:T(8,128)(2,1)S(1)}, u32[]{:S(2)}, u32[]{:S(2)}) collective-permute-start(bf16[32,1536]{1,0:T(8,128)(2,1)S(1)} %add_convert_fusion.refs_1_), channel_id=1, source_target_pairs={{0,12},{4,8},{8,4},{12,0},{1,13},{5,9},{9,5},{13,1},{2,14},{6,10},... | collective-permute-start | bytes 294920 | tf_op jit(solution)/shard_map/ppermute | solution.py:398
  (8 other events, 91.3 us)

commit v8 on v6

--- a/solution.py
+++ b/solution.py
@@ -11,8 +11,8 @@
 F32, BF16 = jnp.float32, jnp.bfloat16
 MIB = 1024 * 1024
 
-CHUNKS = ((3, "end"), (3, "end"), (3, "end"), (3, "end"), (2, "inner"), (2, "inner"))
-GROUPS = {0: ((0,), "relay"), 1: ((1,), "relay"), 2: ((2,), "relay"), 3: ((3,), "relay"), 4: ((4,), "relay"), 5: ((5,), "relay")}
+CHUNKS = ((4, "end"), (4, "end"), (4, "inner"), (4, "inner"))
+GROUPS = {0: ((0,), "relay"), 1: ((1,), "relay"), 2: ((2,), "direct"), 3: ((3,), "direct")}
 
 SUMS = {
     "end": {"m0": (0, 1, None), "m1": (1, 2, "m0"), "m2": (2, 3, "m1")},
@@ -28,13 +28,11 @@
 HELD = {"end": ("a2", "a1", "a0", None), "inner": ("a2", "a0", None, "a1")}
 
 ORDER = (
-    ("g", 0), ("m0", 0), ("g", 4), ("m0", 4), ("g", 2), ("m0", 2), ("m1", 0), ("g", 1),
-    ("m0", 1), ("g", 3), ("m0", 3), ("m1", 2), ("mb", 4), ("m2", 0), ("g", 5), ("m0", 5),
-    ("m1", 1), ("m2", 2), ("h", 0), ("a0", 0), ("m1", 3), ("m1", 4), ("m2", 1), ("h", 2),
-    ("a1", 0), ("m2", 3), ("a0", 2), ("m1", 5), ("a1", 2), ("a2", 0), ("h", 1), ("h", 4),
-    ("a2", 2), ("a0", 4), ("a0", 1), ("a1", 1), ("a2", 4), ("h", 3), ("d", 0), ("a1", 4),
-    ("mb", 5), ("a2", 1), ("d", 2), ("a0", 3), ("a1", 3), ("d", 1), ("h", 5), ("a2", 3),
-    ("d", 4), ("a0", 5), ("a1", 5), ("a2", 5), ("d", 3), ("d", 5),
+    ("g", 0), ("m0", 0), ("g", 1), ("m0", 1), ("g", 3), ("m0", 3), ("m1", 0), ("g", 2),
+    ("m0", 2), ("m1", 1), ("m2", 0), ("mb", 3), ("mb", 2), ("m1", 3), ("m2", 1), ("m1", 2),
+    ("h", 0), ("h", 3), ("h", 1), ("a0", 1), ("h", 2), ("a0", 3), ("a1", 3), ("a2", 3),
+    ("a1", 2), ("d", 3), ("a1", 1), ("a0", 2), ("a2", 2), ("d", 2), ("a0", 0), ("a1", 0),
+    ("a2", 1), ("a2", 0), ("d", 1), ("d", 0),
 )
 
 SMEM = pl.BlockSpec(memory_space=pltpu.SMEM)

time: 137 us -> 130 us (0.949)
  starting transfers between devices: 51.1 us -> 36.1 us
  waiting for transfers between devices: 50.5 us -> 61.6 us
  Pallas kernels: 31.7 us -> 29.4 us
    ppermute x36 -> x24, starting transfers between devices: 43.4 us -> 28.4 us  [hop(): return lax.ppermute(value, ('dp', 'blk'), pairs)]
    ppermute x36 -> x24, waiting for transfers between devices: 38.5 us -> 49.6 us  [hop(): return lax.ppermute(value, ('dp', 'blk'), pairs)]
    pallas_call x43 -> x27, Pallas kernels: 31.7 us -> 29.4 us  [call(): pl.pallas_call(body, out_shape=outs, in_specs=list(specs) + [ANY] * len(a...]
  transfers between devices with their start and end apart: 44 -> 32, of which waited for: 16 -> 13; matrix products, arithmetic and copies ran while one was open for 0% -> 0% of each run, Pallas kernels for 18% -> 16%
where the time goes in v8:
time: 130 us
  waiting for transfers between devices  61.6 us (47%)
  starting transfers between devices  36.1 us (28%)
  Pallas kernels  29.4 us (23%)
  local copies, waits for them, and re-layouts  1.72 us (1%)
    ppermute x24, waiting for transfers between devices, hop(): return lax.ppermute(value, ('dp', 'blk'), pairs)  49.6 us
    pallas_call x27, Pallas kernels, call(): pl.pallas_call(body, out_shape=outs, in_specs=list(specs) + [ANY] * len(a...  29.4 us
    ppermute x24, starting transfers between devices, hop(): return lax.ppermute(value, ('dp', 'blk'), pairs)  28.4 us
    ppermute x3, waiting for transfers between devices, local(): own = own + lax.ppermute(sent[step - 1], 'expert', exchange).astype(F32)  5.04 us
    ppermute x3, waiting for transfers between devices, local(): lax.ppermute(block, 'expert', [(i, i ^ step) for i in range(groups)])  3.77 us
    ppermute x3, starting transfers between devices, local(): own = own + lax.ppermute(sent[step - 1], 'expert', exchange).astype(F32)  3.55 us
    ppermute x3, starting transfers between devices, local(): lax.ppermute(block, 'expert', [(i, i ^ step) for i in range(groups)])  3.55 us
  transfers between devices with their start and end apart: 32, of which 13 were waited for; matrix products, arithmetic and copies ran while one was open for 0% of the time, Pallas kernels for 16%

profile of v8, /device:TPU:0, one launch (start us, length us, event | category | flops | bytes accessed | tf_op | source)
XLA Modules:
  0.0 129.5 jit_solution(6336361921991040835)
XLA Ops:
  0.0 1.0 copy-done
  2.6 1.2 collective-permute-done.refs_2_
  3.8 5.4 %gate_up.4 = (f32[2,2,96,1024]{3,2,1,0:T(8,128)S(1)}, bf16[2,2,96,1024]{3,2,1,0:T(8,128)(2,1)S(1)}) custom-call(s32[1]{0:T(128)} %bitcast.3.refs_0_, bf16[2,48,1536]{2,1,0:T(8,128)(2,1)S(1)} %pick.1.refs_1_, bf16[2,48,1536]{2,1,0:T(8,128)(2,1)S(1)} %collective-permute-done.refs_2_, bf16[2,1536,4096]{2,1,0:T(8,128)(2,1)} %refs_3_.7, ...), custom_call_target="tpu_custom_call" | custom-call | tf_op jit(solution)/shard_map/gate_up/pallas_call | solution.py:50
  9.2 4.9 %collective-permute-start.1 = (bf16[2,2,96,1024]{3,2,1,0:T(8,128)(2,1)S(1)}, bf16[2,2,96,1024]{3,2,1,0:T(8,128)(2,1)S(1)}, u32[]{:S(2)}, u32[]{:S(2)}) collective-permute-start(bf16[2,2,96,1024]{3,2,1,0:T(8,128)(2,1)S(1)} %get-tuple-element.26), channel_id=1, source_target_pairs={{0,1},{19,18},{4,5},{23,22},{8,9},{27,26},{12,13},{31,30}} | collective-permute-start | bytes 2359304 | tf_op jit(solution)/shard_map/ppermute | solution.py:340
  14.1 5.4 %gate_up.5 = (f32[2,2,96,1024]{3,2,1,0:T(8,128)S(1)}, bf16[2,2,96,1024]{3,2,1,0:T(8,128)(2,1)S(1)}) custom-call(s32[1]{0:T(128)} %bitcast.3.refs_0_, bf16[2,48,1536]{2,1,0:T(8,128)(2,1)S(1)} %pick.1.refs_1_, bf16[2,48,1536]{2,1,0:T(8,128)(2,1)S(1)} %collective-permute-done.refs_2_, bf16[2,1536,4096]{2,1,0:T(8,128)(2,1)} %refs_3_.7, ...), custom_call_target="tpu_custom_call" | custom-call | tf_op jit(solution)/shard_map/gate_up/pallas_call | solution.py:50
  19.5 1.3 %collective-permute-start.3 = (bf16[2,2,96,1024]{3,2,1,0:T(8,128)(2,1)S(1)}, bf16[2,2,96,1024]{3,2,1,0:T(8,128)(2,1)S(1)}, u32[]{:S(2)}, u32[]{:S(2)}) collective-permute-start(bf16[2,2,96,1024]{3,2,1,0:T(8,128)(2,1)S(1)} %get-tuple-element.29), channel_id=1, source_target_pairs={{0,1},{19,18},{4,5},{23,22},{8,9},{27,26},{12,13},{31,30}} | collective-permute-start | bytes 2359304 | tf_op jit(solution)/shard_map/ppermute | solution.py:340
  20.8 5.4 %gate_up.6 = (f32[2,2,96,1024]{3,2,1,0:T(8,128)S(1)}, bf16[2,2,96,1024]{3,2,1,0:T(8,128)(2,1)S(1)}) custom-call(s32[1]{0:T(128)} %bitcast.3.refs_0_, bf16[2,48,1536]{2,1,0:T(8,128)(2,1)S(1)} %pick.1.refs_1_, bf16[2,48,1536]{2,1,0:T(8,128)(2,1)S(1)} %collective-permute-done.refs_2_, bf16[2,1536,4096]{2,1,0:T(8,128)(2,1)} %refs_3_.7, ...), custom_call_target="tpu_custom_call" | custom-call | tf_op jit(solution)/shard_map/gate_up/pallas_call | solution.py:50
  26.3 0.7 collective-permute-start.2
  27.0 2.9 %collective-permute-start.7 = (bf16[2,2,96,1024]{3,2,1,0:T(8,128)(2,1)S(1)}, bf16[2,2,96,1024]{3,2,1,0:T(8,128)(2,1)S(1)}, u32[]{:S(2)}, u32[]{:S(2)}) collective-permute-start(bf16[2,2,96,1024]{3,2,1,0:T(8,128)(2,1)S(1)} %get-tuple-element.32), channel_id=1, source_target_pairs={{0,1},{19,18},{4,5},{23,22},{8,9},{27,26},{12,13},{31,30}} | collective-permute-start | bytes 2359304 | tf_op jit(solution)/shard_map/ppermute | solution.py:340
  29.9 6.4 %gate_up.7 = (f32[2,2,96,1024]{3,2,1,0:T(8,128)S(1)}, bf16[2,2,96,1024]{3,2,1,0:T(8,128)(2,1)}) custom-call(s32[1]{0:T(128)} %bitcast.3.refs_0_, bf16[2,48,1536]{2,1,0:T(8,128)(2,1)S(1)} %pick.1.refs_1_, bf16[2,48,1536]{2,1,0:T(8,128)(2,1)S(1)} %collective-permute-done.refs_2_, bf16[2,1536,4096]{2,1,0:T(8,128)(2,1)} %refs_3_.7, ...), custom_call_target="tpu_custom_call" | custom-call | tf_op jit(solution)/shard_map/gate_up/pallas_call | solution.py:50
  36.4 0.8 collective-permute-start.6
  37.2 2.3 %collective-permute-start.5 = (bf16[2,2,96,1024]{3,2,1,0:T(8,128)(2,1)}, bf16[2,2,96,1024]{3,2,1,0:T(8,128)(2,1)S(1)}, u32[]{:S(2)}, u32[]{:S(2)}) collective-permute-start(bf16[2,2,96,1024]{3,2,1,0:T(8,128)(2,1)} %get-tuple-element.31), channel_id=1, source_target_pairs={{0,1},{19,18},{4,5},{23,22},{8,9},{27,26},{12,13},{31,30}} | collective-permute-start | bytes 2359304 | tf_op jit(solution)/shard_map/ppermute | solution.py:340
  39.6 0.8 collective-permute-start.4
  40.5 0.8 collective-permute-start.12
  41.4 0.7 collective-permute-start.13
  42.1 0.8 collective-permute-start.11
  43.0 12.3 %collective-permute-done.5.refs_2_ = bf16[2,2,96,1024]{3,2,1,0:T(8,128)(2,1)S(1)} collective-permute-done((bf16[2,2,96,1024]{3,2,1,0:T(8,128)(2,1)}, bf16[2,2,96,1024]{3,2,1,0:T(8,128)(2,1)S(1)}, u32[]{:S(2)}, u32[]{:S(2)}) %collective-permute-start.5) | collective-permute-done | bytes 786464 | tf_op jit(solution)/shard_map/ppermute | solution.py:340
  55.3 0.7 collective-permute-start.9
  56.0 0.7 collective-permute-start.10
  56.8 1.3 collective-permute-start.17
  58.8 0.7 collective-permute-start.19
  59.5 0.9 collective-permute-start.20
  60.4 1.3 collective-permute-start.14
  61.7 8.4 %collective-permute-done.17.refs_1_ = bf16[2,96,1024]{2,1,0:T(8,128)(2,1)S(1)} collective-permute-done((bf16[2,96,1024]{2,1,0:T(8,128)(2,1)S(1)}, bf16[2,96,1024]{2,1,0:T(8,128)(2,1)S(1)}, u32[]{:S(2)}, u32[]{:S(2)}) %collective-permute-start.17) | collective-permute-done | bytes 393248 | tf_op jit(solution)/shard_map/ppermute | solution.py:340
  70.8 0.7 collective-permute-start.16
  72.3 1.2 down.4
  74.2 11.9 %collective-permute-done.14.refs_1_ = bf16[2,96,1024]{2,1,0:T(8,128)(2,1)S(1)} collective-permute-done((bf16[2,96,1024]{2,1,0:T(8,128)(2,1)S(1)}, bf16[2,96,1024]{2,1,0:T(8,128)(2,1)S(1)}, u32[]{:S(2)}, u32[]{:S(2)}) %collective-permute-start.14) | collective-permute-done | bytes 393248 | tf_op jit(solution)/shard_map/ppermute | solution.py:340
  86.0 1.2 down.5
  87.2 0.7 collective-permute-start.21
  88.0 1.3 collective-permute-start.24
  89.3 1.3 collective-permute-start.23
  90.6 11.4 %collective-permute-done.24.refs_1_ = bf16[2,96,1024]{2,1,0:T(8,128)(2,1)S(1)} collective-permute-done((bf16[2,96,1024]{2,1,0:T(8,128)(2,1)S(1)}, bf16[2,96,1024]{2,1,0:T(8,128)(2,1)S(1)}, u32[]{:S(2)}, u32[]{:S(2)}) %collective-permute-start.24) | collective-permute-done | bytes 393248 | tf_op jit(solution)/shard_map/ppermute | solution.py:340
  102.0 1.2 down.6
  103.2 5.6 %collective-permute-done.23.refs_1_ = bf16[2,96,1024]{2,1,0:T(8,128)(2,1)S(1)} collective-permute-done((bf16[2,96,1024]{2,1,0:T(8,128)(2,1)S(1)}, bf16[2,96,1024]{2,1,0:T(8,128)(2,1)S(1)}, u32[]{:S(2)}, u32[]{:S(2)}) %collective-permute-start.23) | collective-permute-done | bytes 393248 | tf_op jit(solution)/shard_map/ppermute | solution.py:340
  108.8 1.2 down.7
  110.0 2.0 %collective-permute-done.25.refs_4_ = f32[2,48,1536]{2,1,0:T(8,128)S(1)} collective-permute-done((f32[2,48,1536]{2,1,0:T(8,128)S(1)}, f32[2,48,1536]{2,1,0:T(8,128)S(1)}, u32[]{:S(2)}, u32[]{:S(2)}) %collective-permute-start.25) | collective-permute-done | bytes 589856 | tf_op jit(solution)/shard_map/ppermute | solution.py:399
  112.0 0.7 combine.1
  112.8 1.6 %collective-permute-start.28 = (bf16[32,1536]{1,0:T(8,128)(2,1)S(1)}, bf16[32,1536]{1,0:T(8,128)(2,1)S(1)}, u32[]{:S(2)}, u32[]{:S(2)}) collective-permute-start(bf16[32,1536]{1,0:T(8,128)(2,1)S(1)} %get-tuple-element.44), channel_id=1, source_target_pairs={{0,4},{4,0},{8,12},{12,8},{1,5},{5,1},{9,13},{13,9},{2,6},{6,2},{1... | collective-permute-start | bytes 294920 | tf_op jit(solution)/shard_map/ppermute | solution.py:405
  114.4 1.5 %collective-permute-start.27 = (bf16[32,1536]{1,0:T(8,128)(2,1)S(1)}, bf16[32,1536]{1,0:T(8,128)(2,1)S(1)}, u32[]{:S(2)}, u32[]{:S(2)}) collective-permute-start(bf16[32,1536]{1,0:T(8,128)(2,1)S(1)} %get-tuple-element.43), channel_id=1, source_target_pairs={{0,8},{4,12},{8,0},{12,4},{1,9},{5,13},{9,1},{13,5},{2,10},{6,14},... | collective-permute-start | bytes 294920 | tf_op jit(solution)/shard_map/ppermute | solution.py:405
  116.4 1.3 %collective-permute-done.28 = bf16[32,1536]{1,0:T(8,128)(2,1)S(1)} collective-permute-done((bf16[32,1536]{1,0:T(8,128)(2,1)S(1)}, bf16[32,1536]{1,0:T(8,128)(2,1)S(1)}, u32[]{:S(2)}, u32[]{:S(2)}) %collective-permute-start.28) | collective-permute-done | bytes 98336 | tf_op jit(solution)/shard_map/ppermute | solution.py:405
  117.7 2.4 %collective-permute-done.27 = bf16[32,1536]{1,0:T(8,128)(2,1)S(1)} collective-permute-done((bf16[32,1536]{1,0:T(8,128)(2,1)S(1)}, bf16[32,1536]{1,0:T(8,128)(2,1)S(1)}, u32[]{:S(2)}, u32[]{:S(2)}) %collective-permute-start.27) | collective-permute-done | bytes 98336 | tf_op jit(solution)/shard_map/ppermute | solution.py:405
  120.1 1.3 collective-permute-done.26
  121.4 0.9 collective-permute-start.29
  122.4 0.9 collective-permute-start.30
  123.3 1.7 %collective-permute-start.31 = (bf16[32,1536]{1,0:T(8,128)(2,1)S(1)}, bf16[32,1536]{1,0:T(8,128)(2,1)S(1)}, u32[]{:S(2)}, u32[]{:S(2)}) collective-permute-start(bf16[32,1536]{1,0:T(8,128)(2,1)S(1)} %add_convert_fusion.refs_1_), channel_id=1, source_target_pairs={{0,12},{4,8},{8,4},{12,0},{1,13},{5,9},{9,5},{13,1},{2,14},{6,10},... | collective-permute-start | bytes 294920 | tf_op jit(solution)/shard_map/ppermute | solution.py:409
  125.0 2.0 %collective-permute-done.29.refs_2_ = bf16[32,1536]{1,0:T(8,128)(2,1)S(1)} collective-permute-done((bf16[32,1536]{1,0:T(8,128)(2,1)S(1)}, bf16[32,1536]{1,0:T(8,128)(2,1)S(1)}, u32[]{:S(2)}, u32[]{:S(2)}) %collective-permute-start.29) | collective-permute-done | bytes 98336 | tf_op jit(solution)/shard_map/ppermute | solution.py:409
  127.4 1.3 %collective-permute-done.31.refs_4_ = bf16[32,1536]{1,0:T(8,128)(2,1)S(1)} collective-permute-done((bf16[32,1536]{1,0:T(8,128)(2,1)S(1)}, bf16[32,1536]{1,0:T(8,128)(2,1)S(1)}, u32[]{:S(2)}, u32[]{:S(2)}) %collective-permute-start.31) | collective-permute-done | bytes 98336 | tf_op jit(solution)/shard_map/ppermute | solution.py:409
  128.8 0.8 place_blocks.1
  (65 shorter events, 5.5 us)
Async XLA Ops:
  0.0 1.0 copy-start
  1.0 0.7 copy-start.1
  2.0 1.7 %collective-permute-start = (bf16[2,48,1536]{2,1,0:T(8,128)(2,1)S(1)}, bf16[2,48,1536]{2,1,0:T(8,128)(2,1)S(1)}, u32[]{:S(2)}, u32[]{:S(2)}) collective-permute-start(bf16[2,48,1536]{2,1,0:T(8,128)(2,1)S(1)} %pick.1.refs_1_), channel_id=1, source_target_pairs={{0,16},{16,0},{1,17},{17,1},{2,18},{18,2},{3,19},{19,3},{4,20},{20... | collective-permute-start | bytes 884744 | tf_op jit(solution)/shard_map/ppermute | solution.py:344
  9.2 17.1 %collective-permute-start.1 = (bf16[2,2,96,1024]{3,2,1,0:T(8,128)(2,1)S(1)}, bf16[2,2,96,1024]{3,2,1,0:T(8,128)(2,1)S(1)}, u32[]{:S(2)}, u32[]{:S(2)}) collective-permute-start(bf16[2,2,96,1024]{3,2,1,0:T(8,128)(2,1)S(1)} %get-tuple-element.26), channel_id=1, source_target_pairs={{0,1},{19,18},{4,5},{23,22},{8,9},{27,26},{12,13},{31,30}} | collective-permute-start | bytes 2359304 | tf_op jit(solution)/shard_map/ppermute | solution.py:340
  19.5 16.9 %collective-permute-start.3 = (bf16[2,2,96,1024]{3,2,1,0:T(8,128)(2,1)S(1)}, bf16[2,2,96,1024]{3,2,1,0:T(8,128)(2,1)S(1)}, u32[]{:S(2)}, u32[]{:S(2)}) collective-permute-start(bf16[2,2,96,1024]{3,2,1,0:T(8,128)(2,1)S(1)} %get-tuple-element.29), channel_id=1, source_target_pairs={{0,1},{19,18},{4,5},{23,22},{8,9},{27,26},{12,13},{31,30}} | collective-permute-start | bytes 2359304 | tf_op jit(solution)/shard_map/ppermute | solution.py:340
  26.3 13.3 %collective-permute-start.2 = (bf16[2,2,96,1024]{3,2,1,0:T(8,128)(2,1)S(1)}, bf16[2,2,96,1024]{3,2,1,0:T(8,128)(2,1)S(1)}, u32[]{:S(2)}, u32[]{:S(2)}) collective-permute-start(bf16[2,2,96,1024]{3,2,1,0:T(8,128)(2,1)S(1)} %add_to_send.6.refs_5_), channel_id=1, source_target_pairs={{1,2},{18,17},{5,6},{22,21},{9,10},{26,25},{13,14},{30,29}} | collective-permute-start | bytes 2359304 | tf_op jit(solution)/shard_map/ppermute | solution.py:340
  27.0 13.5 %collective-permute-start.7 = (bf16[2,2,96,1024]{3,2,1,0:T(8,128)(2,1)S(1)}, bf16[2,2,96,1024]{3,2,1,0:T(8,128)(2,1)S(1)}, u32[]{:S(2)}, u32[]{:S(2)}) collective-permute-start(bf16[2,2,96,1024]{3,2,1,0:T(8,128)(2,1)S(1)} %get-tuple-element.32), channel_id=1, source_target_pairs={{0,1},{19,18},{4,5},{23,22},{8,9},{27,26},{12,13},{31,30}} | collective-permute-start | bytes 2359304 | tf_op jit(solution)/shard_map/ppermute | solution.py:340
  29.9 42.3 %slice-start = ((s8[25165824]{0:T(1024)(128)(4,1)}), s8[4194304]{0:T(1024)(128)(4,1)S(1)}, s32[]{:S(2)}) async-start(s8[25165824]{0:T(1024)(128)(4,1)} %bitcast.4), calls=%async_computation | async-start | bytes 8388608
  29.9 42.3 %slice-start.1 = ((s8[25165824]{0:T(1024)(128)(4,1)}), s8[4194304]{0:T(1024)(128)(4,1)S(1)}, s32[]{:S(2)}) async-start(s8[25165824]{0:T(1024)(128)(4,1)} %bitcast.4), calls=%async_computation.1 | async-start | bytes 8388608
  29.9 42.3 %slice-start.2 = ((s8[25165824]{0:T(1024)(128)(4,1)}), s8[4194304]{0:T(1024)(128)(4,1)S(1)}, s32[]{:S(2)}) async-start(s8[25165824]{0:T(1024)(128)(4,1)} %bitcast.4), calls=%async_computation.2 | async-start | bytes 8388608
  29.9 42.3 %slice-start.3 = ((s8[25165824]{0:T(1024)(128)(4,1)}), s8[4194304]{0:T(1024)(128)(4,1)S(1)}, s32[]{:S(2)}) async-start(s8[25165824]{0:T(1024)(128)(4,1)} %bitcast.4), calls=%async_computation.3 | async-start | bytes 8388608
  36.4 5.7 %collective-permute-start.6 = (bf16[2,2,96,1024]{3,2,1,0:T(8,128)(2,1)S(1)}, bf16[2,2,96,1024]{3,2,1,0:T(8,128)(2,1)S(1)}, u32[]{:S(2)}, u32[]{:S(2)}) collective-permute-start(bf16[2,2,96,1024]{3,2,1,0:T(8,128)(2,1)S(1)} %add_to_send.7.refs_3_), channel_id=1, source_target_pairs={{1,2},{18,17},{5,6},{22,21},{9,10},{26,25},{13,14},{30,29}} | collective-permute-start | bytes 2359304 | tf_op jit(solution)/shard_map/ppermute | solution.py:340
  37.2 18.0 %collective-permute-start.5 = (bf16[2,2,96,1024]{3,2,1,0:T(8,128)(2,1)}, bf16[2,2,96,1024]{3,2,1,0:T(8,128)(2,1)S(1)}, u32[]{:S(2)}, u32[]{:S(2)}) collective-permute-start(bf16[2,2,96,1024]{3,2,1,0:T(8,128)(2,1)} %get-tuple-element.31), channel_id=1, source_target_pairs={{0,1},{19,18},{4,5},{23,22},{8,9},{27,26},{12,13},{31,30}} | collective-permute-start | bytes 2359304 | tf_op jit(solution)/shard_map/ppermute | solution.py:340
  39.6 32.7 %slice-start.4 = ((s8[25165824]{0:T(1024)(128)(4,1)}), s8[4194304]{0:T(1024)(128)(4,1)S(1)}, s32[]{:S(2)}) async-start(s8[25165824]{0:T(1024)(128)(4,1)} %bitcast.4), calls=%async_computation.4 | async-start | bytes 8388608
  39.6 16.4 %collective-permute-start.4 = (bf16[2,2,96,1024]{3,2,1,0:T(8,128)(2,1)S(1)}, bf16[2,2,96,1024]{3,2,1,0:T(8,128)(2,1)S(1)}, u32[]{:S(2)}, u32[]{:S(2)}) collective-permute-start(bf16[2,2,96,1024]{3,2,1,0:T(8,128)(2,1)S(1)} %add_to_send.8.refs_2_), channel_id=1, source_target_pairs={{2,3},{17,16},{6,7},{21,20},{10,11},{25,24},{14,15},{29,28}} | collective-permute-start | bytes 2359304 | tf_op jit(solution)/shard_map/ppermute | solution.py:340
  40.5 16.2 %collective-permute-start.12 = (bf16[2,2,96,1024]{3,2,1,0:T(8,128)(2,1)S(1)}, bf16[2,2,96,1024]{3,2,1,0:T(8,128)(2,1)S(1)}, u32[]{:S(2)}, u32[]{:S(2)}) collective-permute-start(bf16[2,2,96,1024]{3,2,1,0:T(8,128)(2,1)S(1)} %add_to_send.9.refs_3_), channel_id=1, source_target_pairs={{1,2},{18,17},{5,6},{22,21},{9,10},{26,25},{13,14},{30,29}} | collective-permute-start | bytes 2359304 | tf_op jit(solution)/shard_map/ppermute | solution.py:340
  41.4 15.4 %collective-permute-start.13 = (bf16[2,2,96,1024]{3,2,1,0:T(8,128)(2,1)S(1)}, bf16[2,2,96,1024]{3,2,1,0:T(8,128)(2,1)S(1)}, u32[]{:S(2)}, u32[]{:S(2)}) collective-permute-start(bf16[2,2,96,1024]{3,2,1,0:T(8,128)(2,1)S(1)} %round_to_send.2.refs_2_), channel_id=1, source_target_pairs={{3,2},{16,17},{7,6},{20,21},{11,10},{24,25},{15,14},{28,29}} | collective-permute-start | bytes 2359304 | tf_op jit(solution)/shard_map/ppermute | solution.py:340
  42.1 30.1 %slice-start.5 = ((s8[25165824]{0:T(1024)(128)(4,1)}), s8[4194304]{0:T(1024)(128)(4,1)S(1)}, s32[]{:S(2)}) async-start(s8[25165824]{0:T(1024)(128)(4,1)} %bitcast.4), calls=%async_computation.5 | async-start | bytes 8388608
  42.1 16.6 %collective-permute-start.11 = (bf16[2,2,96,1024]{3,2,1,0:T(8,128)(2,1)S(1)}, bf16[2,2,96,1024]{3,2,1,0:T(8,128)(2,1)S(1)}, u32[]{:S(2)}, u32[]{:S(2)}) collective-permute-start(bf16[2,2,96,1024]{3,2,1,0:T(8,128)(2,1)S(1)} %add_to_send.10.refs_3_), channel_id=1, source_target_pairs={{2,3},{17,16},{6,7},{21,20},{10,11},{25,24},{14,15},{29,28}} | collective-permute-start | bytes 2359304 | tf_op jit(solution)/shard_map/ppermute | solution.py:340
  55.3 4.2 %collective-permute-start.9 = (bf16[2,2,96,1024]{3,2,1,0:T(8,128)(2,1)S(1)}, bf16[2,2,96,1024]{3,2,1,0:T(8,128)(2,1)S(1)}, u32[]{:S(2)}, u32[]{:S(2)}) collective-permute-start(bf16[2,2,96,1024]{3,2,1,0:T(8,128)(2,1)S(1)} %add_to_send.11.refs_3_), channel_id=1, source_target_pairs={{1,2},{18,17},{5,6},{22,21},{9,10},{26,25},{13,14},{30,29}} | collective-permute-start | bytes 2359304 | tf_op jit(solution)/shard_map/ppermute | solution.py:340
  56.0 4.4 %collective-permute-start.10 = (bf16[2,2,96,1024]{3,2,1,0:T(8,128)(2,1)S(1)}, bf16[2,2,96,1024]{3,2,1,0:T(8,128)(2,1)S(1)}, u32[]{:S(2)}, u32[]{:S(2)}) collective-permute-start(bf16[2,2,96,1024]{3,2,1,0:T(8,128)(2,1)S(1)} %round_to_send.3.refs_3_), channel_id=1, source_target_pairs={{3,2},{16,17},{7,6},{20,21},{11,10},{24,25},{15,14},{28,29}} | collective-permute-start | bytes 2359304 | tf_op jit(solution)/shard_map/ppermute | solution.py:340
  56.8 13.3 %collective-permute-start.17 = (bf16[2,96,1024]{2,1,0:T(8,128)(2,1)S(1)}, bf16[2,96,1024]{2,1,0:T(8,128)(2,1)S(1)}, u32[]{:S(2)}, u32[]{:S(2)}) collective-permute-start(bf16[2,96,1024]{2,1,0:T(8,128)(2,1)S(1)} %hidden_values.5.refs_3_), channel_id=1, source_target_pairs={{2,0},{17,19},{6,4},{21,23},{10,8},{25,27},{14,12},{29,31}} | collective-permute-start | bytes 1179656 | tf_op jit(solution)/shard_map/ppermute | solution.py:340
  58.1 12.7 %collective-permute-start.18 = (bf16[2,96,1024]{2,1,0:T(8,128)(2,1)S(1)}, bf16[2,96,1024]{2,1,0:T(8,128)(2,1)S(1)}, u32[]{:S(2)}, u32[]{:S(2)}) collective-permute-start(bf16[2,96,1024]{2,1,0:T(8,128)(2,1)S(1)} %hidden_values.5.refs_3_), channel_id=1, source_target_pairs={{2,1},{17,18},{6,5},{21,22},{10,9},{25,26},{14,13},{29,30}} | collective-permute-start | bytes 1179656 | tf_op jit(solution)/shard_map/ppermute | solution.py:340
  58.8 12.7 %collective-permute-start.19 = (bf16[2,96,1024]{2,1,0:T(8,128)(2,1)S(1)}, bf16[2,96,1024]{2,1,0:T(8,128)(2,1)S(1)}, u32[]{:S(2)}, u32[]{:S(2)}) collective-permute-start(bf16[2,96,1024]{2,1,0:T(8,128)(2,1)S(1)} %hidden_values.5.refs_3_), channel_id=1, source_target_pairs={{2,3},{17,16},{6,7},{21,20},{10,11},{25,24},{14,15},{29,28}} | collective-permute-start | bytes 1179656 | tf_op jit(solution)/shard_map/ppermute | solution.py:340
  59.5 14.0 %collective-permute-start.20 = (bf16[2,96,1024]{2,1,0:T(8,128)(2,1)S(1)}, bf16[2,96,1024]{2,1,0:T(8,128)(2,1)S(1)}, u32[]{:S(2)}, u32[]{:S(2)}) collective-permute-start(bf16[2,96,1024]{2,1,0:T(8,128)(2,1)S(1)} %hidden_values.6.refs_4_), channel_id=1, source_target_pairs={{3,2},{16,17},{7,6},{20,21},{11,10},{24,25},{15,14},{28,29}} | collective-permute-start | bytes 1179656 | tf_op jit(solution)/shard_map/ppermute | solution.py:340
  60.4 25.6 %collective-permute-start.14 = (bf16[2,96,1024]{2,1,0:T(8,128)(2,1)S(1)}, bf16[2,96,1024]{2,1,0:T(8,128)(2,1)S(1)}, u32[]{:S(2)}, u32[]{:S(2)}) collective-permute-start(bf16[2,96,1024]{2,1,0:T(8,128)(2,1)S(1)} %hidden_values.7.refs_6_.refs_3_), channel_id=1, source_target_pairs={{2,0},{17,19},{6,4},{21,23},{10,8},{25,27},{14,12},{29,31}} | collective-permute-start | bytes 1179656 | tf_op jit(solution)/shard_map/ppermute | solution.py:340
  70.1 15.9 %collective-permute-start.15 = (bf16[2,96,1024]{2,1,0:T(8,128)(2,1)S(1)}, bf16[2,96,1024]{2,1,0:T(8,128)(2,1)S(1)}, u32[]{:S(2)}, u32[]{:S(2)}) collective-permute-start(bf16[2,96,1024]{2,1,0:T(8,128)(2,1)S(1)} %hidden_values.7.refs_6_.refs_3_), channel_id=1, source_target_pairs={{2,1},{17,18},{6,5},{21,22},{10,9},{25,26},{14,13},{29,30}} | collective-permute-start | bytes 1179656 | tf_op jit(solution)/shard_map/ppermute | solution.py:340
  70.8 15.2 %collective-permute-start.16 = (bf16[2,96,1024]{2,1,0:T(8,128)(2,1)S(1)}, bf16[2,96,1024]{2,1,0:T(8,128)(2,1)S(1)}, u32[]{:S(2)}, u32[]{:S(2)}) collective-permute-start(bf16[2,96,1024]{2,1,0:T(8,128)(2,1)S(1)} %hidden_values.7.refs_6_.refs_3_), channel_id=1, source_target_pairs={{2,3},{17,16},{6,7},{21,20},{10,11},{25,24},{14,15},{29,28}} | collective-permute-start | bytes 1179656 | tf_op jit(solution)/shard_map/ppermute | solution.py:340
  71.5 15.7 %collective-permute-start.8 = (bf16[2,96,1024]{2,1,0:T(8,128)(2,1)S(1)}, bf16[2,96,1024]{2,1,0:T(8,128)(2,1)S(1)}, u32[]{:S(2)}, u32[]{:S(2)}) collective-permute-start(bf16[2,96,1024]{2,1,0:T(8,128)(2,1)S(1)} %hidden_values.4.refs_4_), channel_id=1, source_target_pairs={{3,2},{16,17},{7,6},{20,21},{11,10},{24,25},{15,14},{28,29}} | collective-permute-start | bytes 1179656 | tf_op jit(solution)/shard_map/ppermute | solution.py:340
  73.5 14.5 %collective-permute-start.22 = (bf16[2,96,1024]{2,1,0:T(8,128)(2,1)S(1)}, bf16[2,96,1024]{2,1,0:T(8,128)(2,1)S(1)}, u32[]{:S(2)}, u32[]{:S(2)}) collective-permute-start(bf16[2,96,1024]{2,1,0:T(8,128)(2,1)S(1)} %pass_on.4.refs_8_.refs_3_), channel_id=1, source_target_pairs={{2,1},{17,18},{6,5},{21,22},{10,9},{25,26},{14,13},{29,30}} | collective-permute-start | bytes 1179656 | tf_op jit(solution)/shard_map/ppermute | solution.py:340
  87.2 2.0 %collective-permute-start.21 = (bf16[2,96,1024]{2,1,0:T(8,128)(2,1)S(1)}, bf16[2,96,1024]{2,1,0:T(8,128)(2,1)S(1)}, u32[]{:S(2)}, u32[]{:S(2)}) collective-permute-start(bf16[2,96,1024]{2,1,0:T(8,128)(2,1)S(1)} %pass_on.5.refs_1_.refs_3_), channel_id=1, source_target_pairs={{2,1},{17,18},{6,5},{21,22},{10,9},{25,26},{14,13},{29,30}} | collective-permute-start | bytes 1179656 | tf_op jit(solution)/shard_map/ppermute | solution.py:340
  88.0 14.0 %collective-permute-start.24 = (bf16[2,96,1024]{2,1,0:T(8,128)(2,1)S(1)}, bf16[2,96,1024]{2,1,0:T(8,128)(2,1)S(1)}, u32[]{:S(2)}, u32[]{:S(2)}) collective-permute-start(bf16[2,96,1024]{2,1,0:T(8,128)(2,1)S(1)} %pass_on.6.refs_1_.refs_2_), channel_id=1, source_target_pairs={{1,0},{18,19},{5,4},{22,23},{9,8},{26,27},{13,12},{30,31}} | collective-permute-start | bytes 1179656 | tf_op jit(solution)/shard_map/ppermute | solution.py:340
  89.3 19.5 %collective-permute-start.23 = (bf16[2,96,1024]{2,1,0:T(8,128)(2,1)S(1)}, bf16[2,96,1024]{2,1,0:T(8,128)(2,1)S(1)}, u32[]{:S(2)}, u32[]{:S(2)}) collective-permute-start(bf16[2,96,1024]{2,1,0:T(8,128)(2,1)S(1)} %pass_on.7.refs_8_.refs_2_), channel_id=1, source_target_pairs={{1,0},{18,19},{5,4},{22,23},{9,8},{26,27},{13,12},{30,31}} | collective-permute-start | bytes 1179656 | tf_op jit(solution)/shard_map/ppermute | solution.py:340
  108.8 3.3 %copy-start.2 = (s32[128,2]{0,1:T(2,128)S(1)}, s32[128,2]{0,1:T(2,128)}, u32[]{:S(2)}) copy-start(s32[128,2]{0,1:T(2,128)} %param.7) | copy-start | bytes 3076
  108.8 3.3 %copy-start.3 = (f32[128,2]{0,1:T(2,128)S(1)}, f32[128,2]{0,1:T(2,128)}, u32[]{:S(2)}) copy-start(f32[128,2]{0,1:T(2,128)} %param.8) | copy-start | bytes 3076
  110.0 2.1 %collective-permute-start.25 = (f32[2,48,1536]{2,1,0:T(8,128)S(1)}, f32[2,48,1536]{2,1,0:T(8,128)S(1)}, u32[]{:S(2)}, u32[]{:S(2)}) collective-permute-start(f32[2,48,1536]{2,1,0:T(8,128)S(1)} %get-tuple-element.40), channel_id=1, source_target_pairs={{0,16},{16,0},{1,17},{17,1},{2,18},{18,2},{3,19},{19,3},{4,20},{20... | collective-permute-start | bytes 1769480 | tf_op jit(solution)/shard_map/ppermute | solution.py:399
  112.8 4.9 %collective-permute-start.28 = (bf16[32,1536]{1,0:T(8,128)(2,1)S(1)}, bf16[32,1536]{1,0:T(8,128)(2,1)S(1)}, u32[]{:S(2)}, u32[]{:S(2)}) collective-permute-start(bf16[32,1536]{1,0:T(8,128)(2,1)S(1)} %get-tuple-element.44), channel_id=1, source_target_pairs={{0,4},{4,0},{8,12},{12,8},{1,5},{5,1},{9,13},{13,9},{2,6},{6,2},{1... | collective-permute-start | bytes 294920 | tf_op jit(solution)/shard_map/ppermute | solution.py:405
  114.4 5.8 %collective-permute-start.27 = (bf16[32,1536]{1,0:T(8,128)(2,1)S(1)}, bf16[32,1536]{1,0:T(8,128)(2,1)S(1)}, u32[]{:S(2)}, u32[]{:S(2)}) collective-permute-start(bf16[32,1536]{1,0:T(8,128)(2,1)S(1)} %get-tuple-element.43), channel_id=1, source_target_pairs={{0,8},{4,12},{8,0},{12,4},{1,9},{5,13},{9,1},{13,5},{2,10},{6,14},... | collective-permute-start | bytes 294920 | tf_op jit(solution)/shard_map/ppermute | solution.py:405
  115.9 5.5 %collective-permute-start.26 = (bf16[32,1536]{1,0:T(8,128)(2,1)S(1)}, bf16[32,1536]{1,0:T(8,128)(2,1)S(1)}, u32[]{:S(2)}, u32[]{:S(2)}) collective-permute-start(bf16[32,1536]{1,0:T(8,128)(2,1)S(1)} %get-tuple-element.42), channel_id=1, source_target_pairs={{0,12},{4,8},{8,4},{12,0},{1,13},{5,9},{9,5},{13,1},{2,14},{6,10},... | collective-permute-start | bytes 294920 | tf_op jit(solution)/shard_map/ppermute | solution.py:405
  121.4 5.6 %collective-permute-start.29 = (bf16[32,1536]{1,0:T(8,128)(2,1)S(1)}, bf16[32,1536]{1,0:T(8,128)(2,1)S(1)}, u32[]{:S(2)}, u32[]{:S(2)}) collective-permute-start(bf16[32,1536]{1,0:T(8,128)(2,1)S(1)} %add_convert_fusion.refs_1_), channel_id=1, source_target_pairs={{0,4},{4,0},{8,12},{12,8},{1,5},{5,1},{9,13},{13,9},{2,6},{6,2},{1... | collective-permute-start | bytes 294920 | tf_op jit(solution)/shard_map/ppermute | solution.py:409
  122.4 5.1 %collective-permute-start.30 = (bf16[32,1536]{1,0:T(8,128)(2,1)S(1)}, bf16[32,1536]{1,0:T(8,128)(2,1)S(1)}, u32[]{:S(2)}, u32[]{:S(2)}) collective-permute-start(bf16[32,1536]{1,0:T(8,128)(2,1)S(1)} %add_convert_fusion.refs_1_), channel_id=1, source_target_pairs={{0,8},{4,12},{8,0},{12,4},{1,9},{5,13},{9,1},{13,5},{2,10},{6,14},... | collective-permute-start | bytes 294920 | tf_op jit(solution)/shard_map/ppermute | solution.py:409
  123.3 5.5 %collective-permute-start.31 = (bf16[32,1536]{1,0:T(8,128)(2,1)S(1)}, bf16[32,1536]{1,0:T(8,128)(2,1)S(1)}, u32[]{:S(2)}, u32[]{:S(2)}) collective-permute-start(bf16[32,1536]{1,0:T(8,128)(2,1)S(1)} %add_convert_fusion.refs_1_), channel_id=1, source_target_pairs={{0,12},{4,8},{8,4},{12,0},{1,13},{5,9},{9,5},{13,1},{2,14},{6,10},... | collective-permute-start | bytes 294920 | tf_op jit(solution)/shard_map/ppermute | solution.py:409

commit v9 on v8

--- a/solution.py
+++ b/solution.py
@@ -12,7 +12,7 @@
 MIB = 1024 * 1024
 
 CHUNKS = ((4, "end"), (4, "end"), (4, "inner"), (4, "inner"))
-GROUPS = {0: ((0,), "relay"), 1: ((1,), "relay"), 2: ((2,), "direct"), 3: ((3,), "direct")}
+GROUPS = {0: ((0,), "relay"), 1: ((1,), "relay"), 2: ((2,), "relay"), 3: ((3,), "relay")}
 
 SUMS = {
     "end": {"m0": (0, 1, None), "m1": (1, 2, "m0"), "m2": (2, 3, "m1")},
@@ -28,11 +28,11 @@
 HELD = {"end": ("a2", "a1", "a0", None), "inner": ("a2", "a0", None, "a1")}
 
 ORDER = (
-    ("g", 0), ("m0", 0), ("g", 1), ("m0", 1), ("g", 3), ("m0", 3), ("m1", 0), ("g", 2),
-    ("m0", 2), ("m1", 1), ("m2", 0), ("mb", 3), ("mb", 2), ("m1", 3), ("m2", 1), ("m1", 2),
-    ("h", 0), ("h", 3), ("h", 1), ("a0", 1), ("h", 2), ("a0", 3), ("a1", 3), ("a2", 3),
-    ("a1", 2), ("d", 3), ("a1", 1), ("a0", 2), ("a2", 2), ("d", 2), ("a0", 0), ("a1", 0),
-    ("a2", 1), ("a2", 0), ("d", 1), ("d", 0),
+    ("g", 1), ("m0", 1), ("g", 0), ("m0", 0), ("g", 3), ("m0", 3), ("m1", 1), ("g", 2),
+    ("m0", 2), ("m1", 0), ("m2", 1), ("m1", 3), ("mb", 2), ("mb", 3), ("m2", 0), ("m1", 2),
+    ("h", 1), ("h", 3), ("h", 0), ("h", 2), ("a0", 3), ("a0", 1), ("a2", 3), ("a0", 0),
+    ("a0", 2), ("a1", 0), ("a1", 1), ("a1", 3), ("d", 3), ("a2", 2), ("a2", 0), ("a1", 2),
+    ("a2", 1), ("d", 2), ("d", 0), ("d", 1),
 )
 
 SMEM = pl.BlockSpec(memory_space=pltpu.SMEM)

time: 130 us -> 121 us (0.931)
  waiting for transfers between devices: 61.6 us -> 53.1 us
    ppermute x24, waiting for transfers between devices: 49.6 us -> 41.1 us  [hop(): return lax.ppermute(value, ('dp', 'blk'), pairs)]
    pallas_call x27 -> x29, Pallas kernels: 29.4 us -> 28.4 us  [call(): pl.pallas_call(body, out_shape=outs, in_specs=list(specs) + [ANY] * len(a...]
  transfers between devices with their start and end apart: 32 -> 32, of which waited for: 13 -> 14; matrix products, arithmetic and copies ran while one was open for 0% -> 0% of each run, Pallas kernels for 16% -> 17%
where the time goes in v9:
time: 121 us; the launch traced here: 120 us
  waiting for transfers between devices  53.1 us (44%)
  starting transfers between devices  36.5 us (30%)
  Pallas kernels  28.4 us (23%)
  local copies, waits for them, and re-layouts  1.71 us (1%)
    ppermute x24, waiting for transfers between devices, hop(): return lax.ppermute(value, ('dp', 'blk'), pairs)  41.1 us
    ppermute x24, starting transfers between devices, hop(): return lax.ppermute(value, ('dp', 'blk'), pairs)  28.8 us
    pallas_call x29, Pallas kernels, call(): pl.pallas_call(body, out_shape=outs, in_specs=list(specs) + [ANY] * len(a...  28.4 us
    ppermute x3, waiting for transfers between devices, local(): own = own + lax.ppermute(sent[step - 1], 'expert', exchange).astype(F32)  5.05 us
    ppermute x3, waiting for transfers between devices, local(): lax.ppermute(block, 'expert', [(i, i ^ step) for i in range(groups)])  3.78 us
    ppermute x3, starting transfers between devices, local(): lax.ppermute(block, 'expert', [(i, i ^ step) for i in range(groups)])  3.55 us
    ppermute x3, starting transfers between devices, local(): own = own + lax.ppermute(sent[step - 1], 'expert', exchange).astype(F32)  3.55 us
  transfers between devices with their start and end apart: 32, of which 14 were waited for; matrix products, arithmetic and copies ran while one was open for 0% of the time, Pallas kernels for 17%

profile of v9, /device:TPU:0, one launch (start us, length us, event | category | flops | bytes accessed | tf_op | source)
XLA Modules:
  0.0 120.4 jit_solution(7872751054680678044)
XLA Ops:
  0.0 1.0 copy-done
  2.6 1.2 %collective-permute-done.refs_2_ = bf16[2,48,1536]{2,1,0:T(8,128)(2,1)S(1)} collective-permute-done((bf16[2,48,1536]{2,1,0:T(8,128)(2,1)S(1)}, bf16[2,48,1536]{2,1,0:T(8,128)(2,1)S(1)}, u32[]{:S(2)}, u32[]{:S(2)}) %collective-permute-start) | collective-permute-done | bytes 294944 | tf_op jit(solution)/shard_map/ppermute | solution.py:344
  3.8 5.4 %gate_up.4 = (f32[2,2,96,1024]{3,2,1,0:T(8,128)S(1)}, bf16[2,2,96,1024]{3,2,1,0:T(8,128)(2,1)S(1)}) custom-call(s32[1]{0:T(128)} %bitcast.3.refs_0_, bf16[2,48,1536]{2,1,0:T(8,128)(2,1)S(1)} %pick.1.refs_1_, bf16[2,48,1536]{2,1,0:T(8,128)(2,1)S(1)} %collective-permute-done.refs_2_, bf16[2,1536,4096]{2,1,0:T(8,128)(2,1)} %refs_3_.7, ...), custom_call_target="tpu_custom_call" | custom-call | tf_op jit(solution)/shard_map/gate_up/pallas_call | solution.py:50
  9.2 4.9 %collective-permute-start.1 = (bf16[2,2,96,1024]{3,2,1,0:T(8,128)(2,1)S(1)}, bf16[2,2,96,1024]{3,2,1,0:T(8,128)(2,1)S(1)}, u32[]{:S(2)}, u32[]{:S(2)}) collective-permute-start(bf16[2,2,96,1024]{3,2,1,0:T(8,128)(2,1)S(1)} %get-tuple-element.26), channel_id=1, source_target_pairs={{0,1},{19,18},{4,5},{23,22},{8,9},{27,26},{12,13},{31,30}} | collective-permute-start | bytes 2359304 | tf_op jit(solution)/shard_map/ppermute | solution.py:340
  14.1 5.4 %gate_up.5 = (f32[2,2,96,1024]{3,2,1,0:T(8,128)S(1)}, bf16[2,2,96,1024]{3,2,1,0:T(8,128)(2,1)S(1)}) custom-call(s32[1]{0:T(128)} %bitcast.3.refs_0_, bf16[2,48,1536]{2,1,0:T(8,128)(2,1)S(1)} %pick.1.refs_1_, bf16[2,48,1536]{2,1,0:T(8,128)(2,1)S(1)} %collective-permute-done.refs_2_, bf16[2,1536,4096]{2,1,0:T(8,128)(2,1)} %refs_3_.7, ...), custom_call_target="tpu_custom_call" | custom-call | tf_op jit(solution)/shard_map/gate_up/pallas_call | solution.py:50
  19.5 1.3 %collective-permute-start.3 = (bf16[2,2,96,1024]{3,2,1,0:T(8,128)(2,1)S(1)}, bf16[2,2,96,1024]{3,2,1,0:T(8,128)(2,1)S(1)}, u32[]{:S(2)}, u32[]{:S(2)}) collective-permute-start(bf16[2,2,96,1024]{3,2,1,0:T(8,128)(2,1)S(1)} %get-tuple-element.29), channel_id=1, source_target_pairs={{0,1},{19,18},{4,5},{23,22},{8,9},{27,26},{12,13},{31,30}} | collective-permute-start | bytes 2359304 | tf_op jit(solution)/shard_map/ppermute | solution.py:340
  20.8 5.4 %gate_up.6 = (f32[2,2,96,1024]{3,2,1,0:T(8,128)S(1)}, bf16[2,2,96,1024]{3,2,1,0:T(8,128)(2,1)S(1)}) custom-call(s32[1]{0:T(128)} %bitcast.3.refs_0_, bf16[2,48,1536]{2,1,0:T(8,128)(2,1)S(1)} %pick.1.refs_1_, bf16[2,48,1536]{2,1,0:T(8,128)(2,1)S(1)} %collective-permute-done.refs_2_, bf16[2,1536,4096]{2,1,0:T(8,128)(2,1)} %refs_3_.7, ...), custom_call_target="tpu_custom_call" | custom-call | tf_op jit(solution)/shard_map/gate_up/pallas_call | solution.py:50
  26.3 0.7 collective-permute-start.2
  27.0 2.9 %collective-permute-start.7 = (bf16[2,2,96,1024]{3,2,1,0:T(8,128)(2,1)S(1)}, bf16[2,2,96,1024]{3,2,1,0:T(8,128)(2,1)S(1)}, u32[]{:S(2)}, u32[]{:S(2)}) collective-permute-start(bf16[2,2,96,1024]{3,2,1,0:T(8,128)(2,1)S(1)} %get-tuple-element.32), channel_id=1, source_target_pairs={{0,1},{19,18},{4,5},{23,22},{8,9},{27,26},{12,13},{31,30}} | collective-permute-start | bytes 2359304 | tf_op jit(solution)/shard_map/ppermute | solution.py:340
  29.9 5.5 %gate_up.7 = (f32[2,2,96,1024]{3,2,1,0:T(8,128)S(1)}, bf16[2,2,96,1024]{3,2,1,0:T(8,128)(2,1)S(1)}) custom-call(s32[1]{0:T(128)} %bitcast.3.refs_0_, bf16[2,48,1536]{2,1,0:T(8,128)(2,1)S(1)} %pick.1.refs_1_, bf16[2,48,1536]{2,1,0:T(8,128)(2,1)S(1)} %collective-permute-done.refs_2_, bf16[2,1536,4096]{2,1,0:T(8,128)(2,1)} %refs_3_.7, ...), custom_call_target="tpu_custom_call" | custom-call | tf_op jit(solution)/shard_map/gate_up/pallas_call | solution.py:50
  35.5 0.8 collective-permute-start.6
  36.3 2.6 %collective-permute-start.5 = (bf16[2,2,96,1024]{3,2,1,0:T(8,128)(2,1)S(1)}, bf16[2,2,96,1024]{3,2,1,0:T(8,128)(2,1)S(1)}, u32[]{:S(2)}, u32[]{:S(2)}) collective-permute-start(bf16[2,2,96,1024]{3,2,1,0:T(8,128)(2,1)S(1)} %get-tuple-element.31), channel_id=1, source_target_pairs={{0,1},{19,18},{4,5},{23,22},{8,9},{27,26},{12,13},{31,30}} | collective-permute-start | bytes 2359304 | tf_op jit(solution)/shard_map/ppermute | solution.py:340
  38.9 0.7 collective-permute-start.4
  39.7 0.7 collective-permute-done.7.refs_2_
  40.4 0.8 collective-permute-start.10
  41.2 0.8 collective-permute-start.11
  42.1 0.7 collective-permute-start.9
  42.8 11.5 %collective-permute-done.5.refs_2_ = bf16[2,2,96,1024]{3,2,1,0:T(8,128)(2,1)S(1)} collective-permute-done((bf16[2,2,96,1024]{3,2,1,0:T(8,128)(2,1)S(1)}, bf16[2,2,96,1024]{3,2,1,0:T(8,128)(2,1)S(1)}, u32[]{:S(2)}, u32[]{:S(2)}) %collective-permute-start.5) | collective-permute-done | bytes 786464 | tf_op jit(solution)/shard_map/ppermute | solution.py:340
  54.3 0.8 collective-permute-start.14
  55.2 0.8 collective-permute-start.15
  56.1 0.7 collective-permute-start.13
  57.5 0.9 collective-permute-start.8
  59.1 1.3 %collective-permute-start.19 = (bf16[2,96,1024]{2,1,0:T(8,128)(2,1)S(1)}, bf16[2,96,1024]{2,1,0:T(8,128)(2,1)S(1)}, u32[]{:S(2)}, u32[]{:S(2)}) collective-permute-start(bf16[2,96,1024]{2,1,0:T(8,128)(2,1)S(1)} %pass_on.6.refs_1_.refs_2_), channel_id=1, source_target_pairs={{1,0},{18,19},{5,4},{22,23},{9,8},{26,27},{13,12},{30,31}} | collective-permute-start | bytes 1179656 | tf_op jit(solution)/shard_map/ppermute | solution.py:340
  60.4 0.7 collective-permute-start.18
  63.3 16.7 %collective-permute-done.19.refs_1_ = bf16[2,96,1024]{2,1,0:T(8,128)(2,1)S(1)} collective-permute-done((bf16[2,96,1024]{2,1,0:T(8,128)(2,1)S(1)}, bf16[2,96,1024]{2,1,0:T(8,128)(2,1)S(1)}, u32[]{:S(2)}, u32[]{:S(2)}) %collective-permute-start.19) | collective-permute-done | bytes 393248 | tf_op jit(solution)/shard_map/ppermute | solution.py:340
  80.0 1.2 down.4
  81.3 1.3 %collective-permute-start.23 = (bf16[2,96,1024]{2,1,0:T(8,128)(2,1)S(1)}, bf16[2,96,1024]{2,1,0:T(8,128)(2,1)S(1)}, u32[]{:S(2)}, u32[]{:S(2)}) collective-permute-start(bf16[2,96,1024]{2,1,0:T(8,128)(2,1)S(1)} %pass_on.9.refs_1_.refs_2_), channel_id=1, source_target_pairs={{1,0},{18,19},{5,4},{22,23},{9,8},{26,27},{13,12},{30,31}} | collective-permute-start | bytes 1179656 | tf_op jit(solution)/shard_map/ppermute | solution.py:340
  82.6 1.3 %collective-permute-start.22 = (bf16[2,96,1024]{2,1,0:T(8,128)(2,1)S(1)}, bf16[2,96,1024]{2,1,0:T(8,128)(2,1)S(1)}, u32[]{:S(2)}, u32[]{:S(2)}) collective-permute-start(bf16[2,96,1024]{2,1,0:T(8,128)(2,1)S(1)} %pass_on.10.refs_1_.refs_2_), channel_id=1, source_target_pairs={{1,0},{18,19},{5,4},{22,23},{9,8},{26,27},{13,12},{30,31}} | collective-permute-start | bytes 1179656 | tf_op jit(solution)/shard_map/ppermute | solution.py:340
  83.9 1.3 %collective-permute-start.21 = (bf16[2,96,1024]{2,1,0:T(8,128)(2,1)S(1)}, bf16[2,96,1024]{2,1,0:T(8,128)(2,1)S(1)}, u32[]{:S(2)}, u32[]{:S(2)}) collective-permute-start(bf16[2,96,1024]{2,1,0:T(8,128)(2,1)S(1)} %pass_on.11.refs_8_.refs_2_), channel_id=1, source_target_pairs={{1,0},{18,19},{5,4},{22,23},{9,8},{26,27},{13,12},{30,31}} | collective-permute-start | bytes 1179656 | tf_op jit(solution)/shard_map/ppermute | solution.py:340
  85.2 6.0 %collective-permute-done.23.refs_1_ = bf16[2,96,1024]{2,1,0:T(8,128)(2,1)S(1)} collective-permute-done((bf16[2,96,1024]{2,1,0:T(8,128)(2,1)S(1)}, bf16[2,96,1024]{2,1,0:T(8,128)(2,1)S(1)}, u32[]{:S(2)}, u32[]{:S(2)}) %collective-permute-start.23) | collective-permute-done | bytes 393248 | tf_op jit(solution)/shard_map/ppermute | solution.py:340
  91.2 1.2 down.5
  92.4 3.0 %collective-permute-done.22.refs_1_ = bf16[2,96,1024]{2,1,0:T(8,128)(2,1)S(1)} collective-permute-done((bf16[2,96,1024]{2,1,0:T(8,128)(2,1)S(1)}, bf16[2,96,1024]{2,1,0:T(8,128)(2,1)S(1)}, u32[]{:S(2)}, u32[]{:S(2)}) %collective-permute-start.22) | collective-permute-done | bytes 393248 | tf_op jit(solution)/shard_map/ppermute | solution.py:340
  95.4 1.2 down.6
  96.6 3.0 %collective-permute-done.21.refs_1_ = bf16[2,96,1024]{2,1,0:T(8,128)(2,1)S(1)} collective-permute-done((bf16[2,96,1024]{2,1,0:T(8,128)(2,1)S(1)}, bf16[2,96,1024]{2,1,0:T(8,128)(2,1)S(1)}, u32[]{:S(2)}, u32[]{:S(2)}) %collective-permute-start.21) | collective-permute-done | bytes 393248 | tf_op jit(solution)/shard_map/ppermute | solution.py:340
  99.6 1.2 down.7
  100.9 2.0 %collective-permute-done.25.refs_4_ = f32[2,48,1536]{2,1,0:T(8,128)S(1)} collective-permute-done((f32[2,48,1536]{2,1,0:T(8,128)S(1)}, f32[2,48,1536]{2,1,0:T(8,128)S(1)}, u32[]{:S(2)}, u32[]{:S(2)}) %collective-permute-start.25) | collective-permute-done | bytes 589856 | tf_op jit(solution)/shard_map/ppermute | solution.py:399
  102.9 0.7 combine.1
  103.7 1.6 %collective-permute-start.28 = (bf16[32,1536]{1,0:T(8,128)(2,1)S(1)}, bf16[32,1536]{1,0:T(8,128)(2,1)S(1)}, u32[]{:S(2)}, u32[]{:S(2)}) collective-permute-start(bf16[32,1536]{1,0:T(8,128)(2,1)S(1)} %get-tuple-element.44), channel_id=1, source_target_pairs={{0,4},{4,0},{8,12},{12,8},{1,5},{5,1},{9,13},{13,9},{2,6},{6,2},{1... | collective-permute-start | bytes 294920 | tf_op jit(solution)/shard_map/ppermute | solution.py:405
  105.2 1.5 %collective-permute-start.27 = (bf16[32,1536]{1,0:T(8,128)(2,1)S(1)}, bf16[32,1536]{1,0:T(8,128)(2,1)S(1)}, u32[]{:S(2)}, u32[]{:S(2)}) collective-permute-start(bf16[32,1536]{1,0:T(8,128)(2,1)S(1)} %get-tuple-element.43), channel_id=1, source_target_pairs={{0,8},{4,12},{8,0},{12,4},{1,9},{5,13},{9,1},{13,5},{2,10},{6,14},... | collective-permute-start | bytes 294920 | tf_op jit(solution)/shard_map/ppermute | solution.py:405
  107.2 1.3 %collective-permute-done.28 = bf16[32,1536]{1,0:T(8,128)(2,1)S(1)} collective-permute-done((bf16[32,1536]{1,0:T(8,128)(2,1)S(1)}, bf16[32,1536]{1,0:T(8,128)(2,1)S(1)}, u32[]{:S(2)}, u32[]{:S(2)}) %collective-permute-start.28) | collective-permute-done | bytes 98336 | tf_op jit(solution)/shard_map/ppermute | solution.py:405
  108.6 2.4 %collective-permute-done.27 = bf16[32,1536]{1,0:T(8,128)(2,1)S(1)} collective-permute-done((bf16[32,1536]{1,0:T(8,128)(2,1)S(1)}, bf16[32,1536]{1,0:T(8,128)(2,1)S(1)}, u32[]{:S(2)}, u32[]{:S(2)}) %collective-permute-start.27) | collective-permute-done | bytes 98336 | tf_op jit(solution)/shard_map/ppermute | solution.py:405
  111.0 1.3 %collective-permute-done.26 = bf16[32,1536]{1,0:T(8,128)(2,1)S(1)} collective-permute-done((bf16[32,1536]{1,0:T(8,128)(2,1)S(1)}, bf16[32,1536]{1,0:T(8,128)(2,1)S(1)}, u32[]{:S(2)}, u32[]{:S(2)}) %collective-permute-start.26) | collective-permute-done | bytes 98336 | tf_op jit(solution)/shard_map/ppermute | solution.py:405
  112.3 0.9 collective-permute-start.29
  113.2 0.9 collective-permute-start.30
  114.1 1.7 %collective-permute-start.31 = (bf16[32,1536]{1,0:T(8,128)(2,1)S(1)}, bf16[32,1536]{1,0:T(8,128)(2,1)S(1)}, u32[]{:S(2)}, u32[]{:S(2)}) collective-permute-start(bf16[32,1536]{1,0:T(8,128)(2,1)S(1)} %add_convert_fusion.refs_1_), channel_id=1, source_target_pairs={{0,12},{4,8},{8,4},{12,0},{1,13},{5,9},{9,5},{13,1},{2,14},{6,10},... | collective-permute-start | bytes 294920 | tf_op jit(solution)/shard_map/ppermute | solution.py:409
  115.9 2.1 %collective-permute-done.29.refs_2_ = bf16[32,1536]{1,0:T(8,128)(2,1)S(1)} collective-permute-done((bf16[32,1536]{1,0:T(8,128)(2,1)S(1)}, bf16[32,1536]{1,0:T(8,128)(2,1)S(1)}, u32[]{:S(2)}, u32[]{:S(2)}) %collective-permute-start.29) | collective-permute-done | bytes 98336 | tf_op jit(solution)/shard_map/ppermute | solution.py:409
  118.3 1.3 %collective-permute-done.31.refs_4_ = bf16[32,1536]{1,0:T(8,128)(2,1)S(1)} collective-permute-done((bf16[32,1536]{1,0:T(8,128)(2,1)S(1)}, bf16[32,1536]{1,0:T(8,128)(2,1)S(1)}, u32[]{:S(2)}, u32[]{:S(2)}) %collective-permute-start.31) | collective-permute-done | bytes 98336 | tf_op jit(solution)/shard_map/ppermute | solution.py:409
  119.6 0.8 place_blocks.1
  (67 shorter events, 6.1 us)
Async XLA Ops:
  0.0 1.0 copy-start
  1.0 0.7 copy-start.1
  2.0 1.7 %collective-permute-start = (bf16[2,48,1536]{2,1,0:T(8,128)(2,1)S(1)}, bf16[2,48,1536]{2,1,0:T(8,128)(2,1)S(1)}, u32[]{:S(2)}, u32[]{:S(2)}) collective-permute-start(bf16[2,48,1536]{2,1,0:T(8,128)(2,1)S(1)} %pick.1.refs_1_), channel_id=1, source_target_pairs={{0,16},{16,0},{1,17},{17,1},{2,18},{18,2},{3,19},{19,3},{4,20},{20... | collective-permute-start | bytes 884744 | tf_op jit(solution)/shard_map/ppermute | solution.py:344
  9.2 17.1 %collective-permute-start.1 = (bf16[2,2,96,1024]{3,2,1,0:T(8,128)(2,1)S(1)}, bf16[2,2,96,1024]{3,2,1,0:T(8,128)(2,1)S(1)}, u32[]{:S(2)}, u32[]{:S(2)}) collective-permute-start(bf16[2,2,96,1024]{3,2,1,0:T(8,128)(2,1)S(1)} %get-tuple-element.26), channel_id=1, source_target_pairs={{0,1},{19,18},{4,5},{23,22},{8,9},{27,26},{12,13},{31,30}} | collective-permute-start | bytes 2359304 | tf_op jit(solution)/shard_map/ppermute | solution.py:340
  19.5 16.0 %collective-permute-start.3 = (bf16[2,2,96,1024]{3,2,1,0:T(8,128)(2,1)S(1)}, bf16[2,2,96,1024]{3,2,1,0:T(8,128)(2,1)S(1)}, u32[]{:S(2)}, u32[]{:S(2)}) collective-permute-start(bf16[2,2,96,1024]{3,2,1,0:T(8,128)(2,1)S(1)} %get-tuple-element.29), channel_id=1, source_target_pairs={{0,1},{19,18},{4,5},{23,22},{8,9},{27,26},{12,13},{31,30}} | collective-permute-start | bytes 2359304 | tf_op jit(solution)/shard_map/ppermute | solution.py:340
  26.3 12.7 %collective-permute-start.2 = (bf16[2,2,96,1024]{3,2,1,0:T(8,128)(2,1)S(1)}, bf16[2,2,96,1024]{3,2,1,0:T(8,128)(2,1)S(1)}, u32[]{:S(2)}, u32[]{:S(2)}) collective-permute-start(bf16[2,2,96,1024]{3,2,1,0:T(8,128)(2,1)S(1)} %add_to_send.6.refs_5_), channel_id=1, source_target_pairs={{1,2},{18,17},{5,6},{22,21},{9,10},{26,25},{13,14},{30,29}} | collective-permute-start | bytes 2359304 | tf_op jit(solution)/shard_map/ppermute | solution.py:340
  27.0 13.4 %collective-permute-start.7 = (bf16[2,2,96,1024]{3,2,1,0:T(8,128)(2,1)S(1)}, bf16[2,2,96,1024]{3,2,1,0:T(8,128)(2,1)S(1)}, u32[]{:S(2)}, u32[]{:S(2)}) collective-permute-start(bf16[2,2,96,1024]{3,2,1,0:T(8,128)(2,1)S(1)} %get-tuple-element.32), channel_id=1, source_target_pairs={{0,1},{19,18},{4,5},{23,22},{8,9},{27,26},{12,13},{31,30}} | collective-permute-start | bytes 2359304 | tf_op jit(solution)/shard_map/ppermute | solution.py:340
  29.9 50.1 %slice-start = ((s8[25165824]{0:T(1024)(128)(4,1)}), s8[4194304]{0:T(1024)(128)(4,1)S(1)}, s32[]{:S(2)}) async-start(s8[25165824]{0:T(1024)(128)(4,1)} %bitcast.4), calls=%async_computation | async-start | bytes 8388608
  29.9 50.1 %slice-start.1 = ((s8[25165824]{0:T(1024)(128)(4,1)}), s8[4194304]{0:T(1024)(128)(4,1)S(1)}, s32[]{:S(2)}) async-start(s8[25165824]{0:T(1024)(128)(4,1)} %bitcast.4), calls=%async_computation.1 | async-start | bytes 8388608
  29.9 50.1 %slice-start.2 = ((s8[25165824]{0:T(1024)(128)(4,1)}), s8[4194304]{0:T(1024)(128)(4,1)S(1)}, s32[]{:S(2)}) async-start(s8[25165824]{0:T(1024)(128)(4,1)} %bitcast.4), calls=%async_computation.2 | async-start | bytes 8388608
  29.9 50.1 %slice-start.3 = ((s8[25165824]{0:T(1024)(128)(4,1)}), s8[4194304]{0:T(1024)(128)(4,1)S(1)}, s32[]{:S(2)}) async-start(s8[25165824]{0:T(1024)(128)(4,1)} %bitcast.4), calls=%async_computation.3 | async-start | bytes 8388608
  35.5 6.6 %collective-permute-start.6 = (bf16[2,2,96,1024]{3,2,1,0:T(8,128)(2,1)S(1)}, bf16[2,2,96,1024]{3,2,1,0:T(8,128)(2,1)S(1)}, u32[]{:S(2)}, u32[]{:S(2)}) collective-permute-start(bf16[2,2,96,1024]{3,2,1,0:T(8,128)(2,1)S(1)} %add_to_send.7.refs_3_), channel_id=1, source_target_pairs={{1,2},{18,17},{5,6},{22,21},{9,10},{26,25},{13,14},{30,29}} | collective-permute-start | bytes 2359304 | tf_op jit(solution)/shard_map/ppermute | solution.py:340
  36.3 18.0 %collective-permute-start.5 = (bf16[2,2,96,1024]{3,2,1,0:T(8,128)(2,1)S(1)}, bf16[2,2,96,1024]{3,2,1,0:T(8,128)(2,1)S(1)}, u32[]{:S(2)}, u32[]{:S(2)}) collective-permute-start(bf16[2,2,96,1024]{3,2,1,0:T(8,128)(2,1)S(1)} %get-tuple-element.31), channel_id=1, source_target_pairs={{0,1},{19,18},{4,5},{23,22},{8,9},{27,26},{12,13},{31,30}} | collective-permute-start | bytes 2359304 | tf_op jit(solution)/shard_map/ppermute | solution.py:340
  38.9 16.2 %collective-permute-start.4 = (bf16[2,2,96,1024]{3,2,1,0:T(8,128)(2,1)S(1)}, bf16[2,2,96,1024]{3,2,1,0:T(8,128)(2,1)S(1)}, u32[]{:S(2)}, u32[]{:S(2)}) collective-permute-start(bf16[2,2,96,1024]{3,2,1,0:T(8,128)(2,1)S(1)} %add_to_send.8.refs_3_), channel_id=1, source_target_pairs={{2,3},{17,16},{6,7},{21,20},{10,11},{25,24},{14,15},{29,28}} | collective-permute-start | bytes 2359304 | tf_op jit(solution)/shard_map/ppermute | solution.py:340
  40.4 39.7 %slice-start.4 = ((s8[25165824]{0:T(1024)(128)(4,1)}), s8[4194304]{0:T(1024)(128)(4,1)S(1)}, s32[]{:S(2)}) async-start(s8[25165824]{0:T(1024)(128)(4,1)} %bitcast.4), calls=%async_computation.4 | async-start | bytes 8388608
  40.4 15.7 %collective-permute-start.10 = (bf16[2,2,96,1024]{3,2,1,0:T(8,128)(2,1)S(1)}, bf16[2,2,96,1024]{3,2,1,0:T(8,128)(2,1)S(1)}, u32[]{:S(2)}, u32[]{:S(2)}) collective-permute-start(bf16[2,2,96,1024]{3,2,1,0:T(8,128)(2,1)S(1)} %add_to_send.9.refs_2_), channel_id=1, source_target_pairs={{1,2},{18,17},{5,6},{22,21},{9,10},{26,25},{13,14},{30,29}} | collective-permute-start | bytes 2359304 | tf_op jit(solution)/shard_map/ppermute | solution.py:340
  41.2 14.9 %collective-permute-start.11 = (bf16[2,2,96,1024]{3,2,1,0:T(8,128)(2,1)S(1)}, bf16[2,2,96,1024]{3,2,1,0:T(8,128)(2,1)S(1)}, u32[]{:S(2)}, u32[]{:S(2)}) collective-permute-start(bf16[2,2,96,1024]{3,2,1,0:T(8,128)(2,1)S(1)} %round_to_send.3.refs_3_), channel_id=1, source_target_pairs={{3,2},{16,17},{7,6},{20,21},{11,10},{24,25},{15,14},{28,29}} | collective-permute-start | bytes 2359304 | tf_op jit(solution)/shard_map/ppermute | solution.py:340
  42.1 14.7 %collective-permute-start.9 = (bf16[2,2,96,1024]{3,2,1,0:T(8,128)(2,1)S(1)}, bf16[2,2,96,1024]{3,2,1,0:T(8,128)(2,1)S(1)}, u32[]{:S(2)}, u32[]{:S(2)}) collective-permute-start(bf16[2,2,96,1024]{3,2,1,0:T(8,128)(2,1)S(1)} %add_to_send.10.refs_3_), channel_id=1, source_target_pairs={{2,3},{17,16},{6,7},{21,20},{10,11},{25,24},{14,15},{29,28}} | collective-permute-start | bytes 2359304 | tf_op jit(solution)/shard_map/ppermute | solution.py:340
  54.3 25.7 %slice-start.5 = ((s8[25165824]{0:T(1024)(128)(4,1)}), s8[4194304]{0:T(1024)(128)(4,1)S(1)}, s32[]{:S(2)}) async-start(s8[25165824]{0:T(1024)(128)(4,1)} %bitcast.4), calls=%async_computation.5 | async-start | bytes 8388608
  54.3 4.0 %collective-permute-start.14 = (bf16[2,2,96,1024]{3,2,1,0:T(8,128)(2,1)S(1)}, bf16[2,2,96,1024]{3,2,1,0:T(8,128)(2,1)S(1)}, u32[]{:S(2)}, u32[]{:S(2)}) collective-permute-start(bf16[2,2,96,1024]{3,2,1,0:T(8,128)(2,1)S(1)} %add_to_send.11.refs_3_), channel_id=1, source_target_pairs={{1,2},{18,17},{5,6},{22,21},{9,10},{26,25},{13,14},{30,29}} | collective-permute-start | bytes 2359304 | tf_op jit(solution)/shard_map/ppermute | solution.py:340
  55.2 3.9 %collective-permute-start.15 = (bf16[2,2,96,1024]{3,2,1,0:T(8,128)(2,1)S(1)}, bf16[2,2,96,1024]{3,2,1,0:T(8,128)(2,1)S(1)}, u32[]{:S(2)}, u32[]{:S(2)}) collective-permute-start(bf16[2,2,96,1024]{3,2,1,0:T(8,128)(2,1)S(1)} %round_to_send.2.refs_2_), channel_id=1, source_target_pairs={{3,2},{16,17},{7,6},{20,21},{11,10},{24,25},{15,14},{28,29}} | collective-permute-start | bytes 2359304 | tf_op jit(solution)/shard_map/ppermute | solution.py:340
  56.1 3.0 %collective-permute-start.13 = (bf16[2,96,1024]{2,1,0:T(8,128)(2,1)S(1)}, bf16[2,96,1024]{2,1,0:T(8,128)(2,1)S(1)}, u32[]{:S(2)}, u32[]{:S(2)}) collective-permute-start(bf16[2,96,1024]{2,1,0:T(8,128)(2,1)S(1)} %hidden_values.5.refs_3_), channel_id=1, source_target_pairs={{2,1},{17,18},{6,5},{21,22},{10,9},{25,26},{14,13},{29,30}} | collective-permute-start | bytes 1179656 | tf_op jit(solution)/shard_map/ppermute | solution.py:340
  56.8 4.3 %collective-permute-start.12 = (bf16[2,96,1024]{2,1,0:T(8,128)(2,1)S(1)}, bf16[2,96,1024]{2,1,0:T(8,128)(2,1)S(1)}, u32[]{:S(2)}, u32[]{:S(2)}) collective-permute-start(bf16[2,96,1024]{2,1,0:T(8,128)(2,1)S(1)} %hidden_values.6.refs_4_), channel_id=1, source_target_pairs={{3,2},{16,17},{7,6},{20,21},{11,10},{24,25},{15,14},{28,29}} | collective-permute-start | bytes 1179656 | tf_op jit(solution)/shard_map/ppermute | solution.py:340
  57.5 4.3 %collective-permute-start.8 = (bf16[2,96,1024]{2,1,0:T(8,128)(2,1)S(1)}, bf16[2,96,1024]{2,1,0:T(8,128)(2,1)S(1)}, u32[]{:S(2)}, u32[]{:S(2)}) collective-permute-start(bf16[2,96,1024]{2,1,0:T(8,128)(2,1)S(1)} %hidden_values.4.refs_4_), channel_id=1, source_target_pairs={{3,2},{16,17},{7,6},{20,21},{11,10},{24,25},{15,14},{28,29}} | collective-permute-start | bytes 1179656 | tf_op jit(solution)/shard_map/ppermute | solution.py:340
  58.4 4.2 %collective-permute-start.20 = (bf16[2,96,1024]{2,1,0:T(8,128)(2,1)S(1)}, bf16[2,96,1024]{2,1,0:T(8,128)(2,1)S(1)}, u32[]{:S(2)}, u32[]{:S(2)}) collective-permute-start(bf16[2,96,1024]{2,1,0:T(8,128)(2,1)S(1)} %hidden_values.5.refs_3_), channel_id=1, source_target_pairs={{2,3},{17,16},{6,7},{21,20},{10,11},{25,24},{14,15},{29,28}} | collective-permute-start | bytes 1179656 | tf_op jit(solution)/shard_map/ppermute | solution.py:340
  59.1 20.9 %collective-permute-start.19 = (bf16[2,96,1024]{2,1,0:T(8,128)(2,1)S(1)}, bf16[2,96,1024]{2,1,0:T(8,128)(2,1)S(1)}, u32[]{:S(2)}, u32[]{:S(2)}) collective-permute-start(bf16[2,96,1024]{2,1,0:T(8,128)(2,1)S(1)} %pass_on.6.refs_1_.refs_2_), channel_id=1, source_target_pairs={{1,0},{18,19},{5,4},{22,23},{9,8},{26,27},{13,12},{30,31}} | collective-permute-start | bytes 1179656 | tf_op jit(solution)/shard_map/ppermute | solution.py:340
  60.4 20.8 %collective-permute-start.18 = (bf16[2,96,1024]{2,1,0:T(8,128)(2,1)S(1)}, bf16[2,96,1024]{2,1,0:T(8,128)(2,1)S(1)}, u32[]{:S(2)}, u32[]{:S(2)}) collective-permute-start(bf16[2,96,1024]{2,1,0:T(8,128)(2,1)S(1)} %hidden_values.7.refs_1_.refs_3_), channel_id=1, source_target_pairs={{2,1},{17,18},{6,5},{21,22},{10,9},{25,26},{14,13},{29,30}} | collective-permute-start | bytes 1179656 | tf_op jit(solution)/shard_map/ppermute | solution.py:340
  61.2 21.4 %collective-permute-start.17 = (bf16[2,96,1024]{2,1,0:T(8,128)(2,1)S(1)}, bf16[2,96,1024]{2,1,0:T(8,128)(2,1)S(1)}, u32[]{:S(2)}, u32[]{:S(2)}) collective-permute-start(bf16[2,96,1024]{2,1,0:T(8,128)(2,1)S(1)} %pass_on.7.refs_1_.refs_3_), channel_id=1, source_target_pairs={{2,1},{17,18},{6,5},{21,22},{10,9},{25,26},{14,13},{29,30}} | collective-permute-start | bytes 1179656 | tf_op jit(solution)/shard_map/ppermute | solution.py:340
  61.9 22.0 %collective-permute-start.16 = (bf16[2,96,1024]{2,1,0:T(8,128)(2,1)S(1)}, bf16[2,96,1024]{2,1,0:T(8,128)(2,1)S(1)}, u32[]{:S(2)}, u32[]{:S(2)}) collective-permute-start(bf16[2,96,1024]{2,1,0:T(8,128)(2,1)S(1)} %pass_on.8.refs_6_.refs_3_), channel_id=1, source_target_pairs={{2,1},{17,18},{6,5},{21,22},{10,9},{25,26},{14,13},{29,30}} | collective-permute-start | bytes 1179656 | tf_op jit(solution)/shard_map/ppermute | solution.py:340
  62.6 22.6 %collective-permute-start.24 = (bf16[2,96,1024]{2,1,0:T(8,128)(2,1)S(1)}, bf16[2,96,1024]{2,1,0:T(8,128)(2,1)S(1)}, u32[]{:S(2)}, u32[]{:S(2)}) collective-permute-start(bf16[2,96,1024]{2,1,0:T(8,128)(2,1)S(1)} %hidden_values.7.refs_1_.refs_3_), channel_id=1, source_target_pairs={{2,3},{17,16},{6,7},{21,20},{10,11},{25,24},{14,15},{29,28}} | collective-permute-start | bytes 1179656 | tf_op jit(solution)/shard_map/ppermute | solution.py:340
  81.3 10.0 %collective-permute-start.23 = (bf16[2,96,1024]{2,1,0:T(8,128)(2,1)S(1)}, bf16[2,96,1024]{2,1,0:T(8,128)(2,1)S(1)}, u32[]{:S(2)}, u32[]{:S(2)}) collective-permute-start(bf16[2,96,1024]{2,1,0:T(8,128)(2,1)S(1)} %pass_on.9.refs_1_.refs_2_), channel_id=1, source_target_pairs={{1,0},{18,19},{5,4},{22,23},{9,8},{26,27},{13,12},{30,31}} | collective-permute-start | bytes 1179656 | tf_op jit(solution)/shard_map/ppermute | solution.py:340
  82.6 12.9 %collective-permute-start.22 = (bf16[2,96,1024]{2,1,0:T(8,128)(2,1)S(1)}, bf16[2,96,1024]{2,1,0:T(8,128)(2,1)S(1)}, u32[]{:S(2)}, u32[]{:S(2)}) collective-permute-start(bf16[2,96,1024]{2,1,0:T(8,128)(2,1)S(1)} %pass_on.10.refs_1_.refs_2_), channel_id=1, source_target_pairs={{1,0},{18,19},{5,4},{22,23},{9,8},{26,27},{13,12},{30,31}} | collective-permute-start | bytes 1179656 | tf_op jit(solution)/shard_map/ppermute | solution.py:340
  83.9 15.7 %collective-permute-start.21 = (bf16[2,96,1024]{2,1,0:T(8,128)(2,1)S(1)}, bf16[2,96,1024]{2,1,0:T(8,128)(2,1)S(1)}, u32[]{:S(2)}, u32[]{:S(2)}) collective-permute-start(bf16[2,96,1024]{2,1,0:T(8,128)(2,1)S(1)} %pass_on.11.refs_8_.refs_2_), channel_id=1, source_target_pairs={{1,0},{18,19},{5,4},{22,23},{9,8},{26,27},{13,12},{30,31}} | collective-permute-start | bytes 1179656 | tf_op jit(solution)/shard_map/ppermute | solution.py:340
  99.6 3.3 %copy-start.2 = (s32[128,2]{0,1:T(2,128)S(1)}, s32[128,2]{0,1:T(2,128)}, u32[]{:S(2)}) copy-start(s32[128,2]{0,1:T(2,128)} %param.7) | copy-start | bytes 3076
  99.6 3.3 %copy-start.3 = (f32[128,2]{0,1:T(2,128)S(1)}, f32[128,2]{0,1:T(2,128)}, u32[]{:S(2)}) copy-start(f32[128,2]{0,1:T(2,128)} %param.8) | copy-start | bytes 3076
  100.8 2.1 %collective-permute-start.25 = (f32[2,48,1536]{2,1,0:T(8,128)S(1)}, f32[2,48,1536]{2,1,0:T(8,128)S(1)}, u32[]{:S(2)}, u32[]{:S(2)}) collective-permute-start(f32[2,48,1536]{2,1,0:T(8,128)S(1)} %get-tuple-element.40), channel_id=1, source_target_pairs={{0,16},{16,0},{1,17},{17,1},{2,18},{18,2},{3,19},{19,3},{4,20},{20... | collective-permute-start | bytes 1769480 | tf_op jit(solution)/shard_map/ppermute | solution.py:399
  103.7 4.9 %collective-permute-start.28 = (bf16[32,1536]{1,0:T(8,128)(2,1)S(1)}, bf16[32,1536]{1,0:T(8,128)(2,1)S(1)}, u32[]{:S(2)}, u32[]{:S(2)}) collective-permute-start(bf16[32,1536]{1,0:T(8,128)(2,1)S(1)} %get-tuple-element.44), channel_id=1, source_target_pairs={{0,4},{4,0},{8,12},{12,8},{1,5},{5,1},{9,13},{13,9},{2,6},{6,2},{1... | collective-permute-start | bytes 294920 | tf_op jit(solution)/shard_map/ppermute | solution.py:405
  105.2 5.8 %collective-permute-start.27 = (bf16[32,1536]{1,0:T(8,128)(2,1)S(1)}, bf16[32,1536]{1,0:T(8,128)(2,1)S(1)}, u32[]{:S(2)}, u32[]{:S(2)}) collective-permute-start(bf16[32,1536]{1,0:T(8,128)(2,1)S(1)} %get-tuple-element.43), channel_id=1, source_target_pairs={{0,8},{4,12},{8,0},{12,4},{1,9},{5,13},{9,1},{13,5},{2,10},{6,14},... | collective-permute-start | bytes 294920 | tf_op jit(solution)/shard_map/ppermute | solution.py:405
  106.7 5.5 %collective-permute-start.26 = (bf16[32,1536]{1,0:T(8,128)(2,1)S(1)}, bf16[32,1536]{1,0:T(8,128)(2,1)S(1)}, u32[]{:S(2)}, u32[]{:S(2)}) collective-permute-start(bf16[32,1536]{1,0:T(8,128)(2,1)S(1)} %get-tuple-element.42), channel_id=1, source_target_pairs={{0,12},{4,8},{8,4},{12,0},{1,13},{5,9},{9,5},{13,1},{2,14},{6,10},... | collective-permute-start | bytes 294920 | tf_op jit(solution)/shard_map/ppermute | solution.py:405
  112.3 5.6 %collective-permute-start.29 = (bf16[32,1536]{1,0:T(8,128)(2,1)S(1)}, bf16[32,1536]{1,0:T(8,128)(2,1)S(1)}, u32[]{:S(2)}, u32[]{:S(2)}) collective-permute-start(bf16[32,1536]{1,0:T(8,128)(2,1)S(1)} %add_convert_fusion.refs_1_), channel_id=1, source_target_pairs={{0,4},{4,0},{8,12},{12,8},{1,5},{5,1},{9,13},{13,9},{2,6},{6,2},{1... | collective-permute-start | bytes 294920 | tf_op jit(solution)/shard_map/ppermute | solution.py:409
  113.2 5.1 %collective-permute-start.30 = (bf16[32,1536]{1,0:T(8,128)(2,1)S(1)}, bf16[32,1536]{1,0:T(8,128)(2,1)S(1)}, u32[]{:S(2)}, u32[]{:S(2)}) collective-permute-start(bf16[32,1536]{1,0:T(8,128)(2,1)S(1)} %add_convert_fusion.refs_1_), channel_id=1, source_target_pairs={{0,8},{4,12},{8,0},{12,4},{1,9},{5,13},{9,1},{13,5},{2,10},{6,14},... | collective-permute-start | bytes 294920 | tf_op jit(solution)/shard_map/ppermute | solution.py:409
  114.1 5.5 %collective-permute-start.31 = (bf16[32,1536]{1,0:T(8,128)(2,1)S(1)}, bf16[32,1536]{1,0:T(8,128)(2,1)S(1)}, u32[]{:S(2)}, u32[]{:S(2)}) collective-permute-start(bf16[32,1536]{1,0:T(8,128)(2,1)S(1)} %add_convert_fusion.refs_1_), channel_id=1, source_target_pairs={{0,12},{4,8},{8,4},{12,0},{1,13},{5,9},{9,5},{13,1},{2,14},{6,10},... | collective-permute-start | bytes 294920 | tf_op jit(solution)/shard_map/ppermute | solution.py:409
